TPU v7x, 32 devices: a whole 2x2x4 slice. The times are simulated.
32 devices in a mesh: mod: 8 (over z, y), rep: 4 (over x, core).
Axes of the slice: x: 2, y: 2, z: 4, core: 2. Of those that a mesh axis runs over, the one named last changes fastest.
Arguments:
- raw_rows: bfloat16 [64, 384, 768], P('mod', 'rep'), may hold values from -6 to 6
- recv_counts: int32 [8, 32], P('mod', 'rep'), may hold values from 0 to 96, as said below
- slot_groups: int32 [8, 3072], P('mod', 'rep'), may hold values from 0 to 4, as said below
- read_counts: int32 [8, 4], P('mod', 'rep'), may hold values from 1 to 4, as said below
- patch_convolution_weight: bfloat16 [768, 768], replicated, may hold values from -0.21875 to 0.21875
- patch_stem_bias_vector: float32 [768], replicated, may hold values from -3 to 3
- language_projection_weight: bfloat16 [768, 768], replicated, may hold values from -0.21875 to 0.21875
- language_bias_vector: float32 [768], replicated, may hold values from -3 to 3
- readout_table: float32 [8, 768], replicated, may hold values from -6 to 6
- attn_gain: float32 [768], replicated, may hold values from 0.5 to 1.5
- attn_bias: float32 [768], replicated, may hold values from -2 to 2
- qkv_weight: bfloat16 [768, 2304], P('mod'), may hold values from -0.21875 to 0.21875
- out_weight: bfloat16 [768, 768], P('mod'), may hold values from -0.875 to 0.875
- mlp_gain: float32 [768], replicated, may hold values from 0.5 to 1.5
- mlp_bias: float32 [768], replicated, may hold values from -2 to 2
- up_weight: bfloat16 [768, 3072], P('mod'), may hold values from -0.21875 to 0.21875
- up_bias: float32 [3072], replicated, may hold values from -2 to 2
- down_weight: bfloat16 [3072, 768], P('mod'), may hold values from -0.109375 to 0.109375
- down_bias: float32 [768], replicated, may hold values from -2 to 2
- out_cotangent: bfloat16 [8, 3104, 768], P('mod', 'rep'), may hold values from -6 to 6
Outputs:
- layer_out: bfloat16 [8, 3104, 768], P('mod', 'rep')
- raw_grad: float32 [64, 384, 768], P('mod', 'rep')
- patch_weight_grad: float32 [768, 768], replicated
- patch_bias_grad: float32 [768], replicated
- lang_weight_grad: float32 [768, 768], replicated
- lang_bias_grad: float32 [768], replicated
- readout_grad: float32 [8, 768], replicated
- attn_gain_grad: float32 [768], replicated
- attn_bias_grad: float32 [768], replicated
- qkv_weight_grad: float32 [768, 2304], P('mod')
- out_weight_grad: float32 [768, 768], P('mod')
- mlp_gain_grad: float32 [768], replicated
- mlp_bias_grad: float32 [768], replicated
- up_weight_grad: float32 [768, 3072], P('mod')
- up_bias_grad: float32 [3072], replicated
- down_weight_grad: float32 [3072, 768], P('mod')
- down_bias_grad: float32 [768], replicated
Inputs may be any that keep to these rules, and one draw needn't show every extreme that they name: `recv_counts`: every sequence receives a full block of 96 live rows from device 0 of mod. `slot_groups`: even values: 0 for language tokens, 2 (t + 1) for observation tokens of time step t. `read_counts`: some sequence has 4.
All inputs are finite; a program needn't handle non-finite values.
Results may differ from a plain program's by a relative error of at most 0.017.
Values may be sent and summed in bfloat16 or wider, within the bound.
No kernel may reach another device: no remote copies, remote signals or barrier semaphores. Data moves between devices by JAX's collectives and lax.ppermute only.
A program may use at most 192 MiB of HBM per device.

v0:
```python
import jax
import jax.numpy as jnp
from jax import lax
from jax.sharding import PartitionSpec as P

D = 768
HEADS = 12
HD = 64
RPS = 4
RD = 8


layer_eps = 1e-06


def layer_norm(stream, norm_gain, norm_bias):
    row_mean = jnp.mean(stream, axis=-1, keepdims=True)
    centred = stream - row_mean
    row_var = jnp.mean(centred * centred, axis=-1, keepdims=True)
    return centred * lax.rsqrt(row_var + layer_eps) * norm_gain + norm_bias


def norm_backward(stream, norm_gain, norm_bias, upstream):
    _, pullback = jax.vjp(layer_norm, stream, norm_gain, norm_bias)
    return pullback(upstream)


def outer_sum(left, right):
    return lax.dot_general(
        left, right, (((0,), (0,)), ((), ())), preferred_element_type=jnp.float32
    )


def times_transposed(left, right):
    return lax.dot_general(
        left, right, (((1,), (1,)), ((), ())), preferred_element_type=jnp.float32
    )


def per_device(
    raw_rows,
    recv_counts,
    slot_groups,
    read_counts,
    patch_convolution_weight,
    patch_stem_bias_vector,
    language_projection_weight,
    language_bias_vector,
    readout_table,
    attn_gain,
    attn_bias,
    qkv_weight,
    out_weight,
    mlp_gain,
    mlp_bias,
    up_weight,
    up_bias,
    down_weight,
    down_bias,
    out_cotangent,
):
    groups_n = lax.axis_size("mod")
    device_pos = lax.axis_index("mod")
    is_image = device_pos < 3 * groups_n // 4
    block_rows = raw_rows.shape[1]
    capacity = groups_n * block_rows
    seq_len = capacity + RD
    scale = HD ** (-0.5)
    stem_weight = jnp.where(is_image, patch_convolution_weight, language_projection_weight)
    stem_bias = jnp.where(is_image, patch_stem_bias_vector, language_bias_vector)
    raw_flat = raw_rows.reshape(capacity, raw_rows.shape[2])
    embedded = (
        jnp.dot(raw_flat, stem_weight, preferred_element_type=jnp.float32) + stem_bias
    ).astype(jnp.bfloat16)
    received = lax.all_to_all(
        embedded.reshape(groups_n, block_rows, D), "mod", split_axis=0, concat_axis=0, tiled=True
    )
    gathered = (
        lax.all_gather(qkv_weight, "mod", axis=0, tiled=True),
        lax.all_gather(out_weight, "mod", axis=0, tiled=True),
        lax.all_gather(up_weight, "mod", axis=0, tiled=True),
        lax.all_gather(down_weight, "mod", axis=0, tiled=True),
    )
    full_qkv, full_out, full_up, full_down = gathered
    slot_index = jnp.arange(capacity)
    live_recv = slot_index % block_rows < jnp.repeat(recv_counts[0], block_rows)
    readout_slot = jnp.arange(RD)
    live_read = readout_slot % RPS < read_counts[0, 0]
    live_slot = jnp.concatenate([live_recv, live_read])
    read_group = 2 * (readout_slot // RPS + 1) + 1
    group_id = jnp.concatenate([slot_groups[0], read_group])
    key_group = group_id[None, :]
    query_group = group_id[:, None]
    visible = (
        live_slot[None, :]
        & (key_group <= query_group)
        & ((key_group % 2 == 0) | (key_group == query_group))
    )
    visible = visible | jnp.eye(seq_len, dtype=jnp.bool_)
    live_float = live_slot.astype(jnp.float32)[:, None]
    stream = jnp.concatenate(
        [received.reshape(capacity, D).astype(jnp.float32), readout_table], axis=0
    )
    normed = layer_norm(stream, attn_gain, attn_bias).astype(jnp.bfloat16)
    qkv_rows = jnp.dot(normed, full_qkv, preferred_element_type=jnp.float32).astype(jnp.bfloat16)

    def head_scores(head_index):
        query_rows = lax.dynamic_slice_in_dim(qkv_rows, head_index * HD, HD, 1)
        key_rows = lax.dynamic_slice_in_dim(qkv_rows, D + head_index * HD, HD, 1)
        value_rows = lax.dynamic_slice_in_dim(qkv_rows, 2 * D + head_index * HD, HD, 1)
        scores = times_transposed(query_rows, key_rows) * scale
        return (query_rows, key_rows, value_rows, jnp.where(visible, scores, -1e30))

    def forward_head(head_index):
        _, _, value_rows, scores = head_scores(head_index)
        row_peak = jnp.max(scores, axis=1, keepdims=True)
        exponent = jnp.exp(scores - row_peak)
        row_total = jnp.sum(exponent, axis=1, keepdims=True)
        attn_probs = (exponent / row_total).astype(jnp.bfloat16)
        head_out = jnp.dot(attn_probs, value_rows, preferred_element_type=jnp.float32)
        return (head_out, row_peak[:, 0] + jnp.log(row_total[:, 0]))

    head_outs, head_lse = lax.map(forward_head, jnp.arange(HEADS))
    mixed_rows = head_outs.transpose(1, 0, 2).reshape(seq_len, D).astype(jnp.bfloat16)
    after_attn = stream + jnp.dot(mixed_rows, full_out, preferred_element_type=jnp.float32)
    normed2 = layer_norm(after_attn, mlp_gain, mlp_bias).astype(jnp.bfloat16)
    hidden_pre = jnp.dot(normed2, full_up, preferred_element_type=jnp.float32) + up_bias
    activated = jax.nn.gelu(hidden_pre).astype(jnp.bfloat16)
    branch = jnp.dot(activated, full_down, preferred_element_type=jnp.float32) + down_bias
    layer_out = ((after_attn + branch) * live_float).astype(jnp.bfloat16)[None]
    back_qkv, back_out, back_up, back_down = gathered
    upstream = out_cotangent[0].astype(jnp.float32) * live_float
    branch_grad = upstream.astype(jnp.bfloat16)
    down_weight_grad = outer_sum(activated, branch_grad)
    down_bias_grad = jnp.sum(branch_grad.astype(jnp.float32), axis=0)
    activ_grad = times_transposed(branch_grad, back_down)
    _, gelu_back = jax.vjp(jax.nn.gelu, hidden_pre)
    hidden_grad = gelu_back(activ_grad)[0].astype(jnp.bfloat16)
    up_weight_grad = outer_sum(normed2, hidden_grad)
    up_bias_grad = jnp.sum(hidden_grad.astype(jnp.float32), axis=0)
    normed2_grad = times_transposed(hidden_grad, back_up)
    norm2_input_grad, mlp_gain_grad, mlp_bias_grad = norm_backward(
        after_attn, mlp_gain, mlp_bias, normed2_grad
    )
    after_grad = upstream + norm2_input_grad
    attn_grad = after_grad.astype(jnp.bfloat16)
    out_weight_grad = outer_sum(mixed_rows, attn_grad)
    mixed_grad = times_transposed(attn_grad, back_out).astype(jnp.bfloat16)

    def backward_head(inputs):
        head_index, lse_row = inputs
        query_rows, key_rows, value_rows, scores = head_scores(head_index)
        probs_full = jnp.exp(scores - lse_row[:, None])
        grad_rows = lax.dynamic_slice_in_dim(mixed_grad, head_index * HD, HD, 1)
        prob_grad = times_transposed(grad_rows, value_rows)
        row_delta = jnp.sum(probs_full * prob_grad, axis=1, keepdims=True)
        score_grad = (probs_full * (prob_grad - row_delta)).astype(jnp.bfloat16)
        query_grad = jnp.dot(score_grad, key_rows, preferred_element_type=jnp.float32) * scale
        key_grad = outer_sum(score_grad, query_rows) * scale
        value_grad = outer_sum(probs_full.astype(jnp.bfloat16), grad_rows)
        return (query_grad, key_grad, value_grad)

    head_grads = lax.map(backward_head, (jnp.arange(HEADS), head_lse))
    qkv_grad = jnp.concatenate(
        [head_part.transpose(1, 0, 2).reshape(seq_len, D) for head_part in head_grads], axis=1
    ).astype(jnp.bfloat16)
    qkv_weight_grad = outer_sum(normed, qkv_grad)
    normed_grad = times_transposed(qkv_grad, back_qkv)
    norm1_input_grad, attn_gain_grad, attn_bias_grad = norm_backward(
        stream, attn_gain, attn_bias, normed_grad
    )
    stream_grad = after_grad + norm1_input_grad
    readout_grad = stream_grad[capacity:]
    embedded_grad = stream_grad[:capacity].astype(jnp.bfloat16).reshape(groups_n, block_rows, D)
    returned = lax.all_to_all(embedded_grad, "mod", split_axis=0, concat_axis=0, tiled=True)
    flat_back = returned.reshape(capacity, D)
    stem_weight_grad = outer_sum(raw_flat, flat_back)
    stem_bias_grad = jnp.sum(flat_back.astype(jnp.float32), axis=0)
    raw_grad = times_transposed(flat_back, stem_weight).reshape(raw_rows.shape)
    patch_weight_grad = jnp.where(is_image, stem_weight_grad, 0.0)
    lang_weight_grad = jnp.where(is_image, 0.0, stem_weight_grad)
    patch_bias_grad = jnp.where(is_image, stem_bias_grad, 0.0)
    lang_bias_grad = jnp.where(is_image, 0.0, stem_bias_grad)
    shards = (
        lax.psum_scatter(
            qkv_weight_grad.astype(jnp.bfloat16), "mod", scatter_dimension=0, tiled=True
        ).astype(jnp.float32),
        lax.psum_scatter(
            out_weight_grad.astype(jnp.bfloat16), "mod", scatter_dimension=0, tiled=True
        ).astype(jnp.float32),
        lax.psum_scatter(
            up_weight_grad.astype(jnp.bfloat16), "mod", scatter_dimension=0, tiled=True
        ).astype(jnp.float32),
        lax.psum_scatter(
            down_weight_grad.astype(jnp.bfloat16), "mod", scatter_dimension=0, tiled=True
        ).astype(jnp.float32),
    )
    shards = (
        lax.psum(shards[0].astype(jnp.bfloat16), "rep").astype(jnp.float32),
        lax.psum(shards[1].astype(jnp.bfloat16), "rep").astype(jnp.float32),
        lax.psum(shards[2].astype(jnp.bfloat16), "rep").astype(jnp.float32),
        lax.psum(shards[3].astype(jnp.bfloat16), "rep").astype(jnp.float32),
    )
    qkv_shard, out_shard, up_shard, down_shard = shards
    summed = lax.psum(
        (
            patch_weight_grad,
            patch_bias_grad,
            lang_weight_grad,
            lang_bias_grad,
            readout_grad,
            attn_gain_grad,
            attn_bias_grad,
            mlp_gain_grad,
            mlp_bias_grad,
            up_bias_grad,
            down_bias_grad,
        ),
        ("mod", "rep"),
    )
    (
        patch_weight_sum,
        patch_bias_sum,
        lang_weight_sum,
        lang_bias_sum,
        readout_sum,
        attn_gain_sum,
        attn_bias_sum,
        mlp_gain_sum,
        mlp_bias_sum,
        up_bias_sum,
        down_bias_sum,
    ) = summed
    return (
        layer_out,
        raw_grad,
        patch_weight_sum,
        patch_bias_sum,
        lang_weight_sum,
        lang_bias_sum,
        readout_sum,
        attn_gain_sum,
        attn_bias_sum,
        qkv_shard,
        out_shard,
        mlp_gain_sum,
        mlp_bias_sum,
        up_shard,
        up_bias_sum,
        down_shard,
        down_bias_sum,
    )


def solution(mesh):
    return jax.shard_map(
        per_device,
        mesh=mesh,
        in_specs=(
            P("mod", "rep", None),
            P("mod", "rep"),
            P("mod", "rep"),
            P("mod", "rep"),
            P(),
            P(),
            P(),
            P(),
            P(),
            P(),
            P(),
            P("mod", None),
            P("mod", None),
            P(),
            P(),
            P("mod", None),
            P(),
            P("mod", None),
            P(),
            P("mod", "rep", None),
        ),
        out_specs=(
            P("mod", "rep", None),
            P("mod", "rep", None),
            P(),
            P(),
            P(),
            P(),
            P(),
            P(),
            P(),
            P("mod", None),
            P("mod", None),
            P(),
            P(),
            P("mod", None),
            P(),
            P("mod", None),
            P(),
        ),
        check_vma=False,
    )
```

profile of v0, /device:TPU:0, one launch (start us, length us, event | category | flops | bytes accessed | tf_op | source)
XLA Modules:
  0.0 1006.9 jit_solution(16712000536364582664)
XLA Ops:
  10.1 3.4 add_convert_fusion.2
  13.5 7.4 all-to-all-start
  23.6 40.2 %all-to-all-done = bf16[8,96,768]{2,1,0:T(8,128)(2,1)} async-done(((bf16[8,96,768]{2,1,0:T(8,128)(2,1)}), bf16[8,96,768]{2,1,0:T(8,128)(2,1)}, u32[]{:S(2)}, u32[]{:S(2)}) %all-to-all-start) | async-done | bytes 1179680 | tf_op jit(solution)/shard_map/all_to_all | solution.py:75
  67.2 30.0 %all-gather.5.cloned.1.call-done = bf16[768,2304]{1,0:T(8,128)(2,1)} async-done(((bf16[96,2304]{1,0:T(8,128)(2,1)}), bf16[768,2304]{1,0:T(8,128)(2,1)}) %all-gather.5.cloned.1.call-update) | async-done | bytes 3538960 | tf_op jit(solution)/shard_map/all_gather | solution.py:79
  97.2 7.0 convolution_convert_fusion
  106.1 100.4 %while.32 = (s32[]{:T(128)}, bf16[12,776,64]{1,2,0:T(8,128)(2,1)}, f32[12,776]{1,0:T(8,128)}, s32[12]{0:T(128)}, bf16[776,2304]{1,0:T(8,128)(2,1)}, /*index=5*/p...) while((s32[]{:T(128)}, bf16[12,776,64]{1,2,0:T(8,128)(2,1)}, ...), condition=%wide.region_5.6_spmd.clone, body=%wide.region_2.5_spmd.clone.sunk | while | flops 163188928 | bytes 8099271 | solution.py:123
  108.3 2.4 fusion.119
  111.1 2.2 fusion.121
  116.6 2.4 fusion.119
  124.9 2.4 fusion.119
  127.7 2.2 fusion.121
  133.3 2.4 fusion.119
  136.1 2.2 fusion.121
  141.6 2.4 fusion.119
  144.4 2.2 fusion.121
  149.9 2.4 fusion.119
  152.7 2.2 fusion.121
  158.3 2.4 fusion.119
  161.1 2.2 fusion.121
  166.6 2.4 fusion.119
  169.4 2.2 fusion.121
  174.9 2.4 fusion.119
  177.8 2.2 fusion.121
  183.3 2.4 fusion.119
  186.1 2.2 fusion.121
  191.6 2.4 fusion.119
  194.5 2.2 fusion.121
  200.0 2.4 fusion.119
  206.4 3.0 fusion.81
  211.9 8.0 all-gather.9.cloned.1.call-done
  219.9 10.9 %fusion.76 = f32[776,3072]{1,0:T(8,128)} fusion(bf16[768,3072]{1,0:T(8,128)(2,1)} %all-gather.9.cloned.1.call-done, f32[776,768]{1,0:T(8,128)} %copy-done.3, f32[768]{0:T(1024)} %param.38, f32[768]{0:T(1024)} %param.37, f32[776]{0:T(1024)} %fusion.63, f32[776]{0:T(1024)S(1)} %broadcast_multiply_fusion), kind=kOutput, calls=%fused_computation.135 | convolution fusion | flops 3664607232 | bytes 16650304 | tf_op jit(solution)/shard_map/dot_general | solution.py:127
  230.8 69.3 %all-gather.11.cloned.1.call-done = bf16[3072,768]{1,0:T(8,128)(2,1)} async-done(((bf16[384,768]{1,0:T(8,128)(2,1)}), bf16[3072,768]{1,0:T(8,128)(2,1)}) %all-gather.11.cloned.1.call-update) | async-done | bytes 4718608 | tf_op jit(solution)/shard_map/all_gather | solution.py:82
  300.1 14.2 %convert_reduce_fusion = (f32[3072]{0:T(1024)}, bf16[776,3072]{1,0:T(8,128)(2,1)S(1)}) fusion(f32[776,3072]{1,0:T(8,128)} %fusion.76, f32[3072]{0:T(1024)} %param.40, bf16[3072,768]{1,0:T(8,128)(2,1)} %all-gather.11.cloned.1.call-done, bf16[1,776,768]{2,1,0:T(8,128)(2,1)} %param.43, f32[776]{0:T(1024)S(1)} %get-tuple-element.345), kind=kOutput, calls=%fused_computation.55 | convolution fusion | flops 3718241280 | bytes 20241440 | tf_op jit(solution)/shard_map/dot_general | solution.py:35
  314.3 4.8 multiply_reduce_fusion.1
  322.5 2.4 convolution_convert_fusion.5
  325.0 3.8 convolution_convert_fusion.4
  333.1 170.0 %while.33 = (s32[]{:T(128)}, bf16[12,776,64]{1,2,0:T(8,128)(2,1)}, bf16[12,776,64]{1,2,0:T(8,128)(2,1)}, bf16[12,776,64]{1,2,0:T(8,128)(2,1)}, s32[12]{0:T(128)}...) while((s32[]{:T(128)}, bf16[12,776,64]{1,2,0:T(8,128)(2,1)}, ...), condition=%wide.region_12.13_spmd.clone, body=%wide.region_10.12_spmd.clone.sunk | while | flops 395126016 | bytes 20562328 | solution.py:163
  337.7 2.8 multiply_reduce_fusion.8
  351.9 2.8 multiply_reduce_fusion.8
  366.1 2.8 multiply_reduce_fusion.8
  380.2 2.8 multiply_reduce_fusion.8
  394.4 2.8 multiply_reduce_fusion.8
  408.5 2.8 multiply_reduce_fusion.8
  422.7 2.8 multiply_reduce_fusion.8
  436.8 2.8 multiply_reduce_fusion.8
  451.0 2.8 multiply_reduce_fusion.8
  465.1 2.8 multiply_reduce_fusion.8
  479.2 2.8 multiply_reduce_fusion.8
  493.4 2.8 multiply_reduce_fusion.8
  503.0 8.4 convolution_convert_fusion.3
  511.5 9.9 convolution_convert_fusion.2
  521.5 12.3 %convolution_convert_fusion.1 = bf16[3072,768]{1,0:T(8,128)(2,1)} fusion(bf16[1,776,768]{2,1,0:T(8,128)(2,1)} %param.43, f32[776]{0:T(1024)S(1)} %get-tuple-element.345, f32[776,3072]{1,0:T(8,128)} %fusion.76, f32[3072]{0:T(1024)} %param.40), kind=kOutput, calls=%fused_computation.58 | convolution fusion | flops 3689613312 | bytes 15461408 | tf_op jit(solution)/shard_map/dot_general | solution.py:29
  533.9 8.0 multiply_reduce_fusion.2
  544.6 31.6 %all_to_all.10 = bf16[8,96,768]{2,1,0:T(8,128)(2,1)S(1)} all-to-all(bf16[8,96,768]{2,1,0:T(8,128)(2,1)S(1)} %bitcast.107), channel_id=1, replica_groups=mesh['mod'=8,'rep'=4] {'mod'}, dimensions={0} | all-to-all | bytes 2359296 | tf_op jit(solution)/shard_map/all_to_all | solution.py:175
  576.2 3.3 fusion.50
  579.9 15.6 %reduce-scatter.5.cloned.1.call-done = bf16[96,2304]{1,0:T(8,128)(2,1)} async-done(((bf16[768,2304]{1,0:T(8,128)(2,1)}), bf16[96,2304]{1,0:T(8,128)(2,1)}) %reduce-scatter.5.cloned.1.call-update) | async-done | bytes 442384 | tf_op jit(solution)/shard_map/reduce_scatter | solution.py:185
  595.5 98.6 %reduce-scatter.9.cloned.1.call-done = bf16[96,3072]{1,0:T(8,128)(2,1)} async-done(((bf16[768,3072]{1,0:T(8,128)(2,1)}), bf16[96,3072]{1,0:T(8,128)(2,1)}) %reduce-scatter.9.cloned.1.call-update) | async-done | bytes 589840 | tf_op jit(solution)/shard_map/reduce_scatter | solution.py:191
  694.1 98.9 %reduce-scatter.11.cloned.1.call-done = bf16[384,768]{1,0:T(8,128)(2,1)} async-done(((bf16[3072,768]{1,0:T(8,128)(2,1)}), bf16[384,768]{1,0:T(8,128)(2,1)}) %reduce-scatter.11.cloned.1.call-update) | async-done | bytes 589840 | tf_op jit(solution)/shard_map/reduce_scatter | solution.py:194
  793.1 12.8 %fusion.52 = bf16[1,776,768]{2,1,0:T(8,128)(2,1)} fusion(f32[776,768]{1,0:T(8,128)} %copy-done.3, bf16[3072,768]{1,0:T(8,128)(2,1)} %all-gather.11.cloned.1.call-done, f32[776]{0:T(1024)S(1)} %get-tuple-element.345, f32[768]{0:T(1024)S(1)} %copy-done.35, f32[776,3072]{1,0:T(8,128)} %fusion.76, f32[3072]{0:T(1024)S(1)} %copy-done.34), kind=kOutput, calls=%fused_computation.90 | convolution fusion | flops 3687849984 | bytes 17848352 | tf_op jit(solution)/shard_map/dot_general | solution.py:129
  806.2 42.2 %all-reduce = (f32[768]{0:T(1024)}, f32[768]{0:T(1024)}, f32[8,768]{1,0:T(8,128)}, f32[768]{0:T(1024)}, f32[768]{0:T(1024)}, /*index=5*/f32[768]{0:T(1024)}, f32[768]{0:T(1024)}, f32[3072]{0:T(1024)}, f32[768]{0:T(1024)}) all-reduce(f32[768]{0:T(1024)S(1)} %get-tuple-element.358, ...), channel_id=1, replica_groups=mesh['mod'=8,'rep'=4] {'mod','rep'}, use_global_device_ids=true, to_apply=%region_17.18 | all-reduce | flops 14592 | bytes 116736 | tf_op jit(solution)/shard_map/psum | solution.py:205
  848.4 3.8 fusion.54
  852.2 92.5 %all-reduce.6.cloned.1.call-done = (f32[768,768]{0,1:T(8,128)}, f32[768,768]{0,1:T(8,128)}) async-done(((f32[768,768]{0,1:T(8,128)}, f32[768,768]{0,1:T(8,128)}), (f32[768,768]{0,1:T(8,128)}, f32[768,768]{0,1:T(8,128)})) %all-reduce.6.cloned.1.call-update) | async-done | bytes 4718608 | tf_op jit(solution)/shard_map/psum | solution.py:205
  944.7 3.2 copy.37
  949.9 42.9 %all-reduce.8.cloned.1.call-done = (bf16[96,2304]{1,0:T(8,128)(2,1)}, bf16[96,768]{1,0:T(8,128)(2,1)}, bf16[96,3072]{1,0:T(8,128)(2,1)}, bf16[384,768]{1,0:T(8,128)(2,1)}) async-done(((bf16[96,2304]{1,0:T(8,128)(2,1)}, bf16[96,768]{1,0:T(8,128)(2,1)}, bf16[96,3072]{1,0:T(8,128)(2,1)}, bf16[384,768]{1,0:T(8,128)(2,1)}), (bf16[96,2304]{1,0:T(8,128)(2,1)}, bf16[96,768]{1,0:T(8,128)(2,1)}, ...) | async-done | bytes 1769488 | tf_op jit(solution)/shard_map/psum | solution.py:199
  (350 shorter events, 201.7 us)
Async XLA Ops:
  7.2 2.9 copy-start
  7.2 90.0 %all-gather.5.cloned.1.call-start = ((), (), s32[]{:S(2)}) async-start(), calls=%async_computation.6 | async-start | bytes 3981312 | tf_op jit(solution)/shard_map/all_gather | solution.py:79
  7.9 198.5 %all-gather.7.cloned.1.call-start = ((), (), s32[]{:S(2)}) async-start(), calls=%async_computation.7 | async-start | bytes 1327104 | tf_op jit(solution)/shard_map/all_gather | solution.py:80
  8.7 211.2 %all-gather.9.cloned.1.call-start = ((), (), s32[]{:S(2)}) async-start(), calls=%async_computation.8 | async-start | bytes 5308416 | tf_op jit(solution)/shard_map/all_gather | solution.py:81
  13.5 8.7 copy-start.32
  13.5 8.9 copy-start.29
  13.5 50.3 %all-to-all-start = ((bf16[8,96,768]{2,1,0:T(8,128)(2,1)}), bf16[8,96,768]{2,1,0:T(8,128)(2,1)}, u32[]{:S(2)}, u32[]{:S(2)}) async-start(bf16[8,96,768]{2,1,0:T(8,128)(2,1)} %bitcast.2), calls=%async_computation | async-start | bytes 2359296 | tf_op jit(solution)/shard_map/all_to_all | solution.py:75
  20.9 279.1 %all-gather.11.cloned.1.call-start = ((), (), s32[]{:S(2)}) async-start(), calls=%async_computation.9 | async-start | bytes 5308416 | tf_op jit(solution)/shard_map/all_gather | solution.py:82
  21.5 558.4 %reduce-scatter.7.cloned.1.call-start = ((), (), s32[]{:S(2)}) async-start(), calls=%async_computation.11 | async-start | bytes 1327104 | tf_op jit(solution)/shard_map/reduce_scatter | solution.py:188
  67.2 37.0 %copy-start.16 = (f32[776]{0:T(1024)}, f32[776]{0:T(1024)S(1)}, u32[]{:S(2)}) copy-start(f32[776]{0:T(1024)S(1)} %fusion.62) | copy-start | bytes 9316
  67.2 38.8 %copy-start.27 = (s32[776]{0:T(1024)S(1)}, s32[776]{0:T(1024)}, u32[]{:S(2)}) copy-start(s32[776]{0:T(1024)} %get-tuple-element.546) | copy-start | bytes 9316
  300.0 14.2 %copy-start.4 = (f32[776,768]{1,0:T(8,128)S(1)}, f32[776,768]{1,0:T(8,128)}, u32[]{:S(2)}) copy-start(f32[776,768]{1,0:T(8,128)} %copy-done.3) | copy-start | bytes 7151620
  300.1 14.2 %copy-start.18 = (f32[776]{0:T(1024)S(1)}, f32[776]{0:T(1024)}, u32[]{:S(2)}) copy-start(f32[776]{0:T(1024)} %fusion.63) | copy-start | bytes 9316
  300.1 14.2 %copy-start.21 = (f32[768]{0:T(1024)S(1)}, f32[768]{0:T(1024)}, u32[]{:S(2)}) copy-start(f32[768]{0:T(1024)} %param.37) | copy-start | bytes 9220
  300.1 14.2 %copy-start.33 = (bf16[768,3072]{1,0:T(8,128)(2,1)S(1)}, bf16[768,3072]{1,0:T(8,128)(2,1)}, u32[]{:S(2)}) copy-start(bf16[768,3072]{1,0:T(8,128)(2,1)} %all-gather.9.cloned.1.call-done) | copy-start | bytes 14155780
  314.3 4.8 copy-start.36
  324.9 270.6 %reduce-scatter.5.cloned.1.call-start = ((), (), s32[]{:S(2)}) async-start(), calls=%async_computation.10 | async-start | bytes 3981312 | tf_op jit(solution)/shard_map/reduce_scatter | solution.py:185
  335.2 2.6 copy-start.28
  335.2 2.6 copy-start.30
  335.2 2.6 copy-start.31
  349.3 2.6 copy-start.28
  349.3 2.6 copy-start.30
  349.3 2.6 copy-start.31
  363.5 2.6 copy-start.28
  363.5 2.6 copy-start.30
  377.7 2.6 copy-start.28
  377.7 2.6 copy-start.30
  377.7 2.6 copy-start.31
  391.8 2.6 copy-start.28
  391.8 2.6 copy-start.30
  406.0 2.6 copy-start.28
  406.0 2.6 copy-start.30
  420.1 2.6 copy-start.28
  420.1 2.6 copy-start.30
  434.2 2.6 copy-start.28
  434.2 2.6 copy-start.30
  448.4 2.6 copy-start.28
  448.4 2.6 copy-start.30
  462.5 2.6 copy-start.28
  462.5 2.6 copy-start.30
  476.7 2.6 copy-start.28
  476.7 2.6 copy-start.30
  490.8 2.6 copy-start.28
  490.8 2.6 copy-start.30
  511.4 182.6 %reduce-scatter.9.cloned.1.call-start = ((), (), s32[]{:S(2)}) async-start(), calls=%async_computation.12 | async-start | bytes 5308416 | tf_op jit(solution)/shard_map/reduce_scatter | solution.py:191
  521.4 271.5 %reduce-scatter.11.cloned.1.call-start = ((), (), s32[]{:S(2)}) async-start(), calls=%async_computation.13 | async-start | bytes 5308416 | tf_op jit(solution)/shard_map/reduce_scatter | solution.py:194
  533.8 8.1 copy-start.15
  533.8 410.9 %all-reduce.6.cloned.1.call-start = ((), (), s32[]{:S(2)}) async-start(), calls=%async_computation.14 | async-start | bytes 9437184 | tf_op jit(solution)/shard_map/psum | solution.py:205
  533.9 8.0 copy-start.13
  533.9 8.0 copy-start.17
  533.9 8.0 copy-start.22
  544.5 35.0 %copy-start.5 = (f32[776,768]{1,0:T(8,128)}, f32[776,768]{1,0:T(8,128)S(1)}, u32[]{:S(2)}) copy-start(f32[776,768]{1,0:T(8,128)S(1)} %add_add_fusion.2) | copy-start | bytes 7151620
  579.6 213.4 %copy-start.34 = (f32[3072]{0:T(1024)S(1)}, f32[3072]{0:T(1024)}, u32[]{:S(2)}) copy-start(f32[3072]{0:T(1024)} %param.40) | copy-start | bytes 36868
  579.6 213.4 %copy-start.35 = (f32[768]{0:T(1024)S(1)}, f32[768]{0:T(1024)}, u32[]{:S(2)}) copy-start(f32[768]{0:T(1024)} %param.42) | copy-start | bytes 9220
  579.6 413.2 %all-reduce.8.cloned.1.call-start = ((), (), s32[]{:S(2)}) async-start(), calls=%async_computation.15 | async-start | bytes 3538944 | tf_op jit(solution)/shard_map/psum | solution.py:199
  793.0 13.2 %slice-start = ((f32[776,768]{1,0:T(8,128)}), f32[8,768]{1,0:T(8,128)S(1)}, s32[]{:S(2)}) async-start(f32[776,768]{1,0:T(8,128)} %copy-done.5), calls=%async_computation.16 | async-start | bytes 49152 | tf_op jit(solution)/shard_map/slice | solution.py:173
  793.0 13.2 %copy-start.19 = (f32[768]{0:T(1024)S(1)}, f32[768]{0:T(1024)}, u32[]{:S(2)}) copy-start(f32[768]{0:T(1024)} %get-tuple-element.355) | copy-start | bytes 9220
  793.0 13.1 %copy-start.20 = (f32[3072]{0:T(1024)S(1)}, f32[3072]{0:T(1024)}, u32[]{:S(2)}) copy-start(f32[3072]{0:T(1024)} %get-tuple-element.363) | copy-start | bytes 36868
  793.0 13.1 %copy-start.23 = (f32[768]{0:T(1024)S(1)}, f32[768]{0:T(1024)}, u32[]{:S(2)}) copy-start(f32[768]{0:T(1024)} %get-tuple-element.282) | copy-start | bytes 9220
  793.0 13.1 %copy-start.24 = (f32[768]{0:T(1024)S(1)}, f32[768]{0:T(1024)}, u32[]{:S(2)}) copy-start(f32[768]{0:T(1024)} %get-tuple-element.286) | copy-start | bytes 9220
  793.1 13.1 %copy-start.25 = (f32[768]{0:T(1024)S(1)}, f32[768]{0:T(1024)}, u32[]{:S(2)}) copy-start(f32[768]{0:T(1024)} %get-tuple-element.284) | copy-start | bytes 9220
  793.1 13.1 %copy-start.26 = (f32[768]{0:T(1024)S(1)}, f32[768]{0:T(1024)}, u32[]{:S(2)}) copy-start(f32[768]{0:T(1024)} %get-tuple-element.287) | copy-start | bytes 9220
  944.7 3.2 copy-start.8
  992.8 5.9 copy-start.11
  (18 other events, 36.9 us)
Sparse Core Ops, SparseCore 0:
  10.2 86.9 all-gather.4
  99.4 39.5 all-gather.6
  141.2 78.6 all-gather.8
  222.0 78.0 all-gather.10
  325.0 62.1 reduce-scatter.6
  511.6 83.8 reduce-scatter.4
  599.1 94.9 reduce-scatter.8
  697.7 95.1 reduce-scatter.10
  799.4 145.3 all-reduce.5
  947.4 45.3 all-reduce.7
where the time goes:
time: 1020 us; the launch traced here: 1010 us
  waiting for transfers between devices  499 us (49%)
  matrix products  295 us (29%)
  blocking collectives  73.8 us (7%)
  local copies, waits for them, and re-layouts  72.3 us (7%)
  other arithmetic  26.1 us (3%)
  loops' own time  17.2 us (2%)
  between operations  15.5 us (2%)
    dot_general x41, matrix products, times_transposed(): lax.dot_general(left, right, (((1,), (1,)), ((), ())), preferred_element_...  117 us
    reduce_scatter x1, waiting for transfers between devices, per_device(): lax.psum_scatter(down_weight_grad.astype(jnp.bfloat16), 'mod', scatter_di...  98.9 us
    reduce_scatter x1, waiting for transfers between devices, per_device(): lax.psum_scatter(up_weight_grad.astype(jnp.bfloat16), 'mod', scatter_dime...  98.6 us
    psum x1, waiting for transfers between devices, per_device(): lax.psum((patch_weight_grad, patch_bias_grad, lang_weight_grad, lang_bias...  92.5 us
    dot_general x29, matrix products, outer_sum(): lax.dot_general(left, right, (((0,), (0,)), ((), ())), preferred_element_...  89.2 us
    all_gather x1, waiting for transfers between devices, per_device(): lax.all_gather(down_weight, 'mod', axis=0, tiled=True)  69.3 us
    psum x1, waiting for transfers between devices, per_device(): lax.psum(shards[0].astype(jnp.bfloat16), 'rep').astype(jnp.float32)  42.9 us
    psum x1, blocking collectives, per_device(): lax.psum((patch_weight_grad, patch_bias_grad, lang_weight_grad, lang_bias...  42.2 us
  transfers between devices with their start and end apart: 11, of which 9 were waited for; matrix products, arithmetic and copies ran while one was open for 36% of the time, Pallas kernels for 0%

commit v1 on v0

v1 whole, which is shorter than its diff:
```python
import functools

import jax
import jax.numpy as jnp
from jax import lax
from jax.experimental import pallas as pl
from jax.experimental.pallas import tpu as pltpu
from jax.sharding import PartitionSpec as P

D = 768
HEADS = 12
HD = 64
RPS = 4
RD = 8
PAD = 16
LANES = 128
CHUNK = 256
FB = 256
EPS = 1e-6
NEG = -1e30
F32 = jnp.float32
BF16 = jnp.bfloat16
AXES = ("mod", "rep")
SCALE = HD ** (-0.5)
VMEM = pl.BlockSpec(memory_space=pltpu.VMEM)
SMEM = pl.BlockSpec(memory_space=pltpu.SMEM)


def nn(left, right):
    return lax.dot_general(left, right, (((1,), (0,)), ((), ())), preferred_element_type=F32)


def nt(left, right):
    return lax.dot_general(left, right, (((1,), (1,)), ((), ())), preferred_element_type=F32)


def tn(left, right):
    return lax.dot_general(left, right, (((0,), (0,)), ((), ())), preferred_element_type=F32)


def chunks(rows):
    count = rows // CHUNK
    return [
        (i * CHUNK, (rows - i * CHUNK) if i == count - 1 else CHUNK) for i in range(count)
    ]


def normalise(rows):
    mean = jnp.mean(rows, axis=-1, keepdims=True)
    centred = rows - mean
    var = jnp.mean(centred * centred, axis=-1, keepdims=True)
    rstd = lax.rsqrt(var + EPS)
    return centred * rstd, rstd


def norm_input_grad(xhat, rstd, gain, upstream):
    scaled = upstream * gain
    first = jnp.mean(scaled, axis=-1, keepdims=True)
    second = jnp.mean(scaled * xhat, axis=-1, keepdims=True)
    return rstd * (scaled - first - xhat * second)


def call(kernel, out_shape, **kw):
    limit = kw.pop("vmem", 56)
    cost = kw.pop("cost", None)
    return pl.pallas_call(
        kernel,
        out_shape=out_shape,
        cost_estimate=cost,
        compiler_params=pltpu.CompilerParams(vmem_limit_bytes=limit * 1024 * 1024),
        **kw,
    )


def cost(flops, nbytes):
    return pl.CostEstimate(flops=int(flops), bytes_accessed=int(nbytes), transcendentals=0)


def struct(shape, dtype):
    return jax.ShapeDtypeStruct(shape, dtype)


def live_of(index, counts, read, block_rows):
    groups_n = counts.shape[1]
    capacity = groups_n * block_rows
    live = index < 0
    for s in range(groups_n):
        live = live | ((index >= s * block_rows) & (index < s * block_rows + counts[0, s]))
    slot = index - capacity
    return live | ((slot >= 0) & (slot < RD) & (slot % RPS < read[0, 0]))


def stem_kernel(cut, raw, wp, bp, wl, bl, table, gain, bias, stream, normed):
    capacity = raw.shape[0]
    step = capacity // 4
    for start in range(0, capacity, step):
        weight, shift = (wp, bp) if start < cut else (wl, bl)
        rows = pl.ds(start, step)
        embedded = (nn(raw[rows, :], weight[...]) + shift[...]).astype(BF16).astype(F32)
        stream[rows, :] = embedded
        xhat, _ = normalise(embedded)
        normed[rows, :] = (xhat * gain[...] + bias[...]).astype(BF16)
    tail = jnp.concatenate([table[...], jnp.zeros((PAD - RD, D), F32)], axis=0)
    stream[pl.ds(capacity, PAD), :] = tail
    xhat, _ = normalise(tail)
    normed[pl.ds(capacity, PAD), :] = (xhat * gain[...] + bias[...]).astype(BF16)


def stems(raw, wp, bp, wl, bl, table, gain, bias):
    capacity = raw.shape[0]
    total = capacity + PAD
    return call(
        functools.partial(stem_kernel, 3 * capacity // 4),
        (struct((total, D), F32), struct((total, D), BF16)),
        in_specs=[VMEM] * 8,
        out_specs=(VMEM, VMEM),
        cost=cost(2 * capacity * D * D, 8 * capacity * D),
    )(raw, wp, bp, wl, bl, table, gain, bias)


def qkv_kernel(rows, weight, out):
    for start, size in chunks(rows.shape[0]):
        out[0, pl.ds(start, size), :] = nn(rows[pl.ds(start, size), :], weight[0]).astype(BF16)


def project_qkv(normed, weights):
    total = normed.shape[0]
    return call(
        qkv_kernel,
        struct((3, total, D), BF16),
        grid=(3,),
        in_specs=[
            pl.BlockSpec((total, D), lambda r: (0, 0)),
            pl.BlockSpec((1, D, D), lambda r: (r, 0, 0)),
        ],
        out_specs=pl.BlockSpec((1, total, D), lambda r: (r, 0, 0)),
        cost=cost(6 * total * D * D, 6 * D * D + 8 * total * D),
    )(normed, weights)


def visible_readout(group_row, live_row):
    capacity = group_row.shape[1]
    query = lax.broadcasted_iota(jnp.int32, (RD, capacity), 0)
    group = 2 * (query // RPS + 1) + 1
    keys = group_row[...]
    seen = live_row & (keys <= group) & ((keys % 2 == 0) | (keys == group))
    return jnp.where(seen, 0.0, NEG)


def visible_between(read):
    query = lax.broadcasted_iota(jnp.int32, (RD, PAD), 0)
    key = lax.broadcasted_iota(jnp.int32, (RD, PAD), 1)
    live = (key < RD) & (key % RPS < read[0, 0])
    seen = (query == key) | (live & (query // RPS == key // RPS))
    return jnp.where(seen, 0.0, NEG)


def tiled(rows):
    return jnp.concatenate([rows] * HEADS, axis=0)


def own_head():
    row = lax.broadcasted_iota(jnp.int32, (HEADS * RD, D), 0) // RD
    lane = lax.broadcasted_iota(jnp.int32, (HEADS * RD, D), 1) // HD
    return row == lane


def fold_heads(stack, mine):
    kept = jnp.where(mine, stack, 0.0)
    total = kept[:RD]
    for head in range(1, HEADS):
        total = total + kept[head * RD : (head + 1) * RD]
    return jnp.concatenate([total, jnp.zeros((PAD - RD, D), F32)], axis=0)


def attend_kernel(
    block_rows, qkv, counts, read, group_row, group_col, mixed, lse, lse_read, mask, lse_cols, tail
):
    step = pl.program_id(0)
    capacity = group_row.shape[1]

    @pl.when(step == 0)
    def _():
        slot_row = lax.broadcasted_iota(jnp.int32, (1, capacity), 1)
        live_row = live_of(slot_row, counts, read, block_rows)
        keys = group_row[...]
        for start in range(0, capacity, CHUNK):
            query = lax.broadcasted_iota(jnp.int32, (CHUNK, capacity), 0) + start
            group = group_col[pl.ds(start, CHUNK), :]
            seen = live_row & (keys <= group) & ((keys % 2 == 0) | (keys == group))
            seen = seen | (query == slot_row)
            mask[pl.ds(start, CHUNK), :] = jnp.where(seen, 0.0, NEG)
        lse_cols[...] = jnp.zeros_like(lse_cols)
        mine = own_head()
        tail_rows = pl.ds(capacity, PAD)
        head_rows = pl.ds(0, capacity)
        query = qkv[0, tail_rows, :].astype(F32)[:RD] * SCALE
        query = jnp.where(mine, tiled(query), 0.0).astype(BF16)
        far = nt(query, qkv[1, head_rows, :]) + tiled(visible_readout(group_row, live_row))
        near = nt(query, qkv[1, tail_rows, :]) + tiled(visible_between(read))
        peak = jnp.maximum(
            jnp.max(far, axis=1, keepdims=True), jnp.max(near, axis=1, keepdims=True)
        )
        far = jnp.exp(far - peak)
        near = jnp.exp(near - peak)
        total = jnp.sum(far, axis=1, keepdims=True) + jnp.sum(near, axis=1, keepdims=True)
        out = nn(far.astype(BF16), qkv[2, head_rows, :]) + nn(
            near.astype(BF16), qkv[2, tail_rows, :]
        )
        tail[...] = fold_heads(out / total, mine)
        lse_read[...] = jnp.broadcast_to(peak + jnp.log(total), lse_read.shape)

    lane = lax.broadcasted_iota(jnp.int32, (1, LANES), 1)
    columns = pl.ds(pl.multiple_of(step * LANES, LANES), LANES)
    keys = qkv[1, pl.ds(0, capacity), columns]
    values = qkv[2, pl.ds(0, capacity), columns]
    for start in range(0, capacity, CHUNK):
        rows = pl.ds(start, CHUNK)
        query = qkv[0, rows, columns] * SCALE
        outs = []
        logs = lse_cols[rows, :]
        for head in range(2):
            chosen = jnp.where(lane // HD == head, query, jnp.zeros_like(query))
            scores = nt(chosen.astype(BF16), keys) + mask[rows, :]
            peak = jnp.max(scores, axis=1, keepdims=True)
            weight = jnp.exp(scores - peak)
            total = jnp.sum(weight, axis=1, keepdims=True)
            outs.append(nn(weight.astype(BF16), values) / total)
            logs = jnp.where(lane == 2 * step + head, peak + jnp.log(total), logs)
        mixed[rows, :] = jnp.where(lane < HD, outs[0], outs[1]).astype(BF16)
        lse_cols[rows, :] = logs
    mixed[pl.ds(capacity, PAD), :] = tail[:, columns].astype(BF16)

    @pl.when(step == pl.num_programs(0) - 1)
    def _():
        lse[...] = lse_cols[...].T[: lse.shape[0], :]


def attend(qkv, counts, read, group_row, group_col, block_rows):
    total = qkv.shape[1]
    capacity = total - PAD
    pairs = HEADS // 2
    return call(
        functools.partial(attend_kernel, block_rows),
        (
            struct((total, D), BF16),
            struct((16, capacity), F32),
            struct((HEADS * RD, LANES), F32),
        ),
        grid=(pairs,),
        in_specs=[VMEM, SMEM, SMEM, VMEM, VMEM],
        out_specs=(pl.BlockSpec((total, LANES), lambda j: (0, j)), VMEM, VMEM),
        scratch_shapes=[
            pltpu.VMEM((capacity, capacity), F32),
            pltpu.VMEM((capacity, LANES), F32),
            pltpu.VMEM((PAD, D), F32),
        ],
        cost=cost(4 * HEADS * capacity * capacity * 256, 8 * total * D),
    )(qkv, counts, read, group_row, group_col)


def attend_back_kernel(
    block_rows,
    qkv,
    mixed,
    grad,
    lse,
    lse_read,
    counts,
    read,
    group_row,
    group_col,
    out,
    mask,
    delta,
    key_more,
    value_more,
    tails,
):
    step = pl.program_id(0)
    capacity = group_row.shape[1]
    tail_rows = pl.ds(capacity, PAD)
    head_rows = pl.ds(0, capacity)

    @pl.when(step == 0)
    def _():
        slot_row = lax.broadcasted_iota(jnp.int32, (1, capacity), 1)
        group = group_row[...]
        for start in range(0, capacity, CHUNK):
            slot = lax.broadcasted_iota(jnp.int32, (CHUNK, 1), 0) + start
            live = live_of(slot, counts, read, block_rows)
            keys = group_col[pl.ds(start, CHUNK), :]
            seen = live & (keys <= group) & ((keys % 2 == 0) | (keys == group))
            seen = seen | (slot == slot_row)
            mask[pl.ds(start, CHUNK), :] = jnp.where(seen, 0.0, NEG)
        head = lax.broadcasted_iota(jnp.int32, (16, D), 0)
        column = lax.broadcasted_iota(jnp.int32, (16, D), 1)
        select = jnp.where(column // HD == head, 1.0, 0.0).astype(BF16)
        for start in range(0, capacity, CHUNK):
            rows = pl.ds(start, CHUNK)
            product = grad[rows, :].astype(F32) * mixed[rows, :].astype(F32)
            high = product.astype(BF16)
            low = (product - high.astype(F32)).astype(BF16)
            delta[:, rows] = nt(select, high) + nt(select, low)

        live_row = live_of(slot_row, counts, read, block_rows)
        mine = own_head()
        query = qkv[0, tail_rows, :].astype(F32)[:RD] * SCALE
        query = jnp.where(mine, tiled(query), 0.0).astype(BF16)
        upper = grad[tail_rows, :].astype(F32)[:RD]
        upper = jnp.where(mine, tiled(upper), 0.0)
        result = tiled(mixed[tail_rows, :].astype(F32)[:RD])
        row_delta = jnp.sum(upper * result, axis=1, keepdims=True)
        upper = upper.astype(BF16)
        logs = lse_read[:, 0:1]
        far = nt(query, qkv[1, head_rows, :]) + tiled(visible_readout(group_row, live_row))
        near = nt(query, qkv[1, tail_rows, :]) + tiled(visible_between(read))
        far = jnp.exp(far - logs)
        near = jnp.exp(near - logs)
        far_grad = (far * (nt(upper, qkv[2, head_rows, :]) - row_delta)).astype(BF16)
        near_grad = (near * (nt(upper, qkv[2, tail_rows, :]) - row_delta)).astype(BF16)
        query_grad = nn(far_grad, qkv[1, head_rows, :]) + nn(near_grad, qkv[1, tail_rows, :])
        tails[0] = fold_heads(query_grad, mine) * SCALE
        tails[1] = tn(near_grad, query)
        tails[2] = tn(near.astype(BF16), upper)
        key_more[...] = tn(far_grad, query)
        value_more[...] = tn(far.astype(BF16), upper)

    lane = lax.broadcasted_iota(jnp.int32, (1, LANES), 1)
    columns = pl.ds(pl.multiple_of(step * LANES, LANES), LANES)
    query = (qkv[0, head_rows, columns] * SCALE).astype(BF16)
    upper = grad[head_rows, columns]
    query_grad = jnp.zeros((capacity, LANES), F32)
    for start in range(0, capacity, CHUNK):
        rows = pl.ds(start, CHUNK)
        all_keys = qkv[1, rows, columns]
        all_values = qkv[2, rows, columns]
        key_parts = []
        value_parts = []
        for head in range(2):
            own = lane // HD == head
            keys = jnp.where(own, all_keys, jnp.zeros_like(all_keys))
            values = jnp.where(own, all_values, jnp.zeros_like(all_values))
            logs = lse[pl.ds(2 * step + head, 1), :]
            row_delta = delta[pl.ds(2 * step + head, 1), :]
            probs = jnp.exp(nt(keys, query) + mask[rows, :] - logs)
            score_grad = (probs * (nt(values, upper) - row_delta)).astype(BF16)
            value_parts.append(nn(probs.astype(BF16), upper))
            key_parts.append(nn(score_grad, query))
            query_grad = query_grad + tn(score_grad, keys)
        key_grad = jnp.where(lane < HD, key_parts[0], key_parts[1]) + key_more[rows, columns]
        value_grad = jnp.where(lane < HD, value_parts[0], value_parts[1]) + value_more[rows, columns]
        out[1, rows, :] = key_grad.astype(BF16)
        out[2, rows, :] = value_grad.astype(BF16)
    out[0, head_rows, :] = (query_grad * SCALE).astype(BF16)
    for part in range(3):
        out[part, tail_rows, :] = tails[part, :, columns].astype(BF16)


def attend_back(qkv, mixed, grad, lse, lse_read, counts, read, group_row, group_col, block_rows):
    total = qkv.shape[1]
    capacity = total - PAD
    pairs = HEADS // 2
    return call(
        functools.partial(attend_back_kernel, block_rows),
        struct((3, total, D), BF16),
        grid=(pairs,),
        in_specs=[VMEM, VMEM, VMEM, VMEM, VMEM, SMEM, SMEM, VMEM, VMEM],
        out_specs=pl.BlockSpec((3, total, LANES), lambda j: (0, 0, j)),
        scratch_shapes=[
            pltpu.VMEM((capacity, capacity), F32),
            pltpu.VMEM((16, capacity), F32),
            pltpu.VMEM((capacity, D), F32),
            pltpu.VMEM((capacity, D), F32),
            pltpu.VMEM((3, PAD, D), F32),
        ],
        cost=cost(10 * HEADS * capacity * capacity * 256, 16 * total * D),
    )(qkv, mixed, grad, lse, lse_read, counts, read, group_row, group_col)


def out_kernel(mixed, weight, stream, gain, bias, after, normed):
    for start, size in chunks(mixed.shape[0]):
        rows = pl.ds(start, size)
        value = stream[rows, :] + nn(mixed[rows, :], weight[0])
        after[rows, :] = value
        xhat, _ = normalise(value)
        normed[rows, :] = (xhat * gain[...] + bias[...]).astype(BF16)


def out_project(mixed, weights, stream, gain, bias):
    total = mixed.shape[0]
    whole = pl.BlockSpec((total, D), lambda i: (0, 0))
    vector = pl.BlockSpec((1, D), lambda i: (0, 0))
    return call(
        out_kernel,
        (struct((total, D), F32), struct((total, D), BF16)),
        grid=(1,),
        in_specs=[whole, pl.BlockSpec((1, D, D), lambda i: (3, 0, 0)), whole, vector, vector],
        out_specs=(whole, whole),
        cost=cost(2 * total * D * D, 12 * total * D),
    )(mixed, weights, stream, gain, bias)


def out_back_kernel(inner, after, branch, gain, weight, grad, grad_low, mixed_grad, gains, biases):
    gain_sum = jnp.zeros((1, D), F32)
    bias_sum = jnp.zeros((1, D), F32)
    for start, size in chunks(inner.shape[0]):
        rows = pl.ds(start, size)
        upstream = inner[rows, :]
        xhat, rstd = normalise(after[rows, :])
        gain_sum = gain_sum + jnp.sum(upstream * xhat, axis=0, keepdims=True)
        bias_sum = bias_sum + jnp.sum(upstream, axis=0, keepdims=True)
        total = branch[rows, :].astype(F32) + norm_input_grad(xhat, rstd, gain[...], upstream)
        grad[rows, :] = total
        low = total.astype(BF16)
        grad_low[rows, :] = low
        mixed_grad[rows, :] = nt(low, weight[0]).astype(BF16)
    gains[...] = gain_sum
    biases[...] = bias_sum


def out_back(inner, after, branch, gain, weights):
    total = inner.shape[0]
    whole = pl.BlockSpec((total, D), lambda i: (0, 0))
    vector = pl.BlockSpec((1, D), lambda i: (0, 0))
    return call(
        out_back_kernel,
        (
            struct((total, D), F32),
            struct((total, D), BF16),
            struct((total, D), BF16),
            struct((1, D), F32),
            struct((1, D), F32),
        ),
        grid=(1,),
        in_specs=[whole, whole, whole, vector, pl.BlockSpec((1, D, D), lambda i: (3, 0, 0))],
        out_specs=(whole, whole, whole, vector, vector),
        cost=cost(2 * total * D * D, 20 * total * D),
    )(inner, after, branch, gain, weights)


def mlp_kernel(
    block_rows,
    after,
    normed,
    cotangent,
    counts,
    read,
    up,
    up_bias,
    down,
    down_bias,
    layer_out,
    up_grad,
    down_grad,
    up_bias_grad,
    inner,
    branch,
    down_bias_grad,
    total_out,
    active,
    hidden_grad,
    live_col,
):
    step = pl.program_id(0)
    total = normed.shape[0]
    slots = cotangent.shape[0]

    @pl.when(step == 0)
    def _():
        index = lax.broadcasted_iota(jnp.int32, (total, 1), 0)
        live = jnp.where(live_of(index, counts, read, block_rows), 1.0, 0.0)
        live_col[...] = live
        upstream = cotangent[...].astype(F32) * live[:slots]
        upstream = jnp.concatenate([upstream, jnp.zeros((total - slots, D), F32)], axis=0)
        branch[...] = upstream.astype(BF16)
        down_bias_grad[...] = jnp.sum(upstream, axis=0, keepdims=True)
        inner[...] = jnp.zeros_like(inner)
        total_out[...] = after[...] + down_bias[...]

    bias_sum = jnp.zeros(up_bias.shape, F32)
    for start, size in chunks(total):
        rows = pl.ds(start, size)
        hidden = nn(normed[rows, :], up[0]) + up_bias[...]
        factor = (2.0 / jnp.pi) ** 0.5
        square = hidden * hidden
        bent = jnp.tanh(hidden * (factor + (factor * 0.044715) * square))
        half = 0.5 * (1.0 + bent)
        act = (hidden * half).astype(BF16)
        slope = half + (0.5 * hidden) * (1.0 - bent * bent) * (
            factor + (3.0 * factor * 0.044715) * square
        )
        back = (nt(branch[rows, :], down[...]) * slope).astype(BF16)
        bias_sum = bias_sum + jnp.sum(back.astype(F32), axis=0, keepdims=True)
        active[rows, :] = act
        hidden_grad[rows, :] = back
        total_out[rows, :] += nn(act, down[...])
        inner[rows, :] += nt(back, up[0])
    up_bias_grad[...] = bias_sum
    down_grad[...] = tn(active[...], branch[...]).astype(BF16)
    up_grad[0] = tn(normed[...], hidden_grad[...]).astype(BF16)

    @pl.when(step == pl.num_programs(0) - 1)
    def _():
        layer_out[...] = (total_out[...] * live_col[...])[:slots].astype(BF16)


def mlp(after, normed, cotangent, counts, read, up, up_bias, down, down_bias, block_rows):
    total = normed.shape[0]
    slots = cotangent.shape[0]
    hidden = up_bias.shape[1]
    per = D // FB
    whole = lambda rows: pl.BlockSpec((rows, D), lambda j: (0, 0))
    return call(
        functools.partial(mlp_kernel, block_rows),
        (
            struct((slots, D), BF16),
            struct((hidden // D, D, D), BF16),
            struct((hidden, D), BF16),
            struct((1, hidden), F32),
            struct((total, D), F32),
            struct((total, D), BF16),
            struct((1, D), F32),
        ),
        grid=(hidden // FB,),
        in_specs=[
            whole(total),
            whole(total),
            whole(slots),
            SMEM,
            SMEM,
            pl.BlockSpec((1, D, FB), lambda j: (j // per, 0, j % per)),
            pl.BlockSpec((1, FB), lambda j: (0, j)),
            pl.BlockSpec((FB, D), lambda j: (j, 0)),
            whole(1),
        ],
        out_specs=(
            whole(slots),
            pl.BlockSpec((1, D, FB), lambda j: (j // per, 0, j % per)),
            pl.BlockSpec((FB, D), lambda j: (j, 0)),
            pl.BlockSpec((1, FB), lambda j: (0, j)),
            whole(total),
            whole(total),
            whole(1),
        ),
        scratch_shapes=[
            pltpu.VMEM((total, D), F32),
            pltpu.VMEM((total, FB), BF16),
            pltpu.VMEM((total, FB), BF16),
            pltpu.VMEM((total, 1), F32),
        ],
        cost=cost(12 * total * D * hidden, 16 * D * hidden),
    )(after, normed, cotangent, counts, read, up, up_bias, down, down_bias)


def qkv_back_kernel(capacity, grads, weights, stream, gain, after_grad, embedded, readout, gains, biases):
    gain_sum = jnp.zeros((1, D), F32)
    bias_sum = jnp.zeros((1, D), F32)
    for start, size in chunks(stream.shape[0]):
        rows = pl.ds(start, size)
        upstream = (
            nt(grads[0, rows, :], weights[0])
            + nt(grads[1, rows, :], weights[1])
            + nt(grads[2, rows, :], weights[2])
        )
        xhat, rstd = normalise(stream[rows, :])
        gain_sum = gain_sum + jnp.sum(upstream * xhat, axis=0, keepdims=True)
        bias_sum = bias_sum + jnp.sum(upstream, axis=0, keepdims=True)
        total = after_grad[rows, :] + norm_input_grad(xhat, rstd, gain[...], upstream)
        inside = min(size, capacity - start)
        embedded[pl.ds(start, inside), :] = total[:inside].astype(BF16)
        if start + size > capacity:
            readout[...] = total[capacity - start : capacity - start + RD]
    gains[...] = gain_sum
    biases[...] = bias_sum


def qkv_back(grads, weights, stream, gain, after_grad):
    total = stream.shape[0]
    capacity = total - PAD
    whole = pl.BlockSpec((total, D), lambda i: (0, 0))
    vector = pl.BlockSpec((1, D), lambda i: (0, 0))
    return call(
        functools.partial(qkv_back_kernel, capacity),
        (
            struct((capacity, D), BF16),
            struct((RD, D), F32),
            struct((1, D), F32),
            struct((1, D), F32),
        ),
        grid=(1,),
        in_specs=[
            pl.BlockSpec((3, total, D), lambda i: (0, 0, 0)),
            pl.BlockSpec((3, D, D), lambda i: (0, 0, 0)),
            whole,
            vector,
            whole,
        ],
        out_specs=(
            pl.BlockSpec((capacity, D), lambda i: (0, 0)),
            pl.BlockSpec((RD, D), lambda i: (0, 0)),
            vector,
            vector,
        ),
        cost=cost(6 * total * D * D, 20 * total * D),
    )(grads, weights, stream, gain, after_grad)


def weight_kernel(normed, mixed, grads, attn_grad, out):
    step = pl.program_id(0)

    @pl.when(step < 3)
    def _():
        out[0] = tn(normed[...], grads[0]).astype(BF16)

    @pl.when(step == 3)
    def _():
        out[0] = tn(mixed[...], attn_grad[...]).astype(BF16)


def weight_grads(normed, mixed, grads, attn_grad):
    total = normed.shape[0]
    whole = pl.BlockSpec((total, D), lambda r: (0, 0))
    return call(
        weight_kernel,
        struct((4, D, D), BF16),
        grid=(4,),
        in_specs=[
            whole,
            whole,
            pl.BlockSpec((1, total, D), lambda r: (jnp.minimum(r, 2), 0, 0)),
            whole,
        ],
        out_specs=pl.BlockSpec((1, D, D), lambda r: (r, 0, 0)),
        cost=cost(8 * total * D * D, 8 * D * D + 12 * total * D),
    )(normed, mixed, grads, attn_grad)


def stem_back_kernel(cut, raw, embedded, out, patch_bias, lang_bias):
    out[0] = tn(raw[:cut, :], embedded[:cut, :]).astype(BF16)
    out[1] = tn(raw[cut:, :], embedded[cut:, :]).astype(BF16)
    patch_bias[...] = jnp.sum(embedded[:cut, :].astype(F32), axis=0, keepdims=True)
    lang_bias[...] = jnp.sum(embedded[cut:, :].astype(F32), axis=0, keepdims=True)


def stem_back(raw, embedded):
    capacity = raw.shape[0]
    return call(
        functools.partial(stem_back_kernel, 3 * capacity // 4),
        (struct((2, D, D), BF16), struct((1, D), F32), struct((1, D), F32)),
        in_specs=[VMEM, VMEM],
        out_specs=(VMEM, VMEM, VMEM),
        cost=cost(2 * capacity * D * D, 8 * capacity * D),
    )(raw, embedded)


def raw_kernel(image, grad, wp, wl, out):
    @pl.when(image[0] != 0)
    def _():
        out[...] = nt(grad[...], wp[...])

    @pl.when(image[0] == 0)
    def _():
        out[...] = nt(grad[...], wl[...])


def raw_back(image, grad, wp, wl):
    return call(
        raw_kernel,
        struct(grad.shape, F32),
        in_specs=[SMEM, VMEM, VMEM, VMEM],
        out_specs=VMEM,
        cost=cost(2 * grad.shape[0] * D * D, 6 * grad.shape[0] * D),
    )(image, grad, wp, wl)


class Grid:
    def __init__(self, mods, reps):
        self.mods, self.reps = mods, reps
        self.mod, self.rep = lax.axis_index("mod"), lax.axis_index("rep")

    def swap(self, value, mod=0, rep=0):
        pairs = [
            (m * self.reps + r, (m ^ mod) * self.reps + (r ^ rep))
            for m in range(self.mods)
            for r in range(self.reps)
        ]
        return lax.ppermute(value, AXES, pairs)

    def bit(self, mod=0, rep=0):
        return ((self.mod & mod) | (self.rep & rep)) != 0

    def joined(self, value, axis, **bit):
        other = self.swap(value, **bit)
        shape = [1] * (value.ndim + 1)
        shape[axis] = 2
        place = jnp.arange(2).reshape(shape) == self.bit(**bit)
        return jnp.where(place, jnp.expand_dims(value, axis), jnp.expand_dims(other, axis))

    def halved(self, value, axis, **bit):
        mine = self.bit(**bit).astype(jnp.int32)
        keep = lax.dynamic_index_in_dim(value, mine, axis, keepdims=False)
        give = lax.dynamic_index_in_dim(value, 1 - mine, axis, keepdims=False)
        return keep + self.swap(give, **bit)


def gather_piece(grid, piece, by_rank):
    rows = piece.shape[0]
    value = grid.joined(piece, 0, mod=2)
    value = grid.joined(value, 0, mod=4)
    value = grid.joined(value, 2, mod=1)
    axis = 0 if by_rank else 3
    value = grid.joined(value, axis, rep=2)
    value = grid.joined(value, axis + 1, rep=1)
    if by_rank:
        return value.reshape(4, grid.mods * rows, D)
    return value.reshape(grid.mods * 4 * rows, D)


def scatter_piece(grid, value, by_rank, y_first):
    if by_rank:
        value = value.reshape(2, 2, 2, 2, 2, -1, D)
        value = grid.halved(value, 1, rep=1)
        axis_x, axis_y = 0, 3
    else:
        value = value.reshape(2, 2, 2, 2, 2, -1, D)
        value = grid.halved(value, 4, rep=1)
        axis_x, axis_y = 3, 2
    if y_first:
        value = grid.halved(value, axis_y, mod=1)
        value = grid.halved(value, axis_x - (axis_x > axis_y), rep=2)
    else:
        value = grid.halved(value, axis_x, rep=2)
        value = grid.halved(value, axis_y - (axis_y > axis_x), mod=1)
    value = grid.halved(value, 0, mod=4)
    return grid.halved(value, 0, mod=2)


def share_ranks(grid, piece):
    value = grid.joined(piece, 0, rep=2)
    value = grid.joined(value, 1, rep=1)
    return value.reshape((4,) + piece.shape)


def sum_everywhere(grid, value):
    for bit in ({"rep": 1}, {"rep": 2}, {"mod": 1}, {"mod": 2}, {"mod": 4}):
        value = value + grid.swap(value, **bit)
    return value


def stem_sum(grid, value):
    shape = value.shape
    value = value.reshape(2, 2, 2, 2, 2, -1, D)
    order = ({"rep": 1}, {"rep": 2}, {"mod": 1}, {"mod": 4}, {"mod": 2})
    for bit in order:
        value = grid.halved(value, 0, **bit)
    for bit in reversed(order):
        value = grid.joined(value, 0, **bit)
    return value.reshape(shape)


def gathered_weights(grid, fast, qkv_weight, out_weight, up_weight, down_weight):
    if not fast:
        qkv = lax.all_gather(qkv_weight, "mod", axis=0, tiled=True)
        out = lax.all_gather(out_weight, "mod", axis=0, tiled=True)
        up = lax.all_gather(up_weight, "mod", axis=0, tiled=True)
        down = lax.all_gather(down_weight, "mod", axis=0, tiled=True)
        first = jnp.concatenate([qkv, out], axis=1)
        by_columns = lambda w: w.reshape(D, -1, D).transpose(1, 0, 2)
        return by_columns(first), by_columns(up), down
    rank = grid.rep
    pick = lambda w: lax.dynamic_slice_in_dim(w, rank * D, D, 1)
    first = gather_piece(grid, pick(jnp.concatenate([qkv_weight, out_weight], axis=1)), True)
    up = gather_piece(grid, pick(up_weight), True)
    quarter = down_weight.shape[0] // 4
    down = gather_piece(
        grid, lax.dynamic_slice_in_dim(down_weight, rank * quarter, quarter, 0), False
    )
    return first, up, down


def reduced_rows(value, fast):
    part = lax.psum_scatter(value, "mod", scatter_dimension=0, tiled=True)
    return lax.psum(part, "rep").astype(F32)


def per_device(
    raw_rows,
    recv_counts,
    slot_groups,
    read_counts,
    patch_convolution_weight,
    patch_stem_bias_vector,
    language_projection_weight,
    language_bias_vector,
    readout_table,
    attn_gain,
    attn_bias,
    qkv_weight,
    out_weight,
    mlp_gain,
    mlp_bias,
    up_weight,
    up_bias,
    down_weight,
    down_bias,
    out_cotangent,
):
    mods, reps = lax.axis_size("mod"), lax.axis_size("rep")
    fast = mods == 8 and reps == 4
    grid = Grid(mods, reps)
    block_rows = raw_rows.shape[1]
    capacity = mods * block_rows
    row = lambda v: v.reshape(1, -1)
    image = (grid.mod < 3 * mods // 4).astype(jnp.int32).reshape(1)
    group_row = slot_groups
    group_col = slot_groups.reshape(capacity, 1)

    received = lax.all_to_all(raw_rows, "mod", split_axis=0, concat_axis=0, tiled=True)
    first, up, down = gathered_weights(grid, fast, qkv_weight, out_weight, up_weight, down_weight)
    rows = received.reshape(capacity, D)
    stream, normed = stems(
        rows,
        patch_convolution_weight,
        row(patch_stem_bias_vector),
        language_projection_weight,
        row(language_bias_vector),
        readout_table,
        row(attn_gain),
        row(attn_bias),
    )
    qkv = project_qkv(normed, first)
    mixed, lse, lse_read = attend(qkv, recv_counts, read_counts, group_row, group_col, block_rows)
    after, normed2 = out_project(mixed, first, stream, row(mlp_gain), row(mlp_bias))
    layer_out, up_grad, down_grad, up_bias_grad, inner, branch, down_bias_grad = mlp(
        after,
        normed2,
        out_cotangent[0],
        recv_counts,
        read_counts,
        up,
        row(up_bias),
        down,
        row(down_bias),
        block_rows,
    )
    after_grad, attn_grad, mixed_grad, mlp_gain_grad, mlp_bias_grad = out_back(
        inner, after, branch, row(mlp_gain), first
    )
    grads = attend_back(
        qkv, mixed, mixed_grad, lse, lse_read, recv_counts, read_counts, group_row, group_col,
        block_rows,
    )
    embedded_grad, readout_grad, attn_gain_grad, attn_bias_grad = qkv_back(
        grads, first, stream, row(attn_gain), after_grad
    )
    first_grad = weight_grads(normed, mixed, grads, attn_grad)
    stem_grad, patch_bias_grad, lang_bias_grad = stem_back(rows, embedded_grad)
    returned = lax.all_to_all(
        embedded_grad.reshape(raw_rows.shape), "mod", split_axis=0, concat_axis=0, tiled=True
    )
    raw_grad = raw_back(
        image,
        returned.reshape(capacity, D),
        patch_convolution_weight,
        language_projection_weight,
    ).reshape(raw_rows.shape)

    small = jnp.concatenate(
        [
            patch_bias_grad,
            lang_bias_grad,
            attn_gain_grad,
            attn_bias_grad,
            mlp_gain_grad,
            mlp_bias_grad,
            down_bias_grad,
            up_bias_grad.reshape(-1, D),
            readout_grad,
        ],
        axis=0,
    )
    if fast:
        up_piece = share_ranks(grid, scatter_piece(grid, up_grad, True, True))
        down_piece = share_ranks(grid, scatter_piece(grid, down_grad, False, False))
        first_piece = share_ranks(grid, scatter_piece(grid, first_grad, True, False))
        flat = lambda p: p.transpose(1, 0, 2).reshape(p.shape[1], -1).astype(F32)
        qkv_sum = flat(first_piece[:3])
        out_sum = first_piece[3].astype(F32)
        up_sum = flat(up_piece)
        down_sum = down_piece.reshape(-1, D).astype(F32)
        small = sum_everywhere(grid, small)
        stem_grad = stem_sum(grid, stem_grad).astype(F32)
    else:
        flat = lambda p: p.transpose(1, 0, 2).reshape(D, -1)
        qkv_sum = reduced_rows(flat(first_grad[:3]), fast)
        out_sum = reduced_rows(first_grad[3], fast)
        up_sum = reduced_rows(flat(up_grad), fast)
        down_sum = reduced_rows(down_grad, fast)
        small = lax.psum(small, AXES)
        stem_grad = lax.psum(stem_grad.astype(F32), AXES)
    ups = up_bias.shape[0] // D
    return (
        layer_out[None],
        raw_grad,
        stem_grad[0],
        small[0],
        stem_grad[1],
        small[1],
        small[7 + ups : 7 + ups + RD],
        small[2],
        small[3],
        qkv_sum,
        out_sum,
        small[4],
        small[5],
        up_sum,
        small[7 : 7 + ups].reshape(-1),
        down_sum,
        small[6],
    )


def solution(mesh):
    both, rows, rep = P("mod", "rep", None), P("mod", None), P()
    pair = P("mod", "rep")
    return jax.shard_map(
        per_device,
        mesh=mesh,
        in_specs=(both, pair, pair, pair)
        + (rep,) * 7
        + (rows, rows, rep, rep, rows, rep, rows, rep, both),
        out_specs=(both, both)
        + (rep,) * 7
        + (rows, rows, rep, rep, rows, rep, rows, rep),
        check_vma=False,
    )
```

time: 1020 us -> 570 us (0.56)
  matrix products: 295 us -> 0 us
  waiting for transfers between devices: 499 us -> 283 us
  Pallas kernels: 0 us -> 142 us
  blocking collectives: 73.8 us -> 0 us
  starting transfers between devices: 8.06 us -> 65.9 us
  local copies, waits for them, and re-layouts: 72.3 us -> 38 us
  loops' own time: 17.2 us -> 0 us
  between operations: 15.5 us -> 2.36 us
    dot_general x99 -> x0, matrix products: 295 us -> none  [the longest x41 117 us: times_transposed(): lax.dot_general(left, right, (((1,), (1,)), ((), ())), preferred_element_...]
    ppermute x0 -> x51, waiting for transfers between devices: none -> 260 us  [swap(): return lax.ppermute(value, AXES, pairs)]
    reduce_scatter x4 -> x0, waiting for transfers between devices: 213 us -> none  [the longest x1 98.9 us: per_device(): lax.psum_scatter(down_weight_grad.astype(jnp.bfloat16), 'mod', scatter_di...]
    pallas_call x0 -> x11, Pallas kernels: none -> 142 us  [the longest x1 41 us: mlp(): call(functools.partial(mlp_kernel, block_rows), (struct((slots, D), BF16)...]
    psum x2 -> x0, waiting for transfers between devices: 135 us -> none  [the longest x1 92.5 us: per_device(): lax.psum((patch_weight_grad, patch_bias_grad, lang_weight_grad, lang_bias...]
    all_gather x4 -> x0, waiting for transfers between devices: 107 us -> none  [the longest x1 69.3 us: per_device(): lax.all_gather(down_weight, 'mod', axis=0, tiled=True)]
    ppermute x0 -> x51, starting transfers between devices: none -> 53.9 us  [swap(): return lax.ppermute(value, AXES, pairs)]
    psum x1 -> x0, blocking collectives: 42.2 us -> none  [per_device(): lax.psum((patch_weight_grad, patch_bias_grad, lang_weight_grad, lang_bias...]
  transfers between devices with their start and end apart: 11 -> 53, of which waited for: 9 -> 33; matrix products, arithmetic and copies ran while one was open for 36% -> 9% of each run, Pallas kernels for 0% -> 9%
where the time goes in v1:
time: 570 us; the launch traced here: 567 us
  waiting for transfers between devices  283 us (50%)
  Pallas kernels  142 us (25%)
  starting transfers between devices  65.9 us (12%)
  local copies, waits for them, and re-layouts  38 us (7%)
  other arithmetic  35.1 us (6%)
    ppermute x51, waiting for transfers between devices, swap(): return lax.ppermute(value, AXES, pairs)  260 us
    ppermute x51, starting transfers between devices, swap(): return lax.ppermute(value, AXES, pairs)  53.9 us
    pallas_call x1, Pallas kernels, mlp(): call(functools.partial(mlp_kernel, block_rows), (struct((slots, D), BF16)...  41 us
    pallas_call x1, Pallas kernels, attend_back(): call(functools.partial(attend_back_kernel, block_rows), struct((3, total,...  28.3 us
    all_to_all x1, waiting for transfers between devices, per_device(): lax.all_to_all(raw_rows, 'mod', split_axis=0, concat_axis=0, tiled=True)  22.8 us
    pallas_call x1, Pallas kernels, attend(): call(functools.partial(attend_kernel, block_rows), (struct((total, D), BF...  20.7 us
    select_n x12, other arithmetic, joined(): jnp.where(place, jnp.expand_dims(value, axis), jnp.expand_dims(other, axis))  17.3 us
    squeeze x20, local copies, waits for them, and re-layouts, halved(): give = lax.dynamic_index_in_dim(value, 1 - mine, axis, keepdims=False)  14.8 us
  transfers between devices with their start and end apart: 53, of which 33 were waited for; matrix products, arithmetic and copies ran while one was open for 9% of the time, Pallas kernels for 9%

profile of v1, /device:TPU:0, one launch (start us, length us, event | category | flops | bytes accessed | tf_op | source)
XLA Modules:
  0.0 567.0 jit_solution(6828839464220360490)
XLA Ops:
  1.7 3.1 collective-permute-start
  5.9 2.1 collective-permute-start.10
  7.9 1.6 collective-permute-done
  9.5 3.2 collective-permute-done.5
  12.6 2.3 collective-permute-done.10
  15.1 2.8 collective-permute-start.1
  18.1 2.8 collective-permute-start.6
  20.9 23.4 %collective-permute-done.1 = bf16[2,96,768]{2,1,0:T(8,128)(2,1)S(1)} collective-permute-done((bf16[2,96,768]{2,1,0:T(8,128)(2,1)S(1)}, bf16[2,96,768]{2,1,0:T(8,128)(2,1)S(1)}, u32[]{:S(2)}, u32[]{:S(2)}) %collective-permute-start.1) | collective-permute-done | bytes 294944 | tf_op jit(solution)/shard_map/ppermute | solution.py:688
  44.3 6.3 %collective-permute-done.11 = bf16[2,96,768]{2,1,0:T(8,128)(2,1)S(1)} collective-permute-done((bf16[2,96,768]{2,1,0:T(8,128)(2,1)S(1)}, bf16[2,96,768]{2,1,0:T(8,128)(2,1)S(1)}, u32[]{:S(2)}, u32[]{:S(2)}) %collective-permute-start.11) | collective-permute-done | bytes 294944 | tf_op jit(solution)/shard_map/ppermute | solution.py:688
  50.6 5.3 collective-permute-done.6
  59.6 12.9 %collective-permute-done.12 = bf16[2,2,96,768]{3,2,1,0:T(8,128)(2,1)S(1)} collective-permute-done((bf16[2,2,96,768]{3,2,1,0:T(8,128)(2,1)S(1)}, bf16[2,2,96,768]{3,2,1,0:T(8,128)(2,1)S(1)}, u32[]{:S(2)}, u32[]{:S(2)}) %collective-permute-start.12) | collective-permute-done | bytes 589856 | tf_op jit(solution)/shard_map/ppermute | solution.py:688
  72.5 12.6 %collective-permute-done.2 = bf16[2,2,96,768]{3,2,1,0:T(8,128)(2,1)S(1)} collective-permute-done((bf16[2,2,96,768]{3,2,1,0:T(8,128)(2,1)S(1)}, bf16[2,2,96,768]{3,2,1,0:T(8,128)(2,1)S(1)}, u32[]{:S(2)}, u32[]{:S(2)}) %collective-permute-start.2) | collective-permute-done | bytes 589856 | tf_op jit(solution)/shard_map/ppermute | solution.py:688
  85.9 10.0 %collective-permute-done.7 = bf16[2,2,96,768]{3,2,1,0:T(8,128)(2,1)} collective-permute-done((bf16[2,2,96,768]{3,2,1,0:T(8,128)(2,1)S(1)}, bf16[2,2,96,768]{3,2,1,0:T(8,128)(2,1)}, u32[]{:S(2)}, u32[]{:S(2)}) %collective-permute-start.7) | collective-permute-done | bytes 589856 | tf_op jit(solution)/shard_map/ppermute | solution.py:688
  95.9 3.0 broadcast_select_fusion.6
  102.1 25.8 %collective-permute-done.13 = bf16[2,2,2,96,768]{4,3,2,1,0:T(8,128)(2,1)} collective-permute-done((bf16[2,2,2,96,768]{4,3,2,1,0:T(8,128)(2,1)S(1)}, bf16[2,2,2,96,768]{4,3,2,1,0:T(8,128)(2,1)}, u32[]{:S(2)}, u32[]{:S(2)}) %collective-permute-start.13) | collective-permute-done | bytes 1179680 | tf_op jit(solution)/shard_map/ppermute | solution.py:688
  127.9 25.3 %collective-permute-done.3 = bf16[2,2,2,96,768]{4,3,2,1,0:T(8,128)(2,1)} collective-permute-done((bf16[2,2,2,96,768]{4,3,2,1,0:T(8,128)(2,1)}, bf16[2,2,2,96,768]{4,3,2,1,0:T(8,128)(2,1)}, u32[]{:S(2)}, u32[]{:S(2)}) %collective-permute-start.3) | collective-permute-done | bytes 1179680 | tf_op jit(solution)/shard_map/ppermute | solution.py:688
  153.2 22.4 %collective-permute-done.8 = bf16[2,2,2,96,768]{4,3,2,1,0:T(8,128)(2,1)} collective-permute-done((bf16[2,2,2,96,768]{4,3,2,1,0:T(8,128)(2,1)S(1)}, bf16[2,2,2,96,768]{4,3,2,1,0:T(8,128)(2,1)}, u32[]{:S(2)}, u32[]{:S(2)}) %collective-permute-start.8) | collective-permute-done | bytes 1179680 | tf_op jit(solution)/shard_map/ppermute | solution.py:688
  175.6 4.8 broadcast_select_fusion.2
  181.0 7.7 %all-to-all-start = ((bf16[8,96,768]{2,1,0:T(8,128)(2,1)}), bf16[8,96,768]{2,1,0:T(8,128)(2,1)}, u32[]{:S(2)}, u32[]{:S(2)}) async-start(bf16[8,96,768]{2,1,0:T(8,128)(2,1)} %param.20), calls=%async_computation | async-start | bytes 2359296 | tf_op jit(solution)/shard_map/all_to_all | solution.py:819
  194.8 22.8 %all-to-all-done = bf16[8,96,768]{2,1,0:T(8,128)(2,1)} async-done(((bf16[8,96,768]{2,1,0:T(8,128)(2,1)}), bf16[8,96,768]{2,1,0:T(8,128)(2,1)}, u32[]{:S(2)}, u32[]{:S(2)}) %all-to-all-start) | async-done | bytes 1179680 | tf_op jit(solution)/shard_map/all_to_all | solution.py:819
  217.6 5.0 shard_map.323
  222.6 2.2 broadcast_in_dim.605
  224.9 2.2 broadcast_in_dim.617
  227.1 2.2 broadcast_in_dim.603
  229.9 4.0 broadcast_select_fusion
  233.9 6.6 %shard_map.324.qkv = bf16[3,784,768]{2,1,0:T(8,128)(2,1)} custom-call(bf16[784,768]{1,0:T(8,128)(2,1)} %get-tuple-element.43.rows.normed, bf16[4,768,768]{2,1,0:T(8,128)(2,1)} %get-tuple-element.96.weight.weights), custom_call_target="tpu_custom_call" | custom-call | flops 2774532096 | bytes 8355840 | tf_op jit(solution)/shard_map/pallas_call | solution.py:128
  240.5 20.7 %shard_map.325 = (bf16[784,768]{1,0:T(8,128)(2,1)}, f32[16,768]{1,0:T(8,128)}, f32[96,128]{1,0:T(8,128)}) custom-call(bf16[3,784,768]{2,1,0:T(8,128)(2,1)} %shard_map.324.qkv, s32[1,8]{1,0:T(1,128)} %counts.5, s32[1,1]{1,0:T(1,128)S(6)} %copy.44.read, s32[1,768]{1,0:T(1,128)} %group_row.3, s32[768,1]{1,0:T(8,128)} %copy.38.group_col), custom_call_target="tpu_custom_call" | custom-call | flops 7247757312 | bytes 4816896 | tf_op jit(solution)/shard_map/pallas_call | solution.py:243
  261.2 5.6 shard_map.326
  266.8 4.3 bitcast_select_fusion.down
  271.1 41.0 %shard_map.327 = (bf16[776,768]{1,0:T(8,128)(2,1)}, bf16[4,768,768]{2,1,0:T(8,128)(2,1)}, bf16[3072,768]{1,0:T(8,128)(2,1)}, f32[1,3072]{1,0:T(1,128)}, f32[784,...) custom-call(f32[784,768]{1,0:T(8,128)} %get-tuple-element.46.after, ...), custom_call_target="tpu_custom_call" | custom-call | flops 22196256768 | bytes 37748736 | tf_op jit(solution)/shard_map/pallas_call | solution.py:514
  312.2 7.4 %shard_map.328 = (f32[784,768]{1,0:T(8,128)}, bf16[784,768]{1,0:T(8,128)(2,1)}, bf16[784,768]{1,0:T(8,128)(2,1)}, f32[1,768]{1,0:T(1,128)}, f32[1,768]{1,0:T(1,128)}) custom-call(f32[784,768]{1,0:T(8,128)} %get-tuple-element.49.inner, f32[784,768]{1,0:T(8,128)} %get-tuple-element.46.after, bf16[784,768]{1,0:T(8,128)(2,1)} %get-tuple-element.50.branch, ...), custom_call_target="tpu_custom_call" | custom-call | flops 924844032 | bytes 12042240 | tf_op jit(solution)/shard_map/pallas_call | solution.py:426
  319.6 28.3 %shard_map.329.grads = bf16[3,784,768]{2,1,0:T(8,128)(2,1)} custom-call(bf16[3,784,768]{2,1,0:T(8,128)(2,1)} %shard_map.324.qkv, bf16[784,768]{1,0:T(8,128)(2,1)} %get-tuple-element.44.mixed, bf16[784,768]{1,0:T(8,128)(2,1)} %get-tuple-element.51.grad, f32[16,768]{1,0:T(8,128)} %get-tuple-element.52.lse, f32[96,128]{1,0:T(8,128)} %get-tuple-element.53.lse_read, ...), custom_call_target="tpu_custom_call" | custom-call | flops 18119393280 | bytes 9633792 | tf_op jit(solution)/shard_map/pallas_call | solution.py:364
  347.9 9.1 %shard_map.330 = (bf16[768,768]{1,0:T(8,128)(2,1)}, f32[8,768]{1,0:T(8,128)}, f32[1,768]{1,0:T(1,128)}, f32[1,768]{1,0:T(1,128)}) custom-call(bf16[3,784,768]{2,1,0:T(8,128)(2,1)} %shard_map.329.grads, bf16[4,768,768]{2,1,0:T(8,128)(2,1)} %get-tuple-element.96.weight.weights, f32[784,768]{1,0:T(8,128)} %get-tuple-element.45.stream, f32[1,768]{1,0:T(1,128)} %reshape.273.gain, ...), custom_call_target="tpu_custom_call" | custom-call | flops 2774532096 | bytes 12042240 | tf_op jit(solution)/shard_map/pallas_call | solution.py:583
  357.0 4.5 shard_map.332
  362.9 2.8 collective-permute-done.15
  368.8 9.4 %shard_map.333 = bf16[4,768,768]{2,1,0:T(8,128)(2,1)} custom-call(bf16[784,768]{1,0:T(8,128)(2,1)} %get-tuple-element.43.rows.normed, bf16[784,768]{1,0:T(8,128)(2,1)} %get-tuple-element.44.mixed, bf16[3,784,768]{2,1,0:T(8,128)(2,1)} %shard_map.329.grads, bf16[784,768]{1,0:T(8,128)(2,1)} %get-tuple-element.66.attn_grad), custom_call_target="tpu_custom_call" | custom-call | flops 3699376128 | bytes 11943936 | tf_op jit(solution)/shard_map/pallas_call | solution.py:624
  378.2 3.2 dynamic-slice_bitcast_fusion.2
  385.9 3.2 dynamic-slice_bitcast_fusion.1
  391.2 2.9 collective-permute-done.26
  394.8 3.2 dynamic-slice_bitcast_fusion
  398.5 2.0 collective-permute-start.28
  400.5 1.9 collective-permute-done.18
  403.9 2.2 collective-permute-start.29
  407.0 4.3 all-to-all-start.1
  412.6 2.0 collective-permute-start.20
  415.2 16.3 %collective-permute-done.20 = bf16[48,768]{1,0:T(8,128)(2,1)S(1)} collective-permute-done((bf16[48,768]{1,0:T(8,128)(2,1)S(1)}, bf16[48,768]{1,0:T(8,128)(2,1)S(1)}, u32[]{:S(2)}, u32[]{:S(2)}) %collective-permute-start.20) | collective-permute-done | bytes 73760 | tf_op jit(solution)/shard_map/ppermute | solution.py:688
  431.6 4.7 collective-permute-start.21
  436.3 2.6 bitcast_add_fusion.2
  441.5 4.3 collective-permute-done.21
  447.3 2.6 bitcast_add_fusion.1
  449.9 3.6 collective-permute-done.22
  456.3 1.7 collective-permute-start.38
  458.1 1.9 bitcast_add_fusion
  462.3 4.7 shard_map.331
  467.0 14.7 %collective-permute-done.23 = bf16[2,2,2,48,768]{4,3,2,1,0:T(8,128)(2,1)S(1)} collective-permute-done((bf16[2,2,2,48,768]{4,3,2,1,0:T(8,128)(2,1)S(1)}, bf16[2,2,2,48,768]{4,3,2,1,0:T(8,128)(2,1)S(1)}, u32[]{:S(2)}, u32[]{:S(2)}) %collective-permute-start.23) | collective-permute-done | bytes 589856 | tf_op jit(solution)/shard_map/ppermute | solution.py:688
  488.4 18.7 %collective-permute-done.45 = bf16[2,2,2,96,768]{4,3,2,1,0:T(8,128)(2,1)} collective-permute-done((bf16[2,2,2,96,768]{4,3,2,1,0:T(8,128)(2,1)}, bf16[2,2,2,96,768]{4,3,2,1,0:T(8,128)(2,1)}, u32[]{:S(2)}, u32[]{:S(2)}) %collective-permute-start.45) | collective-permute-done | bytes 1179680 | tf_op jit(solution)/shard_map/ppermute | solution.py:688
  510.3 6.4 %collective-permute-done.39 = bf16[2,2,96,768]{3,2,1,0:T(8,128)(2,1)S(1)} collective-permute-done((bf16[2,2,96,768]{3,2,1,0:T(8,128)(2,1)S(1)}, bf16[2,2,96,768]{3,2,1,0:T(8,128)(2,1)S(1)}, u32[]{:S(2)}, u32[]{:S(2)}) %collective-permute-start.39) | collective-permute-done | bytes 589856 | tf_op jit(solution)/shard_map/ppermute | solution.py:688
  520.0 15.8 %collective-permute-done.33 = bf16[2,96,768]{2,1,0:T(8,128)(2,1)S(1)} collective-permute-done((bf16[2,96,768]{2,1,0:T(8,128)(2,1)S(1)}, bf16[2,96,768]{2,1,0:T(8,128)(2,1)S(1)}, u32[]{:S(2)}, u32[]{:S(2)}) %collective-permute-start.33) | collective-permute-done | bytes 294944 | tf_op jit(solution)/shard_map/ppermute | solution.py:688
  535.9 6.3 %collective-permute-done.40 = bf16[2,96,768]{2,1,0:T(8,128)(2,1)S(1)} collective-permute-done((bf16[2,96,768]{2,1,0:T(8,128)(2,1)S(1)}, bf16[2,96,768]{2,1,0:T(8,128)(2,1)S(1)}, u32[]{:S(2)}, u32[]{:S(2)}) %collective-permute-start.40) | collective-permute-done | bytes 294944 | tf_op jit(solution)/shard_map/ppermute | solution.py:688
  542.3 3.1 collective-permute-done.47
  545.6 3.0 collective-permute-done.34
  555.2 2.3 collective-permute-done.42
  557.5 1.6 collective-permute-done.49
  559.9 2.5 slice_bitcast_fusion
  (231 shorter events, 67.4 us)
Async XLA Ops:
  1.7 7.8 %collective-permute-start = (bf16[96,768]{1,0:T(8,128)(2,1)S(1)}, bf16[96,768]{1,0:T(8,128)(2,1)S(1)}, u32[]{:S(2)}, u32[]{:S(2)}) collective-permute-start(bf16[96,768]{1,0:T(8,128)(2,1)S(1)} %fusion.1), channel_id=1, source_target_pairs={{0,8},{1,9},{2,10},{3,11},{4,12},{5,13},{6,14},{7,15},{8,0},{9,1},... | collective-permute-start | bytes 442376 | tf_op jit(solution)/shard_map/ppermute | solution.py:688
  4.8 7.8 %collective-permute-start.5 = (bf16[96,768]{1,0:T(8,128)(2,1)S(1)}, bf16[96,768]{1,0:T(8,128)(2,1)S(1)}, u32[]{:S(2)}, u32[]{:S(2)}) collective-permute-start(bf16[96,768]{1,0:T(8,128)(2,1)S(1)} %constant_dynamic-slice_fusion.1), channel_id=1, source_target_pairs={{0,8},{1,9},{2,10},{3,11},{4,12},{5,13},{6,14},{7,15},{8,0},{9,1},... | collective-permute-start | bytes 442376 | tf_op jit(solution)/shard_map/ppermute | solution.py:688
  5.9 9.1 %collective-permute-start.10 = (bf16[96,768]{1,0:T(8,128)(2,1)S(1)}, bf16[96,768]{1,0:T(8,128)(2,1)S(1)}, u32[]{:S(2)}, u32[]{:S(2)}) collective-permute-start(bf16[96,768]{1,0:T(8,128)(2,1)S(1)} %constant_dynamic-slice_fusion), channel_id=1, source_target_pairs={{0,8},{1,9},{2,10},{3,11},{4,12},{5,13},{6,14},{7,15},{8,0},{9,1},... | collective-permute-start | bytes 442376 | tf_op jit(solution)/shard_map/ppermute | solution.py:688
  7.9 42.7 %copy-start.29 = (pred[2]{0:T(512)(128)(4,1)}, pred[2]{0:T(512)(128)(4,1)S(1)}, u32[]{:S(2)}) copy-start(pred[2]{0:T(512)(128)(4,1)S(1)} %iota_compare_fusion) | copy-start | bytes 10
  15.1 29.1 %collective-permute-start.1 = (bf16[2,96,768]{2,1,0:T(8,128)(2,1)S(1)}, bf16[2,96,768]{2,1,0:T(8,128)(2,1)S(1)}, u32[]{:S(2)}, u32[]{:S(2)}) collective-permute-start(bf16[2,96,768]{2,1,0:T(8,128)(2,1)S(1)} %get-tuple-element.94), channel_id=1, source_target_pairs={{0,16},{1,17},{2,18},{3,19},{4,20},{5,21},{6,22},{7,23},{8,24},{9,... | collective-permute-start | bytes 884744 | tf_op jit(solution)/shard_map/ppermute | solution.py:688
  17.9 32.6 %collective-permute-start.11 = (bf16[2,96,768]{2,1,0:T(8,128)(2,1)S(1)}, bf16[2,96,768]{2,1,0:T(8,128)(2,1)S(1)}, u32[]{:S(2)}, u32[]{:S(2)}) collective-permute-start(bf16[2,96,768]{2,1,0:T(8,128)(2,1)S(1)} %get-tuple-element.92), channel_id=1, source_target_pairs={{0,16},{1,17},{2,18},{3,19},{4,20},{5,21},{6,22},{7,23},{8,24},{9,... | collective-permute-start | bytes 884744 | tf_op jit(solution)/shard_map/ppermute | solution.py:688
  18.1 37.8 %collective-permute-start.6 = (bf16[2,96,768]{2,1,0:T(8,128)(2,1)S(1)}, bf16[2,96,768]{2,1,0:T(8,128)(2,1)S(1)}, u32[]{:S(2)}, u32[]{:S(2)}) collective-permute-start(bf16[2,96,768]{2,1,0:T(8,128)(2,1)S(1)} %get-tuple-element.93), channel_id=1, source_target_pairs={{0,16},{1,17},{2,18},{3,19},{4,20},{5,21},{6,22},{7,23},{8,24},{9,... | collective-permute-start | bytes 884744 | tf_op jit(solution)/shard_map/ppermute | solution.py:688
  20.9 37.3 %copy-start.31 = (pred[2]{0:T(512)(128)(4,1)}, pred[2]{0:T(512)(128)(4,1)S(1)}, u32[]{:S(2)}) copy-start(pred[2]{0:T(512)(128)(4,1)S(1)} %iota_compare_fusion.1) | copy-start | bytes 10
  56.1 29.0 %copy-start.9 = (bf16[2,2,96,768]{3,2,1,0:T(8,128)(2,1)}, bf16[2,2,96,768]{3,2,1,0:T(8,128)(2,1)S(1)}, u32[]{:S(2)}) copy-start(bf16[2,2,96,768]{3,2,1,0:T(8,128)(2,1)S(1)} %get-tuple-element.91) | copy-start | bytes 1769476
  56.1 16.3 %collective-permute-start.12 = (bf16[2,2,96,768]{3,2,1,0:T(8,128)(2,1)S(1)}, bf16[2,2,96,768]{3,2,1,0:T(8,128)(2,1)S(1)}, u32[]{:S(2)}, u32[]{:S(2)}) collective-permute-start(bf16[2,2,96,768]{3,2,1,0:T(8,128)(2,1)S(1)} %get-tuple-element.89), channel_id=1, source_target_pairs={{0,4},{1,5},{2,6},{3,7},{4,0},{5,1},{6,2},{7,3},{8,12},{9,13},{10,... | collective-permute-start | bytes 1769480 | tf_op jit(solution)/shard_map/ppermute | solution.py:688
  57.6 27.5 %collective-permute-start.2 = (bf16[2,2,96,768]{3,2,1,0:T(8,128)(2,1)S(1)}, bf16[2,2,96,768]{3,2,1,0:T(8,128)(2,1)S(1)}, u32[]{:S(2)}, u32[]{:S(2)}) collective-permute-start(bf16[2,2,96,768]{3,2,1,0:T(8,128)(2,1)S(1)} %get-tuple-element.91), channel_id=1, source_target_pairs={{0,4},{1,5},{2,6},{3,7},{4,0},{5,1},{6,2},{7,3},{8,12},{9,13},{10,... | collective-permute-start | bytes 1769480 | tf_op jit(solution)/shard_map/ppermute | solution.py:688
  58.2 37.7 %collective-permute-start.7 = (bf16[2,2,96,768]{3,2,1,0:T(8,128)(2,1)S(1)}, bf16[2,2,96,768]{3,2,1,0:T(8,128)(2,1)}, u32[]{:S(2)}, u32[]{:S(2)}) collective-permute-start(bf16[2,2,96,768]{3,2,1,0:T(8,128)(2,1)S(1)} %get-tuple-element.90), channel_id=1, source_target_pairs={{0,4},{1,5},{2,6},{3,7},{4,0},{5,1},{6,2},{7,3},{8,12},{9,13},{10,... | collective-permute-start | bytes 1769480 | tf_op jit(solution)/shard_map/ppermute | solution.py:688
  98.9 54.3 %copy-start.7 = (bf16[2,2,2,96,768]{4,3,2,1,0:T(8,128)(2,1)}, bf16[2,2,2,96,768]{4,3,2,1,0:T(8,128)(2,1)S(1)}, u32[]{:S(2)}) copy-start(bf16[2,2,2,96,768]{4,3,2,1,0:T(8,128)(2,1)S(1)} %get-tuple-element.86) | copy-start | bytes 3538948
  98.9 54.3 %copy-start.8 = (bf16[2,2,2,96,768]{4,3,2,1,0:T(8,128)(2,1)}, bf16[2,2,2,96,768]{4,3,2,1,0:T(8,128)(2,1)S(1)}, u32[]{:S(2)}) copy-start(bf16[2,2,2,96,768]{4,3,2,1,0:T(8,128)(2,1)S(1)} %get-tuple-element.87) | copy-start | bytes 3538948
  98.9 29.0 %collective-permute-start.13 = (bf16[2,2,2,96,768]{4,3,2,1,0:T(8,128)(2,1)S(1)}, bf16[2,2,2,96,768]{4,3,2,1,0:T(8,128)(2,1)}, u32[]{:S(2)}, u32[]{:S(2)}) collective-permute-start(bf16[2,2,2,96,768]{4,3,2,1,0:T(8,128)(2,1)S(1)} %get-tuple-element.86), channel_id=1, source_target_pairs={{0,2},{1,3},{2,0},{3,1},{4,6},{5,7},{6,4},{7,5},{8,10},{9,11},{10,... | collective-permute-start | bytes 3538952 | tf_op jit(solution)/shard_map/ppermute | solution.py:688
  100.1 53.1 %collective-permute-start.3 = (bf16[2,2,2,96,768]{4,3,2,1,0:T(8,128)(2,1)}, bf16[2,2,2,96,768]{4,3,2,1,0:T(8,128)(2,1)}, u32[]{:S(2)}, u32[]{:S(2)}) collective-permute-start(bf16[2,2,2,96,768]{4,3,2,1,0:T(8,128)(2,1)} %get-tuple-element.88), channel_id=1, source_target_pairs={{0,2},{1,3},{2,0},{3,1},{4,6},{5,7},{6,4},{7,5},{8,10},{9,11},{10,... | collective-permute-start | bytes 3538952 | tf_op jit(solution)/shard_map/ppermute | solution.py:688
  100.9 74.7 %collective-permute-start.8 = (bf16[2,2,2,96,768]{4,3,2,1,0:T(8,128)(2,1)S(1)}, bf16[2,2,2,96,768]{4,3,2,1,0:T(8,128)(2,1)}, u32[]{:S(2)}, u32[]{:S(2)}) collective-permute-start(bf16[2,2,2,96,768]{4,3,2,1,0:T(8,128)(2,1)S(1)} %get-tuple-element.87), channel_id=1, source_target_pairs={{0,2},{1,3},{2,0},{3,1},{4,6},{5,7},{6,4},{7,5},{8,10},{9,11},{10,... | collective-permute-start | bytes 3538952 | tf_op jit(solution)/shard_map/ppermute | solution.py:688
  180.4 13.1 %copy-start.19 = (f32[768]{0:T(1024)S(1)}, f32[768]{0:T(1024)}, u32[]{:S(2)}) copy-start(f32[768]{0:T(1024)} %param.34) | copy-start | bytes 9220
  180.4 13.8 %copy-start.20 = (f32[768]{0:T(1024)S(1)}, f32[768]{0:T(1024)}, u32[]{:S(2)}) copy-start(f32[768]{0:T(1024)} %param.38) | copy-start | bytes 9220
  180.5 42.2 %collective-permute-start.4 = (bf16[2,2,2,2,96,768]{5,4,3,2,1,0:T(8,128)(2,1)}, bf16[2,2,2,2,96,768]{5,4,3,2,1,0:T(8,128)(2,1)}, u32[]{:S(2)}, u32[]{:S(2)}) collective-permute-start(bf16[2,2,2,2,96,768]{5,4,3,2,1,0:T(8,128)(2,1)} %get-tuple-element.85), channel_id=1, source_target_pairs={{0,1},{1,0},{2,3},{3,2},{4,5},{5,4},{6,7},{7,6},{8,9},{9,8},{10,11... | collective-permute-start | bytes 7077896 | tf_op jit(solution)/shard_map/ppermute | solution.py:688
  180.5 42.1 %collective-permute-start.9 = (bf16[2,2,2,2,96,768]{5,4,3,2,1,0:T(8,128)(2,1)S(1)}, bf16[2,2,2,2,96,768]{5,4,3,2,1,0:T(8,128)(2,1)}, u32[]{:S(2)}, u32[]{:S(2)}) collective-permute-start(bf16[2,2,2,2,96,768]{5,4,3,2,1,0:T(8,128)(2,1)S(1)} %get-tuple-element.84), channel_id=1, source_target_pairs={{0,1},{1,0},{2,3},{3,2},{4,5},{5,4},{6,7},{7,6},{8,9},{9,8},{10,11... | collective-permute-start | bytes 7077896 | tf_op jit(solution)/shard_map/ppermute | solution.py:688
  181.0 36.6 %all-to-all-start = ((bf16[8,96,768]{2,1,0:T(8,128)(2,1)}), bf16[8,96,768]{2,1,0:T(8,128)(2,1)}, u32[]{:S(2)}, u32[]{:S(2)}) async-start(bf16[8,96,768]{2,1,0:T(8,128)(2,1)} %param.20), calls=%async_computation | async-start | bytes 2359296 | tf_op jit(solution)/shard_map/all_to_all | solution.py:819
  188.8 78.1 %collective-permute-start.14 = (bf16[2,2,2,2,96,768]{5,4,3,2,1,0:T(8,128)(2,1)}, bf16[2,2,2,2,96,768]{5,4,3,2,1,0:T(8,128)(2,1)}, u32[]{:S(2)}, u32[]{:S(2)}) collective-permute-start(bf16[2,2,2,2,96,768]{5,4,3,2,1,0:T(8,128)(2,1)} %get-tuple-element.83), channel_id=1, source_target_pairs={{0,1},{1,0},{2,3},{3,2},{4,5},{5,4},{6,7},{7,6},{8,9},{9,8},{10,11... | collective-permute-start | bytes 7077896 | tf_op jit(solution)/shard_map/ppermute | solution.py:688
  189.0 40.9 %copy-start.33 = (pred[4]{0:T(512)(128)(4,1)}, pred[4]{0:T(512)(128)(4,1)S(1)}, u32[]{:S(2)}) copy-start(pred[4]{0:T(512)(128)(4,1)S(1)} %broadcast_in_dim.589) | copy-start | bytes 16
  362.8 2.9 collective-permute-start.15
  367.2 15.4 %collective-permute-start.16 = (bf16[2,2,2,48,768]{4,3,2,1,0:T(8,128)(2,1)S(1)}, bf16[2,2,2,48,768]{4,3,2,1,0:T(8,128)(2,1)S(1)}, u32[]{:S(2)}, u32[]{:S(2)}) collective-permute-start(bf16[2,2,2,48,768]{4,3,2,1,0:T(8,128)(2,1)S(1)} %dynamic-slice_bitcast_fusion.10), channel_id=1, source_target_pairs={{0,2},{1,3},{2,0},{3,1},{4,6},{5,7},{6,4},{7,5},{8,10},{9,11},{10,... | collective-permute-start | bytes 1769480 | tf_op jit(solution)/shard_map/ppermute | solution.py:688
  381.5 54.8 %collective-permute-start.30 = (bf16[2,2,2,2,96,768]{5,4,3,2,1,0:T(8,128)(2,1)}, bf16[2,2,2,2,96,768]{5,4,3,2,1,0:T(8,128)(2,1)}, u32[]{:S(2)}, u32[]{:S(2)}) collective-permute-start(bf16[2,2,2,2,96,768]{5,4,3,2,1,0:T(8,128)(2,1)} %dynamic-slice_bitcast_fusion.2), channel_id=1, source_target_pairs={{0,1},{1,0},{2,3},{3,2},{4,5},{5,4},{6,7},{7,6},{8,9},{9,8},{10,11... | collective-permute-start | bytes 7077896 | tf_op jit(solution)/shard_map/ppermute | solution.py:688
  382.7 12.0 %collective-permute-start.17 = (bf16[2,2,48,768]{3,2,1,0:T(8,128)(2,1)S(1)}, bf16[2,2,48,768]{3,2,1,0:T(8,128)(2,1)S(1)}, u32[]{:S(2)}, u32[]{:S(2)}) collective-permute-start(bf16[2,2,48,768]{3,2,1,0:T(8,128)(2,1)S(1)} %dynamic-slice_bitcast_fusion.14), channel_id=1, source_target_pairs={{0,4},{1,5},{2,6},{3,7},{4,0},{5,1},{6,2},{7,3},{8,12},{9,13},{10,... | collective-permute-start | bytes 884744 | tf_op jit(solution)/shard_map/ppermute | solution.py:688
  385.8 3.8 collective-permute-start.25
  389.1 58.2 %collective-permute-start.37 = (bf16[2,2,2,2,96,768]{5,4,3,2,1,0:T(8,128)(2,1)}, bf16[2,2,2,2,96,768]{5,4,3,2,1,0:T(8,128)(2,1)}, u32[]{:S(2)}, u32[]{:S(2)}) collective-permute-start(bf16[2,2,2,2,96,768]{5,4,3,2,1,0:T(8,128)(2,1)} %dynamic-slice_bitcast_fusion.1), channel_id=1, source_target_pairs={{0,1},{1,0},{2,3},{3,2},{4,5},{5,4},{6,7},{7,6},{8,9},{9,8},{10,11... | collective-permute-start | bytes 7077896 | tf_op jit(solution)/shard_map/ppermute | solution.py:688
  389.6 4.4 collective-permute-start.26
  394.0 4.4 collective-permute-start.27
  394.8 7.6 %collective-permute-start.18 = (bf16[2,48,768]{2,1,0:T(8,128)(2,1)S(1)}, bf16[2,48,768]{2,1,0:T(8,128)(2,1)S(1)}, u32[]{:S(2)}, u32[]{:S(2)}) collective-permute-start(bf16[2,48,768]{2,1,0:T(8,128)(2,1)S(1)} %dynamic-slice_bitcast_fusion.18), channel_id=1, source_target_pairs={{0,16},{1,17},{2,18},{3,19},{4,20},{5,21},{6,22},{7,23},{8,24},{9,... | collective-permute-start | bytes 442376 | tf_op jit(solution)/shard_map/ppermute | solution.py:688
  398.1 33.4 %copy-start.30 = (pred[2]{0:T(512)(128)(4,1)S(1)}, pred[2]{0:T(512)(128)(4,1)}, u32[]{:S(2)}) copy-start(pred[2]{0:T(512)(128)(4,1)} %copy-done.29) | copy-start | bytes 10
  398.1 60.0 %collective-permute-start.44 = (bf16[2,2,2,2,96,768]{5,4,3,2,1,0:T(8,128)(2,1)}, bf16[2,2,2,2,96,768]{5,4,3,2,1,0:T(8,128)(2,1)}, u32[]{:S(2)}, u32[]{:S(2)}) collective-permute-start(bf16[2,2,2,2,96,768]{5,4,3,2,1,0:T(8,128)(2,1)} %dynamic-slice_bitcast_fusion), channel_id=1, source_target_pairs={{0,1},{1,0},{2,3},{3,2},{4,5},{5,4},{6,7},{7,6},{8,9},{9,8},{10,11... | collective-permute-start | bytes 7077896 | tf_op jit(solution)/shard_map/ppermute | solution.py:688
  398.5 5.4 collective-permute-start.28
  402.4 10.1 %collective-permute-start.19 = (bf16[48,768]{1,0:T(8,128)(2,1)S(1)}, bf16[48,768]{1,0:T(8,128)(2,1)S(1)}, u32[]{:S(2)}, u32[]{:S(2)}) collective-permute-start(bf16[48,768]{1,0:T(8,128)(2,1)S(1)} %dynamic-slice_bitcast_fusion.19), channel_id=1, source_target_pairs={{0,8},{1,9},{2,10},{3,11},{4,12},{5,13},{6,14},{7,15},{8,0},{9,1},... | collective-permute-start | bytes 221192 | tf_op jit(solution)/shard_map/ppermute | solution.py:688
  403.9 7.3 %collective-permute-start.29 = (f32[19,768]{1,0:T(8,128)S(1)}, f32[19,768]{1,0:T(8,128)S(1)}, u32[]{:S(2)}, u32[]{:S(2)}) collective-permute-start(f32[19,768]{1,0:T(8,128)S(1)} %add.180), channel_id=1, source_target_pairs={{0,16},{1,17},{2,18},{3,19},{4,20},{5,21},{6,22},{7,23},{8,24},{9,... | collective-permute-start | bytes 175112 | tf_op jit(solution)/shard_map/ppermute | solution.py:688
  407.0 55.3 %all-to-all-start.1 = ((bf16[8,96,768]{2,1,0:T(8,128)(2,1)}), bf16[8,96,768]{2,1,0:T(8,128)(2,1)}, u32[]{:S(2)}, u32[]{:S(2)}) async-start(bf16[8,96,768]{2,1,0:T(8,128)(2,1)} %bitcast.12), calls=%async_computation.1 | async-start | bytes 2359296 | tf_op jit(solution)/shard_map/all_to_all | solution.py:859
  412.6 18.9 %collective-permute-start.20 = (bf16[48,768]{1,0:T(8,128)(2,1)S(1)}, bf16[48,768]{1,0:T(8,128)(2,1)S(1)}, u32[]{:S(2)}, u32[]{:S(2)}) collective-permute-start(bf16[48,768]{1,0:T(8,128)(2,1)S(1)} %bitcast_add_fusion.19), channel_id=1, source_target_pairs={{0,8},{1,9},{2,10},{3,11},{4,12},{5,13},{6,14},{7,15},{8,0},{9,1},... | collective-permute-start | bytes 221192 | tf_op jit(solution)/shard_map/ppermute | solution.py:688
  431.6 14.2 %collective-permute-start.21 = (bf16[2,48,768]{2,1,0:T(8,128)(2,1)S(1)}, bf16[2,48,768]{2,1,0:T(8,128)(2,1)S(1)}, u32[]{:S(2)}, u32[]{:S(2)}) collective-permute-start(bf16[2,48,768]{2,1,0:T(8,128)(2,1)S(1)} %broadcast_select_fusion.20), channel_id=1, source_target_pairs={{0,16},{1,17},{2,18},{3,19},{4,20},{5,21},{6,22},{7,23},{8,24},{9,... | collective-permute-start | bytes 442376 | tf_op jit(solution)/shard_map/ppermute | solution.py:688
  438.9 19.2 %slice-start = ((s8[4718592]{0:T(1024)(128)(4,1)}), s8[4194304]{0:T(1024)(128)(4,1)S(1)}, s32[]{:S(2)}) async-start(s8[4718592]{0:T(1024)(128)(4,1)} %bitcast.144), calls=%async_computation.2 | async-start | bytes 8388608
  440.0 42.2 %collective-permute-start.31 = (bf16[2,2,2,96,768]{4,3,2,1,0:T(8,128)(2,1)}, bf16[2,2,2,96,768]{4,3,2,1,0:T(8,128)(2,1)}, u32[]{:S(2)}, u32[]{:S(2)}) collective-permute-start(bf16[2,2,2,96,768]{4,3,2,1,0:T(8,128)(2,1)} %dynamic-slice_bitcast_fusion.5), channel_id=1, source_target_pairs={{0,2},{1,3},{2,0},{3,1},{4,6},{5,7},{6,4},{7,5},{8,10},{9,11},{10,... | collective-permute-start | bytes 3538952 | tf_op jit(solution)/shard_map/ppermute | solution.py:688
  445.9 7.6 %collective-permute-start.22 = (bf16[2,2,48,768]{3,2,1,0:T(8,128)(2,1)S(1)}, bf16[2,2,48,768]{3,2,1,0:T(8,128)(2,1)S(1)}, u32[]{:S(2)}, u32[]{:S(2)}) collective-permute-start(bf16[2,2,48,768]{3,2,1,0:T(8,128)(2,1)S(1)} %broadcast_select_fusion.16), channel_id=1, source_target_pairs={{0,4},{1,5},{2,6},{3,7},{4,0},{5,1},{6,2},{7,3},{8,12},{9,13},{10,... | collective-permute-start | bytes 884744 | tf_op jit(solution)/shard_map/ppermute | solution.py:688
  453.6 28.1 %collective-permute-start.23 = (bf16[2,2,2,48,768]{4,3,2,1,0:T(8,128)(2,1)S(1)}, bf16[2,2,2,48,768]{4,3,2,1,0:T(8,128)(2,1)S(1)}, u32[]{:S(2)}, u32[]{:S(2)}) collective-permute-start(bf16[2,2,2,48,768]{4,3,2,1,0:T(8,128)(2,1)S(1)} %broadcast_select_fusion.9), channel_id=1, source_target_pairs={{0,2},{1,3},{2,0},{3,1},{4,6},{5,7},{6,4},{7,5},{8,10},{9,11},{10,... | collective-permute-start | bytes 1769480 | tf_op jit(solution)/shard_map/ppermute | solution.py:688
  456.3 29.0 %collective-permute-start.38 = (bf16[2,2,2,96,768]{4,3,2,1,0:T(8,128)(2,1)}, bf16[2,2,2,96,768]{4,3,2,1,0:T(8,128)(2,1)}, u32[]{:S(2)}, u32[]{:S(2)}) collective-permute-start(bf16[2,2,2,96,768]{4,3,2,1,0:T(8,128)(2,1)} %dynamic-slice_bitcast_fusion.4), channel_id=1, source_target_pairs={{0,4},{1,5},{2,6},{3,7},{4,0},{5,1},{6,2},{7,3},{8,12},{9,13},{10,... | collective-permute-start | bytes 3538952 | tf_op jit(solution)/shard_map/ppermute | solution.py:688
  461.8 45.3 %collective-permute-start.45 = (bf16[2,2,2,96,768]{4,3,2,1,0:T(8,128)(2,1)}, bf16[2,2,2,96,768]{4,3,2,1,0:T(8,128)(2,1)}, u32[]{:S(2)}, u32[]{:S(2)}) collective-permute-start(bf16[2,2,2,96,768]{4,3,2,1,0:T(8,128)(2,1)} %dynamic-slice_bitcast_fusion.3), channel_id=1, source_target_pairs={{0,2},{1,3},{2,0},{3,1},{4,6},{5,7},{6,4},{7,5},{8,10},{9,11},{10,... | collective-permute-start | bytes 3538952 | tf_op jit(solution)/shard_map/ppermute | solution.py:688
  481.9 72.9 %collective-permute-start.24 = (bf16[2,2,2,2,48,768]{5,4,3,2,1,0:T(8,128)(2,1)S(1)}, bf16[2,2,2,2,48,768]{5,4,3,2,1,0:T(8,128)(2,1)S(1)}, u32[]{:S(2)}, u32[]{:S(2)}) collective-permute-start(bf16[2,2,2,2,48,768]{5,4,3,2,1,0:T(8,128)(2,1)S(1)} %broadcast_select_fusion.5), channel_id=1, source_target_pairs={{0,1},{1,0},{2,3},{3,2},{4,5},{5,4},{6,7},{7,6},{8,9},{9,8},{10,11... | collective-permute-start | bytes 3538952 | tf_op jit(solution)/shard_map/ppermute | solution.py:688
  483.8 23.3 %copy-start.5 = (bf16[2,2,2,2,96,768]{5,4,3,2,1,0:T(8,128)(2,1)S(1)}, bf16[2,2,2,2,96,768]{5,4,3,2,1,0:T(8,128)(2,1)}, u32[]{:S(2)}) copy-start(bf16[2,2,2,2,96,768]{5,4,3,2,1,0:T(8,128)(2,1)} %copy-done.4) | copy-start | bytes 7077892
  483.8 26.3 %collective-permute-start.32 = (bf16[2,2,96,768]{3,2,1,0:T(8,128)(2,1)S(1)}, bf16[2,2,96,768]{3,2,1,0:T(8,128)(2,1)S(1)}, u32[]{:S(2)}, u32[]{:S(2)}) collective-permute-start(bf16[2,2,96,768]{3,2,1,0:T(8,128)(2,1)S(1)} %dynamic-slice_bitcast_fusion.9), channel_id=1, source_target_pairs={{0,4},{1,5},{2,6},{3,7},{4,0},{5,1},{6,2},{7,3},{8,12},{9,13},{10,... | collective-permute-start | bytes 1769480 | tf_op jit(solution)/shard_map/ppermute | solution.py:688
  486.8 29.9 %collective-permute-start.39 = (bf16[2,2,96,768]{3,2,1,0:T(8,128)(2,1)S(1)}, bf16[2,2,96,768]{3,2,1,0:T(8,128)(2,1)S(1)}, u32[]{:S(2)}, u32[]{:S(2)}) collective-permute-start(bf16[2,2,96,768]{3,2,1,0:T(8,128)(2,1)S(1)} %dynamic-slice_bitcast_fusion.8), channel_id=1, source_target_pairs={{0,2},{1,3},{2,0},{3,1},{4,6},{5,7},{6,4},{7,5},{8,10},{9,11},{10,... | collective-permute-start | bytes 1769480 | tf_op jit(solution)/shard_map/ppermute | solution.py:688
  508.6 9.9 %collective-permute-start.46 = (bf16[2,2,96,768]{3,2,1,0:T(8,128)(2,1)S(1)}, bf16[2,2,96,768]{3,2,1,0:T(8,128)(2,1)S(1)}, u32[]{:S(2)}, u32[]{:S(2)}) collective-permute-start(bf16[2,2,96,768]{3,2,1,0:T(8,128)(2,1)S(1)} %dynamic-slice_bitcast_fusion.7), channel_id=1, source_target_pairs={{0,4},{1,5},{2,6},{3,7},{4,0},{5,1},{6,2},{7,3},{8,12},{9,13},{10,... | collective-permute-start | bytes 1769480 | tf_op jit(solution)/shard_map/ppermute | solution.py:688
  510.2 25.5 %collective-permute-start.33 = (bf16[2,96,768]{2,1,0:T(8,128)(2,1)S(1)}, bf16[2,96,768]{2,1,0:T(8,128)(2,1)S(1)}, u32[]{:S(2)}, u32[]{:S(2)}) collective-permute-start(bf16[2,96,768]{2,1,0:T(8,128)(2,1)S(1)} %dynamic-slice_bitcast_fusion.13), channel_id=1, source_target_pairs={{0,16},{1,17},{2,18},{3,19},{4,20},{5,21},{6,22},{7,23},{8,24},{9,... | collective-permute-start | bytes 884744 | tf_op jit(solution)/shard_map/ppermute | solution.py:688
  516.8 25.3 %collective-permute-start.40 = (bf16[2,96,768]{2,1,0:T(8,128)(2,1)S(1)}, bf16[2,96,768]{2,1,0:T(8,128)(2,1)S(1)}, u32[]{:S(2)}, u32[]{:S(2)}) collective-permute-start(bf16[2,96,768]{2,1,0:T(8,128)(2,1)S(1)} %dynamic-slice_bitcast_fusion.12), channel_id=1, source_target_pairs={{0,16},{1,17},{2,18},{3,19},{4,20},{5,21},{6,22},{7,23},{8,24},{9,... | collective-permute-start | bytes 884744 | tf_op jit(solution)/shard_map/ppermute | solution.py:688
  518.7 26.8 %collective-permute-start.47 = (bf16[2,96,768]{2,1,0:T(8,128)(2,1)S(1)}, bf16[2,96,768]{2,1,0:T(8,128)(2,1)S(1)}, u32[]{:S(2)}, u32[]{:S(2)}) collective-permute-start(bf16[2,96,768]{2,1,0:T(8,128)(2,1)S(1)} %dynamic-slice_bitcast_fusion.11), channel_id=1, source_target_pairs={{0,16},{1,17},{2,18},{3,19},{4,20},{5,21},{6,22},{7,23},{8,24},{9,... | collective-permute-start | bytes 884744 | tf_op jit(solution)/shard_map/ppermute | solution.py:688
  535.8 12.7 %collective-permute-start.34 = (bf16[96,768]{1,0:T(8,128)(2,1)S(1)}, bf16[96,768]{1,0:T(8,128)(2,1)S(1)}, u32[]{:S(2)}, u32[]{:S(2)}) collective-permute-start(bf16[96,768]{1,0:T(8,128)(2,1)S(1)} %dynamic-slice_bitcast_fusion.17), channel_id=1, source_target_pairs={{0,8},{1,9},{2,10},{3,11},{4,12},{5,13},{6,14},{7,15},{8,0},{9,1},... | collective-permute-start | bytes 442376 | tf_op jit(solution)/shard_map/ppermute | solution.py:688
  542.2 9.4 %collective-permute-start.41 = (bf16[96,768]{1,0:T(8,128)(2,1)S(1)}, bf16[96,768]{1,0:T(8,128)(2,1)S(1)}, u32[]{:S(2)}, u32[]{:S(2)}) collective-permute-start(bf16[96,768]{1,0:T(8,128)(2,1)S(1)} %dynamic-slice_bitcast_fusion.16), channel_id=1, source_target_pairs={{0,8},{1,9},{2,10},{3,11},{4,12},{5,13},{6,14},{7,15},{8,0},{9,1},... | collective-permute-start | bytes 442376 | tf_op jit(solution)/shard_map/ppermute | solution.py:688
  545.5 7.7 %collective-permute-start.48 = (bf16[96,768]{1,0:T(8,128)(2,1)S(1)}, bf16[96,768]{1,0:T(8,128)(2,1)S(1)}, u32[]{:S(2)}, u32[]{:S(2)}) collective-permute-start(bf16[96,768]{1,0:T(8,128)(2,1)S(1)} %dynamic-slice_bitcast_fusion.15), channel_id=1, source_target_pairs={{0,8},{1,9},{2,10},{3,11},{4,12},{5,13},{6,14},{7,15},{8,0},{9,1},... | collective-permute-start | bytes 442376 | tf_op jit(solution)/shard_map/ppermute | solution.py:688
  548.6 6.6 %collective-permute-start.35 = (bf16[96,768]{1,0:T(8,128)(2,1)S(1)}, bf16[96,768]{1,0:T(8,128)(2,1)S(1)}, u32[]{:S(2)}, u32[]{:S(2)}) collective-permute-start(bf16[96,768]{1,0:T(8,128)(2,1)S(1)} %bitcast_add_fusion.17), channel_id=1, source_target_pairs={{0,2},{1,3},{2,0},{3,1},{4,6},{5,7},{6,4},{7,5},{8,10},{9,11},{10,... | collective-permute-start | bytes 442376 | tf_op jit(solution)/shard_map/ppermute | solution.py:688
  551.7 5.9 %collective-permute-start.42 = (bf16[96,768]{1,0:T(8,128)(2,1)S(1)}, bf16[96,768]{1,0:T(8,128)(2,1)S(1)}, u32[]{:S(2)}, u32[]{:S(2)}) collective-permute-start(bf16[96,768]{1,0:T(8,128)(2,1)S(1)} %bitcast_add_fusion.16), channel_id=1, source_target_pairs={{0,2},{1,3},{2,0},{3,1},{4,6},{5,7},{6,4},{7,5},{8,10},{9,11},{10,... | collective-permute-start | bytes 442376 | tf_op jit(solution)/shard_map/ppermute | solution.py:688
  553.3 5.9 %collective-permute-start.49 = (bf16[96,768]{1,0:T(8,128)(2,1)S(1)}, bf16[96,768]{1,0:T(8,128)(2,1)S(1)}, u32[]{:S(2)}, u32[]{:S(2)}) collective-permute-start(bf16[96,768]{1,0:T(8,128)(2,1)S(1)} %bitcast_add_fusion.15), channel_id=1, source_target_pairs={{0,2},{1,3},{2,0},{3,1},{4,6},{5,7},{6,4},{7,5},{8,10},{9,11},{10,... | collective-permute-start | bytes 442376 | tf_op jit(solution)/shard_map/ppermute | solution.py:688
  559.3 3.2 collective-permute-start.36
  559.4 3.1 collective-permute-start.43
  562.4 3.2 collective-permute-start.50
  (27 other events, 167.3 us)

commit v2 on v1

v2 whole, which is shorter than its diff:
```python
import functools

import jax
import jax.numpy as jnp
from jax import lax
from jax.experimental import pallas as pl
from jax.experimental.pallas import tpu as pltpu
from jax.sharding import PartitionSpec as P

D = 768
HEADS = 12
HD = 64
RPS = 4
RD = 8
PAD = 16
PART = D // 2
LANES = 128
CHUNK = 256
FB = 256
EPS = 1e-6
NEG = -1e30
F32 = jnp.float32
BF16 = jnp.bfloat16
AXES = ("mod", "rep")
SCALE = HD ** (-0.5)
VMEM = pl.BlockSpec(memory_space=pltpu.VMEM)
SMEM = pl.BlockSpec(memory_space=pltpu.SMEM)
ANY = pl.BlockSpec(memory_space=pl.ANY)


def nn(left, right):
    return lax.dot_general(left, right, (((1,), (0,)), ((), ())), preferred_element_type=F32)


def nt(left, right):
    return lax.dot_general(left, right, (((1,), (1,)), ((), ())), preferred_element_type=F32)


def tn(left, right):
    return lax.dot_general(left, right, (((0,), (0,)), ((), ())), preferred_element_type=F32)


def line(vector):
    return vector[...].reshape(1, -1)


def chunks(rows):
    count = rows // CHUNK
    return [
        (i * CHUNK, (rows - i * CHUNK) if i == count - 1 else CHUNK) for i in range(count)
    ]


def normalise(rows):
    mean = jnp.mean(rows, axis=-1, keepdims=True)
    centred = rows - mean
    var = jnp.mean(centred * centred, axis=-1, keepdims=True)
    rstd = lax.rsqrt(var + EPS)
    return centred * rstd, rstd


def norm_input_grad(xhat, rstd, gain, upstream):
    scaled = upstream * gain
    first = jnp.mean(scaled, axis=-1, keepdims=True)
    second = jnp.mean(scaled * xhat, axis=-1, keepdims=True)
    return rstd * (scaled - first - xhat * second)


def call(kernel, out_shape, deps=(), **kw):
    limit = kw.pop("vmem", 56)
    estimate = kw.pop("cost", None)
    in_specs = kw.pop("in_specs")
    count, more = len(in_specs), len(deps)

    def body(*refs):
        kernel(*refs[:count], *refs[count + more :])

    built = pl.pallas_call(
        body,
        out_shape=out_shape,
        in_specs=list(in_specs) + [ANY] * more,
        cost_estimate=estimate,
        compiler_params=pltpu.CompilerParams(vmem_limit_bytes=limit * 1024 * 1024),
        **kw,
    )
    return lambda *args: built(*args, *deps)


def cost(us):
    return pl.CostEstimate(flops=int(us * 1.15e9), bytes_accessed=1 << 20, transcendentals=0)


def struct(shape, dtype):
    return jax.ShapeDtypeStruct(shape, dtype)


def live_of(index, counts, read, block_rows):
    groups_n = counts.shape[1]
    capacity = groups_n * block_rows
    live = index < 0
    for s in range(groups_n):
        live = live | ((index >= s * block_rows) & (index < s * block_rows + counts[0, s]))
    slot = index - capacity
    return live | ((slot >= 0) & (slot < RD) & (slot % RPS < read[0, 0]))


def place_bits(place, places):
    if places == 1:
        return 0
    return (place >> 2) + 2 * (place & 3)


def place_of(bits):
    return ((bits & 1) << 2) | (bits >> 1)


def fetch(ids, arrays, want, target, sem):
    places, rows = arrays[0].shape[0], arrays[0].shape[1]
    for k in range(4):

        @pl.when((ids[0] ^ k) == want)
        def _():
            fetch_array(ids, arrays[k], target, sem)


def fetch_array(ids, array, target, sem):
    places, rows = array.shape[0], array.shape[1]
    for place in range(places):
        shard = ids[1] ^ place_bits(place, places)
        start = pl.multiple_of(shard * rows, 16)
        pltpu.make_async_copy(array.at[place], target.at[pl.ds(start, rows), :], sem).start()


def fetched(target, sem):
    pltpu.make_async_copy(target, target, sem).wait()


def stem_kernel(cut, raw, wp, bp, wl, bl, table, gain, bias, stream, normed):
    capacity = raw.shape[0]
    step = capacity // 4
    for start in range(0, capacity, step):
        weight, shift = (wp, bp) if start < cut else (wl, bl)
        rows = pl.ds(start, step)
        embedded = (nn(raw[rows, :], weight[...]) + line(shift)).astype(BF16).astype(F32)
        stream[rows, :] = embedded
        xhat, _ = normalise(embedded)
        normed[rows, :] = (xhat * line(gain) + line(bias)).astype(BF16)
    tail = jnp.concatenate([table[...], jnp.zeros((PAD - RD, D), F32)], axis=0)
    stream[pl.ds(capacity, PAD), :] = tail
    xhat, _ = normalise(tail)
    normed[pl.ds(capacity, PAD), :] = (xhat * line(gain) + line(bias)).astype(BF16)


def stems(raw, wp, bp, wl, bl, table, gain, bias):
    capacity = raw.shape[0]
    total = capacity + PAD
    return call(
        functools.partial(stem_kernel, 3 * capacity // 4),
        (struct((total, D), F32), struct((total, D), BF16)),
        in_specs=[VMEM] * 8,
        out_specs=(VMEM, VMEM),
        cost=cost(5),
    )(raw, wp, bp, wl, bl, table, gain, bias)


def qkv_kernel(ids, rows, w0, w1, w2, w3, out, buffer, sem):
    for r in range(3):
        fetch(ids, (w0, w1, w2, w3), r, buffer.at[r], sem.at[r])
    for r in range(3):
        fetched(buffer.at[r], sem.at[r])
        for start, size in chunks(rows.shape[0]):
            out[r, pl.ds(start, size), :] = nn(rows[pl.ds(start, size), :], buffer[r]).astype(BF16)


def project_qkv(ids, normed, weights, deps=()):
    total = normed.shape[0]
    return call(
        qkv_kernel,
        struct((3, total, D), BF16),
        deps,
        in_specs=[SMEM, VMEM, ANY, ANY, ANY, ANY],
        out_specs=VMEM,
        scratch_shapes=[pltpu.VMEM((3, D, D), BF16), pltpu.SemaphoreType.DMA((3,))],
        cost=cost(7),
    )(ids, normed, *weights)


def visible_readout(group_row, live_row):
    capacity = group_row.shape[1]
    query = lax.broadcasted_iota(jnp.int32, (RD, capacity), 0)
    group = 2 * (query // RPS + 1) + 1
    keys = group_row[...]
    seen = live_row & (keys <= group) & ((keys % 2 == 0) | (keys == group))
    return jnp.where(seen, 0.0, NEG)


def visible_between(read):
    query = lax.broadcasted_iota(jnp.int32, (RD, PAD), 0)
    key = lax.broadcasted_iota(jnp.int32, (RD, PAD), 1)
    live = (key < RD) & (key % RPS < read[0, 0])
    seen = (query == key) | (live & (query // RPS == key // RPS))
    return jnp.where(seen, 0.0, NEG)


def tiled(rows, heads):
    return jnp.concatenate([rows] * heads, axis=0)


def own_head(heads):
    row = lax.broadcasted_iota(jnp.int32, (heads * RD, heads * HD), 0) // RD
    lane = lax.broadcasted_iota(jnp.int32, (heads * RD, heads * HD), 1) // HD
    return row == lane


def fold_heads(stack, mine):
    kept = jnp.where(mine, stack, 0.0)
    total = kept[:RD]
    for start in range(RD, stack.shape[0], RD):
        total = total + kept[start : start + RD]
    return jnp.concatenate([total, jnp.zeros((PAD - RD, stack.shape[1]), F32)], axis=0)


def attend_kernel(
    block_rows, qkv, counts, read, group_row, group_col, mixed, lse, lse_read, mask, lse_cols, tail
):
    step = pl.program_id(0)
    capacity = group_row.shape[1]

    @pl.when(step == 0)
    def _():
        slot_row = lax.broadcasted_iota(jnp.int32, (1, capacity), 1)
        live_row = live_of(slot_row, counts, read, block_rows)
        keys = group_row[...]
        for start in range(0, capacity, CHUNK):
            query = lax.broadcasted_iota(jnp.int32, (CHUNK, capacity), 0) + start
            group = group_col[pl.ds(start, CHUNK), :]
            seen = live_row & (keys <= group) & ((keys % 2 == 0) | (keys == group))
            seen = seen | (query == slot_row)
            mask[pl.ds(start, CHUNK), :] = jnp.where(seen, 0.0, NEG)
        lse_cols[...] = jnp.zeros_like(lse_cols)
        mine = own_head(HEADS)
        tail_rows = pl.ds(capacity, PAD)
        head_rows = pl.ds(0, capacity)
        query = qkv[0, tail_rows, :].astype(F32)[:RD] * SCALE
        query = jnp.where(mine, tiled(query, HEADS), 0.0).astype(BF16)
        far = nt(query, qkv[1, head_rows, :]) + tiled(visible_readout(group_row, live_row), HEADS)
        near = nt(query, qkv[1, tail_rows, :]) + tiled(visible_between(read), HEADS)
        peak = jnp.maximum(
            jnp.max(far, axis=1, keepdims=True), jnp.max(near, axis=1, keepdims=True)
        )
        far = jnp.exp(far - peak)
        near = jnp.exp(near - peak)
        total = jnp.sum(far, axis=1, keepdims=True) + jnp.sum(near, axis=1, keepdims=True)
        out = nn(far.astype(BF16), qkv[2, head_rows, :]) + nn(
            near.astype(BF16), qkv[2, tail_rows, :]
        )
        tail[...] = fold_heads(out / total, mine)
        lse_read[...] = jnp.broadcast_to(peak + jnp.log(total), lse_read.shape)

    lane = lax.broadcasted_iota(jnp.int32, (1, LANES), 1)
    columns = pl.ds(pl.multiple_of(step * LANES, LANES), LANES)
    keys = qkv[1, pl.ds(0, capacity), columns]
    values = qkv[2, pl.ds(0, capacity), columns]
    for start in range(0, capacity, CHUNK):
        rows = pl.ds(start, CHUNK)
        query = qkv[0, rows, columns] * SCALE
        outs = []
        logs = lse_cols[rows, :]
        for head in range(2):
            chosen = jnp.where(lane // HD == head, query, jnp.zeros_like(query))
            scores = nt(chosen.astype(BF16), keys) + mask[rows, :]
            peak = jnp.max(scores, axis=1, keepdims=True)
            weight = jnp.exp(scores - peak)
            total = jnp.sum(weight, axis=1, keepdims=True)
            outs.append(nn(weight.astype(BF16), values) / total)
            logs = jnp.where(lane == 2 * step + head, peak + jnp.log(total), logs)
        mixed[rows, :] = jnp.where(lane < HD, outs[0], outs[1]).astype(BF16)
        lse_cols[rows, :] = logs
    mixed[pl.ds(capacity, PAD), :] = tail[:, columns].astype(BF16)

    @pl.when(step == pl.num_programs(0) - 1)
    def _():
        lse[...] = lse_cols[...].T[: lse.shape[0], :]


def attend(qkv, counts, read, group_row, group_col, block_rows, deps=()):
    total = qkv.shape[1]
    capacity = total - PAD
    pairs = HEADS // 2
    return call(
        functools.partial(attend_kernel, block_rows),
        (
            struct((total, D), BF16),
            struct((16, capacity), F32),
            struct((HEADS * RD, LANES), F32),
        ),
        deps,
        grid=(pairs,),
        in_specs=[VMEM, SMEM, SMEM, VMEM, VMEM],
        out_specs=(pl.BlockSpec((total, LANES), lambda j: (0, j)), VMEM, VMEM),
        scratch_shapes=[
            pltpu.VMEM((capacity, capacity), F32),
            pltpu.VMEM((capacity, LANES), F32),
            pltpu.VMEM((PAD, D), F32),
        ],
        cost=cost(21),
    )(qkv, counts, read, group_row, group_col)


def attend_back_kernel(
    block_rows,
    part,
    qkv,
    mixed,
    grad,
    lse,
    lse_read,
    counts,
    read,
    group_row,
    group_col,
    out,
    mask,
    delta,
    key_more,
    value_more,
    tails,
):
    step = pl.program_id(0)
    capacity = group_row.shape[1]
    tail_rows = pl.ds(capacity, PAD)
    head_rows = pl.ds(0, capacity)
    heads = PART // HD
    mine_columns = pl.ds(part * PART, PART)

    @pl.when(step == 0)
    def _():
        slot_row = lax.broadcasted_iota(jnp.int32, (1, capacity), 1)
        group = group_row[...]
        for start in range(0, capacity, CHUNK):
            slot = lax.broadcasted_iota(jnp.int32, (CHUNK, 1), 0) + start
            live = live_of(slot, counts, read, block_rows)
            keys = group_col[pl.ds(start, CHUNK), :]
            seen = live & (keys <= group) & ((keys % 2 == 0) | (keys == group))
            seen = seen | (slot == slot_row)
            mask[pl.ds(start, CHUNK), :] = jnp.where(seen, 0.0, NEG)
        head = lax.broadcasted_iota(jnp.int32, (8, PART), 0)
        column = lax.broadcasted_iota(jnp.int32, (8, PART), 1)
        select = jnp.where(column // HD == head, 1.0, 0.0).astype(BF16)
        for start in range(0, capacity, CHUNK):
            rows = pl.ds(start, CHUNK)
            product = grad[rows, mine_columns].astype(F32) * mixed[rows, mine_columns].astype(F32)
            high = product.astype(BF16)
            low = (product - high.astype(F32)).astype(BF16)
            delta[:, rows] = nt(select, high) + nt(select, low)

        live_row = live_of(slot_row, counts, read, block_rows)
        mine = own_head(heads)
        query = qkv[0, tail_rows, mine_columns].astype(F32)[:RD] * SCALE
        query = jnp.where(mine, tiled(query, heads), 0.0).astype(BF16)
        upper = grad[tail_rows, mine_columns].astype(F32)[:RD]
        upper = jnp.where(mine, tiled(upper, heads), 0.0)
        result = tiled(mixed[tail_rows, mine_columns].astype(F32)[:RD], heads)
        row_delta = jnp.sum(upper * result, axis=1, keepdims=True)
        upper = upper.astype(BF16)
        logs = lse_read[pl.ds(part * heads * RD, heads * RD), 0:1]
        far = nt(query, qkv[1, head_rows, mine_columns]) + tiled(visible_readout(group_row, live_row), heads)
        near = nt(query, qkv[1, tail_rows, mine_columns]) + tiled(visible_between(read), heads)
        far = jnp.exp(far - logs)
        near = jnp.exp(near - logs)
        far_grad = (far * (nt(upper, qkv[2, head_rows, mine_columns]) - row_delta)).astype(BF16)
        near_grad = (near * (nt(upper, qkv[2, tail_rows, mine_columns]) - row_delta)).astype(BF16)
        query_grad = nn(far_grad, qkv[1, head_rows, mine_columns]) + nn(near_grad, qkv[1, tail_rows, mine_columns])
        tails[0] = fold_heads(query_grad, mine) * SCALE
        tails[1] = tn(near_grad, query)
        tails[2] = tn(near.astype(BF16), upper)
        key_more[...] = tn(far_grad, query)
        value_more[...] = tn(far.astype(BF16), upper)

    lane = lax.broadcasted_iota(jnp.int32, (1, LANES), 1)
    columns = pl.ds(pl.multiple_of(step * LANES, LANES), LANES)
    here = pl.ds(pl.multiple_of(part * PART + step * LANES, LANES), LANES)
    query = (qkv[0, head_rows, here] * SCALE).astype(BF16)
    upper = grad[head_rows, here]
    query_grad = jnp.zeros((capacity, LANES), F32)
    for start in range(0, capacity, CHUNK):
        rows = pl.ds(start, CHUNK)
        all_keys = qkv[1, rows, here]
        all_values = qkv[2, rows, here]
        key_parts = []
        value_parts = []
        for head in range(2):
            own = lane // HD == head
            keys = jnp.where(own, all_keys, jnp.zeros_like(all_keys))
            values = jnp.where(own, all_values, jnp.zeros_like(all_values))
            logs = lse[pl.ds(part * heads + 2 * step + head, 1), :]
            row_delta = delta[pl.ds(2 * step + head, 1), :]
            probs = jnp.exp(nt(keys, query) + mask[rows, :] - logs)
            score_grad = (probs * (nt(values, upper) - row_delta)).astype(BF16)
            value_parts.append(nn(probs.astype(BF16), upper))
            key_parts.append(nn(score_grad, query))
            query_grad = query_grad + tn(score_grad, keys)
        key_grad = jnp.where(lane < HD, key_parts[0], key_parts[1]) + key_more[rows, columns]
        value_grad = jnp.where(lane < HD, value_parts[0], value_parts[1]) + value_more[rows, columns]
        out[1, rows, :] = key_grad.astype(BF16)
        out[2, rows, :] = value_grad.astype(BF16)
    out[0, head_rows, :] = (query_grad * SCALE).astype(BF16)
    for part in range(3):
        out[part, tail_rows, :] = tails[part, :, columns].astype(BF16)


def attend_back(
    qkv, mixed, grad, lse, lse_read, counts, read, group_row, group_col, block_rows, part,
    deps=()
):
    total = qkv.shape[1]
    capacity = total - PAD
    pairs = PART // LANES
    return call(
        functools.partial(attend_back_kernel, block_rows, part),
        struct((3, total, PART), BF16),
        deps,
        grid=(pairs,),
        in_specs=[VMEM, VMEM, VMEM, VMEM, VMEM, SMEM, SMEM, VMEM, VMEM],
        out_specs=pl.BlockSpec((3, total, LANES), lambda j: (0, 0, j)),
        scratch_shapes=[
            pltpu.VMEM((capacity, capacity), F32),
            pltpu.VMEM((8, capacity), F32),
            pltpu.VMEM((capacity, PART), F32),
            pltpu.VMEM((capacity, PART), F32),
            pltpu.VMEM((3, PAD, PART), F32),
        ],
        cost=cost(15),
    )(qkv, mixed, grad, lse, lse_read, counts, read, group_row, group_col)


def out_kernel(ids, mixed, w0, w1, w2, w3, stream, gain, bias, after, normed, buffer, sem):
    fetch(ids, (w0, w1, w2, w3), 3, buffer, sem)
    fetched(buffer, sem)
    for start, size in chunks(mixed.shape[0]):
        rows = pl.ds(start, size)
        value = stream[rows, :] + nn(mixed[rows, :], buffer[...])
        after[rows, :] = value
        xhat, _ = normalise(value)
        normed[rows, :] = (xhat * line(gain) + line(bias)).astype(BF16)


def out_project(ids, mixed, weights, stream, gain, bias, deps=()):
    total = mixed.shape[0]
    return call(
        out_kernel,
        (struct((total, D), F32), struct((total, D), BF16)),
        deps,
        in_specs=[SMEM, VMEM, ANY, ANY, ANY, ANY, VMEM, VMEM, VMEM],
        out_specs=(VMEM, VMEM),
        scratch_shapes=[pltpu.VMEM((D, D), BF16), pltpu.SemaphoreType.DMA],
        cost=cost(6.4),
    )(ids, mixed, *weights, stream, gain, bias)


def out_back_kernel(
    ids, inner, after, branch, gain, w0, w1, w2, w3, grad, grad_low, mixed_grad, sums, buffer, sem
):
    fetch(ids, (w0, w1, w2, w3), 3, buffer, sem)
    fetched(buffer, sem)
    gain_sum = jnp.zeros((1, D), F32)
    bias_sum = jnp.zeros((1, D), F32)
    for start, size in chunks(inner.shape[0]):
        rows = pl.ds(start, size)
        upstream = inner[rows, :]
        xhat, rstd = normalise(after[rows, :])
        gain_sum = gain_sum + jnp.sum(upstream * xhat, axis=0, keepdims=True)
        bias_sum = bias_sum + jnp.sum(upstream, axis=0, keepdims=True)
        total = branch[rows, :].astype(F32) + norm_input_grad(xhat, rstd, line(gain), upstream)
        grad[rows, :] = total
        low = total.astype(BF16)
        grad_low[rows, :] = low
        mixed_grad[rows, :] = nt(low, buffer[...]).astype(BF16)
    sums[0:1, :] = gain_sum
    sums[1:2, :] = bias_sum


def out_back(ids, inner, after, branch, gain, weights, deps=()):
    total = inner.shape[0]
    return call(
        out_back_kernel,
        (
            struct((total, D), F32),
            struct((total, D), BF16),
            struct((total, D), BF16),
            struct((2, D), F32),
        ),
        deps,
        in_specs=[SMEM, VMEM, VMEM, VMEM, VMEM, ANY, ANY, ANY, ANY],
        out_specs=(VMEM, VMEM, VMEM, VMEM),
        scratch_shapes=[pltpu.VMEM((D, D), BF16), pltpu.SemaphoreType.DMA],
        cost=cost(8.5),
    )(ids, inner, after, branch, gain, *weights)


def prepare_kernel(block_rows, cotangent, counts, read, branch, bias_grad):
    total, slots = branch.shape[0], cotangent.shape[0]
    index = lax.broadcasted_iota(jnp.int32, (total, 1), 0)
    live = jnp.where(live_of(index, counts, read, block_rows), 1.0, 0.0)
    upstream = cotangent[...].astype(F32) * live[:slots]
    bias_grad[...] = jnp.sum(upstream, axis=0, keepdims=True)
    upstream = jnp.concatenate([upstream, jnp.zeros((total - slots, D), F32)], axis=0)
    branch[...] = upstream.astype(BF16)


def prepare(cotangent, counts, read, block_rows, total):
    return call(
        functools.partial(prepare_kernel, block_rows),
        (struct((total, D), BF16), struct((1, D), F32)),
        in_specs=[VMEM, SMEM, SMEM],
        out_specs=(VMEM, VMEM),
        cost=cost(3),
    )(cotangent, counts, read)


def mlp_kernel(
    block_rows,
    ks,
    first,
    last,
    slots,
    *refs,
):
    nk = len(ks)
    ids, counts, read, normed, branch, up_bias, down_bias, total_in, inner_in, sums_in = refs[:10]
    weights = refs[10 : 10 + 2 * nk]
    active, hidden_grad, total, inner, sums = refs[10 + 2 * nk : 15 + 2 * nk]
    up, down, sem = refs[-3:]
    step = pl.program_id(0)
    index = step // (D // FB)
    part = step % (D // FB)
    length = normed.shape[0]

    @pl.when(step == 0)
    def _():
        for i in range(nk):
            fetch_array(ids, weights[2 * i], up.at[i], sem.at[i, 0])
            fetch_array(ids, weights[2 * i + 1], down.at[i], sem.at[i, 1])
        sums[...] = sums_in[...]
        if first:
            total[...] = total_in[...] + line(down_bias)
            inner[...] = jnp.zeros_like(inner)
        else:
            total[...] = total_in[...]
            inner[...] = inner_in[...]

    @pl.when(part == 0)
    def _():
        fetched(up.at[index], sem.at[index, 0])
        fetched(down.at[index], sem.at[index, 1])

    columns = pl.ds(pl.multiple_of(part * FB, FB), FB)
    rank = ids[0] ^ ks[0]
    for i in range(1, nk):
        rank = jnp.where(index == i, ids[0] ^ ks[i], rank)
    up_part = up[index, :, columns]
    down_part = down[index, columns, :]
    shift = up_bias[pl.ds(rank, 1), columns]
    bias_sum = jnp.zeros((1, FB), F32)
    for start, size in chunks(length):
        rows = pl.ds(start, size)
        hidden = nn(normed[rows, :], up_part) + shift
        factor = (2.0 / jnp.pi) ** 0.5
        square = hidden * hidden
        bent = jnp.tanh(hidden * (factor + (factor * 0.044715) * square))
        half = 0.5 * (1.0 + bent)
        act = (hidden * half).astype(BF16)
        slope = half + (0.5 * hidden) * (1.0 - bent * bent) * (
            factor + (3.0 * factor * 0.044715) * square
        )
        back = (nt(branch[rows, :], down_part) * slope).astype(BF16)
        bias_sum = bias_sum + jnp.sum(back.astype(F32), axis=0, keepdims=True)
        active[0, rows, :] = act
        hidden_grad[0, rows, :] = back
        total[rows, :] += nn(act, down_part)
        inner[rows, :] += nt(back, up_part)
    sums[pl.ds(rank, 1), columns] = bias_sum

    if last:

        @pl.when(step == pl.num_programs(0) - 1)
        def _():
            at = lax.broadcasted_iota(jnp.int32, (length, 1), 0)
            live = jnp.where(live_of(at, counts, read, block_rows), 1.0, 0.0)
            total[...] = total[...] * live


def mlp(ids, ks, counts, read, normed, branch, up_bias, down_bias, state, weights, block_rows, slots, first, last, deps=()):
    total = normed.shape[0]
    nk = len(ks)
    per = D // FB
    whole = pl.BlockSpec((total, D), lambda j: (0, 0))
    vectors = pl.BlockSpec((4, D), lambda j: (0, 0))
    block = pl.BlockSpec((1, total, FB), lambda j: (j // per, 0, j % per))
    flat = [w for pair in weights for w in pair]
    return call(
        functools.partial(mlp_kernel, block_rows, ks, first, last, slots),
        (
            struct((nk, total, D), BF16),
            struct((nk, total, D), BF16),
            struct((total, D), F32),
            struct((total, D), F32),
            struct((4, D), F32),
        ),
        deps,
        grid=(nk * per,),
        in_specs=[SMEM, SMEM, SMEM, whole, whole, vectors, VMEM, whole, whole, vectors]
        + [ANY] * (2 * nk),
        out_specs=(block, block, whole, whole, vectors),
        scratch_shapes=[
            pltpu.VMEM((nk, D, D), BF16),
            pltpu.VMEM((nk, D, D), BF16),
            pltpu.SemaphoreType.DMA((nk, 2)),
        ],
        cost=cost(20),
    )(ids, counts, read, normed, branch, up_bias, down_bias, *state, *flat)


def put_rows(ids, value, first_row, places, store):
    rows = D // places
    for i in range(value.shape[0] // rows):
        bits = ids[1] ^ (first_row // rows + i)
        store(place_of(bits) if places > 1 else 0, value[i * rows : (i + 1) * rows])


def product_rows(ids, left, right, places, store):
    block = D // 2 if places > 1 else D
    for start in range(0, D, block):
        value = tn(left[:, start : start + block], right[...])
        put_rows(ids, value, start, places, store)


def to_give_kernel(places, count, ids, *refs):
    lefts, rights, out = refs[:count], refs[count : 2 * count], refs[2 * count]
    for i in range(count):

        def store(place, rows, i=i):
            out[i, pl.ds(place, 1)] = rows.astype(BF16)[None]

        product_rows(ids, lefts[i], rights[i], places, store)


def to_keep_kernel(places, y_first, ids, left0, right0, left2, right2, got0, got2, keep, give):
    half = max(places // 2, 1)
    for x, (left, right) in enumerate(((left0, right0), (left2, right2))):

        def store(place, rows, x=x):
            got = (got0, got2)[x]
            summed = (rows + got[pl.ds(place, 1)][0].astype(F32)).astype(BF16)[None]
            y, z = place // half, place % half
            if y_first:

                @pl.when(y == 0)
                def _():
                    keep[x, pl.ds(z, 1)] = summed

                @pl.when(y == 1)
                def _():
                    give[x, pl.ds(z, 1)] = summed
            else:
                (give if x else keep)[y, pl.ds(z, 1)] = summed

        product_rows(ids, left, right, places, store)


def column_spec(total):
    return pl.BlockSpec((total, D), lambda i: (0, 0))


def act_spec(total, index):
    return pl.BlockSpec((None, total, D), lambda i: (index, 0, 0))


def give_products(ids, pairs, specs, places, deps=()):
    count = len(pairs)
    total = pairs[0][0].shape[-2]
    rows = D // places
    return call(
        functools.partial(to_give_kernel, places, count),
        struct((count, places, rows, D), BF16),
        deps,
        grid=(1,),
        in_specs=[SMEM] + [s[0] for s in specs] + [s[1] for s in specs],
        out_specs=pl.BlockSpec((count, places, rows, D), lambda i: (0, 0, 0, 0)),
        cost=cost(6.5),
    )(ids, *[p[0] for p in pairs], *[p[1] for p in pairs])


def keep_products(ids, pairs, specs, got, index, places, y_first, deps=()):
    total = pairs[0][0].shape[-2]
    rows = D // places
    half = struct((2, max(places // 2, 1), rows, D), BF16)
    half_spec = pl.BlockSpec((2, max(places // 2, 1), rows, D), lambda i: (0, 0, 0, 0))
    return call(
        functools.partial(to_keep_kernel, places, y_first),
        (half, half),
        deps,
        grid=(1,),
        in_specs=[
            SMEM,
            specs[0][0],
            specs[0][1],
            specs[1][0],
            specs[1][1],
            pl.BlockSpec((None, places, rows, D), lambda i: (index, 0, 0, 0)),
            pl.BlockSpec((None, places, rows, D), lambda i: (index, 0, 0, 0)),
        ],
        out_specs=(half_spec, half_spec),
        cost=cost(8),
    )(ids, pairs[0][0], pairs[0][1], pairs[1][0], pairs[1][1], *got)


def first_fetch(ids, k, part, normed, mixed, grads, attn_grad, left, right, sem):
    rank = ids[0] ^ k

    @pl.when(rank < 3)
    def _():
        pltpu.make_async_copy(normed, left, sem.at[0]).start()
        pltpu.make_async_copy(grads.at[rank], right, sem.at[1]).start()

    @pl.when(rank == 3)
    def _():
        pltpu.make_async_copy(mixed, left, sem.at[0]).start()
        pltpu.make_async_copy(attn_grad.at[:, pl.ds(part * PART, PART)], right, sem.at[1]).start()


def first_give_kernel(places, part, ids, normed, mixed, grads, attn_grad, out, left, right, sem):
    ks = (1, 3)
    sources = (normed, mixed, grads, attn_grad)
    for i, k in enumerate(ks):
        first_fetch(ids, k, part, *sources, left.at[i], right.at[i], sem.at[i])
    for i, k in enumerate(ks):
        fetched(left.at[i], sem.at[i, 0])
        fetched(right.at[i], sem.at[i, 1])

        def store(place, rows, i=i):
            out[i, pl.ds(place, 1)] = rows.astype(BF16)[None]

        product_rows(ids, left.at[i], right.at[i], places, store)


def first_scratch(total):
    return [
        pltpu.VMEM((2, total, D), BF16),
        pltpu.VMEM((2, total, PART), BF16),
        pltpu.SemaphoreType.DMA((2, 2)),
    ]


def first_give(ids, part, normed, mixed, grads, attn_grad, places, deps=()):
    total = normed.shape[0]
    return call(
        functools.partial(first_give_kernel, places, part),
        struct((2, places, D // places, PART), BF16),
        deps,
        in_specs=[SMEM, ANY, ANY, ANY, ANY],
        out_specs=VMEM,
        scratch_shapes=first_scratch(total),
        cost=cost(5),
    )(ids, normed, mixed, grads, attn_grad)


def first_keep_kernel(
    places, part, y_first, ids, normed, mixed, grads, attn_grad, got, keep, give, left, right, sem
):
    sources = (normed, mixed, grads, attn_grad)
    for i, k in enumerate((0, 2)):
        first_fetch(ids, k, part, *sources, left.at[i], right.at[i], sem.at[i])
    for i in range(2):
        fetched(left.at[i], sem.at[i, 0])
        fetched(right.at[i], sem.at[i, 1])
    to_keep_kernel(
        places, y_first, ids, left.at[0], right.at[0], left.at[1], right.at[1], got.at[0], got.at[1],
        keep, give
    )


def first_keep(ids, part, normed, mixed, grads, attn_grad, got, places, y_first, deps=()):
    total = normed.shape[0]
    half = struct((2, max(places // 2, 1), D // places, PART), BF16)
    return call(
        functools.partial(first_keep_kernel, places, part, y_first),
        (half, half),
        deps,
        in_specs=[SMEM, ANY, ANY, ANY, ANY, VMEM],
        out_specs=(VMEM, VMEM),
        scratch_shapes=first_scratch(total),
        cost=cost(6),
    )(ids, normed, mixed, grads, attn_grad, got)


def qkv_back_kernel(capacity, ids, grads0, grads1, *refs):
    stream, gain, after_grad, embedded, readout, sums, buffer, sem = refs[4:]
    for r in range(3):
        fetch(ids, refs[:4], r, buffer.at[r], sem.at[r])
    for r in range(3):
        fetched(buffer.at[r], sem.at[r])
    gain_sum = jnp.zeros((1, D), F32)
    bias_sum = jnp.zeros((1, D), F32)
    for start, size in chunks(stream.shape[0]):
        rows = pl.ds(start, size)
        upstream = jnp.zeros((size, D), F32)
        for r in range(3):
            grad = jnp.concatenate([grads0[r, rows, :], grads1[r, rows, :]], axis=1)
            upstream = upstream + nt(grad, buffer[r])
        xhat, rstd = normalise(stream[rows, :])
        gain_sum = gain_sum + jnp.sum(upstream * xhat, axis=0, keepdims=True)
        bias_sum = bias_sum + jnp.sum(upstream, axis=0, keepdims=True)
        total = after_grad[rows, :] + norm_input_grad(xhat, rstd, line(gain), upstream)
        inside = min(size, capacity - start)
        embedded[pl.ds(start, inside), :] = total[:inside].astype(BF16)
        if start + size > capacity:
            readout[...] = total[capacity - start : capacity - start + RD]
    sums[0:1, :] = gain_sum
    sums[1:2, :] = bias_sum


def qkv_back(ids, grads, weights, stream, gain, after_grad, deps=()):
    total = stream.shape[0]
    capacity = total - PAD
    return call(
        functools.partial(qkv_back_kernel, capacity),
        (struct((capacity, D), BF16), struct((RD, D), F32), struct((2, D), F32)),
        deps,
        in_specs=[SMEM, VMEM, VMEM] + [ANY] * 4 + [VMEM, VMEM, VMEM],
        out_specs=(VMEM, VMEM, VMEM),
        scratch_shapes=[pltpu.VMEM((3, D, D), BF16), pltpu.SemaphoreType.DMA((3,))],
        cost=cost(10),
    )(ids, *grads, *weights, stream, gain, after_grad)


def stem_back_kernel(cut, places, ids, raw, embedded, keep, give, sums):
    for stem, part in enumerate((slice(0, cut), slice(cut, None))):
        sums[stem : stem + 1, :] = jnp.sum(embedded[part, :].astype(F32), axis=0, keepdims=True)
        value = tn(raw[part, :], embedded[part, :]).astype(BF16)
        if places == 1:
            (give if stem else keep)[...] = value.reshape(keep.shape)
            continue
        rows = D // places // 2
        mine = (ids[0] & 1) == stem
        for i in range(2 * places):
            place = place_of(ids[1] ^ (i // 2))
            x = (i % 2) ^ (ids[0] >> 1)
            at = (x * 2 + (place >> 2)) * 4 + (place & 3)
            piece = value[i * rows : (i + 1) * rows][None]

            @pl.when(mine)
            def _():
                keep[pl.ds(at, 1)] = piece

            @pl.when(jnp.logical_not(mine))
            def _():
                give[pl.ds(at, 1)] = piece


def stem_back(ids, raw, embedded, places, deps=()):
    capacity = raw.shape[0]
    shape = (2 * places, D // (2 * places), D) if places > 1 else (1, D, D)
    return call(
        functools.partial(stem_back_kernel, 3 * capacity // 4, places),
        (struct(shape, BF16), struct(shape, BF16), struct((2, D), F32)),
        deps,
        in_specs=[SMEM, VMEM, VMEM],
        out_specs=(VMEM, VMEM, VMEM),
        cost=cost(6),
    )(ids, raw, embedded)


def stem_out_kernel(ids, own, other, patch, lang):
    rows = own.shape[1]
    for i in range(own.shape[0]):
        shard = ids[1] ^ place_bits(((i >> 2) & 1) * 4 + (i & 3), 8)
        x = (i >> 3) ^ (ids[0] >> 1)
        at = pl.ds(pl.multiple_of((shard * 2 + x) * rows, 16), rows)
        mine, theirs = own[i].astype(F32), other[i].astype(F32)

        @pl.when((ids[0] & 1) == 0)
        def _():
            patch[at, :] = mine
            lang[at, :] = theirs

        @pl.when((ids[0] & 1) == 1)
        def _():
            patch[at, :] = theirs
            lang[at, :] = mine


def stem_out(ids, own, other):
    return call(
        stem_out_kernel,
        (struct((D, D), F32), struct((D, D), F32)),
        in_specs=[SMEM, VMEM, VMEM],
        out_specs=(VMEM, VMEM),
        cost=cost(4.4),
    )(ids, own, other)


def raw_kernel(image, grad, wp, wl, out):
    @pl.when(image[0] != 0)
    def _():
        out[...] = nt(grad[...], wp[...])

    @pl.when(image[0] == 0)
    def _():
        out[...] = nt(grad[...], wl[...])


def raw_back(image, grad, wp, wl, deps=()):
    return call(
        raw_kernel,
        struct(grad.shape, F32),
        deps,
        in_specs=[SMEM, VMEM, VMEM, VMEM],
        out_specs=VMEM,
        cost=cost(4.6),
    )(image, grad, wp, wl)


def first_out_kernel(ids, k0, k2, k13, qkv, out, ranks):
    ranks[0], ranks[2], ranks[1], ranks[3] = k0[...], k2[...], k13[0], k13[1]
    for r in range(3):
        qkv[:, r * D : (r + 1) * D] = ranks[pl.ds(ids[0] ^ r, 1)][0].astype(F32)
    out[...] = ranks[pl.ds(ids[0] ^ 3, 1)][0].astype(F32)


def first_out(ids, k0, k2, k13):
    rows = k0.shape[0]
    return call(
        first_out_kernel,
        (struct((rows, 3 * D), F32), struct((rows, D), F32)),
        in_specs=[SMEM, VMEM, VMEM, VMEM],
        out_specs=(VMEM, VMEM),
        scratch_shapes=[pltpu.VMEM((4, rows, D), BF16)],
        cost=cost(2.3),
    )(ids, k0, k2, k13)


def mlp_out_kernel(places, ids, k0, k2, k13, up, down, ranks):
    ranks[0], ranks[2], ranks[1], ranks[3] = k0[...], k2[...], k13[0], k13[1]
    rows, unit = k0.shape[1], D // places
    for r in range(4):
        both = ranks[pl.ds(ids[0] ^ r, 1)][0]
        value = both[0].astype(F32)
        for s in range(places):
            start = (4 * s + r) * unit
            up[:, start : start + unit] = value[:, s * unit : (s + 1) * unit]
        down[r * rows : (r + 1) * rows, :] = both[1].astype(F32)


def mlp_out(ids, k0, k2, k13, places):
    rows = k0.shape[1]
    return call(
        functools.partial(mlp_out_kernel, places),
        (struct((rows, 4 * D), F32), struct((4 * rows, D), F32)),
        in_specs=[SMEM, VMEM, VMEM, VMEM],
        out_specs=(VMEM, VMEM),
        scratch_shapes=[pltpu.VMEM((4, 2, rows, D), BF16)],
        cost=cost(3.1),
    )(ids, k0, k2, k13)


class Grid:
    def __init__(self, mods, reps):
        self.mods, self.reps = mods, reps
        self.mod, self.rep = lax.axis_index("mod"), lax.axis_index("rep")

    def swap(self, value, mod=0, rep=0):
        pairs = [
            (m * self.reps + r, (m ^ mod) * self.reps + (r ^ rep))
            for m in range(self.mods)
            for r in range(self.reps)
        ]
        return lax.ppermute(value, AXES, pairs)


CORE, X, Y, Z0, Z1 = {"rep": 1}, {"rep": 2}, {"mod": 1}, {"mod": 2}, {"mod": 4}
Z01, XY = {"mod": 6}, {"rep": 2, "mod": 1}


def tie(value, *deps):
    return lax.optimization_barrier((value,) + deps)[0]


def joined(*parts):
    return jnp.concatenate(parts, axis=0)


def gather_z(grid, piece):
    parts = [piece] + [grid.swap(piece, **bit) for bit in (Z0, Z1, Z01)]
    return jnp.stack(parts)


def reduce_z(grid, parts):
    total = parts[0]
    for part, bit in zip(parts[1:], (Z0, Z1, Z01)):
        total = total + grid.swap(part, **bit)
    return total


def per_device(
    raw_rows,
    recv_counts,
    slot_groups,
    read_counts,
    patch_convolution_weight,
    patch_stem_bias_vector,
    language_projection_weight,
    language_bias_vector,
    readout_table,
    attn_gain,
    attn_bias,
    qkv_weight,
    out_weight,
    mlp_gain,
    mlp_bias,
    up_weight,
    up_bias,
    down_weight,
    down_bias,
    out_cotangent,
):
    mods, reps = lax.axis_size("mod"), lax.axis_size("rep")
    fast = mods == 8 and reps == 4
    places = mods if fast else 1
    grid = Grid(mods, reps)
    block_rows = raw_rows.shape[1]
    capacity = mods * block_rows
    total = capacity + PAD
    slots = out_cotangent.shape[1]
    units = up_bias.shape[0] // (4 * mods)
    image = (grid.mod < 3 * mods // 4).astype(jnp.int32).reshape(1)
    rank = grid.rep if fast else jnp.zeros((), jnp.int32)
    ids = jnp.stack([rank, grid.mod if fast else jnp.zeros((), jnp.int32)]).astype(jnp.int32)
    group_row = slot_groups
    group_col = slot_groups.reshape(capacity, 1)
    marks = (recv_counts, read_counts, group_row, group_col)

    by_rank = lambda w: w.reshape(w.shape[0], -1, 4, units).transpose(2, 0, 1, 3).reshape(4, -1, D)
    up_bias_rows = up_bias.reshape(-1, 4, units).transpose(1, 0, 2).reshape(4, D)

    if fast:
        piece = lax.dynamic_slice_in_dim(
            jnp.concatenate([qkv_weight, out_weight], axis=1), rank * D, D, 1
        )
        quarter = down_weight.shape[0] // 4
        piece_up = lax.dynamic_index_in_dim(
            up_weight.reshape(-1, mods, 4, units), rank, 2, keepdims=False
        ).reshape(-1, D)
        piece_down = lax.dynamic_slice_in_dim(down_weight, rank * quarter, quarter, 0)
        first_z = gather_z(grid, piece)
        up_z = gather_z(grid, tie(piece_up, first_z))
        raw_rows = tie(raw_rows, first_z)
    received = lax.all_to_all(raw_rows, "mod", split_axis=0, concat_axis=0, tiled=True)
    rows = received.reshape(capacity, D)
    branch, down_bias_grad = prepare(out_cotangent[0], recv_counts, read_counts, block_rows, total)
    if fast:
        first0 = joined(first_z, grid.swap(first_z, **Y))
        first2 = grid.swap(first0, **X)
        first1 = grid.swap(first0, **CORE)
        first3 = grid.swap(first2, **CORE)
        first = (first0, first1, first2, first3)
        up0 = joined(up_z, grid.swap(tie(up_z, first0), **Y))
        rows, up0 = lax.optimization_barrier((rows, up0))
    else:
        whole = lambda w: lax.all_gather(w, "mod", axis=0, tiled=True)
        every = jnp.concatenate([whole(qkv_weight), whole(out_weight)], axis=1)
        first = tuple(every[None, :, r * D : (r + 1) * D] for r in range(4))
        every = by_rank(whole(up_weight))
        up0, up1, up2, up3 = (every[r : r + 1] for r in range(4))
        every = whole(down_weight).reshape(mods, 4, units, D).transpose(1, 0, 2, 3)
        every = every.reshape(4, D, D)
        down0, down1, down2, down3 = (every[r : r + 1] for r in range(4))

    stream, normed = stems(
        rows,
        patch_convolution_weight,
        patch_stem_bias_vector,
        language_projection_weight,
        language_bias_vector,
        readout_table,
        attn_gain,
        attn_bias,
    )
    deps = ()
    if fast:
        down_z = gather_z(grid, tie(piece_down, rows))
        up2 = grid.swap(tie(up0, first2, rows), **X)
        deps = (down_z,)
    qkv = project_qkv(ids, normed, first)
    mixed, lse, lse_read = attend(qkv, *marks, block_rows, deps)
    deps = ()
    if fast:
        down0 = joined(down_z, grid.swap(tie(down_z, qkv), **Y))
        up1 = grid.swap(tie(up0, qkv), **CORE)
        deps = (down0, up1, up2)
    after, normed2 = out_project(ids, mixed, first, stream, mlp_gain, mlp_bias, deps)
    if fast:
        down2 = grid.swap(tie(down0, up2), **X)
        down1 = grid.swap(down0, **CORE)
        up3 = grid.swap(tie(up2, mixed), **CORE)
        deps = (up3,)
    sums = jnp.zeros((4, D), F32)
    step = lambda ks, state, weights, first_call, last_call, deps: mlp(
        ids, ks, recv_counts, read_counts, normed2, branch, up_bias_rows, down_bias, state,
        weights, block_rows, slots, first_call, last_call, deps,
    )
    active01, hidden01, outer, inner, sums = step(
        (0, 1), (after, after, sums), ((up0, down0), (up1, down1)), True, False, deps
    )
    spec = column_spec(total)
    at = [act_spec(total, i) for i in range(2)]
    deps = ()
    if fast:
        down3 = grid.swap(tie(down2, inner), **CORE)
    give1 = give_products(
        ids, [(normed2, hidden01), (active01, branch)], [(spec, at[1]), (at[1], spec)], places
    )
    active23, hidden23, outer, inner, sums = step(
        (2, 3), (outer, inner, sums), ((up2, down2), (up3, down3)), False, True, (give1,)
    )
    layer_out = outer[:slots].astype(BF16)[None]
    give3 = give_products(
        ids, [(normed2, hidden23), (active23, branch)], [(spec, at[1]), (at[1], spec)], places
    )
    if fast:
        got1, got3 = grid.swap(give1, **CORE), grid.swap(give3, **CORE)
    else:
        got1, got3 = jnp.zeros_like(give1), jnp.zeros_like(give3)
    after_grad, attn_grad, mixed_grad, mlp_sums = out_back(
        ids, inner, after, branch, mlp_gain, first, (give3,)
    )
    keep_down, give_down = keep_products(
        ids, [(active01, branch), (active23, branch)], [(at[0], spec)] * 2, (got1, got3), 1,
        places, False, (attn_grad,)
    )
    keep_up, give_up = keep_products(
        ids, [(normed2, hidden01), (normed2, hidden23)], [(spec, at[0])] * 2, (got1, got3), 0,
        places, True, (keep_down,)
    )
    grads_a = attend_back(
        qkv, mixed, mixed_grad, lse, lse_read, *marks, block_rows, 0, (keep_up,)
    )
    first_a13 = first_give(ids, 0, normed, mixed, grads_a, attn_grad, places)
    deps = (first_a13,)
    if fast:
        got = grid.swap(give_down, **X)
        down_y = (keep_down[0] + got[0], keep_down[1] + got[1])
        got = grid.swap(give_up, **Y)
        up_x = (keep_up[0] + got[0], keep_up[1] + got[1])
        got_a = grid.swap(first_a13, **CORE)
        deps = deps + down_y + up_x
    else:
        got_a = jnp.zeros_like(first_a13)
    grads_b = attend_back(
        qkv, mixed, mixed_grad, lse, lse_read, *marks, block_rows, 1, deps
    )
    deps = (grads_b,)
    if fast:
        got_up = grid.swap(tie(up_x[1], grads_a), **X)
        got_down = grid.swap(tie(down_y[1], grads_a), **Y)
        up_w = [up_x[0][i] + got_up[i] for i in range(4)]
        down_w = [down_y[0][i] + got_down[i] for i in range(4)]
        deps = deps + (got_up, got_down)
    keep_a, give_a = first_keep(
        ids, 0, normed, mixed, grads_a, attn_grad, got_a, places, False, deps
    )
    first_b13 = first_give(ids, 1, normed, mixed, grads_b, attn_grad, places, (keep_a,))
    deps = (first_b13,)
    if fast:
        got_b = grid.swap(first_b13, **CORE)
        deps = deps + (got_b,)
    else:
        got_b = jnp.zeros_like(first_b13)
    embedded_grad, readout_grad, attn_sums = qkv_back(
        ids, (grads_a, grads_b), first, stream, attn_gain, after_grad, deps
    )
    returned = lax.all_to_all(
        embedded_grad.reshape(raw_rows.shape), "mod", split_axis=0, concat_axis=0, tiled=True
    )
    deps = ()
    if fast:
        got = grid.swap(tie(give_a, first_b13), **X)
        own_a, pass_a = keep_a[0] + got[0], keep_a[1] + got[1]
        both = jnp.stack([reduce_z(grid, up_w), reduce_z(grid, down_w)])
        deps = (own_a, pass_a, both)
    stem_keep, stem_give, stem_sums = stem_back(ids, rows, embedded_grad, places, deps)
    keep_b, give_b = first_keep(
        ids, 1, normed, mixed, grads_b, attn_grad, got_b, places, False, (stem_keep,)
    )
    raw_grad = raw_back(
        image,
        returned.reshape(capacity, D),
        patch_convolution_weight,
        language_projection_weight,
    ).reshape(raw_rows.shape)

    small = jnp.concatenate(
        [stem_sums, attn_sums, mlp_sums, down_bias_grad, sums, readout_grad], axis=0
    )
    if fast:
        together = lambda *values: lax.optimization_barrier(values)
        got_y = grid.swap(tie(pass_a, stem_keep), **Y)
        got = grid.swap(stem_give, **CORE)
        got_small = grid.swap(small, **CORE)
        parts = [stem_keep[4 * i : 4 * i + 4] + got[4 * i : 4 * i + 4] for i in range(4)]
        small = small + got_small
        *parts, small, give_b, both = together(*parts, small, give_b, both)
        got = [grid.swap(part, **bit) for part, bit in zip(parts[1:], (Y, X, XY))]
        got_small = grid.swap(small, **X)
        got_x = grid.swap(give_b, **X)
        from_x = grid.swap(both, **X)
        parts = [parts[0][i] + got[0][i] + got[1][i] + got[2][i] for i in range(4)]
        small = small + got_small
        own_b, pass_b = keep_b[0] + got_x[0], keep_b[1] + got_x[1]
        own_a = own_a + got_y
        *parts, small, pass_b, own_b, own_a, from_x, returned_ = together(
            *parts, small, pass_b, own_b, own_a, from_x, returned
        )
        got_y = grid.swap(pass_b, **Y)
        got_small = grid.swap(small, **Y)
        from_core = grid.swap(jnp.stack([both, from_x]), **CORE)
        piece = reduce_z(grid, parts)
        small = small + got_small
        own_b = own_b + got_y
        lasts = [jnp.concatenate([own_a[i], own_b[i]], axis=1) for i in range(4)]
        piece, small, from_core, *lasts = together(piece, small, from_core, *lasts)
        got_small = grid.swap(small, **Z0)
        piece = gather_z(grid, piece)
        small = small + got_small
        last = reduce_z(grid, lasts)
        piece, small, last = together(piece, small, last)
        got_small = grid.swap(small, **Z1)
        last_x = grid.swap(last, **X)
        piece = joined(piece, *[grid.swap(piece, **bit) for bit in (Y, X, XY)])
        small = small + got_small
        piece, last_x = together(piece, last_x)
        last_core = grid.swap(jnp.stack([last, last_x]), **CORE)
        patch_sum, lang_sum = stem_out(ids, piece, grid.swap(piece, **CORE))
        up_sum, down_sum = mlp_out(ids, both, from_x, from_core, places)
        qkv_sum, out_sum = first_out(ids, last, last_x, last_core)
    else:
        reduced = lambda v: lax.psum(
            lax.psum_scatter(v, "mod", scatter_dimension=0, tiled=True), "rep"
        ).astype(F32)
        every = []
        for keep, other, give in ((keep_a, first_a13, give_a), (keep_b, first_b13, give_b)):
            every.append(jnp.stack([keep[0, 0], other[0, 0], give[0, 0], other[1, 0]], axis=1))
        every = reduced(jnp.concatenate(every, axis=2).reshape(D, -1))
        qkv_sum, out_sum = every[:, : 3 * D], every[:, 3 * D :]
        every = jnp.stack([keep_up[0, 0], give1[0, 0], keep_up[1, 0], give3[0, 0]])
        every = every.reshape(4, D, mods, units).transpose(1, 2, 0, 3).reshape(D, -1)
        up_sum = reduced(every)
        every = jnp.stack([keep_down[0, 0], give1[1, 0], give_down[0, 0], give3[1, 0]])
        every = every.reshape(4, mods, units, D).transpose(1, 0, 2, 3).reshape(-1, D)
        down_sum = reduced(every)
        small = lax.psum(small, AXES)
        patch_sum = lax.psum(stem_keep[0].astype(F32), AXES)
        lang_sum = lax.psum(stem_give[0].astype(F32), AXES)
    up_bias_sum = small[7:11].reshape(4, -1, units).transpose(1, 0, 2).reshape(-1)
    return (
        layer_out,
        raw_grad,
        patch_sum,
        small[0],
        lang_sum,
        small[1],
        small[11 : 11 + RD],
        small[2],
        small[3],
        qkv_sum,
        out_sum,
        small[4],
        small[5],
        up_sum,
        up_bias_sum,
        down_sum,
        small[6],
    )


def solution(mesh):
    both, rows, rep = P("mod", "rep", None), P("mod", None), P()
    pair = P("mod", "rep")
    return jax.shard_map(
        per_device,
        mesh=mesh,
        in_specs=(both, pair, pair, pair)
        + (rep,) * 7
        + (rows, rows, rep, rep, rows, rep, rows, rep, both),
        out_specs=(both, both)
        + (rep,) * 7
        + (rows, rows, rep, rep, rows, rep, rows, rep),
        check_vma=False,
    )
```

time: 570 us -> 467 us (0.82)
  waiting for transfers between devices: 283 us -> 137 us
  Pallas kernels: 142 us -> 207 us
  other arithmetic: 35.1 us -> 7.24 us
  starting transfers between devices: 65.9 us -> 87.5 us
  local copies, waits for them, and re-layouts: 38 us -> 23 us
    ppermute x51 -> x65, waiting for transfers between devices: 260 us -> 137 us  [swap(): return lax.ppermute(value, AXES, pairs)]
    pallas_call x11 -> x24, Pallas kernels: 142 us -> 207 us  [call(): return lambda *args: built(*args, *deps)]
    all_to_all x1, waiting for transfers between devices: 22.8 us -> 0.01 us  [per_device(): lax.all_to_all(raw_rows, 'mod', split_axis=0, concat_axis=0, tiled=True)]
    ppermute x51 -> x65, starting transfers between devices: 53.9 us -> 71.6 us  [swap(): return lax.ppermute(value, AXES, pairs)]
    select_n x12 -> x0, other arithmetic: 17.3 us -> none  [joined(): jnp.where(place, jnp.expand_dims(value, axis), jnp.expand_dims(other, axis))]
    squeeze x21 -> x2, local copies, waits for them, and re-layouts: 17.3 us -> 0.06 us  [per_device(): lasts = [jnp.concatenate([own_a[i], own_b[i]], axis=1) for i in range(4)]]
    unnamed x76 -> x107, local copies, waits for them, and re-layouts: 1.62 us -> 11.6 us
    add x25 -> x17, other arithmetic: 13.5 us -> 3.51 us  [the longest x1 1 us: per_device(): down_y = (keep_down[0] + got[0], keep_down[1] + got[1])]
  transfers between devices with their start and end apart: 53 -> 67, of which waited for: 33 -> 26; matrix products, arithmetic and copies ran while one was open for 9% -> 4% of each run, Pallas kernels for 9% -> 34%
where the time goes in v2:
time: 467 us; the launch traced here: 464 us
  Pallas kernels  207 us (44%)
  waiting for transfers between devices  137 us (29%)
  starting transfers between devices  87.5 us (19%)
  local copies, waits for them, and re-layouts  23 us (5%)
  other arithmetic  7.24 us (2%)
    pallas_call x24, Pallas kernels, call(): return lambda *args: built(*args, *deps)  207 us
    ppermute x65, waiting for transfers between devices, swap(): return lax.ppermute(value, AXES, pairs)  137 us
    ppermute x65, starting transfers between devices, swap(): return lax.ppermute(value, AXES, pairs)  71.6 us
    unnamed x107, local copies, waits for them, and re-layouts  11.6 us
  transfers between devices with their start and end apart: 67, of which 26 were waited for; matrix products, arithmetic and copies ran while one was open for 4% of the time, Pallas kernels for 34%

profile of v2, /device:TPU:0, one launch (start us, length us, event | category | flops | bytes accessed | tf_op | source)
XLA Modules:
  0.0 463.9 jit_solution(14874465944229671762)
XLA Ops:
  0.7 1.7 constant_dynamic-update-slice_fusion.4
  2.4 4.0 collective-permute-start.1
  8.7 1.6 copy.39.refs_4_.refs_8_
  12.5 2.6 collective-permute-done.1
  15.1 2.7 collective-permute-done.2
  17.9 7.0 %all-to-all-start = ((bf16[8,96,768]{2,1,0:T(8,128)(2,1)}), bf16[8,96,768]{2,1,0:T(8,128)(2,1)S(1)}, u32[]{:S(2)}, u32[]{:S(2)}) async-start(bf16[8,96,768]{2,1,0:T(8,128)(2,1)} %param.20), calls=%async_computation | async-start | bytes 2359296 | tf_op jit(solution)/shard_map/all_to_all | solution.py:1058
  25.6 3.8 collective-permute-start.5
  29.9 2.0 collective-permute-start.6
  34.0 18.7 %collective-permute-done.6 = bf16[4,96,768]{2,1,0:T(8,128)(2,1)S(1)} collective-permute-done((bf16[4,96,768]{2,1,0:T(8,128)(2,1)S(1)}, bf16[4,96,768]{2,1,0:T(8,128)(2,1)S(1)}, u32[]{:S(2)}, u32[]{:S(2)}) %collective-permute-start.6) | collective-permute-done | bytes 589856 | tf_op jit(solution)/shard_map/ppermute | solution.py:978
  55.1 11.2 %collective-permute-done.4 = bf16[96,768]{1,0:T(8,128)(2,1)S(1)} collective-permute-done((bf16[96,768]{1,0:T(8,128)(2,1)S(1)}, bf16[96,768]{1,0:T(8,128)(2,1)S(1)}, u32[]{:S(2)}, u32[]{:S(2)}) %collective-permute-start.4) | collective-permute-done | bytes 147488 | tf_op jit(solution)/shard_map/ppermute | solution.py:978
  68.0 12.6 %collective-permute-done.7 = bf16[4,96,768]{2,1,0:T(8,128)(2,1)S(1)} collective-permute-done((bf16[4,96,768]{2,1,0:T(8,128)(2,1)S(1)}, bf16[4,96,768]{2,1,0:T(8,128)(2,1)S(1)}, u32[]{:S(2)}, u32[]{:S(2)}) %collective-permute-start.7) | collective-permute-done | bytes 589856 | tf_op jit(solution)/shard_map/ppermute | solution.py:978
  81.7 2.9 collective-permute-start.13
  86.1 5.0 %shard_map.323 = (f32[784,768]{1,0:T(8,128)}, bf16[784,768]{1,0:T(8,128)(2,1)}) custom-call(bf16[768,768]{1,0:T(8,128)(2,1)} %bitcast.157, bf16[768,768]{1,0:T(8,128)(2,1)} %refs_2_.7, f32[768]{0:T(1024)} %refs_2_.6, bf16[768,768]{1,0:T(8,128)(2,1)} %refs_3_.5, f32[768]{0:T(1024)} %refs_4_.2, f32[8,768]{1,0:T(8,128)} %refs_5_.3, f32[768]{0:T(1024)} %refs_8_.3, ...), custom_call_target="tpu_custom_call" | custom-call | flops 5750000128 | bytes 1048576 | tf_op jit(solution)/shard_map/pallas_call | solution.py:86
  92.7 4.1 collective-permute-done.12
  97.0 8.3 %shard_map.324.refs_0_ = bf16[3,784,768]{2,1,0:T(8,128)(2,1)} custom-call(s32[2]{0:T(128)} %pad_add_fusion.refs_0_, bf16[784,768]{1,0:T(8,128)(2,1)} %get-tuple-element.108.refs_1_, bf16[8,96,768]{2,1,0:T(8,128)(2,1)} %constant_dynamic-update-slice_fusion.refs_2_.refs_5_.refs_3_, bf16[8,96,768]{2,1,0:T(8,128)(2,1)} %collective-permute-done.8.refs_3_.refs_6_.refs_4_, ...), custom_call_target="tpu_custom_call" | custom-call | flops 8049999872 | bytes 1048576 | tf_op jit(solution)/shard_map/pallas_call | solution.py:86
  106.7 20.9 %shard_map.325 = (bf16[784,768]{1,0:T(8,128)(2,1)}, f32[16,768]{1,0:T(8,128)}, f32[96,128]{1,0:T(8,128)}) custom-call(bf16[3,784,768]{2,1,0:T(8,128)(2,1)} %shard_map.324.refs_0_, s32[1,8]{1,0:T(1,128)} %refs_5_.5, s32[1,1]{1,0:T(1,128)S(6)} %copy.59.refs_2_.refs_6_, s32[1,768]{1,0:T(1,128)} %refs_7_.7, s32[768,1]{1,0:T(8,128)} %copy.39.refs_4_.refs_8_, ...), custom_call_target="tpu_custom_call" | custom-call | flops 24149999616 | bytes 1048576 | tf_op jit(solution)/shard_map/pallas_call | solution.py:86
  129.3 3.1 shard_map.327
  133.9 6.4 %shard_map.326 = (f32[784,768]{1,0:T(8,128)}, bf16[784,768]{1,0:T(8,128)(2,1)}) custom-call(s32[2]{0:T(128)} %pad_add_fusion.refs_0_, bf16[784,768]{1,0:T(8,128)(2,1)} %get-tuple-element.110.refs_1_.refs_2_, bf16[8,96,768]{2,1,0:T(8,128)(2,1)} %constant_dynamic-update-slice_fusion.refs_2_.refs_5_.refs_3_, ...), custom_call_target="tpu_custom_call" | custom-call | flops 7360000000 | bytes 1048576 | tf_op jit(solution)/shard_map/pallas_call | solution.py:86
  140.9 19.8 %shard_map.328 = (bf16[2,784,768]{2,1,0:T(8,128)(2,1)}, bf16[2,784,768]{2,1,0:T(8,128)(2,1)}, f32[784,768]{1,0:T(8,128)}, f32[784,768]{1,0:T(8,128)}, f32[4,768]{1,0:T(4,128)}) custom-call(s32[2]{0:T(128)} %pad_add_fusion.refs_0_, s32[1,8]{1,0:T(1,128)} %refs_5_.5, s32[1,1]{1,0:T(1,128)S(6)} %copy.59.refs_2_.refs_6_, ...), custom_call_target="tpu_custom_call" | custom-call | flops 23000000512 | bytes 1048576 | tf_op jit(solution)/shard_map/pallas_call | solution.py:86
  160.8 6.7 %shard_map.329.refs_14_ = bf16[2,8,96,768]{3,2,1,0:T(8,128)(2,1)} custom-call(s32[2]{0:T(128)} %pad_add_fusion.refs_0_, bf16[784,768]{1,0:T(8,128)(2,1)} %get-tuple-element.116.refs_3_.refs_1_, bf16[2,784,768]{2,1,0:T(8,128)(2,1)} %get-tuple-element.125.refs_2_.refs_1_, bf16[2,784,768]{2,1,0:T(8,128)(2,1)} %get-tuple-element.126.refs_3_.refs_2_, ...), custom_call_target="tpu_custom_call" | custom-call | flops 7474999808 | bytes 1048576 | tf_op jit(solution)/shard_map/pallas_call | solution.py:86
  168.7 20.7 %shard_map.330 = (bf16[2,784,768]{2,1,0:T(8,128)(2,1)}, bf16[2,784,768]{2,1,0:T(8,128)(2,1)}, f32[784,768]{1,0:T(8,128)}, f32[784,768]{1,0:T(8,128)}, f32[4,768]{1,0:T(4,128)}) custom-call(s32[2]{0:T(128)} %pad_add_fusion.refs_0_, s32[1,8]{1,0:T(1,128)} %refs_5_.5, s32[1,1]{1,0:T(1,128)S(6)} %copy.59.refs_2_.refs_6_, ...), custom_call_target="tpu_custom_call" | custom-call | flops 23000000512 | bytes 1048576 | tf_op jit(solution)/shard_map/pallas_call | solution.py:86
  189.4 6.4 %shard_map.331.refs_9_ = bf16[2,8,96,768]{3,2,1,0:T(8,128)(2,1)} custom-call(s32[2]{0:T(128)} %pad_add_fusion.refs_0_, bf16[784,768]{1,0:T(8,128)(2,1)} %get-tuple-element.116.refs_3_.refs_1_, bf16[2,784,768]{2,1,0:T(8,128)(2,1)} %get-tuple-element.129.refs_2_.refs_3_, bf16[2,784,768]{2,1,0:T(8,128)(2,1)} %get-tuple-element.130.refs_3_.refs_4_, ...), custom_call_target="tpu_custom_call" | custom-call | flops 7474999808 | bytes 1048576 | tf_op jit(solution)/shard_map/pallas_call | solution.py:86
  196.2 8.4 %shard_map.332 = (f32[784,768]{1,0:T(8,128)}, bf16[784,768]{1,0:T(8,128)(2,1)}, bf16[784,768]{1,0:T(8,128)(2,1)}, f32[2,768]{1,0:T(2,128)}) custom-call(s32[2]{0:T(128)} %pad_add_fusion.refs_0_, f32[784,768]{1,0:T(8,128)} %get-tuple-element.128.refs_1_, f32[784,768]{1,0:T(8,128)} %get-tuple-element.118.refs_7_.refs_8_.refs_2_, ...), custom_call_target="tpu_custom_call" | custom-call | flops 9774999552 | bytes 1048576 | tf_op jit(solution)/shard_map/pallas_call | solution.py:86
  206.8 6.8 %shard_map.333 = (bf16[2,4,96,768]{3,2,1,0:T(8,128)(2,1)}, bf16[2,4,96,768]{3,2,1,0:T(8,128)(2,1)}) custom-call(s32[2]{0:T(128)} %pad_add_fusion.refs_0_, bf16[2,784,768]{2,1,0:T(8,128)(2,1)} %get-tuple-element.125.refs_2_.refs_1_, bf16[784,768]{1,0:T(8,128)(2,1)} %get-tuple-element.117.refs_4_.refs_3_.refs_2_, ...), custom_call_target="tpu_custom_call" | custom-call | flops 9200000000 | bytes 1048576 | tf_op jit(solution)/shard_map/pallas_call | solution.py:86
  213.6 9.2 %shard_map.334 = (bf16[2,4,96,768]{3,2,1,0:T(8,128)(2,1)}, bf16[2,4,96,768]{3,2,1,0:T(8,128)(2,1)}) custom-call(s32[2]{0:T(128)} %pad_add_fusion.refs_0_, bf16[784,768]{1,0:T(8,128)(2,1)} %get-tuple-element.116.refs_3_.refs_1_, bf16[2,784,768]{2,1,0:T(8,128)(2,1)} %get-tuple-element.126.refs_3_.refs_2_, bf16[784,768]{1,0:T(8,128)(2,1)} %get-tuple-element.116.refs_3_.refs_1_, ...), custom_call_target="tpu_custom_call" | custom-call | flops 9200000000 | bytes 1048576 | tf_op jit(solution)/shard_map/pallas_call | solution.py:86
  225.0 16.2 %shard_map.335.refs_3_.refs_1_ = bf16[3,784,384]{2,1,0:T(8,128)(2,1)} custom-call(bf16[3,784,768]{2,1,0:T(8,128)(2,1)} %shard_map.324.refs_0_, bf16[784,768]{1,0:T(8,128)(2,1)} %get-tuple-element.110.refs_1_.refs_2_, bf16[784,768]{1,0:T(8,128)(2,1)} %get-tuple-element.131.refs_2_, f32[16,768]{1,0:T(8,128)} %get-tuple-element.132.refs_3_, ...), custom_call_target="tpu_custom_call" | custom-call | flops 17250000896 | bytes 1048576 | tf_op jit(solution)/shard_map/pallas_call | solution.py:86
  241.2 5.2 %shard_map.336.refs_9_ = bf16[2,8,96,384]{3,2,1,0:T(8,128)(2,1)} custom-call(s32[2]{0:T(128)} %pad_add_fusion.refs_0_, bf16[784,768]{1,0:T(8,128)(2,1)} %get-tuple-element.108.refs_1_, bf16[784,768]{1,0:T(8,128)(2,1)} %get-tuple-element.110.refs_1_.refs_2_, bf16[3,784,384]{2,1,0:T(8,128)(2,1)} %shard_map.335.refs_3_.refs_1_, ...), custom_call_target="tpu_custom_call" | custom-call | flops 5750000128 | bytes 1048576 | tf_op jit(solution)/shard_map/pallas_call | solution.py:86
  246.5 4.5 collective-permute-done.24
  255.2 16.3 %shard_map.337.refs_6_.refs_3_.refs_2_ = bf16[3,784,384]{2,1,0:T(8,128)(2,1)} custom-call(bf16[3,784,768]{2,1,0:T(8,128)(2,1)} %shard_map.324.refs_0_, bf16[784,768]{1,0:T(8,128)(2,1)} %get-tuple-element.110.refs_1_.refs_2_, bf16[784,768]{1,0:T(8,128)(2,1)} %get-tuple-element.131.refs_2_, f32[16,768]{1,0:T(8,128)} %get-tuple-element.132.refs_3_, ...), custom_call_target="tpu_custom_call" | custom-call | flops 17250000896 | bytes 1048576 | tf_op jit(solution)/shard_map/pallas_call | solution.py:86
  273.6 6.0 %shard_map.338 = (bf16[2,4,96,384]{3,2,1,0:T(8,128)(2,1)}, bf16[2,4,96,384]{3,2,1,0:T(8,128)(2,1)}) custom-call(s32[2]{0:T(128)} %pad_add_fusion.refs_0_, bf16[784,768]{1,0:T(8,128)(2,1)} %get-tuple-element.108.refs_1_, bf16[784,768]{1,0:T(8,128)(2,1)} %get-tuple-element.110.refs_1_.refs_2_, bf16[3,784,384]{2,1,0:T(8,128)(2,1)} %shard_map.335.refs_3_.refs_1_, ...), custom_call_target="tpu_custom_call" | custom-call | flops 6899999744 | bytes 1048576 | tf_op jit(solution)/shard_map/pallas_call | solution.py:86
  279.6 5.2 %shard_map.339.refs_10_ = bf16[2,8,96,384]{3,2,1,0:T(8,128)(2,1)} custom-call(s32[2]{0:T(128)} %pad_add_fusion.refs_0_, bf16[784,768]{1,0:T(8,128)(2,1)} %get-tuple-element.108.refs_1_, bf16[784,768]{1,0:T(8,128)(2,1)} %get-tuple-element.110.refs_1_.refs_2_, bf16[3,784,384]{2,1,0:T(8,128)(2,1)} %shard_map.337.refs_6_.refs_3_.refs_2_, ...), custom_call_target="tpu_custom_call" | custom-call | flops 5750000128 | bytes 1048576 | tf_op jit(solution)/shard_map/pallas_call | solution.py:86
  285.3 2.3 collective-permute-start.32
  289.9 1.7 collective-permute-done.30
  291.6 5.7 %collective-permute-start.35 = (bf16[96,768]{1,0:T(8,128)(2,1)S(1)}, bf16[96,768]{1,0:T(8,128)(2,1)S(1)}, u32[]{:S(2)}, u32[]{:S(2)}) collective-permute-start(bf16[96,768]{1,0:T(8,128)(2,1)S(1)} %get-tuple-element.218), channel_id=1, source_target_pairs={{0,24},{1,25},{2,26},{3,27},{4,28},{5,29},{6,30},{7,31},{8,16},{9,... | collective-permute-start | bytes 442376 | tf_op jit(solution)/shard_map/ppermute | solution.py:978
  297.3 3.8 collective-permute-start.34
  301.1 7.9 %collective-permute-done.31 = bf16[96,768]{1,0:T(8,128)(2,1)S(1)} collective-permute-done((bf16[96,768]{1,0:T(8,128)(2,1)S(1)}, bf16[96,768]{1,0:T(8,128)(2,1)S(1)}, u32[]{:S(2)}, u32[]{:S(2)}) %collective-permute-start.31) | collective-permute-done | bytes 147488 | tf_op jit(solution)/shard_map/ppermute | solution.py:978
  309.7 4.9 %collective-permute-done.34 = bf16[96,768]{1,0:T(8,128)(2,1)S(1)} collective-permute-done((bf16[96,768]{1,0:T(8,128)(2,1)S(1)}, bf16[96,768]{1,0:T(8,128)(2,1)S(1)}, u32[]{:S(2)}, u32[]{:S(2)}) %collective-permute-start.34) | collective-permute-done | bytes 147488 | tf_op jit(solution)/shard_map/ppermute | solution.py:978
  315.4 3.5 collective-permute-done.29
  320.8 10.2 %shard_map.340 = (bf16[768,768]{1,0:T(8,128)(2,1)}, f32[8,768]{1,0:T(8,128)}, f32[2,768]{1,0:T(2,128)}) custom-call(s32[2]{0:T(128)} %pad_add_fusion.refs_0_, bf16[3,784,384]{2,1,0:T(8,128)(2,1)} %shard_map.335.refs_3_.refs_1_, bf16[3,784,384]{2,1,0:T(8,128)(2,1)} %shard_map.337.refs_6_.refs_3_.refs_2_, ...), custom_call_target="tpu_custom_call" | custom-call | flops 11500000256 | bytes 1048576 | tf_op jit(solution)/shard_map/pallas_call | solution.py:86
  331.0 5.8 %shard_map.342 = (bf16[16,48,768]{2,1,0:T(8,128)(2,1)}, bf16[16,48,768]{2,1,0:T(8,128)(2,1)}, f32[2,768]{1,0:T(2,128)}) custom-call(s32[2]{0:T(128)} %pad_add_fusion.refs_0_, bf16[768,768]{1,0:T(8,128)(2,1)} %bitcast.158, bf16[768,768]{1,0:T(8,128)(2,1)} %get-tuple-element.143.refs_2_, bf16[4,96,384]{2,1,0:T(8,128)(2,1)} %get-tuple-element.221.refs_3_, ...), custom_call_target="tpu_custom_call" | custom-call | flops 6899999744 | bytes 1048576 | tf_op jit(solution)/shard_map/pallas_call | solution.py:86
  336.9 8.8 %all-to-all-start.1 = ((bf16[8,96,768]{2,1,0:T(8,128)(2,1)}), bf16[8,96,768]{2,1,0:T(8,128)(2,1)S(1)}, u32[]{:S(2)}, u32[]{:S(2)}) async-start(bf16[8,96,768]{2,1,0:T(8,128)(2,1)} %bitcast.24), calls=%async_computation.1 | async-start | bytes 2359296 | tf_op jit(solution)/shard_map/all_to_all | solution.py:1182
  346.3 1.9 collective-permute-start.43
  348.2 5.9 %shard_map.343 = (bf16[2,4,96,384]{3,2,1,0:T(8,128)(2,1)}, bf16[2,4,96,384]{3,2,1,0:T(8,128)(2,1)}) custom-call(s32[2]{0:T(128)} %pad_add_fusion.refs_0_, bf16[784,768]{1,0:T(8,128)(2,1)} %get-tuple-element.108.refs_1_, bf16[784,768]{1,0:T(8,128)(2,1)} %get-tuple-element.110.refs_1_.refs_2_, bf16[3,784,384]{2,1,0:T(8,128)(2,1)} %shard_map.337.refs_6_.refs_3_.refs_2_, ...), custom_call_target="tpu_custom_call" | custom-call | flops 6899999744 | bytes 1048576 | tf_op jit(solution)/shard_map/pallas_call | solution.py:86
  357.4 1.8 collective-permute-start.40
  359.3 9.1 %collective-permute-done.43 = bf16[4,96,384]{2,1,0:T(8,128)(2,1)S(1)} collective-permute-done((bf16[4,96,384]{2,1,0:T(8,128)(2,1)S(1)}, bf16[4,96,384]{2,1,0:T(8,128)(2,1)S(1)}, u32[]{:S(2)}, u32[]{:S(2)}) %collective-permute-start.43) | collective-permute-done | bytes 294944 | tf_op jit(solution)/shard_map/ppermute | solution.py:978
  369.1 15.7 %collective-permute-done.41 = f32[19,768]{1,0:T(8,128)S(1)} collective-permute-done((f32[19,768]{1,0:T(8,128)S(1)}, f32[19,768]{1,0:T(8,128)S(1)}, u32[]{:S(2)}, u32[]{:S(2)}) %collective-permute-start.41) | collective-permute-done | bytes 58400 | tf_op jit(solution)/shard_map/ppermute | solution.py:978
  385.6 7.0 %collective-permute-done.44.refs_2_ = bf16[2,96,768]{2,1,0:T(8,128)(2,1)S(1)} collective-permute-done((bf16[2,96,768]{2,1,0:T(8,128)(2,1)S(1)}, bf16[2,96,768]{2,1,0:T(8,128)(2,1)S(1)}, u32[]{:S(2)}, u32[]{:S(2)}) %collective-permute-start.44) | collective-permute-done | bytes 294944 | tf_op jit(solution)/shard_map/ppermute | solution.py:978
  392.7 1.8 collective-permute-start.45
  394.5 2.4 collective-permute-start.46
  399.3 2.8 collective-permute-done.48
  403.1 2.2 collective-permute-done.50
  405.5 3.5 collective-permute-start.53
  411.9 4.5 collective-permute-done.54
  416.5 1.7 collective-permute-start.57
  418.4 2.7 collective-permute-done.55
  421.0 5.5 %collective-permute-done.56 = bf16[96,768]{1,0:T(8,128)(2,1)S(1)} collective-permute-done((bf16[96,768]{1,0:T(8,128)(2,1)S(1)}, bf16[96,768]{1,0:T(8,128)(2,1)S(1)}, u32[]{:S(2)}, u32[]{:S(2)}) %collective-permute-start.56) | collective-permute-done | bytes 147488 | tf_op jit(solution)/shard_map/ppermute | solution.py:978
  430.9 2.8 fusion
  433.7 3.6 collective-permute-done.60
  437.2 2.6 collective-permute-done.59
  441.5 4.6 shard_map.341
  446.6 3.1 shard_map.346
  449.7 3.4 collective-permute-done.63
  455.9 2.2 shard_map.345
  459.2 4.5 shard_map.344
  (254 shorter events, 61.3 us)
Async XLA Ops:
  2.4 12.7 %collective-permute-start.1 = (bf16[96,768]{1,0:T(8,128)(2,1)S(1)}, bf16[96,768]{1,0:T(8,128)(2,1)S(1)}, u32[]{:S(2)}, u32[]{:S(2)}) collective-permute-start(bf16[96,768]{1,0:T(8,128)(2,1)S(1)} %get-tuple-element.199), channel_id=1, source_target_pairs={{0,16},{1,17},{2,18},{3,19},{4,20},{5,21},{6,22},{7,23},{8,24},{9,... | collective-permute-start | bytes 442376 | tf_op jit(solution)/shard_map/ppermute | solution.py:978
  6.5 8.7 %collective-permute-start = (bf16[96,768]{1,0:T(8,128)(2,1)S(1)}, bf16[96,768]{1,0:T(8,128)(2,1)S(1)}, u32[]{:S(2)}, u32[]{:S(2)}) collective-permute-start(bf16[96,768]{1,0:T(8,128)(2,1)S(1)} %get-tuple-element.199), channel_id=1, source_target_pairs={{0,8},{1,9},{2,10},{3,11},{4,12},{5,13},{6,14},{7,15},{8,0},{9,1},... | collective-permute-start | bytes 442376 | tf_op jit(solution)/shard_map/ppermute | solution.py:978
  8.0 9.8 %collective-permute-start.2 = (bf16[96,768]{1,0:T(8,128)(2,1)S(1)}, bf16[96,768]{1,0:T(8,128)(2,1)S(1)}, u32[]{:S(2)}, u32[]{:S(2)}) collective-permute-start(bf16[96,768]{1,0:T(8,128)(2,1)S(1)} %get-tuple-element.199), channel_id=1, source_target_pairs={{0,24},{1,25},{2,26},{3,27},{4,28},{5,29},{6,30},{7,31},{8,16},{9,... | collective-permute-start | bytes 442376 | tf_op jit(solution)/shard_map/ppermute | solution.py:978
  17.9 63.7 %all-to-all-start = ((bf16[8,96,768]{2,1,0:T(8,128)(2,1)}), bf16[8,96,768]{2,1,0:T(8,128)(2,1)S(1)}, u32[]{:S(2)}, u32[]{:S(2)}) async-start(bf16[8,96,768]{2,1,0:T(8,128)(2,1)} %param.20), calls=%async_computation | async-start | bytes 2359296 | tf_op jit(solution)/shard_map/all_to_all | solution.py:1058
  25.6 29.5 %collective-permute-start.5 = (bf16[96,768]{1,0:T(8,128)(2,1)S(1)}, bf16[96,768]{1,0:T(8,128)(2,1)S(1)}, u32[]{:S(2)}, u32[]{:S(2)}) collective-permute-start(bf16[96,768]{1,0:T(8,128)(2,1)S(1)} %reshape.111), channel_id=1, source_target_pairs={{0,24},{1,25},{2,26},{3,27},{4,28},{5,29},{6,30},{7,31},{8,16},{9,... | collective-permute-start | bytes 442376 | tf_op jit(solution)/shard_map/ppermute | solution.py:978
  29.4 36.9 %collective-permute-start.4 = (bf16[96,768]{1,0:T(8,128)(2,1)S(1)}, bf16[96,768]{1,0:T(8,128)(2,1)S(1)}, u32[]{:S(2)}, u32[]{:S(2)}) collective-permute-start(bf16[96,768]{1,0:T(8,128)(2,1)S(1)} %reshape.111), channel_id=1, source_target_pairs={{0,16},{1,17},{2,18},{3,19},{4,20},{5,21},{6,22},{7,23},{8,24},{9,... | collective-permute-start | bytes 442376 | tf_op jit(solution)/shard_map/ppermute | solution.py:978
  29.4 36.9 %collective-permute-start.3 = (bf16[96,768]{1,0:T(8,128)(2,1)S(1)}, bf16[96,768]{1,0:T(8,128)(2,1)S(1)}, u32[]{:S(2)}, u32[]{:S(2)}) collective-permute-start(bf16[96,768]{1,0:T(8,128)(2,1)S(1)} %reshape.111), channel_id=1, source_target_pairs={{0,8},{1,9},{2,10},{3,11},{4,12},{5,13},{6,14},{7,15},{8,0},{9,1},... | collective-permute-start | bytes 442376 | tf_op jit(solution)/shard_map/ppermute | solution.py:978
  29.9 22.8 %collective-permute-start.6 = (bf16[4,96,768]{2,1,0:T(8,128)(2,1)S(1)}, bf16[4,96,768]{2,1,0:T(8,128)(2,1)S(1)}, u32[]{:S(2)}, u32[]{:S(2)}) collective-permute-start(bf16[4,96,768]{2,1,0:T(8,128)(2,1)S(1)} %pad_maximum_fusion.1), channel_id=1, source_target_pairs={{0,4},{1,5},{2,6},{3,7},{4,0},{5,1},{6,2},{7,3},{8,12},{9,13},{10,... | collective-permute-start | bytes 1769480 | tf_op jit(solution)/shard_map/ppermute | solution.py:978
  53.6 27.7 %collective-permute-start.9 = (bf16[8,96,768]{2,1,0:T(8,128)(2,1)}, bf16[8,96,768]{2,1,0:T(8,128)(2,1)}, u32[]{:S(2)}, u32[]{:S(2)}) collective-permute-start(bf16[8,96,768]{2,1,0:T(8,128)(2,1)} %constant_dynamic-update-slice_fusion.refs_2_.refs_5_.refs_3_), channel_id=1, source_target_pairs={{0,2},{1,3},{2,0},{3,1},{4,6},{5,7},{6,4},{7,5},{8,10},{9,11},{10,... | collective-permute-start | bytes 3538952 | tf_op jit(solution)/shard_map/ppermute | solution.py:978
  66.4 14.2 %collective-permute-start.7 = (bf16[4,96,768]{2,1,0:T(8,128)(2,1)S(1)}, bf16[4,96,768]{2,1,0:T(8,128)(2,1)S(1)}, u32[]{:S(2)}, u32[]{:S(2)}) collective-permute-start(bf16[4,96,768]{2,1,0:T(8,128)(2,1)S(1)} %pad_maximum_fusion.2), channel_id=1, source_target_pairs={{0,4},{1,5},{2,6},{3,7},{4,0},{5,1},{6,2},{7,3},{8,12},{9,13},{10,... | collective-permute-start | bytes 1769480 | tf_op jit(solution)/shard_map/ppermute | solution.py:978
  67.9 29.1 %collective-permute-start.8 = (bf16[8,96,768]{2,1,0:T(8,128)(2,1)}, bf16[8,96,768]{2,1,0:T(8,128)(2,1)}, u32[]{:S(2)}, u32[]{:S(2)}) collective-permute-start(bf16[8,96,768]{2,1,0:T(8,128)(2,1)} %constant_dynamic-update-slice_fusion.refs_2_.refs_5_.refs_3_), channel_id=1, source_target_pairs={{0,1},{1,0},{2,3},{3,2},{4,5},{5,4},{6,7},{7,6},{8,9},{9,8},{10,11... | collective-permute-start | bytes 3538952 | tf_op jit(solution)/shard_map/ppermute | solution.py:978
  81.6 15.4 %collective-permute-start.10 = (bf16[8,96,768]{2,1,0:T(8,128)(2,1)}, bf16[8,96,768]{2,1,0:T(8,128)(2,1)}, u32[]{:S(2)}, u32[]{:S(2)}) collective-permute-start(bf16[8,96,768]{2,1,0:T(8,128)(2,1)} %collective-permute-done.9.refs_4_.refs_7_.refs_5_), channel_id=1, source_target_pairs={{0,1},{1,0},{2,3},{3,2},{4,5},{5,4},{6,7},{7,6},{8,9},{9,8},{10,11... | collective-permute-start | bytes 3538952 | tf_op jit(solution)/shard_map/ppermute | solution.py:978
  81.7 9.5 %collective-permute-start.13 = (bf16[96,768]{1,0:T(8,128)(2,1)S(1)}, bf16[96,768]{1,0:T(8,128)(2,1)S(1)}, u32[]{:S(2)}, u32[]{:S(2)}) collective-permute-start(bf16[96,768]{1,0:T(8,128)(2,1)S(1)} %constant_dynamic-slice_fusion), channel_id=1, source_target_pairs={{0,24},{1,25},{2,26},{3,27},{4,28},{5,29},{6,30},{7,31},{8,16},{9,... | collective-permute-start | bytes 442376 | tf_op jit(solution)/shard_map/ppermute | solution.py:978
  84.5 12.3 %collective-permute-start.12 = (bf16[96,768]{1,0:T(8,128)(2,1)S(1)}, bf16[96,768]{1,0:T(8,128)(2,1)S(1)}, u32[]{:S(2)}, u32[]{:S(2)}) collective-permute-start(bf16[96,768]{1,0:T(8,128)(2,1)S(1)} %constant_dynamic-slice_fusion), channel_id=1, source_target_pairs={{0,16},{1,17},{2,18},{3,19},{4,20},{5,21},{6,22},{7,23},{8,24},{9,... | collective-permute-start | bytes 442376 | tf_op jit(solution)/shard_map/ppermute | solution.py:978
  84.5 12.3 %collective-permute-start.11 = (bf16[96,768]{1,0:T(8,128)(2,1)S(1)}, bf16[96,768]{1,0:T(8,128)(2,1)S(1)}, u32[]{:S(2)}, u32[]{:S(2)}) collective-permute-start(bf16[96,768]{1,0:T(8,128)(2,1)S(1)} %constant_dynamic-slice_fusion), channel_id=1, source_target_pairs={{0,8},{1,9},{2,10},{3,11},{4,12},{5,13},{6,14},{7,15},{8,0},{9,1},... | collective-permute-start | bytes 442376 | tf_op jit(solution)/shard_map/ppermute | solution.py:978
  91.1 36.5 %collective-permute-start.16 = (bf16[8,96,768]{2,1,0:T(8,128)(2,1)S(1)}, bf16[8,96,768]{2,1,0:T(8,128)(2,1)}, u32[]{:S(2)}, u32[]{:S(2)}) collective-permute-start(bf16[8,96,768]{2,1,0:T(8,128)(2,1)S(1)} %copy-done.28), channel_id=1, source_target_pairs={{0,2},{1,3},{2,0},{3,1},{4,6},{5,7},{6,4},{7,5},{8,10},{9,11},{10,... | collective-permute-start | bytes 3538952 | tf_op jit(solution)/shard_map/ppermute | solution.py:978
  105.3 22.9 %collective-permute-start.14 = (bf16[4,96,768]{2,1,0:T(8,128)(2,1)S(1)}, bf16[4,96,768]{2,1,0:T(8,128)(2,1)S(1)}, u32[]{:S(2)}, u32[]{:S(2)}) collective-permute-start(bf16[4,96,768]{2,1,0:T(8,128)(2,1)S(1)} %pad_maximum_fusion.3.refs_5_), channel_id=1, source_target_pairs={{0,4},{1,5},{2,6},{3,7},{4,0},{5,1},{6,2},{7,3},{8,12},{9,13},{10,... | collective-permute-start | bytes 1769480 | tf_op jit(solution)/shard_map/ppermute | solution.py:978
  106.7 27.2 %collective-permute-start.15 = (bf16[8,96,768]{2,1,0:T(8,128)(2,1)S(1)}, bf16[8,96,768]{2,1,0:T(8,128)(2,1)}, u32[]{:S(2)}, u32[]{:S(2)}) collective-permute-start(bf16[8,96,768]{2,1,0:T(8,128)(2,1)S(1)} %copy-done.28), channel_id=1, source_target_pairs={{0,1},{1,0},{2,3},{3,2},{4,5},{5,4},{6,7},{7,6},{8,9},{9,8},{10,11... | collective-permute-start | bytes 3538952 | tf_op jit(solution)/shard_map/ppermute | solution.py:978
  127.7 12.6 %collective-permute-start.18 = (bf16[8,96,768]{2,1,0:T(8,128)(2,1)}, bf16[8,96,768]{2,1,0:T(8,128)(2,1)}, u32[]{:S(2)}, u32[]{:S(2)}) collective-permute-start(bf16[8,96,768]{2,1,0:T(8,128)(2,1)} %collective-permute-done.16.refs_11_.refs_10_), channel_id=1, source_target_pairs={{0,1},{1,0},{2,3},{3,2},{4,5},{5,4},{6,7},{7,6},{8,9},{9,8},{10,11... | collective-permute-start | bytes 3538952 | tf_op jit(solution)/shard_map/ppermute | solution.py:978
  128.3 12.0 %collective-permute-start.17 = (bf16[8,96,768]{2,1,0:T(8,128)(2,1)S(1)}, bf16[8,96,768]{2,1,0:T(8,128)(2,1)}, u32[]{:S(2)}, u32[]{:S(2)}) collective-permute-start(bf16[8,96,768]{2,1,0:T(8,128)(2,1)S(1)} %constant_dynamic-update-slice_fusion.10.refs_9_.refs_11_), channel_id=1, source_target_pairs={{0,1},{1,0},{2,3},{3,2},{4,5},{5,4},{6,7},{7,6},{8,9},{9,8},{10,11... | collective-permute-start | bytes 3538952 | tf_op jit(solution)/shard_map/ppermute | solution.py:978
  132.3 28.3 %collective-permute-start.19 = (bf16[8,96,768]{2,1,0:T(8,128)(2,1)S(1)}, bf16[8,96,768]{2,1,0:T(8,128)(2,1)S(1)}, u32[]{:S(2)}, u32[]{:S(2)}) collective-permute-start(bf16[8,96,768]{2,1,0:T(8,128)(2,1)S(1)} %constant_dynamic-update-slice_fusion.10.refs_9_.refs_11_), channel_id=1, source_target_pairs={{0,2},{1,3},{2,0},{3,1},{4,6},{5,7},{6,4},{7,5},{8,10},{9,11},{10,... | collective-permute-start | bytes 3538952 | tf_op jit(solution)/shard_map/ppermute | solution.py:978
  160.7 7.0 %collective-permute-start.20 = (bf16[8,96,768]{2,1,0:T(8,128)(2,1)S(1)}, bf16[8,96,768]{2,1,0:T(8,128)(2,1)S(1)}, u32[]{:S(2)}, u32[]{:S(2)}) collective-permute-start(bf16[8,96,768]{2,1,0:T(8,128)(2,1)S(1)} %collective-permute-done.19.refs_11_), channel_id=1, source_target_pairs={{0,1},{1,0},{2,3},{3,2},{4,5},{5,4},{6,7},{7,6},{8,9},{9,8},{10,11... | collective-permute-start | bytes 3538952 | tf_op jit(solution)/shard_map/ppermute | solution.py:978
  167.5 37.1 %collective-permute-start.21 = (bf16[2,8,96,768]{3,2,1,0:T(8,128)(2,1)}, bf16[2,8,96,768]{3,2,1,0:T(8,128)(2,1)S(1)}, u32[]{:S(2)}, u32[]{:S(2)}) collective-permute-start(bf16[2,8,96,768]{3,2,1,0:T(8,128)(2,1)} %shard_map.329.refs_14_), channel_id=1, source_target_pairs={{0,1},{1,0},{2,3},{3,2},{4,5},{5,4},{6,7},{7,6},{8,9},{9,8},{10,11... | collective-permute-start | bytes 7077896 | tf_op jit(solution)/shard_map/ppermute | solution.py:978
  195.8 8.8 %collective-permute-start.22 = (bf16[2,8,96,768]{3,2,1,0:T(8,128)(2,1)}, bf16[2,8,96,768]{3,2,1,0:T(8,128)(2,1)S(1)}, u32[]{:S(2)}, u32[]{:S(2)}) collective-permute-start(bf16[2,8,96,768]{3,2,1,0:T(8,128)(2,1)} %shard_map.331.refs_9_), channel_id=1, source_target_pairs={{0,1},{1,0},{2,3},{3,2},{4,5},{5,4},{6,7},{7,6},{8,9},{9,8},{10,11... | collective-permute-start | bytes 7077896 | tf_op jit(solution)/shard_map/ppermute | solution.py:978
  222.8 28.2 %collective-permute-start.24 = (bf16[2,4,96,768]{3,2,1,0:T(8,128)(2,1)}, bf16[2,4,96,768]{3,2,1,0:T(8,128)(2,1)S(1)}, u32[]{:S(2)}, u32[]{:S(2)}) collective-permute-start(bf16[2,4,96,768]{3,2,1,0:T(8,128)(2,1)} %get-tuple-element.138), channel_id=1, source_target_pairs={{0,4},{1,5},{2,6},{3,7},{4,0},{5,1},{6,2},{7,3},{8,12},{9,13},{10,... | collective-permute-start | bytes 3538952 | tf_op jit(solution)/shard_map/ppermute | solution.py:978
  223.5 29.8 %collective-permute-start.23 = (bf16[2,4,96,768]{3,2,1,0:T(8,128)(2,1)S(1)}, bf16[2,4,96,768]{3,2,1,0:T(8,128)(2,1)S(1)}, u32[]{:S(2)}, u32[]{:S(2)}) collective-permute-start(bf16[2,4,96,768]{3,2,1,0:T(8,128)(2,1)S(1)} %copy-done.42), channel_id=1, source_target_pairs={{0,2},{1,3},{2,0},{3,1},{4,6},{5,7},{6,4},{7,5},{8,10},{9,11},{10,... | collective-permute-start | bytes 3538952 | tf_op jit(solution)/shard_map/ppermute | solution.py:978
  246.4 25.1 %collective-permute-start.25 = (bf16[2,8,96,384]{3,2,1,0:T(8,128)(2,1)}, bf16[2,8,96,384]{3,2,1,0:T(8,128)(2,1)S(1)}, u32[]{:S(2)}, u32[]{:S(2)}) collective-permute-start(bf16[2,8,96,384]{3,2,1,0:T(8,128)(2,1)} %shard_map.336.refs_9_), channel_id=1, source_target_pairs={{0,1},{1,0},{2,3},{3,2},{4,5},{5,4},{6,7},{7,6},{8,9},{9,8},{10,11... | collective-permute-start | bytes 3538952 | tf_op jit(solution)/shard_map/ppermute | solution.py:978
  252.0 19.6 %collective-permute-start.26 = (bf16[4,96,768]{2,1,0:T(8,128)(2,1)S(1)}, bf16[4,96,768]{2,1,0:T(8,128)(2,1)S(1)}, u32[]{:S(2)}, u32[]{:S(2)}) collective-permute-start(bf16[4,96,768]{2,1,0:T(8,128)(2,1)S(1)} %get-tuple-element.140.refs_13_), channel_id=1, source_target_pairs={{0,2},{1,3},{2,0},{3,1},{4,6},{5,7},{6,4},{7,5},{8,10},{9,11},{10,... | collective-permute-start | bytes 1769480 | tf_op jit(solution)/shard_map/ppermute | solution.py:978
  254.4 17.2 %collective-permute-start.27 = (bf16[4,96,768]{2,1,0:T(8,128)(2,1)S(1)}, bf16[4,96,768]{2,1,0:T(8,128)(2,1)S(1)}, u32[]{:S(2)}, u32[]{:S(2)}) collective-permute-start(bf16[4,96,768]{2,1,0:T(8,128)(2,1)S(1)} %get-tuple-element.141.refs_11_), channel_id=1, source_target_pairs={{0,4},{1,5},{2,6},{3,7},{4,0},{5,1},{6,2},{7,3},{8,12},{9,13},{10,... | collective-permute-start | bytes 1769480 | tf_op jit(solution)/shard_map/ppermute | solution.py:978
  284.8 34.9 %collective-permute-start.28 = (bf16[2,8,96,384]{3,2,1,0:T(8,128)(2,1)}, bf16[2,8,96,384]{3,2,1,0:T(8,128)(2,1)S(1)}, u32[]{:S(2)}, u32[]{:S(2)}) collective-permute-start(bf16[2,8,96,384]{3,2,1,0:T(8,128)(2,1)} %shard_map.339.refs_10_), channel_id=1, source_target_pairs={{0,1},{1,0},{2,3},{3,2},{4,5},{5,4},{6,7},{7,6},{8,9},{9,8},{10,11... | collective-permute-start | bytes 3538952 | tf_op jit(solution)/shard_map/ppermute | solution.py:978
  285.0 6.6 %collective-permute-start.30 = (bf16[96,768]{1,0:T(8,128)(2,1)S(1)}, bf16[96,768]{1,0:T(8,128)(2,1)S(1)}, u32[]{:S(2)}, u32[]{:S(2)}) collective-permute-start(bf16[96,768]{1,0:T(8,128)(2,1)S(1)} %get-tuple-element.214), channel_id=1, source_target_pairs={{0,8},{1,9},{2,10},{3,11},{4,12},{5,13},{6,14},{7,15},{8,0},{9,1},... | collective-permute-start | bytes 442376 | tf_op jit(solution)/shard_map/ppermute | solution.py:978
  285.3 12.0 %collective-permute-start.32 = (bf16[96,768]{1,0:T(8,128)(2,1)S(1)}, bf16[96,768]{1,0:T(8,128)(2,1)S(1)}, u32[]{:S(2)}, u32[]{:S(2)}) collective-permute-start(bf16[96,768]{1,0:T(8,128)(2,1)S(1)} %get-tuple-element.215), channel_id=1, source_target_pairs={{0,24},{1,25},{2,26},{3,27},{4,28},{5,29},{6,30},{7,31},{8,16},{9,... | collective-permute-start | bytes 442376 | tf_op jit(solution)/shard_map/ppermute | solution.py:978
  287.6 21.4 %collective-permute-start.31 = (bf16[96,768]{1,0:T(8,128)(2,1)S(1)}, bf16[96,768]{1,0:T(8,128)(2,1)S(1)}, u32[]{:S(2)}, u32[]{:S(2)}) collective-permute-start(bf16[96,768]{1,0:T(8,128)(2,1)S(1)} %get-tuple-element.216), channel_id=1, source_target_pairs={{0,16},{1,17},{2,18},{3,19},{4,20},{5,21},{6,22},{7,23},{8,24},{9,... | collective-permute-start | bytes 442376 | tf_op jit(solution)/shard_map/ppermute | solution.py:978
  288.6 21.1 %collective-permute-start.33 = (bf16[96,768]{1,0:T(8,128)(2,1)S(1)}, bf16[96,768]{1,0:T(8,128)(2,1)S(1)}, u32[]{:S(2)}, u32[]{:S(2)}) collective-permute-start(bf16[96,768]{1,0:T(8,128)(2,1)S(1)} %get-tuple-element.217), channel_id=1, source_target_pairs={{0,8},{1,9},{2,10},{3,11},{4,12},{5,13},{6,14},{7,15},{8,0},{9,1},... | collective-permute-start | bytes 442376 | tf_op jit(solution)/shard_map/ppermute | solution.py:978
  291.6 18.1 %collective-permute-start.35 = (bf16[96,768]{1,0:T(8,128)(2,1)S(1)}, bf16[96,768]{1,0:T(8,128)(2,1)S(1)}, u32[]{:S(2)}, u32[]{:S(2)}) collective-permute-start(bf16[96,768]{1,0:T(8,128)(2,1)S(1)} %get-tuple-element.218), channel_id=1, source_target_pairs={{0,24},{1,25},{2,26},{3,27},{4,28},{5,29},{6,30},{7,31},{8,16},{9,... | collective-permute-start | bytes 442376 | tf_op jit(solution)/shard_map/ppermute | solution.py:978
  297.3 17.3 %collective-permute-start.34 = (bf16[96,768]{1,0:T(8,128)(2,1)S(1)}, bf16[96,768]{1,0:T(8,128)(2,1)S(1)}, u32[]{:S(2)}, u32[]{:S(2)}) collective-permute-start(bf16[96,768]{1,0:T(8,128)(2,1)S(1)} %get-tuple-element.219), channel_id=1, source_target_pairs={{0,16},{1,17},{2,18},{3,19},{4,20},{5,21},{6,22},{7,23},{8,24},{9,... | collective-permute-start | bytes 442376 | tf_op jit(solution)/shard_map/ppermute | solution.py:978
  309.0 9.9 %collective-permute-start.29 = (bf16[2,4,96,384]{3,2,1,0:T(8,128)(2,1)S(1)}, bf16[2,4,96,384]{3,2,1,0:T(8,128)(2,1)S(1)}, u32[]{:S(2)}, u32[]{:S(2)}) collective-permute-start(bf16[2,4,96,384]{3,2,1,0:T(8,128)(2,1)S(1)} %copy-done.45), channel_id=1, source_target_pairs={{0,2},{1,3},{2,0},{3,1},{4,6},{5,7},{6,4},{7,5},{8,10},{9,11},{10,... | collective-permute-start | bytes 1769480 | tf_op jit(solution)/shard_map/ppermute | solution.py:978
  336.8 17.4 %collective-permute-start.36 = (bf16[16,48,768]{2,1,0:T(8,128)(2,1)}, bf16[16,48,768]{2,1,0:T(8,128)(2,1)S(1)}, u32[]{:S(2)}, u32[]{:S(2)}) collective-permute-start(bf16[16,48,768]{2,1,0:T(8,128)(2,1)} %get-tuple-element.147), channel_id=1, source_target_pairs={{0,1},{1,0},{2,3},{3,2},{4,5},{5,4},{6,7},{7,6},{8,9},{9,8},{10,11... | collective-permute-start | bytes 3538952 | tf_op jit(solution)/shard_map/ppermute | solution.py:978
  336.9 55.8 %all-to-all-start.1 = ((bf16[8,96,768]{2,1,0:T(8,128)(2,1)}), bf16[8,96,768]{2,1,0:T(8,128)(2,1)S(1)}, u32[]{:S(2)}, u32[]{:S(2)}) async-start(bf16[8,96,768]{2,1,0:T(8,128)(2,1)} %bitcast.24), calls=%async_computation.1 | async-start | bytes 2359296 | tf_op jit(solution)/shard_map/all_to_all | solution.py:1182
  346.0 8.1 %collective-permute-start.37 = (f32[19,768]{1,0:T(8,128)S(1)}, f32[19,768]{1,0:T(8,128)S(1)}, u32[]{:S(2)}, u32[]{:S(2)}) collective-permute-start(f32[19,768]{1,0:T(8,128)S(1)} %concatenate.37), channel_id=1, source_target_pairs={{0,1},{1,0},{2,3},{3,2},{4,5},{5,4},{6,7},{7,6},{8,9},{9,8},{10,11... | collective-permute-start | bytes 175112 | tf_op jit(solution)/shard_map/ppermute | solution.py:978
  346.3 22.0 %collective-permute-start.43 = (bf16[4,96,384]{2,1,0:T(8,128)(2,1)S(1)}, bf16[4,96,384]{2,1,0:T(8,128)(2,1)S(1)}, u32[]{:S(2)}, u32[]{:S(2)}) collective-permute-start(bf16[4,96,384]{2,1,0:T(8,128)(2,1)S(1)} %copy-done.23), channel_id=1, source_target_pairs={{0,4},{1,5},{2,6},{3,7},{4,0},{5,1},{6,2},{7,3},{8,12},{9,13},{10,... | collective-permute-start | bytes 884744 | tf_op jit(solution)/shard_map/ppermute | solution.py:978
  355.2 30.3 %collective-permute-start.42 = (bf16[2,4,96,384]{3,2,1,0:T(8,128)(2,1)S(1)}, bf16[2,4,96,384]{3,2,1,0:T(8,128)(2,1)S(1)}, u32[]{:S(2)}, u32[]{:S(2)}) collective-permute-start(bf16[2,4,96,384]{3,2,1,0:T(8,128)(2,1)S(1)} %copy-done.46), channel_id=1, source_target_pairs={{0,2},{1,3},{2,0},{3,1},{4,6},{5,7},{6,4},{7,5},{8,10},{9,11},{10,... | collective-permute-start | bytes 1769480 | tf_op jit(solution)/shard_map/ppermute | solution.py:978
  355.8 29.6 %collective-permute-start.38 = (bf16[4,48,768]{2,1,0:T(8,128)(2,1)S(1)}, bf16[4,48,768]{2,1,0:T(8,128)(2,1)S(1)}, u32[]{:S(2)}, u32[]{:S(2)}) collective-permute-start(bf16[4,48,768]{2,1,0:T(8,128)(2,1)S(1)} %get-tuple-element.156), channel_id=1, source_target_pairs={{0,4},{1,5},{2,6},{3,7},{4,0},{5,1},{6,2},{7,3},{8,12},{9,13},{10,... | collective-permute-start | bytes 884744 | tf_op jit(solution)/shard_map/ppermute | solution.py:978
  356.0 29.4 %collective-permute-start.39 = (bf16[4,48,768]{2,1,0:T(8,128)(2,1)S(1)}, bf16[4,48,768]{2,1,0:T(8,128)(2,1)S(1)}, u32[]{:S(2)}, u32[]{:S(2)}) collective-permute-start(bf16[4,48,768]{2,1,0:T(8,128)(2,1)S(1)} %get-tuple-element.157), channel_id=1, source_target_pairs={{0,2},{1,3},{2,0},{3,1},{4,6},{5,7},{6,4},{7,5},{8,10},{9,11},{10,... | collective-permute-start | bytes 884744 | tf_op jit(solution)/shard_map/ppermute | solution.py:978
  357.4 28.0 %collective-permute-start.40 = (bf16[4,48,768]{2,1,0:T(8,128)(2,1)S(1)}, bf16[4,48,768]{2,1,0:T(8,128)(2,1)S(1)}, u32[]{:S(2)}, u32[]{:S(2)}) collective-permute-start(bf16[4,48,768]{2,1,0:T(8,128)(2,1)S(1)} %get-tuple-element.158), channel_id=1, source_target_pairs={{0,6},{1,7},{2,4},{3,5},{4,2},{5,3},{6,0},{7,1},{8,14},{9,15},{10,... | collective-permute-start | bytes 884744 | tf_op jit(solution)/shard_map/ppermute | solution.py:978
  368.4 16.4 %collective-permute-start.41 = (f32[19,768]{1,0:T(8,128)S(1)}, f32[19,768]{1,0:T(8,128)S(1)}, u32[]{:S(2)}, u32[]{:S(2)}) collective-permute-start(f32[19,768]{1,0:T(8,128)S(1)} %add.266), channel_id=1, source_target_pairs={{0,2},{1,3},{2,0},{3,1},{4,6},{5,7},{6,4},{7,5},{8,10},{9,11},{10,... | collective-permute-start | bytes 175112 | tf_op jit(solution)/shard_map/ppermute | solution.py:978
  384.8 7.9 %collective-permute-start.44 = (bf16[2,96,768]{2,1,0:T(8,128)(2,1)S(1)}, bf16[2,96,768]{2,1,0:T(8,128)(2,1)S(1)}, u32[]{:S(2)}, u32[]{:S(2)}) collective-permute-start(bf16[2,96,768]{2,1,0:T(8,128)(2,1)S(1)} %copy-done.11), channel_id=1, source_target_pairs={{0,2},{1,3},{2,0},{3,1},{4,6},{5,7},{6,4},{7,5},{8,10},{9,11},{10,... | collective-permute-start | bytes 884744 | tf_op jit(solution)/shard_map/ppermute | solution.py:978
  392.7 9.4 %collective-permute-start.45 = (bf16[48,768]{1,0:T(8,128)(2,1)S(1)}, bf16[48,768]{1,0:T(8,128)(2,1)S(1)}, u32[]{:S(2)}, u32[]{:S(2)}) collective-permute-start(bf16[48,768]{1,0:T(8,128)(2,1)S(1)} %get-tuple-element.165), channel_id=1, source_target_pairs={{0,8},{1,9},{2,10},{3,11},{4,12},{5,13},{6,14},{7,15},{8,0},{9,1},... | collective-permute-start | bytes 221192 | tf_op jit(solution)/shard_map/ppermute | solution.py:978
  394.5 7.6 %collective-permute-start.46 = (bf16[48,768]{1,0:T(8,128)(2,1)S(1)}, bf16[48,768]{1,0:T(8,128)(2,1)S(1)}, u32[]{:S(2)}, u32[]{:S(2)}) collective-permute-start(bf16[48,768]{1,0:T(8,128)(2,1)S(1)} %get-tuple-element.166), channel_id=1, source_target_pairs={{0,16},{1,17},{2,18},{3,19},{4,20},{5,21},{6,22},{7,23},{8,24},{9,... | collective-permute-start | bytes 221192 | tf_op jit(solution)/shard_map/ppermute | solution.py:978
  397.8 7.4 %collective-permute-start.50 = (bf16[4,96,384]{2,1,0:T(8,128)(2,1)S(1)}, bf16[4,96,384]{2,1,0:T(8,128)(2,1)S(1)}, u32[]{:S(2)}, u32[]{:S(2)}) collective-permute-start(bf16[4,96,384]{2,1,0:T(8,128)(2,1)S(1)} %get-tuple-element.172), channel_id=1, source_target_pairs={{0,4},{1,5},{2,6},{3,7},{4,0},{5,1},{6,2},{7,3},{8,12},{9,13},{10,... | collective-permute-start | bytes 884744 | tf_op jit(solution)/shard_map/ppermute | solution.py:978
  405.5 11.0 %collective-permute-start.53 = (bf16[48,768]{1,0:T(8,128)(2,1)S(1)}, bf16[48,768]{1,0:T(8,128)(2,1)S(1)}, u32[]{:S(2)}, u32[]{:S(2)}) collective-permute-start(bf16[48,768]{1,0:T(8,128)(2,1)S(1)} %add_add_fusion.1), channel_id=1, source_target_pairs={{0,24},{1,25},{2,26},{3,27},{4,28},{5,29},{6,30},{7,31},{8,16},{9,... | collective-permute-start | bytes 221192 | tf_op jit(solution)/shard_map/ppermute | solution.py:978
  409.0 7.5 %collective-permute-start.54 = (f32[19,768]{1,0:T(8,128)S(1)}, f32[19,768]{1,0:T(8,128)S(1)}, u32[]{:S(2)}, u32[]{:S(2)}) collective-permute-start(f32[19,768]{1,0:T(8,128)S(1)} %add.292), channel_id=1, source_target_pairs={{0,8},{1,9},{2,10},{3,11},{4,12},{5,13},{6,14},{7,15},{8,0},{9,1},... | collective-permute-start | bytes 175112 | tf_op jit(solution)/shard_map/ppermute | solution.py:978
  409.0 9.2 %collective-permute-start.52 = (bf16[48,768]{1,0:T(8,128)(2,1)S(1)}, bf16[48,768]{1,0:T(8,128)(2,1)S(1)}, u32[]{:S(2)}, u32[]{:S(2)}) collective-permute-start(bf16[48,768]{1,0:T(8,128)(2,1)S(1)} %add_add_fusion.1), channel_id=1, source_target_pairs={{0,16},{1,17},{2,18},{3,19},{4,20},{5,21},{6,22},{7,23},{8,24},{9,... | collective-permute-start | bytes 221192 | tf_op jit(solution)/shard_map/ppermute | solution.py:978
  409.9 8.4 %collective-permute-start.51 = (bf16[48,768]{1,0:T(8,128)(2,1)S(1)}, bf16[48,768]{1,0:T(8,128)(2,1)S(1)}, u32[]{:S(2)}, u32[]{:S(2)}) collective-permute-start(bf16[48,768]{1,0:T(8,128)(2,1)S(1)} %add_add_fusion.1), channel_id=1, source_target_pairs={{0,8},{1,9},{2,10},{3,11},{4,12},{5,13},{6,14},{7,15},{8,0},{9,1},... | collective-permute-start | bytes 221192 | tf_op jit(solution)/shard_map/ppermute | solution.py:978
  411.0 10.0 %collective-permute-start.55 = (bf16[96,768]{1,0:T(8,128)(2,1)S(1)}, bf16[96,768]{1,0:T(8,128)(2,1)S(1)}, u32[]{:S(2)}, u32[]{:S(2)}) collective-permute-start(bf16[96,768]{1,0:T(8,128)(2,1)S(1)} %get-tuple-element.176), channel_id=1, source_target_pairs={{0,8},{1,9},{2,10},{3,11},{4,12},{5,13},{6,14},{7,15},{8,0},{9,1},... | collective-permute-start | bytes 442376 | tf_op jit(solution)/shard_map/ppermute | solution.py:978
  416.5 10.0 %collective-permute-start.56 = (bf16[96,768]{1,0:T(8,128)(2,1)S(1)}, bf16[96,768]{1,0:T(8,128)(2,1)S(1)}, u32[]{:S(2)}, u32[]{:S(2)}) collective-permute-start(bf16[96,768]{1,0:T(8,128)(2,1)S(1)} %get-tuple-element.177), channel_id=1, source_target_pairs={{0,16},{1,17},{2,18},{3,19},{4,20},{5,21},{6,22},{7,23},{8,24},{9,... | collective-permute-start | bytes 442376 | tf_op jit(solution)/shard_map/ppermute | solution.py:978
  416.5 10.0 %collective-permute-start.57 = (bf16[96,768]{1,0:T(8,128)(2,1)S(1)}, bf16[96,768]{1,0:T(8,128)(2,1)S(1)}, u32[]{:S(2)}, u32[]{:S(2)}) collective-permute-start(bf16[96,768]{1,0:T(8,128)(2,1)S(1)} %get-tuple-element.178), channel_id=1, source_target_pairs={{0,24},{1,25},{2,26},{3,27},{4,28},{5,29},{6,30},{7,31},{8,16},{9,... | collective-permute-start | bytes 442376 | tf_op jit(solution)/shard_map/ppermute | solution.py:978
  426.6 10.7 %collective-permute-start.60 = (bf16[4,48,768]{2,1,0:T(8,128)(2,1)S(1)}, bf16[4,48,768]{2,1,0:T(8,128)(2,1)S(1)}, u32[]{:S(2)}, u32[]{:S(2)}) collective-permute-start(bf16[4,48,768]{2,1,0:T(8,128)(2,1)S(1)} %pad_maximum_fusion.6), channel_id=1, source_target_pairs={{0,6},{1,7},{2,4},{3,5},{4,2},{5,3},{6,0},{7,1},{8,14},{9,15},{10,... | collective-permute-start | bytes 884744 | tf_op jit(solution)/shard_map/ppermute | solution.py:978
  427.9 12.0 %collective-permute-start.59 = (bf16[4,48,768]{2,1,0:T(8,128)(2,1)S(1)}, bf16[4,48,768]{2,1,0:T(8,128)(2,1)S(1)}, u32[]{:S(2)}, u32[]{:S(2)}) collective-permute-start(bf16[4,48,768]{2,1,0:T(8,128)(2,1)S(1)} %pad_maximum_fusion.6), channel_id=1, source_target_pairs={{0,2},{1,3},{2,0},{3,1},{4,6},{5,7},{6,4},{7,5},{8,10},{9,11},{10,... | collective-permute-start | bytes 884744 | tf_op jit(solution)/shard_map/ppermute | solution.py:978
  429.2 10.7 %collective-permute-start.58 = (bf16[4,48,768]{2,1,0:T(8,128)(2,1)S(1)}, bf16[4,48,768]{2,1,0:T(8,128)(2,1)S(1)}, u32[]{:S(2)}, u32[]{:S(2)}) collective-permute-start(bf16[4,48,768]{2,1,0:T(8,128)(2,1)S(1)} %pad_maximum_fusion.6), channel_id=1, source_target_pairs={{0,4},{1,5},{2,6},{3,7},{4,0},{5,1},{6,2},{7,3},{8,12},{9,13},{10,... | collective-permute-start | bytes 884744 | tf_op jit(solution)/shard_map/ppermute | solution.py:978
  430.1 11.3 %collective-permute-start.61 = (bf16[96,768]{1,0:T(8,128)(2,1)S(1)}, bf16[96,768]{1,0:T(8,128)(2,1)S(1)}, u32[]{:S(2)}, u32[]{:S(2)}) collective-permute-start(bf16[96,768]{1,0:T(8,128)(2,1)S(1)} %add_add_fusion.refs_1_), channel_id=1, source_target_pairs={{0,2},{1,3},{2,0},{3,1},{4,6},{5,7},{6,4},{7,5},{8,10},{9,11},{10,... | collective-permute-start | bytes 442376 | tf_op jit(solution)/shard_map/ppermute | solution.py:978
  441.5 16.7 %collective-permute-start.62 = (bf16[16,48,768]{2,1,0:T(8,128)(2,1)S(1)}, bf16[16,48,768]{2,1,0:T(8,128)(2,1)S(1)}, u32[]{:S(2)}, u32[]{:S(2)}) collective-permute-start(bf16[16,48,768]{2,1,0:T(8,128)(2,1)S(1)} %pad_maximum_fusion.refs_1_), channel_id=1, source_target_pairs={{0,1},{1,0},{2,3},{3,2},{4,5},{5,4},{6,7},{7,6},{8,9},{9,8},{10,11... | collective-permute-start | bytes 3538952 | tf_op jit(solution)/shard_map/ppermute | solution.py:978
  446.0 7.1 %collective-permute-start.63 = (f32[19,768]{1,0:T(8,128)S(1)}, f32[19,768]{1,0:T(8,128)S(1)}, u32[]{:S(2)}, u32[]{:S(2)}) collective-permute-start(f32[19,768]{1,0:T(8,128)S(1)} %add.294), channel_id=1, source_target_pairs={{0,16},{1,17},{2,18},{3,19},{4,20},{5,21},{6,22},{7,23},{8,24},{9,... | collective-permute-start | bytes 175112 | tf_op jit(solution)/shard_map/ppermute | solution.py:978
  446.1 9.1 %collective-permute-start.64 = (bf16[2,96,768]{2,1,0:T(8,128)(2,1)S(1)}, bf16[2,96,768]{2,1,0:T(8,128)(2,1)S(1)}, u32[]{:S(2)}, u32[]{:S(2)}) collective-permute-start(bf16[2,96,768]{2,1,0:T(8,128)(2,1)S(1)} %pad_maximum_fusion.7), channel_id=1, source_target_pairs={{0,1},{1,0},{2,3},{3,2},{4,5},{5,4},{6,7},{7,6},{8,9},{9,8},{10,11... | collective-permute-start | bytes 884744 | tf_op jit(solution)/shard_map/ppermute | solution.py:978
  (51 other events, 389.5 us)

commit v3 on v2

--- a/solution.py
+++ b/solution.py
@@ -14,9 +14,10 @@
 RD = 8
 PAD = 16
 PART = D // 2
+SMALL = 24
 LANES = 128
-CHUNK = 256
-FB = 256
+CHUNK = 384
+FB = 768
 EPS = 1e-6
 NEG = -1e30
 F32 = jnp.float32
@@ -67,7 +68,7 @@
 
 
 def call(kernel, out_shape, deps=(), **kw):
-    limit = kw.pop("vmem", 56)
+    limit = kw.pop("vmem", 20)
     estimate = kw.pop("cost", None)
     in_specs = kw.pop("in_specs")
     count, more = len(in_specs), len(deps)
@@ -123,11 +124,11 @@
             fetch_array(ids, arrays[k], target, sem)
 
 
-def fetch_array(ids, array, target, sem):
+def fetch_array(ids, array, target, sem, in_order=False):
     places, rows = array.shape[0], array.shape[1]
     for place in range(places):
-        shard = ids[1] ^ place_bits(place, places)
-        start = pl.multiple_of(shard * rows, 16)
+        shard = place if in_order else ids[1] ^ place_bits(place, places)
+        start = shard * rows if in_order else pl.multiple_of(shard * rows, 16)
         pltpu.make_async_copy(array.at[place], target.at[pl.ds(start, rows), :], sem).start()
 
 
@@ -540,7 +541,7 @@
     def _():
         for i in range(nk):
             fetch_array(ids, weights[2 * i], up.at[i], sem.at[i, 0])
-            fetch_array(ids, weights[2 * i + 1], down.at[i], sem.at[i, 1])
+            fetch_array(ids, weights[2 * i + 1], down.at[i], sem.at[i, 1], True)
         sums[...] = sums_in[...]
         if first:
             total[...] = total_in[...] + line(down_bias)
@@ -765,33 +766,38 @@
     )(ids, normed, mixed, grads, attn_grad)
 
 
-def first_keep_kernel(
-    places, part, y_first, ids, normed, mixed, grads, attn_grad, got, keep, give, left, right, sem
-):
+def first_keep_kernel(places, part, y_first, ids, normed, mixed, grads, attn_grad, got, *refs):
+    keep, give, left, right, sem = refs[-5:]
     sources = (normed, mixed, grads, attn_grad)
     for i, k in enumerate((0, 2)):
         first_fetch(ids, k, part, *sources, left.at[i], right.at[i], sem.at[i])
     for i in range(2):
         fetched(left.at[i], sem.at[i, 0])
         fetched(right.at[i], sem.at[i, 1])
+    if len(refs) > 5:
+        before = refs[0]
+        give[:, :, :, :PART] = before[...]
+        give = give.at[:, :, :, pl.ds(PART, PART)]
     to_keep_kernel(
         places, y_first, ids, left.at[0], right.at[0], left.at[1], right.at[1], got.at[0], got.at[1],
         keep, give
     )
 
 
-def first_keep(ids, part, normed, mixed, grads, attn_grad, got, places, y_first, deps=()):
+def first_keep(
+    ids, part, normed, mixed, grads, attn_grad, got, places, y_first, deps=(), before=None
+):
     total = normed.shape[0]
     half = struct((2, max(places // 2, 1), D // places, PART), BF16)
     return call(
         functools.partial(first_keep_kernel, places, part, y_first),
-        (half, half),
+        (half, half if before is None else struct(half.shape[:3] + (D,), BF16)),
         deps,
-        in_specs=[SMEM, ANY, ANY, ANY, ANY, VMEM],
+        in_specs=[SMEM, ANY, ANY, ANY, ANY, VMEM] + [VMEM] * (before is not None),
         out_specs=(VMEM, VMEM),
         scratch_shapes=first_scratch(total),
         cost=cost(6),
-    )(ids, normed, mixed, grads, attn_grad, got)
+    )(ids, normed, mixed, grads, attn_grad, got, *([] if before is None else [before]))
 
 
 def qkv_back_kernel(capacity, ids, grads0, grads1, *refs):
@@ -834,68 +840,98 @@
     )(ids, *grads, *weights, stream, gain, after_grad)
 
 
-def stem_back_kernel(cut, places, ids, raw, embedded, keep, give, sums):
+def stem_back_kernel(cut, places, ids, raw, embedded, *refs):
+    keep, give = refs[-4:-2], refs[-2:]
+    rows = D // places // 2
+    small = [part[...] for part in refs[:-4]]
+    sums = [
+        jnp.sum(embedded[part, :].astype(F32), axis=0, keepdims=True)
+        for part in (slice(0, cut), slice(cut, None))
+    ]
+    small = jnp.concatenate(sums + small, axis=0)
+    small = jnp.concatenate([small, jnp.zeros((SMALL - small.shape[0], D), F32)], axis=0)
     for stem, part in enumerate((slice(0, cut), slice(cut, None))):
-        sums[stem : stem + 1, :] = jnp.sum(embedded[part, :].astype(F32), axis=0, keepdims=True)
-        value = tn(raw[part, :], embedded[part, :]).astype(BF16)
-        if places == 1:
-            (give if stem else keep)[...] = value.reshape(keep.shape)
-            continue
-        rows = D // places // 2
+        value = tn(raw[part, :], embedded[part, :])
         mine = (ids[0] & 1) == stem
         for i in range(2 * places):
             place = place_of(ids[1] ^ (i // 2))
             x = (i % 2) ^ (ids[0] >> 1)
-            at = (x * 2 + (place >> 2)) * 4 + (place & 3)
-            piece = value[i * rows : (i + 1) * rows][None]
-
-            @pl.when(mine)
-            def _():
-                keep[pl.ds(at, 1)] = piece
-
-            @pl.when(jnp.logical_not(mine))
-            def _():
-                give[pl.ds(at, 1)] = piece
-
-
-def stem_back(ids, raw, embedded, places, deps=()):
+            more = jnp.zeros((8, D), F32)
+            if stem == 0 and 8 * i < SMALL:
+                more = small[8 * i : 8 * i + 8]
+            piece = jnp.concatenate([value[i * rows : (i + 1) * rows], more], axis=0)
+            piece = piece.astype(BF16)[None]
+
+            for side in range(2):
+
+                @pl.when(mine & (x == side))
+                def _():
+                    keep[side][pl.ds(place, 1)] = piece
+
+                @pl.when(jnp.logical_not(mine) & (x == side))
+                def _():
+                    give[side][pl.ds(place, 1)] = piece
+
+
+def stem_back_plain_kernel(cut, raw, embedded, *refs):
+    keep, give, out = refs[-3:]
+    sums = [
+        jnp.sum(embedded[part, :].astype(F32), axis=0, keepdims=True)
+        for part in (slice(0, cut), slice(cut, None))
+    ]
+    small = jnp.concatenate(sums + [part[...] for part in refs[:-3]], axis=0)
+    out[...] = jnp.concatenate([small, jnp.zeros((SMALL - small.shape[0], D), F32)], axis=0)
+    keep[0] = tn(raw[:cut, :], embedded[:cut, :]).astype(BF16)
+    give[0] = tn(raw[cut:, :], embedded[cut:, :]).astype(BF16)
+
+
+def stem_back(ids, raw, embedded, small, places, deps=()):
     capacity = raw.shape[0]
-    shape = (2 * places, D // (2 * places), D) if places > 1 else (1, D, D)
-    return call(
-        functools.partial(stem_back_kernel, 3 * capacity // 4, places),
-        (struct(shape, BF16), struct(shape, BF16), struct((2, D), F32)),
+    cut = 3 * capacity // 4
+    if places == 1:
+        return call(
+            functools.partial(stem_back_plain_kernel, cut),
+            (struct((1, D, D), BF16), struct((1, D, D), BF16), struct((SMALL, D), F32)),
+            deps,
+            in_specs=[VMEM, VMEM] + [VMEM] * len(small),
+            out_specs=(VMEM, VMEM, VMEM),
+            cost=cost(6),
+        )(raw, embedded, *small)
+    shape = (places, D // (2 * places) + 8, D)
+    return call(
+        functools.partial(stem_back_kernel, cut, places),
+        (struct(shape, BF16),) * 4,
         deps,
-        in_specs=[SMEM, VMEM, VMEM],
-        out_specs=(VMEM, VMEM, VMEM),
+        in_specs=[SMEM, VMEM, VMEM] + [VMEM] * len(small),
+        out_specs=(VMEM,) * 4,
         cost=cost(6),
-    )(ids, raw, embedded)
-
-
-def stem_out_kernel(ids, own, other, patch, lang):
-    rows = own.shape[1]
+    )(ids, raw, embedded, *small)
+
+
+def stem_out_kernel(ids, own, other, patch, lang, small):
+    rows = own.shape[1] - 8
     for i in range(own.shape[0]):
         shard = ids[1] ^ place_bits(((i >> 2) & 1) * 4 + (i & 3), 8)
         x = (i >> 3) ^ (ids[0] >> 1)
-        at = pl.ds(pl.multiple_of((shard * 2 + x) * rows, 16), rows)
+        slot = shard * 2 + x
+        at = pl.ds(pl.multiple_of(slot * rows, 16), rows)
         mine, theirs = own[i].astype(F32), other[i].astype(F32)
-
-        @pl.when((ids[0] & 1) == 0)
+        first = (ids[0] & 1) == 0
+        pieces = jnp.where(first, mine, theirs), jnp.where(first, theirs, mine)
+        patch[at, :] = pieces[0][:rows]
+        lang[at, :] = pieces[1][:rows]
+
+        @pl.when(slot * 8 < SMALL)
         def _():
-            patch[at, :] = mine
-            lang[at, :] = theirs
-
-        @pl.when((ids[0] & 1) == 1)
-        def _():
-            patch[at, :] = theirs
-            lang[at, :] = mine
+            small[pl.ds(pl.multiple_of(slot * 8, 8), 8), :] = pieces[0][rows:]
 
 
 def stem_out(ids, own, other):
     return call(
         stem_out_kernel,
-        (struct((D, D), F32), struct((D, D), F32)),
+        (struct((D, D), F32), struct((D, D), F32), struct((SMALL, D), F32)),
         in_specs=[SMEM, VMEM, VMEM],
-        out_specs=(VMEM, VMEM),
+        out_specs=(VMEM, VMEM, VMEM),
         cost=cost(4.4),
     )(ids, own, other)
 
@@ -993,6 +1029,16 @@
 def gather_z(grid, piece):
     parts = [piece] + [grid.swap(piece, **bit) for bit in (Z0, Z1, Z01)]
     return jnp.stack(parts)
+
+
+def double_z(grid, piece):
+    value = jnp.stack([piece, grid.swap(piece, **Z0)])
+    return joined(value, grid.swap(value, **Z1))
+
+
+def halve_z(grid, value):
+    value = value[:2] + grid.swap(value[2:], **Z1)
+    return value[0] + grid.swap(value[1], **Z0)
 
 
 def reduce_z(grid, parts):
@@ -1053,19 +1099,20 @@
         ).reshape(-1, D)
         piece_down = lax.dynamic_slice_in_dim(down_weight, rank * quarter, quarter, 0)
         first_z = gather_z(grid, piece)
+        first_y = grid.swap(first_z, **Y)
+        first_x = grid.swap(first_z, **X)
         up_z = gather_z(grid, tie(piece_up, first_z))
-        raw_rows = tie(raw_rows, first_z)
+        raw_rows = tie(raw_rows, first_y, up_z)
     received = lax.all_to_all(raw_rows, "mod", split_axis=0, concat_axis=0, tiled=True)
     rows = received.reshape(capacity, D)
     branch, down_bias_grad = prepare(out_cotangent[0], recv_counts, read_counts, block_rows, total)
     if fast:
-        first0 = joined(first_z, grid.swap(first_z, **Y))
-        first2 = grid.swap(first0, **X)
+        first0 = joined(first_z, first_y)
+        first2 = joined(first_x, grid.swap(first_y, **X))
         first1 = grid.swap(first0, **CORE)
         first3 = grid.swap(first2, **CORE)
         first = (first0, first1, first2, first3)
-        up0 = joined(up_z, grid.swap(tie(up_z, first0), **Y))
-        rows, up0 = lax.optimization_barrier((rows, up0))
+        down0 = lax.all_gather(piece_down, "mod", axis=0)
     else:
         whole = lambda w: lax.all_gather(w, "mod", axis=0, tiled=True)
         every = jnp.concatenate([whole(qkv_weight), whole(out_weight)], axis=1)
@@ -1086,24 +1133,22 @@
         attn_gain,
         attn_bias,
     )
+    if fast:
+        down2 = grid.swap(tie(down0, first1, first3), **X)
+    qkv = project_qkv(ids, normed, first)
     deps = ()
-    if fast:
-        down_z = gather_z(grid, tie(piece_down, rows))
-        up2 = grid.swap(tie(up0, first2, rows), **X)
-        deps = (down_z,)
-    qkv = project_qkv(ids, normed, first)
     mixed, lse, lse_read = attend(qkv, *marks, block_rows, deps)
     deps = ()
     if fast:
-        down0 = joined(down_z, grid.swap(tie(down_z, qkv), **Y))
-        up1 = grid.swap(tie(up0, qkv), **CORE)
-        deps = (down0, up1, up2)
+        down1 = grid.swap(tie(down0, up_z), **CORE)
+        up0 = joined(up_z, grid.swap(tie(up_z, first_y), **Y))
+        deps = (up0, down1, down2)
     after, normed2 = out_project(ids, mixed, first, stream, mlp_gain, mlp_bias, deps)
+    deps = ()
     if fast:
-        down2 = grid.swap(tie(down0, up2), **X)
-        down1 = grid.swap(down0, **CORE)
-        up3 = grid.swap(tie(up2, mixed), **CORE)
-        deps = (up3,)
+        up1 = grid.swap(up0, **CORE)
+        up2 = grid.swap(tie(up0, down2, down1), **X)
+        down3 = grid.swap(tie(down2, mixed), **CORE)
     sums = jnp.zeros((4, D), F32)
     step = lambda ks, state, weights, first_call, last_call, deps: mlp(
         ids, ks, recv_counts, read_counts, normed2, branch, up_bias_rows, down_bias, state,
@@ -1116,7 +1161,7 @@
     at = [act_spec(total, i) for i in range(2)]
     deps = ()
     if fast:
-        down3 = grid.swap(tie(down2, inner), **CORE)
+        up3 = grid.swap(tie(up2, inner), **CORE)
     give1 = give_products(
         ids, [(normed2, hidden01), (active01, branch)], [(spec, at[1]), (at[1], spec)], places
     )
@@ -1159,96 +1204,83 @@
     grads_b = attend_back(
         qkv, mixed, mixed_grad, lse, lse_read, *marks, block_rows, 1, deps
     )
-    deps = (grads_b,)
+    first_b13 = first_give(ids, 1, normed, mixed, grads_b, attn_grad, places)
+    keep_a, give_a = first_keep(
+        ids, 0, normed, mixed, grads_a, attn_grad, got_a, places, False, (first_b13,)
+    )
+    got_b = grid.swap(first_b13, **CORE) if fast else jnp.zeros_like(first_b13)
+    deps = (keep_a,)
     if fast:
         got_up = grid.swap(tie(up_x[1], grads_a), **X)
         got_down = grid.swap(tie(down_y[1], grads_a), **Y)
-        up_w = [up_x[0][i] + got_up[i] for i in range(4)]
-        down_w = [down_y[0][i] + got_down[i] for i in range(4)]
-        deps = deps + (got_up, got_down)
-    keep_a, give_a = first_keep(
-        ids, 0, normed, mixed, grads_a, attn_grad, got_a, places, False, deps
-    )
-    first_b13 = first_give(ids, 1, normed, mixed, grads_b, attn_grad, places, (keep_a,))
-    deps = (first_b13,)
-    if fast:
-        got_b = grid.swap(first_b13, **CORE)
-        deps = deps + (got_b,)
-    else:
-        got_b = jnp.zeros_like(first_b13)
+        both = jnp.stack([up_x[0] + got_up, down_y[0] + got_down], axis=1)
+        deps = deps + (both,)
+    keep_b, give_b = first_keep(
+        ids, 1, normed, mixed, grads_b, attn_grad, got_b, places, False, deps, give_a
+    )
     embedded_grad, readout_grad, attn_sums = qkv_back(
-        ids, (grads_a, grads_b), first, stream, attn_gain, after_grad, deps
+        ids, (grads_a, grads_b), first, stream, attn_gain, after_grad, (keep_b,)
     )
     returned = lax.all_to_all(
         embedded_grad.reshape(raw_rows.shape), "mod", split_axis=0, concat_axis=0, tiled=True
     )
-    deps = ()
-    if fast:
-        got = grid.swap(tie(give_a, first_b13), **X)
-        own_a, pass_a = keep_a[0] + got[0], keep_a[1] + got[1]
-        both = jnp.stack([reduce_z(grid, up_w), reduce_z(grid, down_w)])
-        deps = (own_a, pass_a, both)
-    stem_keep, stem_give, stem_sums = stem_back(ids, rows, embedded_grad, places, deps)
-    keep_b, give_b = first_keep(
-        ids, 1, normed, mixed, grads_b, attn_grad, got_b, places, False, (stem_keep,)
-    )
-    raw_grad = raw_back(
-        image,
-        returned.reshape(capacity, D),
-        patch_convolution_weight,
-        language_projection_weight,
-    ).reshape(raw_rows.shape)
-
-    small = jnp.concatenate(
-        [stem_sums, attn_sums, mlp_sums, down_bias_grad, sums, readout_grad], axis=0
-    )
+    small = (attn_sums, mlp_sums, down_bias_grad, sums, readout_grad)
+    stem_parts = stem_back(ids, rows, embedded_grad, small, places)
+
     if fast:
         together = lambda *values: lax.optimization_barrier(values)
-        got_y = grid.swap(tie(pass_a, stem_keep), **Y)
-        got = grid.swap(stem_give, **CORE)
-        got_small = grid.swap(small, **CORE)
-        parts = [stem_keep[4 * i : 4 * i + 4] + got[4 * i : 4 * i + 4] for i in range(4)]
-        small = small + got_small
-        *parts, small, give_b, both = together(*parts, small, give_b, both)
+        got_z = grid.swap(both[2:], **Z1)
+        got_x = grid.swap(give_b, **X)
+        got = [grid.swap(give, **CORE) for give in stem_parts[2:]]
+        parts = [
+            stem_parts[x][4 * y : 4 * y + 4] + got[x][4 * y : 4 * y + 4]
+            for x in range(2)
+            for y in range(2)
+        ]
+        own = jnp.concatenate([keep_a[0], keep_b[0]], axis=2) + got_x[0]
+        away = jnp.concatenate([keep_a[1], keep_b[1]], axis=2) + got_x[1]
+        both = both[:2] + got_z
+        *parts, own, away, both = together(*parts, own, away, both)
         got = [grid.swap(part, **bit) for part, bit in zip(parts[1:], (Y, X, XY))]
-        got_small = grid.swap(small, **X)
-        got_x = grid.swap(give_b, **X)
-        from_x = grid.swap(both, **X)
         parts = [parts[0][i] + got[0][i] + got[1][i] + got[2][i] for i in range(4)]
-        small = small + got_small
-        own_b, pass_b = keep_b[0] + got_x[0], keep_b[1] + got_x[1]
-        own_a = own_a + got_y
-        *parts, small, pass_b, own_b, own_a, from_x, returned_ = together(
-            *parts, small, pass_b, own_b, own_a, from_x, returned
+        *parts, away, own, returned, both = together(*parts, away, own, returned, both)
+        got_both = grid.swap(both[1], **Z0)
+        got_y = grid.swap(away, **Y)
+        piece = reduce_z(grid, parts)
+        last = own + got_y
+        both = both[0] + got_both
+        piece, last, both = together(piece, last, both)
+        both_x = grid.swap(both, **X)
+        got_z = grid.swap(last[2:], **Z1)
+        piece = gather_z(grid, piece)
+        last = last[:2] + got_z
+        raw_grad = raw_back(
+            image,
+            returned.reshape(capacity, D),
+            patch_convolution_weight,
+            language_projection_weight,
         )
-        got_y = grid.swap(pass_b, **Y)
-        got_small = grid.swap(small, **Y)
-        from_core = grid.swap(jnp.stack([both, from_x]), **CORE)
-        piece = reduce_z(grid, parts)
-        small = small + got_small
-        own_b = own_b + got_y
-        lasts = [jnp.concatenate([own_a[i], own_b[i]], axis=1) for i in range(4)]
-        piece, small, from_core, *lasts = together(piece, small, from_core, *lasts)
-        got_small = grid.swap(small, **Z0)
-        piece = gather_z(grid, piece)
-        small = small + got_small
-        last = reduce_z(grid, lasts)
-        piece, small, last = together(piece, small, last)
-        got_small = grid.swap(small, **Z1)
+        piece, last, raw_grad, layer_out, both_x = together(
+            piece, last, raw_grad, layer_out, both_x
+        )
+        both_core = grid.swap(jnp.stack([both, both_x]), **CORE)
+        got_z = grid.swap(last[1], **Z0)
+        piece = joined(piece, *[grid.swap(piece, **bit) for bit in (Y, X, XY)])
+        last = last[0] + got_z
+        piece, last, both_core = together(piece, last, both_core)
+        up_sum, down_sum = mlp_out(ids, both, both_x, both_core, places)
         last_x = grid.swap(last, **X)
-        piece = joined(piece, *[grid.swap(piece, **bit) for bit in (Y, X, XY)])
-        small = small + got_small
-        piece, last_x = together(piece, last_x)
+        theirs = grid.swap(piece, **CORE)
+        theirs, last_x, up_sum = together(theirs, last_x, up_sum)
         last_core = grid.swap(jnp.stack([last, last_x]), **CORE)
-        patch_sum, lang_sum = stem_out(ids, piece, grid.swap(piece, **CORE))
-        up_sum, down_sum = mlp_out(ids, both, from_x, from_core, places)
+        patch_sum, lang_sum, small = stem_out(ids, piece, theirs)
         qkv_sum, out_sum = first_out(ids, last, last_x, last_core)
     else:
         reduced = lambda v: lax.psum(
             lax.psum_scatter(v, "mod", scatter_dimension=0, tiled=True), "rep"
         ).astype(F32)
         every = []
-        for keep, other, give in ((keep_a, first_a13, give_a), (keep_b, first_b13, give_b)):
+        for keep, other, give in ((keep_a, first_a13, give_a), (keep_b, first_b13, give_b[..., PART:])):
             every.append(jnp.stack([keep[0, 0], other[0, 0], give[0, 0], other[1, 0]], axis=1))
         every = reduced(jnp.concatenate(every, axis=2).reshape(D, -1))
         qkv_sum, out_sum = every[:, : 3 * D], every[:, 3 * D :]
@@ -1258,9 +1290,17 @@
         every = jnp.stack([keep_down[0, 0], give1[1, 0], give_down[0, 0], give3[1, 0]])
         every = every.reshape(4, mods, units, D).transpose(1, 0, 2, 3).reshape(-1, D)
         down_sum = reduced(every)
+        stem_keep, stem_give, small = stem_parts
         small = lax.psum(small, AXES)
         patch_sum = lax.psum(stem_keep[0].astype(F32), AXES)
         lang_sum = lax.psum(stem_give[0].astype(F32), AXES)
+        raw_grad = raw_back(
+            image,
+            returned.reshape(capacity, D),
+            patch_convolution_weight,
+            language_projection_weight,
+        )
+    raw_grad = raw_grad.reshape(raw_rows.shape)
     up_bias_sum = small[7:11].reshape(4, -1, units).transpose(1, 0, 2).reshape(-1)
     return (
         layer_out,

time: 467 us -> 402 us (0.86)
  Pallas kernels: 207 us -> 135 us
  starting transfers between devices: 87.5 us -> 62.3 us
  between operations: 2.58 us -> 16.1 us
  local copies, waits for them, and re-layouts: 23 us -> 29.4 us
  waiting for transfers between devices: 137 us -> 142 us
    pallas_call x24, Pallas kernels: 207 us -> 135 us  [call(): return lambda *args: built(*args, *deps)]
    ppermute x65 -> x51, starting transfers between devices: 71.6 us -> 54.8 us  [swap(): return lax.ppermute(value, AXES, pairs)]
    unnamed x107 -> x112, local copies, waits for them, and re-layouts: 11.6 us -> 17.3 us
    all_to_all x1, starting transfers between devices: 8.82 us -> 3.56 us  [per_device(): lax.all_to_all(embedded_grad.reshape(raw_rows.shape), 'mod', split_axis=0...]
    ppermute x65 -> x51, waiting for transfers between devices: 137 us -> 141 us  [swap(): return lax.ppermute(value, AXES, pairs)]
  transfers between devices with their start and end apart: 67 -> 54, of which waited for: 26 -> 24; matrix products, arithmetic and copies ran while one was open for 4% -> 7% of each run, Pallas kernels for 34% -> 32%
where the time goes in v3:
time: 402 us; the launch traced here: 396 us
  waiting for transfers between devices  142 us (35%)
  Pallas kernels  135 us (34%)
  starting transfers between devices  62.3 us (15%)
  local copies, waits for them, and re-layouts  29.4 us (7%)
  between operations  16.1 us (4%)
  other arithmetic  10.6 us (3%)
    ppermute x51, waiting for transfers between devices, swap(): return lax.ppermute(value, AXES, pairs)  141 us
    pallas_call x24, Pallas kernels, call(): return lambda *args: built(*args, *deps)  135 us
    ppermute x51, starting transfers between devices, swap(): return lax.ppermute(value, AXES, pairs)  54.8 us
    unnamed x112, local copies, waits for them, and re-layouts  17.3 us
  transfers between devices with their start and end apart: 54, of which 24 were waited for; matrix products, arithmetic and copies ran while one was open for 7% of the time, Pallas kernels for 32%

profile of v3, /device:TPU:0, one launch (start us, length us, event | category | flops | bytes accessed | tf_op | source)
XLA Modules:
  0.0 395.5 jit_solution(13577702066835566830)
XLA Ops:
  7.3 1.7 constant_dynamic-update-slice_fusion.4
  9.0 4.0 %collective-permute-start.1 = (bf16[96,768]{1,0:T(8,128)(2,1)S(1)}, bf16[96,768]{1,0:T(8,128)(2,1)S(1)}, u32[]{:S(2)}, u32[]{:S(2)}) collective-permute-start(bf16[96,768]{1,0:T(8,128)(2,1)S(1)} %get-tuple-element.197), channel_id=1, source_target_pairs={{0,16},{1,17},{2,18},{3,19},{4,20},{5,21},{6,22},{7,23},{8,24},{9,... | collective-permute-start | bytes 442376 | tf_op jit(solution)/shard_map/ppermute | solution.py:1014
  14.6 7.1 %collective-permute-done.1 = bf16[96,768]{1,0:T(8,128)(2,1)S(1)} collective-permute-done((bf16[96,768]{1,0:T(8,128)(2,1)S(1)}, bf16[96,768]{1,0:T(8,128)(2,1)S(1)}, u32[]{:S(2)}, u32[]{:S(2)}) %collective-permute-start.1) | collective-permute-done | bytes 147488 | tf_op jit(solution)/shard_map/ppermute | solution.py:1014
  21.7 2.7 collective-permute-done.2
  29.6 2.5 collective-permute-start.6
  32.2 2.2 collective-permute-start.5
  37.7 1.6 collective-permute-done.3
  40.8 9.8 %collective-permute-done.5 = bf16[96,768]{1,0:T(8,128)(2,1)S(1)} collective-permute-done((bf16[96,768]{1,0:T(8,128)(2,1)S(1)}, bf16[96,768]{1,0:T(8,128)(2,1)S(1)}, u32[]{:S(2)}, u32[]{:S(2)}) %collective-permute-start.5) | collective-permute-done | bytes 147488 | tf_op jit(solution)/shard_map/ppermute | solution.py:1014
  51.6 3.9 all-to-all-start
  56.1 1.9 constant_dynamic-update-slice_fusion.refs_2_.refs_5_.refs_3_
  59.3 2.7 collective-permute-done.9
  69.2 19.3 %collective-permute-done.11 = bf16[4,96,768]{2,1,0:T(8,128)(2,1)S(1)} collective-permute-done((bf16[4,96,768]{2,1,0:T(8,128)(2,1)}, bf16[4,96,768]{2,1,0:T(8,128)(2,1)S(1)}, u32[]{:S(2)}, u32[]{:S(2)}) %collective-permute-start.11) | collective-permute-done | bytes 589856 | tf_op jit(solution)/shard_map/ppermute | solution.py:1014
  95.2 1.6 shard_map.323
  96.9 6.2 %shard_map.324.refs_0_ = bf16[3,784,768]{2,1,0:T(8,128)(2,1)S(1)} custom-call(s32[2]{0:T(128)S(1)} %pad_add_fusion.refs_0_, bf16[784,768]{1,0:T(8,128)(2,1)S(1)} %get-tuple-element.103.refs_1_, bf16[8,96,768]{2,1,0:T(8,128)(2,1)} %constant_dynamic-update-slice_fusion.refs_2_.refs_5_.refs_3_, ...), custom_call_target="tpu_custom_call" | custom-call | flops 8049999872 | bytes 1048576 | tf_op jit(solution)/shard_map/pallas_call | solution.py:87
  103.1 15.3 %shard_map.325 = (bf16[784,768]{1,0:T(8,128)(2,1)S(1)}, f32[16,768]{1,0:T(8,128)S(1)}, f32[96,128]{1,0:T(8,128)S(1)}) custom-call(bf16[3,784,768]{2,1,0:T(8,128)(2,1)S(1)} %shard_map.324.refs_0_, s32[1,8]{1,0:T(1,128)S(1)} %copy-done.22, s32[1,1]{1,0:T(1,128)S(6)} %copy.56.refs_2_.refs_6_, s32[1,768]{1,0:T(1,128)S(1)} %copy-done.5, ...), custom_call_target="tpu_custom_call" | custom-call | flops 24149999616 | bytes 1048576 | tf_op jit(solution)/shard_map/pallas_call | solution.py:87
  119.7 3.8 shard_map.326
  123.6 11.1 %shard_map.328 = (bf16[2,784,768]{2,1,0:T(8,128)(2,1)S(1)}, bf16[2,784,768]{2,1,0:T(8,128)(2,1)S(1)}, f32[784,768]{1,0:T(8,128)S(1)}, f32[784,768]{1,0:T(8,128)S(1)}, f32[4,768]{1,0:T(4,128)S(1)}) custom-call(s32[2]{0:T(128)S(1)} %pad_add_fusion.refs_0_, s32[1,8]{1,0:T(1,128)S(1)} %copy-done.22, s32[1,1]{1,0:T(1,128)S(6)} %copy.56.refs_2_.refs_6_, ...), custom_call_target="tpu_custom_call" | custom-call | flops 23000000512 | bytes 1048576 | tf_op jit(solution)/shard_map/pallas_call | solution.py:87
  134.7 11.4 %collective-permute-done.15.refs_10_ = bf16[8,96,768]{2,1,0:T(8,128)(2,1)S(1)} collective-permute-done((bf16[8,96,768]{2,1,0:T(8,128)(2,1)}, bf16[8,96,768]{2,1,0:T(8,128)(2,1)S(1)}, u32[]{:S(2)}, u32[]{:S(2)}) %collective-permute-start.15) | collective-permute-done | bytes 1179680 | tf_op jit(solution)/shard_map/ppermute | solution.py:1014
  146.1 3.2 shard_map.329.refs_14_
  149.9 14.9 %shard_map.330 = (bf16[2,784,768]{2,1,0:T(8,128)(2,1)S(1)}, bf16[2,784,768]{2,1,0:T(8,128)(2,1)S(1)}, f32[784,768]{1,0:T(8,128)S(1)}, f32[784,768]{1,0:T(8,128)S(1)}, f32[4,768]{1,0:T(4,128)S(1)}) custom-call(s32[2]{0:T(128)S(1)} %pad_add_fusion.refs_0_, s32[1,8]{1,0:T(1,128)S(1)} %copy-done.22, s32[1,1]{1,0:T(1,128)S(6)} %copy.56.refs_2_.refs_6_, ...), custom_call_target="tpu_custom_call" | custom-call | flops 23000000512 | bytes 1048576 | tf_op jit(solution)/shard_map/pallas_call | solution.py:87
  164.8 3.2 shard_map.331.refs_9_
  168.6 1.7 copy-done.36
  170.2 4.7 %shard_map.332 = (f32[784,768]{1,0:T(8,128)S(1)}, bf16[784,768]{1,0:T(8,128)(2,1)S(1)}, bf16[784,768]{1,0:T(8,128)(2,1)S(1)}, f32[2,768]{1,0:T(2,128)S(1)}) custom-call(s32[2]{0:T(128)S(1)} %pad_add_fusion.refs_0_, f32[784,768]{1,0:T(8,128)S(1)} %copy-done.36, f32[784,768]{1,0:T(8,128)S(1)} %get-tuple-element.111.refs_7_.refs_8_.refs_2_, ...), custom_call_target="tpu_custom_call" | custom-call | flops 9774999552 | bytes 1048576 | tf_op jit(solution)/shard_map/pallas_call | solution.py:87
  175.0 3.3 shard_map.333
  178.3 5.1 %shard_map.334 = (bf16[2,4,96,768]{3,2,1,0:T(8,128)(2,1)S(1)}, bf16[2,4,96,768]{3,2,1,0:T(8,128)(2,1)S(1)}) custom-call(s32[2]{0:T(128)S(1)} %pad_add_fusion.refs_0_, bf16[784,768]{1,0:T(8,128)(2,1)S(1)} %copy-done.34, bf16[2,784,768]{2,1,0:T(8,128)(2,1)S(1)} %get-tuple-element.119.refs_3_.refs_2_, bf16[784,768]{1,0:T(8,128)(2,1)S(1)} %copy-done.34, ...), custom_call_target="tpu_custom_call" | custom-call | flops 9200000000 | bytes 1048576 | tf_op jit(solution)/shard_map/pallas_call | solution.py:87
  185.1 1.8 collective-permute-start.20
  186.9 13.0 %shard_map.335.refs_3_.refs_1_ = bf16[3,784,384]{2,1,0:T(8,128)(2,1)S(1)} custom-call(bf16[3,784,768]{2,1,0:T(8,128)(2,1)S(1)} %shard_map.324.refs_0_, bf16[784,768]{1,0:T(8,128)(2,1)S(1)} %copy-done.32, bf16[784,768]{1,0:T(8,128)(2,1)S(1)} %get-tuple-element.123.refs_2_, f32[16,768]{1,0:T(8,128)S(1)} %get-tuple-element.124.refs_3_, ...), custom_call_target="tpu_custom_call" | custom-call | flops 17250000896 | bytes 1048576 | tf_op jit(solution)/shard_map/pallas_call | solution.py:87
  199.9 12.1 %collective-permute-done.21 = bf16[2,4,96,768]{3,2,1,0:T(8,128)(2,1)S(1)} collective-permute-done((bf16[2,4,96,768]{3,2,1,0:T(8,128)(2,1)S(1)}, bf16[2,4,96,768]{3,2,1,0:T(8,128)(2,1)S(1)}, u32[]{:S(2)}, u32[]{:S(2)}) %collective-permute-start.21) | collective-permute-done | bytes 1179680 | tf_op jit(solution)/shard_map/ppermute | solution.py:1014
  212.0 1.7 collective-permute-start.24
  215.4 3.3 shard_map.336.refs_9_
  218.8 8.3 %collective-permute-done.24 = bf16[4,96,768]{2,1,0:T(8,128)(2,1)S(1)} collective-permute-done((bf16[4,96,768]{2,1,0:T(8,128)(2,1)S(1)}, bf16[4,96,768]{2,1,0:T(8,128)(2,1)S(1)}, u32[]{:S(2)}, u32[]{:S(2)}) %collective-permute-start.24) | collective-permute-done | bytes 589856 | tf_op jit(solution)/shard_map/ppermute | solution.py:1014
  228.6 13.1 %shard_map.337.refs_3_.refs_2_ = bf16[3,784,384]{2,1,0:T(8,128)(2,1)S(1)} custom-call(bf16[3,784,768]{2,1,0:T(8,128)(2,1)S(1)} %shard_map.324.refs_0_, bf16[784,768]{1,0:T(8,128)(2,1)S(1)} %copy-done.32, bf16[784,768]{1,0:T(8,128)(2,1)S(1)} %get-tuple-element.123.refs_2_, f32[16,768]{1,0:T(8,128)S(1)} %get-tuple-element.124.refs_3_, ...), custom_call_target="tpu_custom_call" | custom-call | flops 17250000896 | bytes 1048576 | tf_op jit(solution)/shard_map/pallas_call | solution.py:87
  241.7 3.3 shard_map.338.refs_6_
  246.0 2.3 collective-permute-start.29
  248.4 3.2 shard_map.339
  251.6 3.2 shard_map.340
  255.9 7.9 %shard_map.341 = (bf16[768,768]{1,0:T(8,128)(2,1)}, f32[8,768]{1,0:T(8,128)S(1)}, f32[2,768]{1,0:T(2,128)S(1)}) custom-call(s32[2]{0:T(128)S(1)} %pad_add_fusion.refs_0_, bf16[3,784,384]{2,1,0:T(8,128)(2,1)S(1)} %shard_map.335.refs_3_.refs_1_, bf16[3,784,384]{2,1,0:T(8,128)(2,1)S(1)} %shard_map.337.refs_3_.refs_2_, ...), custom_call_target="tpu_custom_call" | custom-call | flops 11500000256 | bytes 1048576 | tf_op jit(solution)/shard_map/pallas_call | solution.py:87
  264.9 3.6 all-to-all-start.1
  268.5 1.9 collective-permute-start.28
  273.2 4.5 %shard_map.342 = (bf16[8,56,768]{2,1,0:T(8,128)(2,1)S(1)}, bf16[8,56,768]{2,1,0:T(8,128)(2,1)S(1)}, bf16[8,56,768]{2,1,0:T(8,128)(2,1)S(1)}, bf16[8,56,768]{2,1,0:T(8,128)(2,1)S(1)}) custom-call(s32[2]{0:T(128)S(1)} %pad_add_fusion.refs_0_, bf16[768,768]{1,0:T(8,128)(2,1)S(1)} %bitcast.87, bf16[768,768]{1,0:T(8,128)(2,1)} %get-tuple-element.137.refs_2_, ...), custom_call_target="tpu_custom_call" | custom-call | flops 6899999744 | bytes 1048576 | tf_op jit(solution)/shard_map/pallas_call | solution.py:87
  281.9 14.9 %collective-permute-done.28 = bf16[2,4,96,768]{3,2,1,0:T(8,128)(2,1)S(1)} collective-permute-done((bf16[2,4,96,768]{3,2,1,0:T(8,128)(2,1)}, bf16[2,4,96,768]{3,2,1,0:T(8,128)(2,1)S(1)}, u32[]{:S(2)}, u32[]{:S(2)}) %collective-permute-start.28) | collective-permute-done | bytes 1179680 | tf_op jit(solution)/shard_map/ppermute | solution.py:1014
  299.5 1.7 collective-permute-start.31
  301.4 6.9 %collective-permute-done.30 = bf16[4,56,768]{2,1,0:T(8,128)(2,1)} collective-permute-done((bf16[4,56,768]{2,1,0:T(8,128)(2,1)}, bf16[4,56,768]{2,1,0:T(8,128)(2,1)}, u32[]{:S(2)}, u32[]{:S(2)}) %collective-permute-start.30) | collective-permute-done | bytes 344096 | tf_op jit(solution)/shard_map/ppermute | solution.py:1014
  308.3 2.5 collective-permute-done.31
  310.8 5.3 %collective-permute-done.32 = bf16[4,56,768]{2,1,0:T(8,128)(2,1)} collective-permute-done((bf16[4,56,768]{2,1,0:T(8,128)(2,1)}, bf16[4,56,768]{2,1,0:T(8,128)(2,1)}, u32[]{:S(2)}, u32[]{:S(2)}) %collective-permute-start.32) | collective-permute-done | bytes 344096 | tf_op jit(solution)/shard_map/ppermute | solution.py:1014
  316.1 2.0 fusion.11
  319.4 2.4 collective-permute-start.34
  324.4 2.8 fusion
  327.3 2.0 collective-permute-done.35
  329.3 2.8 collective-permute-done.37
  332.2 3.0 collective-permute-done.36
  335.3 2.8 collective-permute-start.40
  339.8 2.1 collective-permute-start.41
  342.0 2.5 shard_map.343
  346.0 5.5 %collective-permute-done.39 = bf16[56,768]{1,0:T(8,128)(2,1)S(1)} collective-permute-done((bf16[56,768]{1,0:T(8,128)(2,1)S(1)}, bf16[56,768]{1,0:T(8,128)(2,1)S(1)}, u32[]{:S(2)}, u32[]{:S(2)}) %collective-permute-start.39) | collective-permute-done | bytes 86048 | tf_op jit(solution)/shard_map/ppermute | solution.py:1014
  351.6 3.9 collective-permute-done.41
  355.8 2.4 collective-permute-start.45
  359.3 2.7 collective-permute-done.46
  362.0 5.6 %collective-permute-done.45 = bf16[4,56,768]{2,1,0:T(8,128)(2,1)S(1)} collective-permute-done((bf16[4,56,768]{2,1,0:T(8,128)(2,1)S(1)}, bf16[4,56,768]{2,1,0:T(8,128)(2,1)S(1)}, u32[]{:S(2)}, u32[]{:S(2)}) %collective-permute-start.45) | collective-permute-done | bytes 344096 | tf_op jit(solution)/shard_map/ppermute | solution.py:1014
  367.6 7.0 %collective-permute-done.44 = bf16[4,56,768]{2,1,0:T(8,128)(2,1)S(1)} collective-permute-done((bf16[4,56,768]{2,1,0:T(8,128)(2,1)S(1)}, bf16[4,56,768]{2,1,0:T(8,128)(2,1)S(1)}, u32[]{:S(2)}, u32[]{:S(2)}) %collective-permute-start.44) | collective-permute-done | bytes 344096 | tf_op jit(solution)/shard_map/ppermute | solution.py:1014
  376.4 2.4 shard_map.344
  378.7 2.4 collective-permute-done.49.refs_2_
  381.3 3.3 shard_map.345
  386.6 1.6 shard_map.346
  (229 shorter events, 60.7 us)
Async XLA Ops:
  7.2 82.3 %all-gather.3.cloned.1.call-start = ((), (), s32[]{:S(2)}) async-start(), calls=%async_computation.2 | async-start | bytes 1327104 | tf_op jit(solution)/shard_map/all_gather | solution.py:1115
  9.0 12.7 %collective-permute-start.1 = (bf16[96,768]{1,0:T(8,128)(2,1)S(1)}, bf16[96,768]{1,0:T(8,128)(2,1)S(1)}, u32[]{:S(2)}, u32[]{:S(2)}) collective-permute-start(bf16[96,768]{1,0:T(8,128)(2,1)S(1)} %get-tuple-element.197), channel_id=1, source_target_pairs={{0,16},{1,17},{2,18},{3,19},{4,20},{5,21},{6,22},{7,23},{8,24},{9,... | collective-permute-start | bytes 442376 | tf_op jit(solution)/shard_map/ppermute | solution.py:1014
  13.0 8.7 %collective-permute-start = (bf16[96,768]{1,0:T(8,128)(2,1)S(1)}, bf16[96,768]{1,0:T(8,128)(2,1)S(1)}, u32[]{:S(2)}, u32[]{:S(2)}) collective-permute-start(bf16[96,768]{1,0:T(8,128)(2,1)S(1)} %get-tuple-element.197), channel_id=1, source_target_pairs={{0,8},{1,9},{2,10},{3,11},{4,12},{5,13},{6,14},{7,15},{8,0},{9,1},... | collective-permute-start | bytes 442376 | tf_op jit(solution)/shard_map/ppermute | solution.py:1014
  14.6 9.8 %collective-permute-start.2 = (bf16[96,768]{1,0:T(8,128)(2,1)S(1)}, bf16[96,768]{1,0:T(8,128)(2,1)S(1)}, u32[]{:S(2)}, u32[]{:S(2)}) collective-permute-start(bf16[96,768]{1,0:T(8,128)(2,1)S(1)} %get-tuple-element.197), channel_id=1, source_target_pairs={{0,24},{1,25},{2,26},{3,27},{4,28},{5,29},{6,30},{7,31},{8,16},{9,... | collective-permute-start | bytes 442376 | tf_op jit(solution)/shard_map/ppermute | solution.py:1014
  24.5 14.8 %collective-permute-start.3 = (bf16[4,96,768]{2,1,0:T(8,128)(2,1)S(1)}, bf16[4,96,768]{2,1,0:T(8,128)(2,1)}, u32[]{:S(2)}, u32[]{:S(2)}) collective-permute-start(bf16[4,96,768]{2,1,0:T(8,128)(2,1)S(1)} %pad_maximum_fusion.2), channel_id=1, source_target_pairs={{0,4},{1,5},{2,6},{3,7},{4,0},{5,1},{6,2},{7,3},{8,12},{9,13},{10,... | collective-permute-start | bytes 1769480 | tf_op jit(solution)/shard_map/ppermute | solution.py:1014
  29.6 11.2 %collective-permute-start.6 = (bf16[96,768]{1,0:T(8,128)(2,1)S(1)}, bf16[96,768]{1,0:T(8,128)(2,1)S(1)}, u32[]{:S(2)}, u32[]{:S(2)}) collective-permute-start(bf16[96,768]{1,0:T(8,128)(2,1)S(1)} %reshape.90), channel_id=1, source_target_pairs={{0,24},{1,25},{2,26},{3,27},{4,28},{5,29},{6,30},{7,31},{8,16},{9,... | collective-permute-start | bytes 442376 | tf_op jit(solution)/shard_map/ppermute | solution.py:1014
  32.2 18.5 %collective-permute-start.5 = (bf16[96,768]{1,0:T(8,128)(2,1)S(1)}, bf16[96,768]{1,0:T(8,128)(2,1)S(1)}, u32[]{:S(2)}, u32[]{:S(2)}) collective-permute-start(bf16[96,768]{1,0:T(8,128)(2,1)S(1)} %reshape.90), channel_id=1, source_target_pairs={{0,16},{1,17},{2,18},{3,19},{4,20},{5,21},{6,22},{7,23},{8,24},{9,... | collective-permute-start | bytes 442376 | tf_op jit(solution)/shard_map/ppermute | solution.py:1014
  34.4 16.3 %collective-permute-start.4 = (bf16[96,768]{1,0:T(8,128)(2,1)S(1)}, bf16[96,768]{1,0:T(8,128)(2,1)S(1)}, u32[]{:S(2)}, u32[]{:S(2)}) collective-permute-start(bf16[96,768]{1,0:T(8,128)(2,1)S(1)} %reshape.90), channel_id=1, source_target_pairs={{0,8},{1,9},{2,10},{3,11},{4,12},{5,13},{6,14},{7,15},{8,0},{9,1},... | collective-permute-start | bytes 442376 | tf_op jit(solution)/shard_map/ppermute | solution.py:1014
  34.8 23.2 %collective-permute-start.8 = (bf16[4,96,768]{2,1,0:T(8,128)(2,1)S(1)}, bf16[4,96,768]{2,1,0:T(8,128)(2,1)}, u32[]{:S(2)}, u32[]{:S(2)}) collective-permute-start(bf16[4,96,768]{2,1,0:T(8,128)(2,1)S(1)} %pad_maximum_fusion.2), channel_id=1, source_target_pairs={{0,2},{1,3},{2,0},{3,1},{4,6},{5,7},{6,4},{7,5},{8,10},{9,11},{10,... | collective-permute-start | bytes 1769480 | tf_op jit(solution)/shard_map/ppermute | solution.py:1014
  39.3 22.7 %collective-permute-start.9 = (bf16[4,96,768]{2,1,0:T(8,128)(2,1)}, bf16[4,96,768]{2,1,0:T(8,128)(2,1)}, u32[]{:S(2)}, u32[]{:S(2)}) collective-permute-start(bf16[4,96,768]{2,1,0:T(8,128)(2,1)} %collective-permute-done.3), channel_id=1, source_target_pairs={{0,2},{1,3},{2,0},{3,1},{4,6},{5,7},{6,4},{7,5},{8,10},{9,11},{10,... | collective-permute-start | bytes 1769480 | tf_op jit(solution)/shard_map/ppermute | solution.py:1014
  51.6 41.1 %all-to-all-start = ((bf16[8,96,768]{2,1,0:T(8,128)(2,1)}), bf16[8,96,768]{2,1,0:T(8,128)(2,1)S(1)}, u32[]{:S(2)}, u32[]{:S(2)}) async-start(bf16[8,96,768]{2,1,0:T(8,128)(2,1)} %param.20), calls=%async_computation | async-start | bytes 2359296 | tf_op jit(solution)/shard_map/all_to_all | solution.py:1106
  58.1 31.9 %collective-permute-start.7 = (bf16[8,96,768]{2,1,0:T(8,128)(2,1)}, bf16[8,96,768]{2,1,0:T(8,128)(2,1)}, u32[]{:S(2)}, u32[]{:S(2)}) collective-permute-start(bf16[8,96,768]{2,1,0:T(8,128)(2,1)} %constant_dynamic-update-slice_fusion.refs_2_.refs_5_.refs_3_), channel_id=1, source_target_pairs={{0,1},{1,0},{2,3},{3,2},{4,5},{5,4},{6,7},{7,6},{8,9},{9,8},{10,11... | collective-permute-start | bytes 3538952 | tf_op jit(solution)/shard_map/ppermute | solution.py:1014
  63.1 105.4 %copy-start.3 = (bf16[8,96,768]{2,1,0:T(8,128)(2,1)}, bf16[8,96,768]{2,1,0:T(8,128)(2,1)S(1)}, u32[]{:S(2)}) copy-start(bf16[8,96,768]{2,1,0:T(8,128)(2,1)S(1)} %constant_dynamic-update-slice_fusion.5.refs_4_.refs_7_.refs_5_) | copy-start | bytes 3538948
  63.1 26.8 %collective-permute-start.10 = (bf16[8,96,768]{2,1,0:T(8,128)(2,1)S(1)}, bf16[8,96,768]{2,1,0:T(8,128)(2,1)}, u32[]{:S(2)}, u32[]{:S(2)}) collective-permute-start(bf16[8,96,768]{2,1,0:T(8,128)(2,1)S(1)} %constant_dynamic-update-slice_fusion.5.refs_4_.refs_7_.refs_5_), channel_id=1, source_target_pairs={{0,1},{1,0},{2,3},{3,2},{4,5},{5,4},{6,7},{7,6},{8,9},{9,8},{10,11... | collective-permute-start | bytes 3538952 | tf_op jit(solution)/shard_map/ppermute | solution.py:1014
  65.6 23.8 %copy-start.39 = (f32[1,768]{1,0:T(1,128)}, f32[1,768]{1,0:T(1,128)S(1)}, u32[]{:S(2)}) copy-start(f32[1,768]{1,0:T(1,128)S(1)} %get-tuple-element.140.refs_5_) | copy-start | bytes 9220
  66.0 26.6 %copy-start.13 = (f32[8,768]{1,0:T(8,128)S(1)}, f32[8,768]{1,0:T(8,128)}, u32[]{:S(2)}) copy-start(f32[8,768]{1,0:T(8,128)} %refs_5_.3) | copy-start | bytes 73732
  66.0 26.6 %copy-start.14 = (f32[768]{0:T(1024)S(1)}, f32[768]{0:T(1024)}, u32[]{:S(2)}) copy-start(f32[768]{0:T(1024)} %refs_2_.6) | copy-start | bytes 9220
  66.0 26.6 %copy-start.15 = (f32[768]{0:T(1024)S(1)}, f32[768]{0:T(1024)}, u32[]{:S(2)}) copy-start(f32[768]{0:T(1024)} %refs_4_.2) | copy-start | bytes 9220
  66.0 26.6 %copy-start.16 = (f32[768]{0:T(1024)S(1)}, f32[768]{0:T(1024)}, u32[]{:S(2)}) copy-start(f32[768]{0:T(1024)} %refs_7_.4) | copy-start | bytes 9220
  66.0 26.6 %copy-start.20 = (f32[768]{0:T(1024)S(1)}, f32[768]{0:T(1024)}, u32[]{:S(2)}) copy-start(f32[768]{0:T(1024)} %refs_8_.3) | copy-start | bytes 9220
  66.7 21.8 %collective-permute-start.11 = (bf16[4,96,768]{2,1,0:T(8,128)(2,1)}, bf16[4,96,768]{2,1,0:T(8,128)(2,1)S(1)}, u32[]{:S(2)}, u32[]{:S(2)}) collective-permute-start(bf16[4,96,768]{2,1,0:T(8,128)(2,1)} %pad_maximum_fusion.3), channel_id=1, source_target_pairs={{0,4},{1,5},{2,6},{3,7},{4,0},{5,1},{6,2},{7,3},{8,12},{9,13},{10,... | collective-permute-start | bytes 1769480 | tf_op jit(solution)/shard_map/ppermute | solution.py:1014
  89.4 34.2 %collective-permute-start.14 = (bf16[8,96,768]{2,1,0:T(8,128)(2,1)}, bf16[8,96,768]{2,1,0:T(8,128)(2,1)}, u32[]{:S(2)}, u32[]{:S(2)}) collective-permute-start(bf16[8,96,768]{2,1,0:T(8,128)(2,1)} %constant_dynamic-update-slice_fusion.7.refs_9_.refs_10_), channel_id=1, source_target_pairs={{0,1},{1,0},{2,3},{3,2},{4,5},{5,4},{6,7},{7,6},{8,9},{9,8},{10,11... | collective-permute-start | bytes 3538952 | tf_op jit(solution)/shard_map/ppermute | solution.py:1014
  89.5 28.9 %collective-permute-start.12 = (bf16[8,96,768]{2,1,0:T(8,128)(2,1)}, bf16[8,96,768]{2,1,0:T(8,128)(2,1)}, u32[]{:S(2)}, u32[]{:S(2)}) collective-permute-start(bf16[8,96,768]{2,1,0:T(8,128)(2,1)} %bitcast.95), channel_id=1, source_target_pairs={{0,1},{1,0},{2,3},{3,2},{4,5},{5,4},{6,7},{7,6},{8,9},{9,8},{10,11... | collective-permute-start | bytes 3538952 | tf_op jit(solution)/shard_map/ppermute | solution.py:1014
  89.9 28.5 %collective-permute-start.13 = (bf16[8,96,768]{2,1,0:T(8,128)(2,1)}, bf16[8,96,768]{2,1,0:T(8,128)(2,1)}, u32[]{:S(2)}, u32[]{:S(2)}) collective-permute-start(bf16[8,96,768]{2,1,0:T(8,128)(2,1)} %bitcast.96), channel_id=1, source_target_pairs={{0,2},{1,3},{2,0},{3,1},{4,6},{5,7},{6,4},{7,5},{8,10},{9,11},{10,... | collective-permute-start | bytes 3538952 | tf_op jit(solution)/shard_map/ppermute | solution.py:1014
  96.9 22.8 %copy-start.23 = (f32[784,768]{1,0:T(8,128)}, f32[784,768]{1,0:T(8,128)S(1)}, u32[]{:S(2)}) copy-start(f32[784,768]{1,0:T(8,128)S(1)} %get-tuple-element.105.refs_6_.refs_7_) | copy-start | bytes 7225348
  118.4 27.7 %collective-permute-start.15 = (bf16[8,96,768]{2,1,0:T(8,128)(2,1)}, bf16[8,96,768]{2,1,0:T(8,128)(2,1)S(1)}, u32[]{:S(2)}, u32[]{:S(2)}) collective-permute-start(bf16[8,96,768]{2,1,0:T(8,128)(2,1)} %constant_dynamic-update-slice_fusion.7.refs_9_.refs_10_), channel_id=1, source_target_pairs={{0,2},{1,3},{2,0},{3,1},{4,6},{5,7},{6,4},{7,5},{8,10},{9,11},{10,... | collective-permute-start | bytes 3538952 | tf_op jit(solution)/shard_map/ppermute | solution.py:1014
  119.7 30.2 %collective-permute-start.17 = (bf16[8,96,768]{2,1,0:T(8,128)(2,1)}, bf16[8,96,768]{2,1,0:T(8,128)(2,1)S(1)}, u32[]{:S(2)}, u32[]{:S(2)}) collective-permute-start(bf16[8,96,768]{2,1,0:T(8,128)(2,1)} %collective-permute-done.13.refs_11_), channel_id=1, source_target_pairs={{0,1},{1,0},{2,3},{3,2},{4,5},{5,4},{6,7},{7,6},{8,9},{9,8},{10,11... | collective-permute-start | bytes 3538952 | tf_op jit(solution)/shard_map/ppermute | solution.py:1014
  123.5 41.3 %copy-start.33 = (bf16[784,768]{1,0:T(8,128)(2,1)}, bf16[784,768]{1,0:T(8,128)(2,1)S(1)}, u32[]{:S(2)}) copy-start(bf16[784,768]{1,0:T(8,128)(2,1)S(1)} %get-tuple-element.109.refs_3_.refs_1_) | copy-start | bytes 3612676
  146.1 3.8 collective-permute-start.16
  149.3 25.6 %collective-permute-start.18 = (bf16[2,8,96,768]{3,2,1,0:T(8,128)(2,1)S(1)}, bf16[2,8,96,768]{3,2,1,0:T(8,128)(2,1)S(1)}, u32[]{:S(2)}, u32[]{:S(2)}) collective-permute-start(bf16[2,8,96,768]{3,2,1,0:T(8,128)(2,1)S(1)} %shard_map.329.refs_14_), channel_id=1, source_target_pairs={{0,1},{1,0},{2,3},{3,2},{4,5},{5,4},{6,7},{7,6},{8,9},{9,8},{10,11... | collective-permute-start | bytes 7077896 | tf_op jit(solution)/shard_map/ppermute | solution.py:1014
  168.5 6.4 %collective-permute-start.19 = (bf16[2,8,96,768]{3,2,1,0:T(8,128)(2,1)S(1)}, bf16[2,8,96,768]{3,2,1,0:T(8,128)(2,1)S(1)}, u32[]{:S(2)}, u32[]{:S(2)}) collective-permute-start(bf16[2,8,96,768]{3,2,1,0:T(8,128)(2,1)S(1)} %shard_map.331.refs_9_), channel_id=1, source_target_pairs={{0,1},{1,0},{2,3},{3,2},{4,5},{5,4},{6,7},{7,6},{8,9},{9,8},{10,11... | collective-permute-start | bytes 7077896 | tf_op jit(solution)/shard_map/ppermute | solution.py:1014
  183.5 28.5 %collective-permute-start.21 = (bf16[2,4,96,768]{3,2,1,0:T(8,128)(2,1)S(1)}, bf16[2,4,96,768]{3,2,1,0:T(8,128)(2,1)S(1)}, u32[]{:S(2)}, u32[]{:S(2)}) collective-permute-start(bf16[2,4,96,768]{3,2,1,0:T(8,128)(2,1)S(1)} %get-tuple-element.130), channel_id=1, source_target_pairs={{0,4},{1,5},{2,6},{3,7},{4,0},{5,1},{6,2},{7,3},{8,12},{9,13},{10,... | collective-permute-start | bytes 3538952 | tf_op jit(solution)/shard_map/ppermute | solution.py:1014
  185.1 28.6 %collective-permute-start.20 = (bf16[2,4,96,768]{3,2,1,0:T(8,128)(2,1)S(1)}, bf16[2,4,96,768]{3,2,1,0:T(8,128)(2,1)S(1)}, u32[]{:S(2)}, u32[]{:S(2)}) collective-permute-start(bf16[2,4,96,768]{3,2,1,0:T(8,128)(2,1)S(1)} %get-tuple-element.129), channel_id=1, source_target_pairs={{0,2},{1,3},{2,0},{3,1},{4,6},{5,7},{6,4},{7,5},{8,10},{9,11},{10,... | collective-permute-start | bytes 3538952 | tf_op jit(solution)/shard_map/ppermute | solution.py:1014
  212.0 15.1 %collective-permute-start.24 = (bf16[4,96,768]{2,1,0:T(8,128)(2,1)S(1)}, bf16[4,96,768]{2,1,0:T(8,128)(2,1)S(1)}, u32[]{:S(2)}, u32[]{:S(2)}) collective-permute-start(bf16[4,96,768]{2,1,0:T(8,128)(2,1)S(1)} %fusion.6.refs_13_), channel_id=1, source_target_pairs={{0,2},{1,3},{2,0},{3,1},{4,6},{5,7},{6,4},{7,5},{8,10},{9,11},{10,... | collective-permute-start | bytes 1769480 | tf_op jit(solution)/shard_map/ppermute | solution.py:1014
  213.8 14.7 %collective-permute-start.25 = (bf16[4,96,768]{2,1,0:T(8,128)(2,1)S(1)}, bf16[4,96,768]{2,1,0:T(8,128)(2,1)S(1)}, u32[]{:S(2)}, u32[]{:S(2)}) collective-permute-start(bf16[4,96,768]{2,1,0:T(8,128)(2,1)S(1)} %fusion.8.refs_11_), channel_id=1, source_target_pairs={{0,4},{1,5},{2,6},{3,7},{4,0},{5,1},{6,2},{7,3},{8,12},{9,13},{10,... | collective-permute-start | bytes 1769480 | tf_op jit(solution)/shard_map/ppermute | solution.py:1014
  218.7 29.7 %collective-permute-start.23 = (bf16[2,8,96,384]{3,2,1,0:T(8,128)(2,1)S(1)}, bf16[2,8,96,384]{3,2,1,0:T(8,128)(2,1)S(1)}, u32[]{:S(2)}, u32[]{:S(2)}) collective-permute-start(bf16[2,8,96,384]{3,2,1,0:T(8,128)(2,1)S(1)} %shard_map.336.refs_9_), channel_id=1, source_target_pairs={{0,1},{1,0},{2,3},{3,2},{4,5},{5,4},{6,7},{7,6},{8,9},{9,8},{10,11... | collective-permute-start | bytes 3538952 | tf_op jit(solution)/shard_map/ppermute | solution.py:1014
  245.0 6.6 %collective-permute-start.22 = (bf16[2,8,96,384]{3,2,1,0:T(8,128)(2,1)S(1)}, bf16[2,8,96,384]{3,2,1,0:T(8,128)(2,1)S(1)}, u32[]{:S(2)}, u32[]{:S(2)}) collective-permute-start(bf16[2,8,96,384]{3,2,1,0:T(8,128)(2,1)S(1)} %shard_map.338.refs_6_), channel_id=1, source_target_pairs={{0,1},{1,0},{2,3},{3,2},{4,5},{5,4},{6,7},{7,6},{8,9},{9,8},{10,11... | collective-permute-start | bytes 3538952 | tf_op jit(solution)/shard_map/ppermute | solution.py:1014
  246.0 32.5 %collective-permute-start.29 = (bf16[2,2,96,768]{3,2,1,0:T(8,128)(2,1)}, bf16[2,2,96,768]{3,2,1,0:T(8,128)(2,1)}, u32[]{:S(2)}, u32[]{:S(2)}) collective-permute-start(bf16[2,2,96,768]{3,2,1,0:T(8,128)(2,1)} %fusion.3), channel_id=1, source_target_pairs={{0,16},{1,17},{2,18},{3,19},{4,20},{5,21},{6,22},{7,23},{8,24},{9,... | collective-permute-start | bytes 1769480 | tf_op jit(solution)/shard_map/ppermute | solution.py:1014
  264.9 53.1 %all-to-all-start.1 = ((bf16[8,96,768]{2,1,0:T(8,128)(2,1)}), bf16[8,96,768]{2,1,0:T(8,128)(2,1)S(1)}, u32[]{:S(2)}, u32[]{:S(2)}) async-start(bf16[8,96,768]{2,1,0:T(8,128)(2,1)} %bitcast.31), calls=%async_computation.1 | async-start | bytes 2359296 | tf_op jit(solution)/shard_map/all_to_all | solution.py:1224
  268.5 28.3 %collective-permute-start.28 = (bf16[2,4,96,768]{3,2,1,0:T(8,128)(2,1)}, bf16[2,4,96,768]{3,2,1,0:T(8,128)(2,1)S(1)}, u32[]{:S(2)}, u32[]{:S(2)}) collective-permute-start(bf16[2,4,96,768]{3,2,1,0:T(8,128)(2,1)} %copy-done.12), channel_id=1, source_target_pairs={{0,2},{1,3},{2,0},{3,1},{4,6},{5,7},{6,4},{7,5},{8,10},{9,11},{10,... | collective-permute-start | bytes 3538952 | tf_op jit(solution)/shard_map/ppermute | solution.py:1014
  277.7 2.4 collective-permute-start.26
  277.9 3.1 collective-permute-start.27
  297.9 25.1 %copy-start.49 = (bf16[4,96,768]{2,1,0:T(8,128)(2,1)S(1)}, bf16[4,96,768]{2,1,0:T(8,128)(2,1)}, u32[]{:S(2)}) copy-start(bf16[4,96,768]{2,1,0:T(8,128)(2,1)} %get-tuple-element.160) | copy-start | bytes 1769476
  297.9 10.4 %collective-permute-start.30 = (bf16[4,56,768]{2,1,0:T(8,128)(2,1)}, bf16[4,56,768]{2,1,0:T(8,128)(2,1)}, u32[]{:S(2)}, u32[]{:S(2)}) collective-permute-start(bf16[4,56,768]{2,1,0:T(8,128)(2,1)} %get-tuple-element.149), channel_id=1, source_target_pairs={{0,4},{1,5},{2,6},{3,7},{4,0},{5,1},{6,2},{7,3},{8,12},{9,13},{10,... | collective-permute-start | bytes 1032200 | tf_op jit(solution)/shard_map/ppermute | solution.py:1014
  299.5 11.3 %collective-permute-start.31 = (bf16[4,56,768]{2,1,0:T(8,128)(2,1)}, bf16[4,56,768]{2,1,0:T(8,128)(2,1)}, u32[]{:S(2)}, u32[]{:S(2)}) collective-permute-start(bf16[4,56,768]{2,1,0:T(8,128)(2,1)} %get-tuple-element.150), channel_id=1, source_target_pairs={{0,2},{1,3},{2,0},{3,1},{4,6},{5,7},{6,4},{7,5},{8,10},{9,11},{10,... | collective-permute-start | bytes 1032200 | tf_op jit(solution)/shard_map/ppermute | solution.py:1014
  301.2 14.8 %collective-permute-start.32 = (bf16[4,56,768]{2,1,0:T(8,128)(2,1)}, bf16[4,56,768]{2,1,0:T(8,128)(2,1)}, u32[]{:S(2)}, u32[]{:S(2)}) collective-permute-start(bf16[4,56,768]{2,1,0:T(8,128)(2,1)} %get-tuple-element.151), channel_id=1, source_target_pairs={{0,6},{1,7},{2,4},{3,5},{4,2},{5,3},{6,0},{7,1},{8,14},{9,15},{10,... | collective-permute-start | bytes 1032200 | tf_op jit(solution)/shard_map/ppermute | solution.py:1014
  318.1 9.2 %collective-permute-start.33 = (bf16[56,768]{1,0:T(8,128)(2,1)}, bf16[56,768]{1,0:T(8,128)(2,1)S(1)}, u32[]{:S(2)}, u32[]{:S(2)}) collective-permute-start(bf16[56,768]{1,0:T(8,128)(2,1)} %get-tuple-element.156), channel_id=1, source_target_pairs={{0,8},{1,9},{2,10},{3,11},{4,12},{5,13},{6,14},{7,15},{8,0},{9,1},... | collective-permute-start | bytes 258056 | tf_op jit(solution)/shard_map/ppermute | solution.py:1014
  319.4 7.8 %collective-permute-start.34 = (bf16[56,768]{1,0:T(8,128)(2,1)}, bf16[56,768]{1,0:T(8,128)(2,1)S(1)}, u32[]{:S(2)}, u32[]{:S(2)}) collective-permute-start(bf16[56,768]{1,0:T(8,128)(2,1)} %get-tuple-element.157), channel_id=1, source_target_pairs={{0,16},{1,17},{2,18},{3,19},{4,20},{5,21},{6,22},{7,23},{8,24},{9,... | collective-permute-start | bytes 258056 | tf_op jit(solution)/shard_map/ppermute | solution.py:1014
  321.8 7.5 %collective-permute-start.35 = (bf16[56,768]{1,0:T(8,128)(2,1)}, bf16[56,768]{1,0:T(8,128)(2,1)S(1)}, u32[]{:S(2)}, u32[]{:S(2)}) collective-permute-start(bf16[56,768]{1,0:T(8,128)(2,1)} %get-tuple-element.158), channel_id=1, source_target_pairs={{0,24},{1,25},{2,26},{3,27},{4,28},{5,29},{6,30},{7,31},{8,16},{9,... | collective-permute-start | bytes 258056 | tf_op jit(solution)/shard_map/ppermute | solution.py:1014
  322.5 9.6 %collective-permute-start.37 = (bf16[2,96,768]{2,1,0:T(8,128)(2,1)S(1)}, bf16[2,96,768]{2,1,0:T(8,128)(2,1)S(1)}, u32[]{:S(2)}, u32[]{:S(2)}) collective-permute-start(bf16[2,96,768]{2,1,0:T(8,128)(2,1)S(1)} %slice_bitcast_fusion.2), channel_id=1, source_target_pairs={{0,8},{1,9},{2,10},{3,11},{4,12},{5,13},{6,14},{7,15},{8,0},{9,1},... | collective-permute-start | bytes 884744 | tf_op jit(solution)/shard_map/ppermute | solution.py:1014
  323.0 12.2 %collective-permute-start.36 = (bf16[4,96,768]{2,1,0:T(8,128)(2,1)S(1)}, bf16[4,96,768]{2,1,0:T(8,128)(2,1)S(1)}, u32[]{:S(2)}, u32[]{:S(2)}) collective-permute-start(bf16[4,96,768]{2,1,0:T(8,128)(2,1)S(1)} %copy-done.49), channel_id=1, source_target_pairs={{0,4},{1,5},{2,6},{3,7},{4,0},{5,1},{6,2},{7,3},{8,12},{9,13},{10,... | collective-permute-start | bytes 1769480 | tf_op jit(solution)/shard_map/ppermute | solution.py:1014
  335.3 10.6 %collective-permute-start.40 = (bf16[56,768]{1,0:T(8,128)(2,1)S(1)}, bf16[56,768]{1,0:T(8,128)(2,1)S(1)}, u32[]{:S(2)}, u32[]{:S(2)}) collective-permute-start(bf16[56,768]{1,0:T(8,128)(2,1)S(1)} %add_add_fusion), channel_id=1, source_target_pairs={{0,24},{1,25},{2,26},{3,27},{4,28},{5,29},{6,30},{7,31},{8,16},{9,... | collective-permute-start | bytes 258056 | tf_op jit(solution)/shard_map/ppermute | solution.py:1014
  338.2 13.4 %collective-permute-start.39 = (bf16[56,768]{1,0:T(8,128)(2,1)S(1)}, bf16[56,768]{1,0:T(8,128)(2,1)S(1)}, u32[]{:S(2)}, u32[]{:S(2)}) collective-permute-start(bf16[56,768]{1,0:T(8,128)(2,1)S(1)} %add_add_fusion), channel_id=1, source_target_pairs={{0,16},{1,17},{2,18},{3,19},{4,20},{5,21},{6,22},{7,23},{8,24},{9,... | collective-permute-start | bytes 258056 | tf_op jit(solution)/shard_map/ppermute | solution.py:1014
  338.5 13.0 %collective-permute-start.38 = (bf16[56,768]{1,0:T(8,128)(2,1)S(1)}, bf16[56,768]{1,0:T(8,128)(2,1)S(1)}, u32[]{:S(2)}, u32[]{:S(2)}) collective-permute-start(bf16[56,768]{1,0:T(8,128)(2,1)S(1)} %add_add_fusion), channel_id=1, source_target_pairs={{0,8},{1,9},{2,10},{3,11},{4,12},{5,13},{6,14},{7,15},{8,0},{9,1},... | collective-permute-start | bytes 258056 | tf_op jit(solution)/shard_map/ppermute | solution.py:1014
  339.8 15.7 %collective-permute-start.41 = (bf16[2,96,768]{2,1,0:T(8,128)(2,1)S(1)}, bf16[2,96,768]{2,1,0:T(8,128)(2,1)S(1)}, u32[]{:S(2)}, u32[]{:S(2)}) collective-permute-start(bf16[2,96,768]{2,1,0:T(8,128)(2,1)S(1)} %slice.212), channel_id=1, source_target_pairs={{0,16},{1,17},{2,18},{3,19},{4,20},{5,21},{6,22},{7,23},{8,24},{9,... | collective-permute-start | bytes 884744 | tf_op jit(solution)/shard_map/ppermute | solution.py:1014
  344.5 11.1 %collective-permute-start.42 = (bf16[2,96,768]{2,1,0:T(8,128)(2,1)S(1)}, bf16[2,96,768]{2,1,0:T(8,128)(2,1)S(1)}, u32[]{:S(2)}, u32[]{:S(2)}) collective-permute-start(bf16[2,96,768]{2,1,0:T(8,128)(2,1)S(1)} %bitcast_add_fusion.refs_1_), channel_id=1, source_target_pairs={{0,2},{1,3},{2,0},{3,1},{4,6},{5,7},{6,4},{7,5},{8,10},{9,11},{10,... | collective-permute-start | bytes 884744 | tf_op jit(solution)/shard_map/ppermute | solution.py:1014
  355.6 19.2 %collective-permute-start.47 = (bf16[2,2,96,768]{3,2,1,0:T(8,128)(2,1)S(1)}, bf16[2,2,96,768]{3,2,1,0:T(8,128)(2,1)S(1)}, u32[]{:S(2)}, u32[]{:S(2)}) collective-permute-start(bf16[2,2,96,768]{3,2,1,0:T(8,128)(2,1)S(1)} %pad_maximum_fusion.4), channel_id=1, source_target_pairs={{0,1},{1,0},{2,3},{3,2},{4,5},{5,4},{6,7},{7,6},{8,9},{9,8},{10,11... | collective-permute-start | bytes 1769480 | tf_op jit(solution)/shard_map/ppermute | solution.py:1014
  355.7 6.3 %collective-permute-start.46 = (bf16[96,768]{1,0:T(8,128)(2,1)S(1)}, bf16[96,768]{1,0:T(8,128)(2,1)S(1)}, u32[]{:S(2)}, u32[]{:S(2)}) collective-permute-start(bf16[96,768]{1,0:T(8,128)(2,1)S(1)} %slice_bitcast_fusion.7), channel_id=1, source_target_pairs={{0,8},{1,9},{2,10},{3,11},{4,12},{5,13},{6,14},{7,15},{8,0},{9,1},... | collective-permute-start | bytes 442376 | tf_op jit(solution)/shard_map/ppermute | solution.py:1014
  355.8 11.9 %collective-permute-start.45 = (bf16[4,56,768]{2,1,0:T(8,128)(2,1)S(1)}, bf16[4,56,768]{2,1,0:T(8,128)(2,1)S(1)}, u32[]{:S(2)}, u32[]{:S(2)}) collective-permute-start(bf16[4,56,768]{2,1,0:T(8,128)(2,1)S(1)} %pad_maximum_fusion.5), channel_id=1, source_target_pairs={{0,6},{1,7},{2,4},{3,5},{4,2},{5,3},{6,0},{7,1},{8,14},{9,15},{10,... | collective-permute-start | bytes 1032200 | tf_op jit(solution)/shard_map/ppermute | solution.py:1014
  358.1 16.5 %collective-permute-start.44 = (bf16[4,56,768]{2,1,0:T(8,128)(2,1)S(1)}, bf16[4,56,768]{2,1,0:T(8,128)(2,1)S(1)}, u32[]{:S(2)}, u32[]{:S(2)}) collective-permute-start(bf16[4,56,768]{2,1,0:T(8,128)(2,1)S(1)} %pad_maximum_fusion.5), channel_id=1, source_target_pairs={{0,2},{1,3},{2,0},{3,1},{4,6},{5,7},{6,4},{7,5},{8,10},{9,11},{10,... | collective-permute-start | bytes 1032200 | tf_op jit(solution)/shard_map/ppermute | solution.py:1014
  358.8 15.9 %collective-permute-start.43 = (bf16[4,56,768]{2,1,0:T(8,128)(2,1)S(1)}, bf16[4,56,768]{2,1,0:T(8,128)(2,1)S(1)}, u32[]{:S(2)}, u32[]{:S(2)}) collective-permute-start(bf16[4,56,768]{2,1,0:T(8,128)(2,1)S(1)} %pad_maximum_fusion.5), channel_id=1, source_target_pairs={{0,4},{1,5},{2,6},{3,7},{4,0},{5,1},{6,2},{7,3},{8,12},{9,13},{10,... | collective-permute-start | bytes 1032200 | tf_op jit(solution)/shard_map/ppermute | solution.py:1014
  374.8 6.3 %collective-permute-start.48 = (bf16[16,56,768]{2,1,0:T(8,128)(2,1)S(1)}, bf16[16,56,768]{2,1,0:T(8,128)(2,1)S(1)}, u32[]{:S(2)}, u32[]{:S(2)}) collective-permute-start(bf16[16,56,768]{2,1,0:T(8,128)(2,1)S(1)} %pad_maximum_fusion.1.refs_1_), channel_id=1, source_target_pairs={{0,1},{1,0},{2,3},{3,2},{4,5},{5,4},{6,7},{7,6},{8,9},{9,8},{10,11... | collective-permute-start | bytes 4128776 | tf_op jit(solution)/shard_map/ppermute | solution.py:1014
  374.9 6.3 %collective-permute-start.49 = (bf16[96,768]{1,0:T(8,128)(2,1)S(1)}, bf16[96,768]{1,0:T(8,128)(2,1)S(1)}, u32[]{:S(2)}, u32[]{:S(2)}) collective-permute-start(bf16[96,768]{1,0:T(8,128)(2,1)S(1)} %bitcast_add_fusion.1.refs_1_), channel_id=1, source_target_pairs={{0,2},{1,3},{2,0},{3,1},{4,6},{5,7},{6,4},{7,5},{8,10},{9,11},{10,... | collective-permute-start | bytes 442376 | tf_op jit(solution)/shard_map/ppermute | solution.py:1014
  381.2 5.4 %collective-permute-start.50 = (bf16[2,96,768]{2,1,0:T(8,128)(2,1)S(1)}, bf16[2,96,768]{2,1,0:T(8,128)(2,1)S(1)}, u32[]{:S(2)}, u32[]{:S(2)}) collective-permute-start(bf16[2,96,768]{2,1,0:T(8,128)(2,1)S(1)} %pad_maximum_fusion.6), channel_id=1, source_target_pairs={{0,1},{1,0},{2,3},{3,2},{4,5},{5,4},{6,7},{7,6},{8,9},{9,8},{10,11... | collective-permute-start | bytes 884744 | tf_op jit(solution)/shard_map/ppermute | solution.py:1014
  (42 other events, 228.4 us)
Sparse Core Ops, SparseCore 0:
  26.9 53.8 all-gather.2

commit v4 on v3

--- a/solution.py
+++ b/solution.py
@@ -1113,6 +1113,8 @@
         first3 = grid.swap(first2, **CORE)
         first = (first0, first1, first2, first3)
         down0 = lax.all_gather(piece_down, "mod", axis=0)
+        piece_down = lax.dynamic_slice_in_dim(down_weight, (rank ^ 2) * quarter, quarter, 0)
+        down2 = lax.all_gather(piece_down, "mod", axis=0)
     else:
         whole = lambda w: lax.all_gather(w, "mod", axis=0, tiled=True)
         every = jnp.concatenate([whole(qkv_weight), whole(out_weight)], axis=1)
@@ -1134,20 +1136,19 @@
         attn_bias,
     )
     if fast:
-        down2 = grid.swap(tie(down0, first1, first3), **X)
+        up0 = joined(up_z, grid.swap(tie(up_z, first_y), **Y))
     qkv = project_qkv(ids, normed, first)
     deps = ()
     mixed, lse, lse_read = attend(qkv, *marks, block_rows, deps)
     deps = ()
     if fast:
         down1 = grid.swap(tie(down0, up_z), **CORE)
-        up0 = joined(up_z, grid.swap(tie(up_z, first_y), **Y))
-        deps = (up0, down1, down2)
+        up2 = grid.swap(tie(up0, first1, first3), **X)
+        deps = (up0, down1)
     after, normed2 = out_project(ids, mixed, first, stream, mlp_gain, mlp_bias, deps)
     deps = ()
     if fast:
         up1 = grid.swap(up0, **CORE)
-        up2 = grid.swap(tie(up0, down2, down1), **X)
         down3 = grid.swap(tie(down2, mixed), **CORE)
     sums = jnp.zeros((4, D), F32)
     step = lambda ks, state, weights, first_call, last_call, deps: mlp(
@@ -1198,7 +1199,6 @@
         got = grid.swap(give_up, **Y)
         up_x = (keep_up[0] + got[0], keep_up[1] + got[1])
         got_a = grid.swap(first_a13, **CORE)
-        deps = deps + down_y + up_x
     else:
         got_a = jnp.zeros_like(first_a13)
     grads_b = attend_back(
@@ -1243,7 +1243,7 @@
         *parts, own, away, both = together(*parts, own, away, both)
         got = [grid.swap(part, **bit) for part, bit in zip(parts[1:], (Y, X, XY))]
         parts = [parts[0][i] + got[0][i] + got[1][i] + got[2][i] for i in range(4)]
-        *parts, away, own, returned, both = together(*parts, away, own, returned, both)
+        *parts, away, own, both = together(*parts, away, own, both)
         got_both = grid.swap(both[1], **Z0)
         got_y = grid.swap(away, **Y)
         piece = reduce_z(grid, parts)
@@ -1260,14 +1260,12 @@
             patch_convolution_weight,
             language_projection_weight,
         )
-        piece, last, raw_grad, layer_out, both_x = together(
-            piece, last, raw_grad, layer_out, both_x
-        )
+        piece, last, layer_out, both_x = together(piece, last, layer_out, both_x)
         both_core = grid.swap(jnp.stack([both, both_x]), **CORE)
         got_z = grid.swap(last[1], **Z0)
         piece = joined(piece, *[grid.swap(piece, **bit) for bit in (Y, X, XY)])
         last = last[0] + got_z
-        piece, last, both_core = together(piece, last, both_core)
+        piece, last, both_core, raw_grad = together(piece, last, both_core, raw_grad)
         up_sum, down_sum = mlp_out(ids, both, both_x, both_core, places)
         last_x = grid.swap(last, **X)
         theirs = grid.swap(piece, **CORE)

time: 402 us -> 374 us (0.930)
  waiting for transfers between devices: 142 us -> 105 us
    ppermute x51 -> x50, waiting for transfers between devices: 141 us -> 105 us  [swap(): return lax.ppermute(value, AXES, pairs)]
    unnamed x112 -> x84, local copies, waits for them, and re-layouts: 17.3 us -> 19.1 us
    ppermute x51 -> x50, starting transfers between devices: 54.8 us -> 54.3 us  [swap(): return lax.ppermute(value, AXES, pairs)]
  transfers between devices with their start and end apart: 54 -> 54, of which waited for: 24 -> 18; matrix products, arithmetic and copies ran while one was open for 7% -> 9% of each run, Pallas kernels for 32% -> 34%
where the time goes in v4:
time: 374 us; the launch traced here: 367 us
  Pallas kernels  135 us (36%)
  waiting for transfers between devices  105 us (28%)
  starting transfers between devices  64.9 us (17%)
  local copies, waits for them, and re-layouts  32.9 us (9%)
  between operations  15.9 us (4%)
  other arithmetic  14.4 us (4%)
    pallas_call x24, Pallas kernels, call(): return lambda *args: built(*args, *deps)  135 us
    ppermute x50, waiting for transfers between devices, swap(): return lax.ppermute(value, AXES, pairs)  105 us
    ppermute x50, starting transfers between devices, swap(): return lax.ppermute(value, AXES, pairs)  54.3 us
    unnamed x84, local copies, waits for them, and re-layouts  19.1 us
  transfers between devices with their start and end apart: 54, of which 18 were waited for; matrix products, arithmetic and copies ran while one was open for 9% of the time, Pallas kernels for 34%

profile of v4, /device:TPU:0, one launch (start us, length us, event | category | flops | bytes accessed | tf_op | source)
XLA Modules:
  0.0 367.4 jit_solution(5542530619920148291)
XLA Ops:
  7.2 1.7 constant_dynamic-slice_fusion
  9.0 1.7 constant_dynamic-update-slice_fusion.4
  10.7 4.0 %collective-permute-start.1 = (bf16[96,768]{1,0:T(8,128)(2,1)S(1)}, bf16[96,768]{1,0:T(8,128)(2,1)S(1)}, u32[]{:S(2)}, u32[]{:S(2)}) collective-permute-start(bf16[96,768]{1,0:T(8,128)(2,1)S(1)} %get-tuple-element.189), channel_id=1, source_target_pairs={{0,16},{1,17},{2,18},{3,19},{4,20},{5,21},{6,22},{7,23},{8,24},{9,... | collective-permute-start | bytes 442376 | tf_op jit(solution)/shard_map/ppermute | solution.py:1014
  14.8 1.6 collective-permute-start
  16.3 7.1 %collective-permute-done.1 = bf16[96,768]{1,0:T(8,128)(2,1)S(1)} collective-permute-done((bf16[96,768]{1,0:T(8,128)(2,1)S(1)}, bf16[96,768]{1,0:T(8,128)(2,1)S(1)}, u32[]{:S(2)}, u32[]{:S(2)}) %collective-permute-start.1) | collective-permute-done | bytes 147488 | tf_op jit(solution)/shard_map/ppermute | solution.py:1014
  23.4 2.8 collective-permute-done.2
  26.3 1.6 collective-permute-start.3
  30.8 4.0 %collective-permute-start.6 = (bf16[96,768]{1,0:T(8,128)(2,1)S(1)}, bf16[96,768]{1,0:T(8,128)(2,1)S(1)}, u32[]{:S(2)}, u32[]{:S(2)}) collective-permute-start(bf16[96,768]{1,0:T(8,128)(2,1)S(1)} %reshape.90), channel_id=1, source_target_pairs={{0,24},{1,25},{2,26},{3,27},{4,28},{5,29},{6,30},{7,31},{8,16},{9,... | collective-permute-start | bytes 442376 | tf_op jit(solution)/shard_map/ppermute | solution.py:1014
  34.8 4.7 %collective-permute-start.5 = (bf16[96,768]{1,0:T(8,128)(2,1)S(1)}, bf16[96,768]{1,0:T(8,128)(2,1)S(1)}, u32[]{:S(2)}, u32[]{:S(2)}) collective-permute-start(bf16[96,768]{1,0:T(8,128)(2,1)S(1)} %reshape.90), channel_id=1, source_target_pairs={{0,16},{1,17},{2,18},{3,19},{4,20},{5,21},{6,22},{7,23},{8,24},{9,... | collective-permute-start | bytes 442376 | tf_op jit(solution)/shard_map/ppermute | solution.py:1014
  43.3 12.6 %collective-permute-done.5 = bf16[96,768]{1,0:T(8,128)(2,1)S(1)} collective-permute-done((bf16[96,768]{1,0:T(8,128)(2,1)S(1)}, bf16[96,768]{1,0:T(8,128)(2,1)S(1)}, u32[]{:S(2)}, u32[]{:S(2)}) %collective-permute-start.5) | collective-permute-done | bytes 147488 | tf_op jit(solution)/shard_map/ppermute | solution.py:1014
  56.0 1.8 pad_maximum_fusion.3
  57.8 6.9 %all-to-all-start = ((bf16[8,96,768]{2,1,0:T(8,128)(2,1)}), bf16[8,96,768]{2,1,0:T(8,128)(2,1)S(1)}, u32[]{:S(2)}, u32[]{:S(2)}) async-start(bf16[8,96,768]{2,1,0:T(8,128)(2,1)} %param.20), calls=%async_computation | async-start | bytes 2359296 | tf_op jit(solution)/shard_map/all_to_all | solution.py:1106
  65.4 1.9 constant_dynamic-update-slice_fusion.refs_2_.refs_5_.refs_3_
  73.6 2.0 collective-permute-start.11
  75.6 1.6 constant_dynamic-update-slice_fusion.10
  78.5 15.0 %collective-permute-done.11 = bf16[4,96,768]{2,1,0:T(8,128)(2,1)S(1)} collective-permute-done((bf16[4,96,768]{2,1,0:T(8,128)(2,1)}, bf16[4,96,768]{2,1,0:T(8,128)(2,1)S(1)}, u32[]{:S(2)}, u32[]{:S(2)}) %collective-permute-start.11) | collective-permute-done | bytes 589856 | tf_op jit(solution)/shard_map/ppermute | solution.py:1014
  94.9 1.5 collective-permute-start.14
  99.0 1.7 shard_map.323
  100.7 1.5 copy-done.22
  102.1 6.1 %shard_map.324.refs_0_ = bf16[3,784,768]{2,1,0:T(8,128)(2,1)S(1)} custom-call(s32[2]{0:T(128)S(1)} %pad_add_fusion.refs_0_, bf16[784,768]{1,0:T(8,128)(2,1)S(1)} %get-tuple-element.101.refs_1_, bf16[8,96,768]{2,1,0:T(8,128)(2,1)} %constant_dynamic-update-slice_fusion.refs_2_.refs_5_.refs_3_, ...), custom_call_target="tpu_custom_call" | custom-call | flops 8049999872 | bytes 1048576 | tf_op jit(solution)/shard_map/pallas_call | solution.py:87
  108.3 15.3 %shard_map.325 = (bf16[784,768]{1,0:T(8,128)(2,1)S(1)}, f32[16,768]{1,0:T(8,128)S(1)}, f32[96,128]{1,0:T(8,128)S(1)}) custom-call(bf16[3,784,768]{2,1,0:T(8,128)(2,1)S(1)} %shard_map.324.refs_0_, s32[1,8]{1,0:T(1,128)S(1)} %copy-done.17, s32[1,1]{1,0:T(1,128)S(6)} %copy.56.refs_2_.refs_6_, s32[1,768]{1,0:T(1,128)S(1)} %copy-done.1, ...), custom_call_target="tpu_custom_call" | custom-call | flops 24149999616 | bytes 1048576 | tf_op jit(solution)/shard_map/pallas_call | solution.py:87
  123.6 1.9 copy-done.20
  126.5 1.7 copy-done.23
  129.5 3.7 %shard_map.326 = (f32[784,768]{1,0:T(8,128)S(1)}, bf16[784,768]{1,0:T(8,128)(2,1)S(1)}) custom-call(s32[2]{0:T(128)S(1)} %pad_add_fusion.refs_0_, bf16[784,768]{1,0:T(8,128)(2,1)S(1)} %copy-done.28, bf16[8,96,768]{2,1,0:T(8,128)(2,1)} %constant_dynamic-update-slice_fusion.refs_2_.refs_5_.refs_3_, ...), custom_call_target="tpu_custom_call" | custom-call | flops 7360000000 | bytes 1048576 | tf_op jit(solution)/shard_map/pallas_call | solution.py:87
  133.3 11.1 %shard_map.328 = (bf16[2,784,768]{2,1,0:T(8,128)(2,1)S(1)}, bf16[2,784,768]{2,1,0:T(8,128)(2,1)S(1)}, f32[784,768]{1,0:T(8,128)S(1)}, f32[784,768]{1,0:T(8,128)S(1)}, f32[4,768]{1,0:T(4,128)S(1)}) custom-call(s32[2]{0:T(128)S(1)} %pad_add_fusion.refs_0_, s32[1,8]{1,0:T(1,128)S(1)} %copy-done.17, s32[1,1]{1,0:T(1,128)S(6)} %copy.56.refs_2_.refs_6_, ...), custom_call_target="tpu_custom_call" | custom-call | flops 23000000512 | bytes 1048576 | tf_op jit(solution)/shard_map/pallas_call | solution.py:87
  145.2 3.2 shard_map.329.refs_14_
  148.5 15.0 %shard_map.330 = (bf16[2,784,768]{2,1,0:T(8,128)(2,1)S(1)}, bf16[2,784,768]{2,1,0:T(8,128)(2,1)S(1)}, f32[784,768]{1,0:T(8,128)S(1)}, f32[784,768]{1,0:T(8,128)S(1)}, f32[4,768]{1,0:T(4,128)S(1)}) custom-call(s32[2]{0:T(128)S(1)} %pad_add_fusion.refs_0_, s32[1,8]{1,0:T(1,128)S(1)} %copy-done.17, s32[1,1]{1,0:T(1,128)S(6)} %copy.56.refs_2_.refs_6_, ...), custom_call_target="tpu_custom_call" | custom-call | flops 23000000512 | bytes 1048576 | tf_op jit(solution)/shard_map/pallas_call | solution.py:87
  163.6 3.2 shard_map.331.refs_9_
  167.3 4.5 %shard_map.332 = (f32[784,768]{1,0:T(8,128)S(1)}, bf16[784,768]{1,0:T(8,128)(2,1)S(1)}, bf16[784,768]{1,0:T(8,128)(2,1)S(1)}, f32[2,768]{1,0:T(2,128)S(1)}) custom-call(s32[2]{0:T(128)S(1)} %pad_add_fusion.refs_0_, f32[784,768]{1,0:T(8,128)S(1)} %get-tuple-element.117.refs_1_, f32[784,768]{1,0:T(8,128)S(1)} %get-tuple-element.108.refs_7_.refs_8_.refs_2_, ...), custom_call_target="tpu_custom_call" | custom-call | flops 9774999552 | bytes 1048576 | tf_op jit(solution)/shard_map/pallas_call | solution.py:87
  171.8 3.3 shard_map.333
  175.2 5.1 %shard_map.334 = (bf16[2,4,96,768]{3,2,1,0:T(8,128)(2,1)S(1)}, bf16[2,4,96,768]{3,2,1,0:T(8,128)(2,1)S(1)}) custom-call(s32[2]{0:T(128)S(1)} %pad_add_fusion.refs_0_, bf16[784,768]{1,0:T(8,128)(2,1)S(1)} %copy-done.33, bf16[2,784,768]{2,1,0:T(8,128)(2,1)S(1)} %get-tuple-element.116.refs_3_.refs_2_, bf16[784,768]{1,0:T(8,128)(2,1)S(1)} %copy-done.33, ...), custom_call_target="tpu_custom_call" | custom-call | flops 9200000000 | bytes 1048576 | tf_op jit(solution)/shard_map/pallas_call | solution.py:87
  181.4 13.0 %shard_map.335.refs_3_.refs_1_ = bf16[3,784,384]{2,1,0:T(8,128)(2,1)S(1)} custom-call(bf16[3,784,768]{2,1,0:T(8,128)(2,1)S(1)} %copy-done.21, bf16[784,768]{1,0:T(8,128)(2,1)S(1)} %copy-done.29, bf16[784,768]{1,0:T(8,128)(2,1)S(1)} %get-tuple-element.120.refs_2_, f32[16,768]{1,0:T(8,128)S(1)} %get-tuple-element.121.refs_3_, ...), custom_call_target="tpu_custom_call" | custom-call | flops 17250000896 | bytes 1048576 | tf_op jit(solution)/shard_map/pallas_call | solution.py:87
  194.5 3.3 shard_map.336.refs_9_
  197.8 13.0 %shard_map.337.refs_3_.refs_2_ = bf16[3,784,384]{2,1,0:T(8,128)(2,1)S(1)} custom-call(bf16[3,784,768]{2,1,0:T(8,128)(2,1)S(1)} %copy-done.21, bf16[784,768]{1,0:T(8,128)(2,1)S(1)} %copy-done.29, bf16[784,768]{1,0:T(8,128)(2,1)S(1)} %get-tuple-element.120.refs_2_, f32[16,768]{1,0:T(8,128)S(1)} %get-tuple-element.121.refs_3_, ...), custom_call_target="tpu_custom_call" | custom-call | flops 17250000896 | bytes 1048576 | tf_op jit(solution)/shard_map/pallas_call | solution.py:87
  210.8 3.5 shard_map.338.refs_6_
  216.4 1.8 collective-permute-start.24
  218.2 3.2 shard_map.339
  221.4 9.1 %collective-permute-done.22 = bf16[4,96,768]{2,1,0:T(8,128)(2,1)S(1)} collective-permute-done((bf16[4,96,768]{2,1,0:T(8,128)(2,1)S(1)}, bf16[4,96,768]{2,1,0:T(8,128)(2,1)S(1)}, u32[]{:S(2)}, u32[]{:S(2)}) %collective-permute-start.22) | collective-permute-done | bytes 589856 | tf_op jit(solution)/shard_map/ppermute | solution.py:1014
  231.6 3.3 collective-permute-start.28
  235.1 3.2 shard_map.340
  238.8 7.6 %shard_map.341 = (bf16[768,768]{1,0:T(8,128)(2,1)}, f32[8,768]{1,0:T(8,128)S(1)}, f32[2,768]{1,0:T(2,128)S(1)}) custom-call(s32[2]{0:T(128)S(1)} %pad_add_fusion.refs_0_, bf16[3,784,384]{2,1,0:T(8,128)(2,1)S(1)} %shard_map.335.refs_3_.refs_1_, bf16[3,784,384]{2,1,0:T(8,128)(2,1)S(1)} %shard_map.337.refs_3_.refs_2_, ...), custom_call_target="tpu_custom_call" | custom-call | flops 11500000256 | bytes 1048576 | tf_op jit(solution)/shard_map/pallas_call | solution.py:87
  246.4 4.7 %shard_map.342 = (bf16[8,56,768]{2,1,0:T(8,128)(2,1)S(1)}, bf16[8,56,768]{2,1,0:T(8,128)(2,1)S(1)}, bf16[8,56,768]{2,1,0:T(8,128)(2,1)S(1)}, bf16[8,56,768]{2,1,0:T(8,128)(2,1)S(1)}) custom-call(s32[2]{0:T(128)S(1)} %pad_add_fusion.refs_0_, bf16[768,768]{1,0:T(8,128)(2,1)S(1)} %bitcast.94, bf16[768,768]{1,0:T(8,128)(2,1)} %get-tuple-element.134.refs_2_, ...), custom_call_target="tpu_custom_call" | custom-call | flops 6899999744 | bytes 1048576 | tf_op jit(solution)/shard_map/pallas_call | solution.py:87
  251.9 8.3 %collective-permute-done.28 = bf16[2,2,96,768]{3,2,1,0:T(8,128)(2,1)S(1)} collective-permute-done((bf16[2,2,96,768]{3,2,1,0:T(8,128)(2,1)S(1)}, bf16[2,2,96,768]{3,2,1,0:T(8,128)(2,1)S(1)}, u32[]{:S(2)}, u32[]{:S(2)}) %collective-permute-start.28) | collective-permute-done | bytes 589856 | tf_op jit(solution)/shard_map/ppermute | solution.py:1014
  262.0 3.0 collective-permute-done.27
  266.1 1.5 collective-permute-start.29
  269.6 3.6 all-to-all-start.1
  273.2 17.9 %collective-permute-done.29 = bf16[4,56,768]{2,1,0:T(8,128)(2,1)S(1)} collective-permute-done((bf16[4,56,768]{2,1,0:T(8,128)(2,1)}, bf16[4,56,768]{2,1,0:T(8,128)(2,1)S(1)}, u32[]{:S(2)}, u32[]{:S(2)}) %collective-permute-start.29) | collective-permute-done | bytes 344096 | tf_op jit(solution)/shard_map/ppermute | solution.py:1014
  291.1 1.9 fusion.15
  293.0 4.4 %collective-permute-start.34 = (bf16[56,768]{1,0:T(8,128)(2,1)}, bf16[56,768]{1,0:T(8,128)(2,1)S(1)}, u32[]{:S(2)}, u32[]{:S(2)}) collective-permute-start(bf16[56,768]{1,0:T(8,128)(2,1)} %get-tuple-element.155), channel_id=1, source_target_pairs={{0,24},{1,25},{2,26},{3,27},{4,28},{5,29},{6,30},{7,31},{8,16},{9,... | collective-permute-start | bytes 258056 | tf_op jit(solution)/shard_map/ppermute | solution.py:1014
  297.4 1.9 collective-permute-start.35
  300.0 6.1 %collective-permute-done.33 = bf16[56,768]{1,0:T(8,128)(2,1)S(1)} collective-permute-done((bf16[56,768]{1,0:T(8,128)(2,1)}, bf16[56,768]{1,0:T(8,128)(2,1)S(1)}, u32[]{:S(2)}, u32[]{:S(2)}) %collective-permute-start.33) | collective-permute-done | bytes 86048 | tf_op jit(solution)/shard_map/ppermute | solution.py:1014
  306.1 3.3 collective-permute-done.36
  311.7 3.3 collective-permute-start.37
  315.2 2.8 fusion
  319.1 6.0 %collective-permute-done.38 = bf16[56,768]{1,0:T(8,128)(2,1)S(1)} collective-permute-done((bf16[56,768]{1,0:T(8,128)(2,1)S(1)}, bf16[56,768]{1,0:T(8,128)(2,1)S(1)}, u32[]{:S(2)}, u32[]{:S(2)}) %collective-permute-start.38) | collective-permute-done | bytes 86048 | tf_op jit(solution)/shard_map/ppermute | solution.py:1014
  325.8 2.6 collective-permute-done.40
  328.5 2.1 collective-permute-start.44
  334.9 2.5 shard_map.343
  339.1 1.7 collective-permute-done.44
  340.8 4.4 %collective-permute-done.43 = bf16[4,56,768]{2,1,0:T(8,128)(2,1)} collective-permute-done((bf16[4,56,768]{2,1,0:T(8,128)(2,1)}, bf16[4,56,768]{2,1,0:T(8,128)(2,1)}, u32[]{:S(2)}, u32[]{:S(2)}) %collective-permute-start.43) | collective-permute-done | bytes 344096 | tf_op jit(solution)/shard_map/ppermute | solution.py:1014
  348.2 2.4 shard_map.344
  350.6 2.5 collective-permute-done.48.refs_2_
  353.2 3.3 shard_map.345
  358.5 1.6 shard_map.346
  (202 shorter events, 48.9 us)
Async XLA Ops:
  7.2 87.2 %all-gather.5.cloned.1.call-start = ((), (), s32[]{:S(2)}) async-start(), calls=%async_computation.2 | async-start | bytes 1327104 | tf_op jit(solution)/shard_map/all_gather | solution.py:1115
  9.0 19.6 %copy-start.36 = (bf16[96,3072]{1,0:T(8,128)(2,1)S(1)}, bf16[96,3072]{1,0:T(8,128)(2,1)}, u32[]{:S(2)}) copy-start(bf16[96,3072]{1,0:T(8,128)(2,1)} %param.35) | copy-start | bytes 1769476
  9.0 117.5 %all-gather.7.cloned.1.call-start = ((), (), s32[]{:S(2)}) async-start(), calls=%async_computation.3 | async-start | bytes 1327104 | tf_op jit(solution)/shard_map/all_gather | solution.py:1117
  10.7 12.7 %collective-permute-start.1 = (bf16[96,768]{1,0:T(8,128)(2,1)S(1)}, bf16[96,768]{1,0:T(8,128)(2,1)S(1)}, u32[]{:S(2)}, u32[]{:S(2)}) collective-permute-start(bf16[96,768]{1,0:T(8,128)(2,1)S(1)} %get-tuple-element.189), channel_id=1, source_target_pairs={{0,16},{1,17},{2,18},{3,19},{4,20},{5,21},{6,22},{7,23},{8,24},{9,... | collective-permute-start | bytes 442376 | tf_op jit(solution)/shard_map/ppermute | solution.py:1014
  14.8 8.7 %collective-permute-start = (bf16[96,768]{1,0:T(8,128)(2,1)S(1)}, bf16[96,768]{1,0:T(8,128)(2,1)S(1)}, u32[]{:S(2)}, u32[]{:S(2)}) collective-permute-start(bf16[96,768]{1,0:T(8,128)(2,1)S(1)} %get-tuple-element.189), channel_id=1, source_target_pairs={{0,8},{1,9},{2,10},{3,11},{4,12},{5,13},{6,14},{7,15},{8,0},{9,1},... | collective-permute-start | bytes 442376 | tf_op jit(solution)/shard_map/ppermute | solution.py:1014
  16.3 9.9 %collective-permute-start.2 = (bf16[96,768]{1,0:T(8,128)(2,1)S(1)}, bf16[96,768]{1,0:T(8,128)(2,1)S(1)}, u32[]{:S(2)}, u32[]{:S(2)}) collective-permute-start(bf16[96,768]{1,0:T(8,128)(2,1)S(1)} %get-tuple-element.189), channel_id=1, source_target_pairs={{0,24},{1,25},{2,26},{3,27},{4,28},{5,29},{6,30},{7,31},{8,16},{9,... | collective-permute-start | bytes 442376 | tf_op jit(solution)/shard_map/ppermute | solution.py:1014
  26.3 16.4 %collective-permute-start.3 = (bf16[4,96,768]{2,1,0:T(8,128)(2,1)S(1)}, bf16[4,96,768]{2,1,0:T(8,128)(2,1)}, u32[]{:S(2)}, u32[]{:S(2)}) collective-permute-start(bf16[4,96,768]{2,1,0:T(8,128)(2,1)S(1)} %pad_maximum_fusion.2), channel_id=1, source_target_pairs={{0,4},{1,5},{2,6},{3,7},{4,0},{5,1},{6,2},{7,3},{8,12},{9,13},{10,... | collective-permute-start | bytes 1769480 | tf_op jit(solution)/shard_map/ppermute | solution.py:1014
  30.8 12.5 %collective-permute-start.6 = (bf16[96,768]{1,0:T(8,128)(2,1)S(1)}, bf16[96,768]{1,0:T(8,128)(2,1)S(1)}, u32[]{:S(2)}, u32[]{:S(2)}) collective-permute-start(bf16[96,768]{1,0:T(8,128)(2,1)S(1)} %reshape.90), channel_id=1, source_target_pairs={{0,24},{1,25},{2,26},{3,27},{4,28},{5,29},{6,30},{7,31},{8,16},{9,... | collective-permute-start | bytes 442376 | tf_op jit(solution)/shard_map/ppermute | solution.py:1014
  34.8 21.2 %collective-permute-start.5 = (bf16[96,768]{1,0:T(8,128)(2,1)S(1)}, bf16[96,768]{1,0:T(8,128)(2,1)S(1)}, u32[]{:S(2)}, u32[]{:S(2)}) collective-permute-start(bf16[96,768]{1,0:T(8,128)(2,1)S(1)} %reshape.90), channel_id=1, source_target_pairs={{0,16},{1,17},{2,18},{3,19},{4,20},{5,21},{6,22},{7,23},{8,24},{9,... | collective-permute-start | bytes 442376 | tf_op jit(solution)/shard_map/ppermute | solution.py:1014
  39.5 16.5 %collective-permute-start.4 = (bf16[96,768]{1,0:T(8,128)(2,1)S(1)}, bf16[96,768]{1,0:T(8,128)(2,1)}, u32[]{:S(2)}, u32[]{:S(2)}) collective-permute-start(bf16[96,768]{1,0:T(8,128)(2,1)S(1)} %reshape.90), channel_id=1, source_target_pairs={{0,8},{1,9},{2,10},{3,11},{4,12},{5,13},{6,14},{7,15},{8,0},{9,1},... | collective-permute-start | bytes 442376 | tf_op jit(solution)/shard_map/ppermute | solution.py:1014
  40.0 27.3 %collective-permute-start.8 = (bf16[4,96,768]{2,1,0:T(8,128)(2,1)S(1)}, bf16[4,96,768]{2,1,0:T(8,128)(2,1)}, u32[]{:S(2)}, u32[]{:S(2)}) collective-permute-start(bf16[4,96,768]{2,1,0:T(8,128)(2,1)S(1)} %pad_maximum_fusion.2), channel_id=1, source_target_pairs={{0,2},{1,3},{2,0},{3,1},{4,6},{5,7},{6,4},{7,5},{8,10},{9,11},{10,... | collective-permute-start | bytes 1769480 | tf_op jit(solution)/shard_map/ppermute | solution.py:1014
  42.7 25.8 %collective-permute-start.9 = (bf16[4,96,768]{2,1,0:T(8,128)(2,1)}, bf16[4,96,768]{2,1,0:T(8,128)(2,1)}, u32[]{:S(2)}, u32[]{:S(2)}) collective-permute-start(bf16[4,96,768]{2,1,0:T(8,128)(2,1)} %collective-permute-done.3), channel_id=1, source_target_pairs={{0,2},{1,3},{2,0},{3,1},{4,6},{5,7},{6,4},{7,5},{8,10},{9,11},{10,... | collective-permute-start | bytes 1769480 | tf_op jit(solution)/shard_map/ppermute | solution.py:1014
  57.8 38.6 %all-to-all-start = ((bf16[8,96,768]{2,1,0:T(8,128)(2,1)}), bf16[8,96,768]{2,1,0:T(8,128)(2,1)S(1)}, u32[]{:S(2)}, u32[]{:S(2)}) async-start(bf16[8,96,768]{2,1,0:T(8,128)(2,1)} %param.20), calls=%async_computation | async-start | bytes 2359296 | tf_op jit(solution)/shard_map/all_to_all | solution.py:1106
  67.3 27.6 %collective-permute-start.7 = (bf16[8,96,768]{2,1,0:T(8,128)(2,1)}, bf16[8,96,768]{2,1,0:T(8,128)(2,1)}, u32[]{:S(2)}, u32[]{:S(2)}) collective-permute-start(bf16[8,96,768]{2,1,0:T(8,128)(2,1)} %constant_dynamic-update-slice_fusion.refs_2_.refs_5_.refs_3_), channel_id=1, source_target_pairs={{0,1},{1,0},{2,3},{3,2},{4,5},{5,4},{6,7},{7,6},{8,9},{9,8},{10,11... | collective-permute-start | bytes 3538952 | tf_op jit(solution)/shard_map/ppermute | solution.py:1014
  69.6 25.3 %collective-permute-start.10 = (bf16[8,96,768]{2,1,0:T(8,128)(2,1)S(1)}, bf16[8,96,768]{2,1,0:T(8,128)(2,1)}, u32[]{:S(2)}, u32[]{:S(2)}) collective-permute-start(bf16[8,96,768]{2,1,0:T(8,128)(2,1)S(1)} %constant_dynamic-update-slice_fusion.5.refs_4_.refs_7_.refs_5_), channel_id=1, source_target_pairs={{0,1},{1,0},{2,3},{3,2},{4,5},{5,4},{6,7},{7,6},{8,9},{9,8},{10,11... | collective-permute-start | bytes 3538952 | tf_op jit(solution)/shard_map/ppermute | solution.py:1014
  72.9 23.5 %copy-start.9 = (f32[8,768]{1,0:T(8,128)S(1)}, f32[8,768]{1,0:T(8,128)}, u32[]{:S(2)}) copy-start(f32[8,768]{1,0:T(8,128)} %refs_5_.3) | copy-start | bytes 73732
  72.9 23.5 %copy-start.10 = (f32[768]{0:T(1024)S(1)}, f32[768]{0:T(1024)}, u32[]{:S(2)}) copy-start(f32[768]{0:T(1024)} %refs_2_.6) | copy-start | bytes 9220
  72.9 23.5 %copy-start.11 = (f32[768]{0:T(1024)S(1)}, f32[768]{0:T(1024)}, u32[]{:S(2)}) copy-start(f32[768]{0:T(1024)} %refs_4_.2) | copy-start | bytes 9220
  72.9 23.5 %copy-start.12 = (f32[768]{0:T(1024)S(1)}, f32[768]{0:T(1024)}, u32[]{:S(2)}) copy-start(f32[768]{0:T(1024)} %refs_7_.4) | copy-start | bytes 9220
  72.9 23.5 %copy-start.16 = (f32[768]{0:T(1024)S(1)}, f32[768]{0:T(1024)}, u32[]{:S(2)}) copy-start(f32[768]{0:T(1024)} %refs_8_.3) | copy-start | bytes 9220
  73.6 19.9 %collective-permute-start.11 = (bf16[4,96,768]{2,1,0:T(8,128)(2,1)}, bf16[4,96,768]{2,1,0:T(8,128)(2,1)S(1)}, u32[]{:S(2)}, u32[]{:S(2)}) collective-permute-start(bf16[4,96,768]{2,1,0:T(8,128)(2,1)} %pad_maximum_fusion.3), channel_id=1, source_target_pairs={{0,4},{1,5},{2,6},{3,7},{4,0},{5,1},{6,2},{7,3},{8,12},{9,13},{10,... | collective-permute-start | bytes 1769480 | tf_op jit(solution)/shard_map/ppermute | solution.py:1014
  94.3 38.9 %collective-permute-start.13 = (bf16[8,96,768]{2,1,0:T(8,128)(2,1)}, bf16[8,96,768]{2,1,0:T(8,128)(2,1)}, u32[]{:S(2)}, u32[]{:S(2)}) collective-permute-start(bf16[8,96,768]{2,1,0:T(8,128)(2,1)} %constant_dynamic-update-slice_fusion.7.refs_9_.refs_10_), channel_id=1, source_target_pairs={{0,1},{1,0},{2,3},{3,2},{4,5},{5,4},{6,7},{7,6},{8,9},{9,8},{10,11... | collective-permute-start | bytes 3538952 | tf_op jit(solution)/shard_map/ppermute | solution.py:1014
  94.4 32.1 %collective-permute-start.12 = (bf16[8,96,768]{2,1,0:T(8,128)(2,1)}, bf16[8,96,768]{2,1,0:T(8,128)(2,1)}, u32[]{:S(2)}, u32[]{:S(2)}) collective-permute-start(bf16[8,96,768]{2,1,0:T(8,128)(2,1)} %bitcast.102), channel_id=1, source_target_pairs={{0,1},{1,0},{2,3},{3,2},{4,5},{5,4},{6,7},{7,6},{8,9},{9,8},{10,11... | collective-permute-start | bytes 3538952 | tf_op jit(solution)/shard_map/ppermute | solution.py:1014
  94.9 49.6 %collective-permute-start.14 = (bf16[8,96,768]{2,1,0:T(8,128)(2,1)}, bf16[8,96,768]{2,1,0:T(8,128)(2,1)}, u32[]{:S(2)}, u32[]{:S(2)}) collective-permute-start(bf16[8,96,768]{2,1,0:T(8,128)(2,1)} %constant_dynamic-update-slice_fusion.7.refs_9_.refs_10_), channel_id=1, source_target_pairs={{0,2},{1,3},{2,0},{3,1},{4,6},{5,7},{6,4},{7,5},{8,10},{9,11},{10,... | collective-permute-start | bytes 3538952 | tf_op jit(solution)/shard_map/ppermute | solution.py:1014
  108.3 18.2 %copy-start.13 = (f32[768]{0:T(1024)S(1)}, f32[768]{0:T(1024)}, u32[]{:S(2)}) copy-start(f32[768]{0:T(1024)} %refs_8_.2) | copy-start | bytes 9220
  108.3 18.2 %copy-start.15 = (f32[768]{0:T(1024)S(1)}, f32[768]{0:T(1024)}, u32[]{:S(2)}) copy-start(f32[768]{0:T(1024)} %refs_4_.3) | copy-start | bytes 9220
  126.5 22.0 %collective-permute-start.16 = (bf16[8,96,768]{2,1,0:T(8,128)(2,1)}, bf16[8,96,768]{2,1,0:T(8,128)(2,1)S(1)}, u32[]{:S(2)}, u32[]{:S(2)}) collective-permute-start(bf16[8,96,768]{2,1,0:T(8,128)(2,1)} %bitcast.104), channel_id=1, source_target_pairs={{0,1},{1,0},{2,3},{3,2},{4,5},{5,4},{6,7},{7,6},{8,9},{9,8},{10,11... | collective-permute-start | bytes 3538952 | tf_op jit(solution)/shard_map/ppermute | solution.py:1014
  133.2 30.3 %copy-start.32 = (bf16[784,768]{1,0:T(8,128)(2,1)}, bf16[784,768]{1,0:T(8,128)(2,1)S(1)}, u32[]{:S(2)}) copy-start(bf16[784,768]{1,0:T(8,128)(2,1)S(1)} %get-tuple-element.106.refs_3_.refs_1_) | copy-start | bytes 3612676
  144.4 4.1 %collective-permute-start.15 = (bf16[8,96,768]{2,1,0:T(8,128)(2,1)}, bf16[8,96,768]{2,1,0:T(8,128)(2,1)S(1)}, u32[]{:S(2)}, u32[]{:S(2)}) collective-permute-start(bf16[8,96,768]{2,1,0:T(8,128)(2,1)} %collective-permute-done.14.refs_10_), channel_id=1, source_target_pairs={{0,1},{1,0},{2,3},{3,2},{4,5},{5,4},{6,7},{7,6},{8,9},{9,8},{10,11... | collective-permute-start | bytes 3538952 | tf_op jit(solution)/shard_map/ppermute | solution.py:1014
  148.4 23.4 %collective-permute-start.17 = (bf16[2,8,96,768]{3,2,1,0:T(8,128)(2,1)S(1)}, bf16[2,8,96,768]{3,2,1,0:T(8,128)(2,1)S(1)}, u32[]{:S(2)}, u32[]{:S(2)}) collective-permute-start(bf16[2,8,96,768]{3,2,1,0:T(8,128)(2,1)S(1)} %shard_map.329.refs_14_), channel_id=1, source_target_pairs={{0,1},{1,0},{2,3},{3,2},{4,5},{5,4},{6,7},{7,6},{8,9},{9,8},{10,11... | collective-permute-start | bytes 7077896 | tf_op jit(solution)/shard_map/ppermute | solution.py:1014
  166.8 5.0 %collective-permute-start.18 = (bf16[2,8,96,768]{3,2,1,0:T(8,128)(2,1)S(1)}, bf16[2,8,96,768]{3,2,1,0:T(8,128)(2,1)S(1)}, u32[]{:S(2)}, u32[]{:S(2)}) collective-permute-start(bf16[2,8,96,768]{3,2,1,0:T(8,128)(2,1)S(1)} %shard_map.331.refs_9_), channel_id=1, source_target_pairs={{0,1},{1,0},{2,3},{3,2},{4,5},{5,4},{6,7},{7,6},{8,9},{9,8},{10,11... | collective-permute-start | bytes 7077896 | tf_op jit(solution)/shard_map/ppermute | solution.py:1014
  180.3 34.7 %collective-permute-start.21 = (bf16[2,4,96,768]{3,2,1,0:T(8,128)(2,1)S(1)}, bf16[2,4,96,768]{3,2,1,0:T(8,128)(2,1)S(1)}, u32[]{:S(2)}, u32[]{:S(2)}) collective-permute-start(bf16[2,4,96,768]{3,2,1,0:T(8,128)(2,1)S(1)} %get-tuple-element.129), channel_id=1, source_target_pairs={{0,4},{1,5},{2,6},{3,7},{4,0},{5,1},{6,2},{7,3},{8,12},{9,13},{10,... | collective-permute-start | bytes 3538952 | tf_op jit(solution)/shard_map/ppermute | solution.py:1014
  180.6 34.4 %collective-permute-start.23 = (bf16[2,4,96,768]{3,2,1,0:T(8,128)(2,1)S(1)}, bf16[2,4,96,768]{3,2,1,0:T(8,128)(2,1)S(1)}, u32[]{:S(2)}, u32[]{:S(2)}) collective-permute-start(bf16[2,4,96,768]{3,2,1,0:T(8,128)(2,1)S(1)} %get-tuple-element.131), channel_id=1, source_target_pairs={{0,2},{1,3},{2,0},{3,1},{4,6},{5,7},{6,4},{7,5},{8,10},{9,11},{10,... | collective-permute-start | bytes 3538952 | tf_op jit(solution)/shard_map/ppermute | solution.py:1014
  181.4 13.1 %copy-start.26 = (bf16[784,768]{1,0:T(8,128)(2,1)S(1)}, bf16[784,768]{1,0:T(8,128)(2,1)}, u32[]{:S(2)}) copy-start(bf16[784,768]{1,0:T(8,128)(2,1)} %copy-done.25) | copy-start | bytes 3612676
  197.8 20.5 %collective-permute-start.20 = (bf16[2,8,96,384]{3,2,1,0:T(8,128)(2,1)S(1)}, bf16[2,8,96,384]{3,2,1,0:T(8,128)(2,1)S(1)}, u32[]{:S(2)}, u32[]{:S(2)}) collective-permute-start(bf16[2,8,96,384]{3,2,1,0:T(8,128)(2,1)S(1)} %shard_map.336.refs_9_), channel_id=1, source_target_pairs={{0,1},{1,0},{2,3},{3,2},{4,5},{5,4},{6,7},{7,6},{8,9},{9,8},{10,11... | collective-permute-start | bytes 3538952 | tf_op jit(solution)/shard_map/ppermute | solution.py:1014
  214.3 20.8 %collective-permute-start.19 = (bf16[2,8,96,384]{3,2,1,0:T(8,128)(2,1)S(1)}, bf16[2,8,96,384]{3,2,1,0:T(8,128)(2,1)S(1)}, u32[]{:S(2)}, u32[]{:S(2)}) collective-permute-start(bf16[2,8,96,384]{3,2,1,0:T(8,128)(2,1)S(1)} %shard_map.338.refs_6_), channel_id=1, source_target_pairs={{0,1},{1,0},{2,3},{3,2},{4,5},{5,4},{6,7},{7,6},{8,9},{9,8},{10,11... | collective-permute-start | bytes 3538952 | tf_op jit(solution)/shard_map/ppermute | solution.py:1014
  215.1 15.3 %collective-permute-start.22 = (bf16[4,96,768]{2,1,0:T(8,128)(2,1)S(1)}, bf16[4,96,768]{2,1,0:T(8,128)(2,1)S(1)}, u32[]{:S(2)}, u32[]{:S(2)}) collective-permute-start(bf16[4,96,768]{2,1,0:T(8,128)(2,1)S(1)} %fusion.10), channel_id=1, source_target_pairs={{0,2},{1,3},{2,0},{3,1},{4,6},{5,7},{6,4},{7,5},{8,10},{9,11},{10,... | collective-permute-start | bytes 1769480 | tf_op jit(solution)/shard_map/ppermute | solution.py:1014
  216.4 15.1 %collective-permute-start.24 = (bf16[4,96,768]{2,1,0:T(8,128)(2,1)S(1)}, bf16[4,96,768]{2,1,0:T(8,128)(2,1)S(1)}, u32[]{:S(2)}, u32[]{:S(2)}) collective-permute-start(bf16[4,96,768]{2,1,0:T(8,128)(2,1)S(1)} %fusion.6), channel_id=1, source_target_pairs={{0,4},{1,5},{2,6},{3,7},{4,0},{5,1},{6,2},{7,3},{8,12},{9,13},{10,... | collective-permute-start | bytes 1769480 | tf_op jit(solution)/shard_map/ppermute | solution.py:1014
  231.6 28.6 %collective-permute-start.28 = (bf16[2,2,96,768]{3,2,1,0:T(8,128)(2,1)S(1)}, bf16[2,2,96,768]{3,2,1,0:T(8,128)(2,1)S(1)}, u32[]{:S(2)}, u32[]{:S(2)}) collective-permute-start(bf16[2,2,96,768]{3,2,1,0:T(8,128)(2,1)S(1)} %fusion.3), channel_id=1, source_target_pairs={{0,16},{1,17},{2,18},{3,19},{4,20},{5,21},{6,22},{7,23},{8,24},{9,... | collective-permute-start | bytes 1769480 | tf_op jit(solution)/shard_map/ppermute | solution.py:1014
  238.4 26.7 %collective-permute-start.27 = (bf16[2,4,96,768]{3,2,1,0:T(8,128)(2,1)S(1)}, bf16[2,4,96,768]{3,2,1,0:T(8,128)(2,1)S(1)}, u32[]{:S(2)}, u32[]{:S(2)}) collective-permute-start(bf16[2,4,96,768]{3,2,1,0:T(8,128)(2,1)S(1)} %get-tuple-element.144), channel_id=1, source_target_pairs={{0,2},{1,3},{2,0},{3,1},{4,6},{5,7},{6,4},{7,5},{8,10},{9,11},{10,... | collective-permute-start | bytes 3538952 | tf_op jit(solution)/shard_map/ppermute | solution.py:1014
  251.1 9.2 %collective-permute-start.25 = (bf16[8,56,768]{2,1,0:T(8,128)(2,1)S(1)}, bf16[8,56,768]{2,1,0:T(8,128)(2,1)S(1)}, u32[]{:S(2)}, u32[]{:S(2)}) collective-permute-start(bf16[8,56,768]{2,1,0:T(8,128)(2,1)S(1)} %get-tuple-element.141), channel_id=1, source_target_pairs={{0,1},{1,0},{2,3},{3,2},{4,5},{5,4},{6,7},{7,6},{8,9},{9,8},{10,11... | collective-permute-start | bytes 2064392 | tf_op jit(solution)/shard_map/ppermute | solution.py:1014
  251.2 9.9 %collective-permute-start.26 = (bf16[8,56,768]{2,1,0:T(8,128)(2,1)S(1)}, bf16[8,56,768]{2,1,0:T(8,128)(2,1)S(1)}, u32[]{:S(2)}, u32[]{:S(2)}) collective-permute-start(bf16[8,56,768]{2,1,0:T(8,128)(2,1)S(1)} %get-tuple-element.143), channel_id=1, source_target_pairs={{0,1},{1,0},{2,3},{3,2},{4,5},{5,4},{6,7},{7,6},{8,9},{9,8},{10,11... | collective-permute-start | bytes 2064392 | tf_op jit(solution)/shard_map/ppermute | solution.py:1014
  266.1 24.9 %collective-permute-start.29 = (bf16[4,56,768]{2,1,0:T(8,128)(2,1)}, bf16[4,56,768]{2,1,0:T(8,128)(2,1)S(1)}, u32[]{:S(2)}, u32[]{:S(2)}) collective-permute-start(bf16[4,56,768]{2,1,0:T(8,128)(2,1)} %get-tuple-element.146), channel_id=1, source_target_pairs={{0,4},{1,5},{2,6},{3,7},{4,0},{5,1},{6,2},{7,3},{8,12},{9,13},{10,... | collective-permute-start | bytes 1032200 | tf_op jit(solution)/shard_map/ppermute | solution.py:1014
  267.6 23.4 %collective-permute-start.30 = (bf16[4,56,768]{2,1,0:T(8,128)(2,1)}, bf16[4,56,768]{2,1,0:T(8,128)(2,1)}, u32[]{:S(2)}, u32[]{:S(2)}) collective-permute-start(bf16[4,56,768]{2,1,0:T(8,128)(2,1)} %get-tuple-element.147), channel_id=1, source_target_pairs={{0,2},{1,3},{2,0},{3,1},{4,6},{5,7},{6,4},{7,5},{8,10},{9,11},{10,... | collective-permute-start | bytes 1032200 | tf_op jit(solution)/shard_map/ppermute | solution.py:1014
  268.4 22.7 %collective-permute-start.31 = (bf16[4,56,768]{2,1,0:T(8,128)(2,1)}, bf16[4,56,768]{2,1,0:T(8,128)(2,1)}, u32[]{:S(2)}, u32[]{:S(2)}) collective-permute-start(bf16[4,56,768]{2,1,0:T(8,128)(2,1)} %get-tuple-element.148), channel_id=1, source_target_pairs={{0,6},{1,7},{2,4},{3,5},{4,2},{5,3},{6,0},{7,1},{8,14},{9,15},{10,... | collective-permute-start | bytes 1032200 | tf_op jit(solution)/shard_map/ppermute | solution.py:1014
  269.6 64.0 %all-to-all-start.1 = ((bf16[8,96,768]{2,1,0:T(8,128)(2,1)}), bf16[8,96,768]{2,1,0:T(8,128)(2,1)S(1)}, u32[]{:S(2)}, u32[]{:S(2)}) async-start(bf16[8,96,768]{2,1,0:T(8,128)(2,1)} %bitcast.44), calls=%async_computation.1 | async-start | bytes 2359296 | tf_op jit(solution)/shard_map/all_to_all | solution.py:1224
  293.0 7.0 %collective-permute-start.32 = (bf16[56,768]{1,0:T(8,128)(2,1)}, bf16[56,768]{1,0:T(8,128)(2,1)S(1)}, u32[]{:S(2)}, u32[]{:S(2)}) collective-permute-start(bf16[56,768]{1,0:T(8,128)(2,1)} %get-tuple-element.153), channel_id=1, source_target_pairs={{0,8},{1,9},{2,10},{3,11},{4,12},{5,13},{6,14},{7,15},{8,0},{9,1},... | collective-permute-start | bytes 258056 | tf_op jit(solution)/shard_map/ppermute | solution.py:1014
  293.0 13.1 %collective-permute-start.33 = (bf16[56,768]{1,0:T(8,128)(2,1)}, bf16[56,768]{1,0:T(8,128)(2,1)S(1)}, u32[]{:S(2)}, u32[]{:S(2)}) collective-permute-start(bf16[56,768]{1,0:T(8,128)(2,1)} %get-tuple-element.154), channel_id=1, source_target_pairs={{0,16},{1,17},{2,18},{3,19},{4,20},{5,21},{6,22},{7,23},{8,24},{9,... | collective-permute-start | bytes 258056 | tf_op jit(solution)/shard_map/ppermute | solution.py:1014
  293.0 13.1 %collective-permute-start.34 = (bf16[56,768]{1,0:T(8,128)(2,1)}, bf16[56,768]{1,0:T(8,128)(2,1)S(1)}, u32[]{:S(2)}, u32[]{:S(2)}) collective-permute-start(bf16[56,768]{1,0:T(8,128)(2,1)} %get-tuple-element.155), channel_id=1, source_target_pairs={{0,24},{1,25},{2,26},{3,27},{4,28},{5,29},{6,30},{7,31},{8,16},{9,... | collective-permute-start | bytes 258056 | tf_op jit(solution)/shard_map/ppermute | solution.py:1014
  297.4 12.1 %collective-permute-start.35 = (bf16[4,96,768]{2,1,0:T(8,128)(2,1)}, bf16[4,96,768]{2,1,0:T(8,128)(2,1)}, u32[]{:S(2)}, u32[]{:S(2)}) collective-permute-start(bf16[4,96,768]{2,1,0:T(8,128)(2,1)} %get-tuple-element.157), channel_id=1, source_target_pairs={{0,4},{1,5},{2,6},{3,7},{4,0},{5,1},{6,2},{7,3},{8,12},{9,13},{10,... | collective-permute-start | bytes 1769480 | tf_op jit(solution)/shard_map/ppermute | solution.py:1014
  299.3 10.1 %collective-permute-start.36 = (bf16[2,96,768]{2,1,0:T(8,128)(2,1)S(1)}, bf16[2,96,768]{2,1,0:T(8,128)(2,1)S(1)}, u32[]{:S(2)}, u32[]{:S(2)}) collective-permute-start(bf16[2,96,768]{2,1,0:T(8,128)(2,1)S(1)} %slice_bitcast_fusion.2), channel_id=1, source_target_pairs={{0,8},{1,9},{2,10},{3,11},{4,12},{5,13},{6,14},{7,15},{8,0},{9,1},... | collective-permute-start | bytes 884744 | tf_op jit(solution)/shard_map/ppermute | solution.py:1014
  310.6 8.4 %collective-permute-start.39 = (bf16[56,768]{1,0:T(8,128)(2,1)S(1)}, bf16[56,768]{1,0:T(8,128)(2,1)S(1)}, u32[]{:S(2)}, u32[]{:S(2)}) collective-permute-start(bf16[56,768]{1,0:T(8,128)(2,1)S(1)} %add_add_fusion), channel_id=1, source_target_pairs={{0,24},{1,25},{2,26},{3,27},{4,28},{5,29},{6,30},{7,31},{8,16},{9,... | collective-permute-start | bytes 258056 | tf_op jit(solution)/shard_map/ppermute | solution.py:1014
  311.6 13.5 %collective-permute-start.38 = (bf16[56,768]{1,0:T(8,128)(2,1)S(1)}, bf16[56,768]{1,0:T(8,128)(2,1)S(1)}, u32[]{:S(2)}, u32[]{:S(2)}) collective-permute-start(bf16[56,768]{1,0:T(8,128)(2,1)S(1)} %add_add_fusion), channel_id=1, source_target_pairs={{0,16},{1,17},{2,18},{3,19},{4,20},{5,21},{6,22},{7,23},{8,24},{9,... | collective-permute-start | bytes 258056 | tf_op jit(solution)/shard_map/ppermute | solution.py:1014
  311.7 13.3 %collective-permute-start.37 = (bf16[56,768]{1,0:T(8,128)(2,1)S(1)}, bf16[56,768]{1,0:T(8,128)(2,1)S(1)}, u32[]{:S(2)}, u32[]{:S(2)}) collective-permute-start(bf16[56,768]{1,0:T(8,128)(2,1)S(1)} %add_add_fusion), channel_id=1, source_target_pairs={{0,8},{1,9},{2,10},{3,11},{4,12},{5,13},{6,14},{7,15},{8,0},{9,1},... | collective-permute-start | bytes 258056 | tf_op jit(solution)/shard_map/ppermute | solution.py:1014
  315.1 13.3 %collective-permute-start.40 = (bf16[2,96,768]{2,1,0:T(8,128)(2,1)S(1)}, bf16[2,96,768]{2,1,0:T(8,128)(2,1)S(1)}, u32[]{:S(2)}, u32[]{:S(2)}) collective-permute-start(bf16[2,96,768]{2,1,0:T(8,128)(2,1)S(1)} %slice.212), channel_id=1, source_target_pairs={{0,16},{1,17},{2,18},{3,19},{4,20},{5,21},{6,22},{7,23},{8,24},{9,... | collective-permute-start | bytes 884744 | tf_op jit(solution)/shard_map/ppermute | solution.py:1014
  318.0 10.5 %collective-permute-start.41 = (bf16[2,96,768]{2,1,0:T(8,128)(2,1)S(1)}, bf16[2,96,768]{2,1,0:T(8,128)(2,1)S(1)}, u32[]{:S(2)}, u32[]{:S(2)}) collective-permute-start(bf16[2,96,768]{2,1,0:T(8,128)(2,1)S(1)} %bitcast_add_fusion.refs_1_), channel_id=1, source_target_pairs={{0,2},{1,3},{2,0},{3,1},{4,6},{5,7},{6,4},{7,5},{8,10},{9,11},{10,... | collective-permute-start | bytes 884744 | tf_op jit(solution)/shard_map/ppermute | solution.py:1014
  328.5 12.3 %collective-permute-start.44 = (bf16[4,56,768]{2,1,0:T(8,128)(2,1)}, bf16[4,56,768]{2,1,0:T(8,128)(2,1)}, u32[]{:S(2)}, u32[]{:S(2)}) collective-permute-start(bf16[4,56,768]{2,1,0:T(8,128)(2,1)} %pad_maximum_fusion.5), channel_id=1, source_target_pairs={{0,6},{1,7},{2,4},{3,5},{4,2},{5,3},{6,0},{7,1},{8,14},{9,15},{10,... | collective-permute-start | bytes 1032200 | tf_op jit(solution)/shard_map/ppermute | solution.py:1014
  330.6 14.6 %collective-permute-start.43 = (bf16[4,56,768]{2,1,0:T(8,128)(2,1)}, bf16[4,56,768]{2,1,0:T(8,128)(2,1)}, u32[]{:S(2)}, u32[]{:S(2)}) collective-permute-start(bf16[4,56,768]{2,1,0:T(8,128)(2,1)} %pad_maximum_fusion.5), channel_id=1, source_target_pairs={{0,2},{1,3},{2,0},{3,1},{4,6},{5,7},{6,4},{7,5},{8,10},{9,11},{10,... | collective-permute-start | bytes 1032200 | tf_op jit(solution)/shard_map/ppermute | solution.py:1014
  331.3 13.9 %collective-permute-start.42 = (bf16[4,56,768]{2,1,0:T(8,128)(2,1)}, bf16[4,56,768]{2,1,0:T(8,128)(2,1)}, u32[]{:S(2)}, u32[]{:S(2)}) collective-permute-start(bf16[4,56,768]{2,1,0:T(8,128)(2,1)} %pad_maximum_fusion.5), channel_id=1, source_target_pairs={{0,4},{1,5},{2,6},{3,7},{4,0},{5,1},{6,2},{7,3},{8,12},{9,13},{10,... | collective-permute-start | bytes 1032200 | tf_op jit(solution)/shard_map/ppermute | solution.py:1014
  332.7 5.5 %collective-permute-start.45 = (bf16[96,768]{1,0:T(8,128)(2,1)}, bf16[96,768]{1,0:T(8,128)(2,1)}, u32[]{:S(2)}, u32[]{:S(2)}) collective-permute-start(bf16[96,768]{1,0:T(8,128)(2,1)} %slice_bitcast_fusion.7), channel_id=1, source_target_pairs={{0,8},{1,9},{2,10},{3,11},{4,12},{5,13},{6,14},{7,15},{8,0},{9,1},... | collective-permute-start | bytes 442376 | tf_op jit(solution)/shard_map/ppermute | solution.py:1014
  333.6 13.1 %collective-permute-start.46 = (bf16[2,2,96,768]{3,2,1,0:T(8,128)(2,1)}, bf16[2,2,96,768]{3,2,1,0:T(8,128)(2,1)S(1)}, u32[]{:S(2)}, u32[]{:S(2)}) collective-permute-start(bf16[2,2,96,768]{3,2,1,0:T(8,128)(2,1)} %pad_maximum_fusion.4), channel_id=1, source_target_pairs={{0,1},{1,0},{2,3},{3,2},{4,5},{5,4},{6,7},{7,6},{8,9},{9,8},{10,11... | collective-permute-start | bytes 1769480 | tf_op jit(solution)/shard_map/ppermute | solution.py:1014
  346.7 6.3 %collective-permute-start.47 = (bf16[16,56,768]{2,1,0:T(8,128)(2,1)S(1)}, bf16[16,56,768]{2,1,0:T(8,128)(2,1)S(1)}, u32[]{:S(2)}, u32[]{:S(2)}) collective-permute-start(bf16[16,56,768]{2,1,0:T(8,128)(2,1)S(1)} %pad_maximum_fusion.1.refs_1_), channel_id=1, source_target_pairs={{0,1},{1,0},{2,3},{3,2},{4,5},{5,4},{6,7},{7,6},{8,9},{9,8},{10,11... | collective-permute-start | bytes 4128776 | tf_op jit(solution)/shard_map/ppermute | solution.py:1014
  346.8 6.3 %collective-permute-start.48 = (bf16[96,768]{1,0:T(8,128)(2,1)S(1)}, bf16[96,768]{1,0:T(8,128)(2,1)S(1)}, u32[]{:S(2)}, u32[]{:S(2)}) collective-permute-start(bf16[96,768]{1,0:T(8,128)(2,1)S(1)} %bitcast_add_fusion.1.refs_1_), channel_id=1, source_target_pairs={{0,2},{1,3},{2,0},{3,1},{4,6},{5,7},{6,4},{7,5},{8,10},{9,11},{10,... | collective-permute-start | bytes 442376 | tf_op jit(solution)/shard_map/ppermute | solution.py:1014
  353.1 5.4 %collective-permute-start.49 = (bf16[2,96,768]{2,1,0:T(8,128)(2,1)S(1)}, bf16[2,96,768]{2,1,0:T(8,128)(2,1)S(1)}, u32[]{:S(2)}, u32[]{:S(2)}) collective-permute-start(bf16[2,96,768]{2,1,0:T(8,128)(2,1)S(1)} %pad_maximum_fusion.6), channel_id=1, source_target_pairs={{0,1},{1,0},{2,3},{3,2},{4,5},{5,4},{6,7},{7,6},{8,9},{9,8},{10,11... | collective-permute-start | bytes 884744 | tf_op jit(solution)/shard_map/ppermute | solution.py:1014
  (28 other events, 87.9 us)
Sparse Core Ops, SparseCore 0:
  10.8 49.4 all-gather.4
  63.0 46.8 all-gather.6

commit v5 on v4

--- a/solution.py
+++ b/solution.py
@@ -68,7 +68,7 @@
 
 
 def call(kernel, out_shape, deps=(), **kw):
-    limit = kw.pop("vmem", 20)
+    limit = kw.pop("vmem", 16)
     estimate = kw.pop("cost", None)
     in_specs = kw.pop("in_specs")
     count, more = len(in_specs), len(deps)

time: 374 us -> 374 us (level)
    unnamed x84 -> x76, local copies, waits for them, and re-layouts: 19.1 us -> 19 us
where the time goes in v5:
time: 374 us; the launch traced here: 367 us
  Pallas kernels  135 us (36%)
  waiting for transfers between devices  105 us (28%)
  starting transfers between devices  64.8 us (17%)
  local copies, waits for them, and re-layouts  32.8 us (9%)
  between operations  15.9 us (4%)
  other arithmetic  14.4 us (4%)
    pallas_call x24, Pallas kernels, call(): return lambda *args: built(*args, *deps)  135 us
    ppermute x50, waiting for transfers between devices, swap(): return lax.ppermute(value, AXES, pairs)  105 us
    ppermute x50, starting transfers between devices, swap(): return lax.ppermute(value, AXES, pairs)  54.3 us
    unnamed x76, local copies, waits for them, and re-layouts  19 us
  transfers between devices with their start and end apart: 54, of which 18 were waited for; matrix products, arithmetic and copies ran while one was open for 9% of the time, Pallas kernels for 34%

profile of v5, /device:TPU:0, one launch (start us, length us, event | category | flops | bytes accessed | tf_op | source)
XLA Modules:
  0.0 367.1 jit_solution(702693487618122153)
XLA Ops:
  7.2 1.7 constant_dynamic-slice_fusion
  9.0 1.7 constant_dynamic-update-slice_fusion.4
  10.7 4.0 %collective-permute-start.1 = (bf16[96,768]{1,0:T(8,128)(2,1)S(1)}, bf16[96,768]{1,0:T(8,128)(2,1)S(1)}, u32[]{:S(2)}, u32[]{:S(2)}) collective-permute-start(bf16[96,768]{1,0:T(8,128)(2,1)S(1)} %get-tuple-element.189), channel_id=1, source_target_pairs={{0,16},{1,17},{2,18},{3,19},{4,20},{5,21},{6,22},{7,23},{8,24},{9,... | collective-permute-start | bytes 442376 | tf_op jit(solution)/shard_map/ppermute | solution.py:1014
  14.8 1.6 collective-permute-start
  16.3 7.1 %collective-permute-done.1 = bf16[96,768]{1,0:T(8,128)(2,1)S(1)} collective-permute-done((bf16[96,768]{1,0:T(8,128)(2,1)S(1)}, bf16[96,768]{1,0:T(8,128)(2,1)S(1)}, u32[]{:S(2)}, u32[]{:S(2)}) %collective-permute-start.1) | collective-permute-done | bytes 147488 | tf_op jit(solution)/shard_map/ppermute | solution.py:1014
  23.4 2.8 collective-permute-done.2
  26.3 1.6 collective-permute-start.3
  30.8 4.0 %collective-permute-start.6 = (bf16[96,768]{1,0:T(8,128)(2,1)S(1)}, bf16[96,768]{1,0:T(8,128)(2,1)S(1)}, u32[]{:S(2)}, u32[]{:S(2)}) collective-permute-start(bf16[96,768]{1,0:T(8,128)(2,1)S(1)} %reshape.90), channel_id=1, source_target_pairs={{0,24},{1,25},{2,26},{3,27},{4,28},{5,29},{6,30},{7,31},{8,16},{9,... | collective-permute-start | bytes 442376 | tf_op jit(solution)/shard_map/ppermute | solution.py:1014
  34.8 4.7 %collective-permute-start.5 = (bf16[96,768]{1,0:T(8,128)(2,1)S(1)}, bf16[96,768]{1,0:T(8,128)(2,1)S(1)}, u32[]{:S(2)}, u32[]{:S(2)}) collective-permute-start(bf16[96,768]{1,0:T(8,128)(2,1)S(1)} %reshape.90), channel_id=1, source_target_pairs={{0,16},{1,17},{2,18},{3,19},{4,20},{5,21},{6,22},{7,23},{8,24},{9,... | collective-permute-start | bytes 442376 | tf_op jit(solution)/shard_map/ppermute | solution.py:1014
  43.3 12.6 %collective-permute-done.5 = bf16[96,768]{1,0:T(8,128)(2,1)S(1)} collective-permute-done((bf16[96,768]{1,0:T(8,128)(2,1)S(1)}, bf16[96,768]{1,0:T(8,128)(2,1)S(1)}, u32[]{:S(2)}, u32[]{:S(2)}) %collective-permute-start.5) | collective-permute-done | bytes 147488 | tf_op jit(solution)/shard_map/ppermute | solution.py:1014
  56.0 1.8 pad_maximum_fusion.3
  57.8 6.9 %all-to-all-start = ((bf16[8,96,768]{2,1,0:T(8,128)(2,1)}), bf16[8,96,768]{2,1,0:T(8,128)(2,1)S(1)}, u32[]{:S(2)}, u32[]{:S(2)}) async-start(bf16[8,96,768]{2,1,0:T(8,128)(2,1)} %param.20), calls=%async_computation | async-start | bytes 2359296 | tf_op jit(solution)/shard_map/all_to_all | solution.py:1106
  65.4 1.9 constant_dynamic-update-slice_fusion.refs_2_.refs_5_.refs_3_
  73.6 2.0 collective-permute-start.11
  75.6 1.6 constant_dynamic-update-slice_fusion.10
  78.5 15.0 %collective-permute-done.11 = bf16[4,96,768]{2,1,0:T(8,128)(2,1)S(1)} collective-permute-done((bf16[4,96,768]{2,1,0:T(8,128)(2,1)}, bf16[4,96,768]{2,1,0:T(8,128)(2,1)S(1)}, u32[]{:S(2)}, u32[]{:S(2)}) %collective-permute-start.11) | collective-permute-done | bytes 589856 | tf_op jit(solution)/shard_map/ppermute | solution.py:1014
  94.9 1.5 collective-permute-start.14
  99.0 1.7 shard_map.323
  100.7 1.5 copy-done.22
  102.2 6.1 %shard_map.324.refs_0_ = bf16[3,784,768]{2,1,0:T(8,128)(2,1)S(1)} custom-call(s32[2]{0:T(128)S(1)} %pad_add_fusion.refs_0_, bf16[784,768]{1,0:T(8,128)(2,1)S(1)} %get-tuple-element.101.refs_1_, bf16[8,96,768]{2,1,0:T(8,128)(2,1)} %constant_dynamic-update-slice_fusion.refs_2_.refs_5_.refs_3_, ...), custom_call_target="tpu_custom_call" | custom-call | flops 8049999872 | bytes 1048576 | tf_op jit(solution)/shard_map/pallas_call | solution.py:87
  108.3 15.3 %shard_map.325 = (bf16[784,768]{1,0:T(8,128)(2,1)S(1)}, f32[16,768]{1,0:T(8,128)S(1)}, f32[96,128]{1,0:T(8,128)S(1)}) custom-call(bf16[3,784,768]{2,1,0:T(8,128)(2,1)S(1)} %shard_map.324.refs_0_, s32[1,8]{1,0:T(1,128)S(1)} %copy-done.17, s32[1,1]{1,0:T(1,128)S(6)} %copy.56.refs_2_.refs_6_, s32[1,768]{1,0:T(1,128)S(1)} %copy-done.1, ...), custom_call_target="tpu_custom_call" | custom-call | flops 24149999616 | bytes 1048576 | tf_op jit(solution)/shard_map/pallas_call | solution.py:87
  123.6 1.8 copy-done.20
  126.5 1.7 copy-done.23
  129.5 3.7 %shard_map.326 = (f32[784,768]{1,0:T(8,128)S(1)}, bf16[784,768]{1,0:T(8,128)(2,1)S(1)}) custom-call(s32[2]{0:T(128)S(1)} %pad_add_fusion.refs_0_, bf16[784,768]{1,0:T(8,128)(2,1)S(1)} %copy-done.28, bf16[8,96,768]{2,1,0:T(8,128)(2,1)} %constant_dynamic-update-slice_fusion.refs_2_.refs_5_.refs_3_, ...), custom_call_target="tpu_custom_call" | custom-call | flops 7360000000 | bytes 1048576 | tf_op jit(solution)/shard_map/pallas_call | solution.py:87
  133.3 11.0 %shard_map.328 = (bf16[2,784,768]{2,1,0:T(8,128)(2,1)S(1)}, bf16[2,784,768]{2,1,0:T(8,128)(2,1)S(1)}, f32[784,768]{1,0:T(8,128)S(1)}, f32[784,768]{1,0:T(8,128)S(1)}, f32[4,768]{1,0:T(4,128)S(1)}) custom-call(s32[2]{0:T(128)S(1)} %pad_add_fusion.refs_0_, s32[1,8]{1,0:T(1,128)S(1)} %copy-done.17, s32[1,1]{1,0:T(1,128)S(6)} %copy.56.refs_2_.refs_6_, ...), custom_call_target="tpu_custom_call" | custom-call | flops 23000000512 | bytes 1048576 | tf_op jit(solution)/shard_map/pallas_call | solution.py:87
  145.1 3.2 shard_map.329.refs_14_
  148.4 14.9 %shard_map.330 = (bf16[2,784,768]{2,1,0:T(8,128)(2,1)S(1)}, bf16[2,784,768]{2,1,0:T(8,128)(2,1)S(1)}, f32[784,768]{1,0:T(8,128)S(1)}, f32[784,768]{1,0:T(8,128)S(1)}, f32[4,768]{1,0:T(4,128)S(1)}) custom-call(s32[2]{0:T(128)S(1)} %pad_add_fusion.refs_0_, s32[1,8]{1,0:T(1,128)S(1)} %copy-done.17, s32[1,1]{1,0:T(1,128)S(6)} %copy.56.refs_2_.refs_6_, ...), custom_call_target="tpu_custom_call" | custom-call | flops 23000000512 | bytes 1048576 | tf_op jit(solution)/shard_map/pallas_call | solution.py:87
  163.3 3.2 shard_map.331.refs_9_
  167.1 4.5 %shard_map.332 = (f32[784,768]{1,0:T(8,128)S(1)}, bf16[784,768]{1,0:T(8,128)(2,1)S(1)}, bf16[784,768]{1,0:T(8,128)(2,1)S(1)}, f32[2,768]{1,0:T(2,128)S(1)}) custom-call(s32[2]{0:T(128)S(1)} %pad_add_fusion.refs_0_, f32[784,768]{1,0:T(8,128)S(1)} %get-tuple-element.117.refs_1_, f32[784,768]{1,0:T(8,128)S(1)} %get-tuple-element.108.refs_7_.refs_8_.refs_2_, ...), custom_call_target="tpu_custom_call" | custom-call | flops 9774999552 | bytes 1048576 | tf_op jit(solution)/shard_map/pallas_call | solution.py:87
  171.6 3.3 shard_map.333
  174.9 5.1 %shard_map.334 = (bf16[2,4,96,768]{3,2,1,0:T(8,128)(2,1)S(1)}, bf16[2,4,96,768]{3,2,1,0:T(8,128)(2,1)S(1)}) custom-call(s32[2]{0:T(128)S(1)} %pad_add_fusion.refs_0_, bf16[784,768]{1,0:T(8,128)(2,1)S(1)} %get-tuple-element.106.refs_3_.refs_1_, bf16[2,784,768]{2,1,0:T(8,128)(2,1)S(1)} %get-tuple-element.116.refs_3_.refs_2_, ...), custom_call_target="tpu_custom_call" | custom-call | flops 9200000000 | bytes 1048576 | tf_op jit(solution)/shard_map/pallas_call | solution.py:87
  181.2 13.0 %shard_map.335.refs_3_.refs_1_ = bf16[3,784,384]{2,1,0:T(8,128)(2,1)S(1)} custom-call(bf16[3,784,768]{2,1,0:T(8,128)(2,1)S(1)} %copy-done.21, bf16[784,768]{1,0:T(8,128)(2,1)S(1)} %copy-done.29, bf16[784,768]{1,0:T(8,128)(2,1)S(1)} %get-tuple-element.120.refs_2_, f32[16,768]{1,0:T(8,128)S(1)} %get-tuple-element.121.refs_3_, ...), custom_call_target="tpu_custom_call" | custom-call | flops 17250000896 | bytes 1048576 | tf_op jit(solution)/shard_map/pallas_call | solution.py:87
  194.2 3.3 shard_map.336.refs_9_
  197.6 13.0 %shard_map.337.refs_3_.refs_2_ = bf16[3,784,384]{2,1,0:T(8,128)(2,1)S(1)} custom-call(bf16[3,784,768]{2,1,0:T(8,128)(2,1)S(1)} %copy-done.21, bf16[784,768]{1,0:T(8,128)(2,1)S(1)} %copy-done.29, bf16[784,768]{1,0:T(8,128)(2,1)S(1)} %get-tuple-element.120.refs_2_, f32[16,768]{1,0:T(8,128)S(1)} %get-tuple-element.121.refs_3_, ...), custom_call_target="tpu_custom_call" | custom-call | flops 17250000896 | bytes 1048576 | tf_op jit(solution)/shard_map/pallas_call | solution.py:87
  210.6 3.5 shard_map.338.refs_6_
  216.1 1.9 collective-permute-start.24
  217.9 3.2 shard_map.339
  221.1 9.0 %collective-permute-done.22 = bf16[4,96,768]{2,1,0:T(8,128)(2,1)S(1)} collective-permute-done((bf16[4,96,768]{2,1,0:T(8,128)(2,1)S(1)}, bf16[4,96,768]{2,1,0:T(8,128)(2,1)S(1)}, u32[]{:S(2)}, u32[]{:S(2)}) %collective-permute-start.22) | collective-permute-done | bytes 589856 | tf_op jit(solution)/shard_map/ppermute | solution.py:1014
  231.4 3.3 collective-permute-start.28
  234.8 3.2 shard_map.340
  238.5 7.5 %shard_map.341 = (bf16[768,768]{1,0:T(8,128)(2,1)}, f32[8,768]{1,0:T(8,128)S(1)}, f32[2,768]{1,0:T(2,128)S(1)}) custom-call(s32[2]{0:T(128)S(1)} %pad_add_fusion.refs_0_, bf16[3,784,384]{2,1,0:T(8,128)(2,1)S(1)} %shard_map.335.refs_3_.refs_1_, bf16[3,784,384]{2,1,0:T(8,128)(2,1)S(1)} %shard_map.337.refs_3_.refs_2_, ...), custom_call_target="tpu_custom_call" | custom-call | flops 11500000256 | bytes 1048576 | tf_op jit(solution)/shard_map/pallas_call | solution.py:87
  246.0 4.7 %shard_map.342 = (bf16[8,56,768]{2,1,0:T(8,128)(2,1)S(1)}, bf16[8,56,768]{2,1,0:T(8,128)(2,1)S(1)}, bf16[8,56,768]{2,1,0:T(8,128)(2,1)S(1)}, bf16[8,56,768]{2,1,0:T(8,128)(2,1)S(1)}) custom-call(s32[2]{0:T(128)S(1)} %pad_add_fusion.refs_0_, bf16[768,768]{1,0:T(8,128)(2,1)S(1)} %bitcast.94, bf16[768,768]{1,0:T(8,128)(2,1)} %get-tuple-element.134.refs_2_, ...), custom_call_target="tpu_custom_call" | custom-call | flops 6899999744 | bytes 1048576 | tf_op jit(solution)/shard_map/pallas_call | solution.py:87
  251.5 8.4 %collective-permute-done.28 = bf16[2,2,96,768]{3,2,1,0:T(8,128)(2,1)S(1)} collective-permute-done((bf16[2,2,96,768]{3,2,1,0:T(8,128)(2,1)S(1)}, bf16[2,2,96,768]{3,2,1,0:T(8,128)(2,1)S(1)}, u32[]{:S(2)}, u32[]{:S(2)}) %collective-permute-start.28) | collective-permute-done | bytes 589856 | tf_op jit(solution)/shard_map/ppermute | solution.py:1014
  261.7 3.0 collective-permute-done.27
  265.8 1.5 collective-permute-start.29
  269.3 3.6 all-to-all-start.1
  272.9 17.9 %collective-permute-done.29 = bf16[4,56,768]{2,1,0:T(8,128)(2,1)S(1)} collective-permute-done((bf16[4,56,768]{2,1,0:T(8,128)(2,1)}, bf16[4,56,768]{2,1,0:T(8,128)(2,1)S(1)}, u32[]{:S(2)}, u32[]{:S(2)}) %collective-permute-start.29) | collective-permute-done | bytes 344096 | tf_op jit(solution)/shard_map/ppermute | solution.py:1014
  290.8 1.9 fusion.15
  292.7 4.4 %collective-permute-start.34 = (bf16[56,768]{1,0:T(8,128)(2,1)}, bf16[56,768]{1,0:T(8,128)(2,1)S(1)}, u32[]{:S(2)}, u32[]{:S(2)}) collective-permute-start(bf16[56,768]{1,0:T(8,128)(2,1)} %get-tuple-element.155), channel_id=1, source_target_pairs={{0,24},{1,25},{2,26},{3,27},{4,28},{5,29},{6,30},{7,31},{8,16},{9,... | collective-permute-start | bytes 258056 | tf_op jit(solution)/shard_map/ppermute | solution.py:1014
  297.1 1.9 collective-permute-start.35
  299.7 6.1 %collective-permute-done.33 = bf16[56,768]{1,0:T(8,128)(2,1)S(1)} collective-permute-done((bf16[56,768]{1,0:T(8,128)(2,1)}, bf16[56,768]{1,0:T(8,128)(2,1)S(1)}, u32[]{:S(2)}, u32[]{:S(2)}) %collective-permute-start.33) | collective-permute-done | bytes 86048 | tf_op jit(solution)/shard_map/ppermute | solution.py:1014
  305.8 3.3 collective-permute-done.36
  311.5 3.3 collective-permute-start.37
  314.9 2.8 fusion
  318.8 6.0 %collective-permute-done.38 = bf16[56,768]{1,0:T(8,128)(2,1)S(1)} collective-permute-done((bf16[56,768]{1,0:T(8,128)(2,1)S(1)}, bf16[56,768]{1,0:T(8,128)(2,1)S(1)}, u32[]{:S(2)}, u32[]{:S(2)}) %collective-permute-start.38) | collective-permute-done | bytes 86048 | tf_op jit(solution)/shard_map/ppermute | solution.py:1014
  325.5 2.6 collective-permute-done.40
  328.2 2.1 collective-permute-start.44
  334.7 2.5 shard_map.343
  338.8 1.7 collective-permute-done.44
  340.5 4.4 %collective-permute-done.43 = bf16[4,56,768]{2,1,0:T(8,128)(2,1)} collective-permute-done((bf16[4,56,768]{2,1,0:T(8,128)(2,1)}, bf16[4,56,768]{2,1,0:T(8,128)(2,1)}, u32[]{:S(2)}, u32[]{:S(2)}) %collective-permute-start.43) | collective-permute-done | bytes 344096 | tf_op jit(solution)/shard_map/ppermute | solution.py:1014
  347.9 2.4 shard_map.344
  350.3 2.5 collective-permute-done.48.refs_2_
  352.9 3.3 shard_map.345
  358.2 1.6 shard_map.346
  (194 shorter events, 48.8 us)
Async XLA Ops:
  7.2 87.2 %all-gather.5.cloned.1.call-start = ((), (), s32[]{:S(2)}) async-start(), calls=%async_computation.2 | async-start | bytes 1327104 | tf_op jit(solution)/shard_map/all_gather | solution.py:1115
  9.0 19.6 %copy-start.32 = (bf16[96,3072]{1,0:T(8,128)(2,1)S(1)}, bf16[96,3072]{1,0:T(8,128)(2,1)}, u32[]{:S(2)}) copy-start(bf16[96,3072]{1,0:T(8,128)(2,1)} %param.35) | copy-start | bytes 1769476
  9.0 117.5 %all-gather.7.cloned.1.call-start = ((), (), s32[]{:S(2)}) async-start(), calls=%async_computation.3 | async-start | bytes 1327104 | tf_op jit(solution)/shard_map/all_gather | solution.py:1117
  10.7 12.7 %collective-permute-start.1 = (bf16[96,768]{1,0:T(8,128)(2,1)S(1)}, bf16[96,768]{1,0:T(8,128)(2,1)S(1)}, u32[]{:S(2)}, u32[]{:S(2)}) collective-permute-start(bf16[96,768]{1,0:T(8,128)(2,1)S(1)} %get-tuple-element.189), channel_id=1, source_target_pairs={{0,16},{1,17},{2,18},{3,19},{4,20},{5,21},{6,22},{7,23},{8,24},{9,... | collective-permute-start | bytes 442376 | tf_op jit(solution)/shard_map/ppermute | solution.py:1014
  14.8 8.7 %collective-permute-start = (bf16[96,768]{1,0:T(8,128)(2,1)S(1)}, bf16[96,768]{1,0:T(8,128)(2,1)S(1)}, u32[]{:S(2)}, u32[]{:S(2)}) collective-permute-start(bf16[96,768]{1,0:T(8,128)(2,1)S(1)} %get-tuple-element.189), channel_id=1, source_target_pairs={{0,8},{1,9},{2,10},{3,11},{4,12},{5,13},{6,14},{7,15},{8,0},{9,1},... | collective-permute-start | bytes 442376 | tf_op jit(solution)/shard_map/ppermute | solution.py:1014
  16.3 9.9 %collective-permute-start.2 = (bf16[96,768]{1,0:T(8,128)(2,1)S(1)}, bf16[96,768]{1,0:T(8,128)(2,1)S(1)}, u32[]{:S(2)}, u32[]{:S(2)}) collective-permute-start(bf16[96,768]{1,0:T(8,128)(2,1)S(1)} %get-tuple-element.189), channel_id=1, source_target_pairs={{0,24},{1,25},{2,26},{3,27},{4,28},{5,29},{6,30},{7,31},{8,16},{9,... | collective-permute-start | bytes 442376 | tf_op jit(solution)/shard_map/ppermute | solution.py:1014
  26.3 16.4 %collective-permute-start.3 = (bf16[4,96,768]{2,1,0:T(8,128)(2,1)S(1)}, bf16[4,96,768]{2,1,0:T(8,128)(2,1)}, u32[]{:S(2)}, u32[]{:S(2)}) collective-permute-start(bf16[4,96,768]{2,1,0:T(8,128)(2,1)S(1)} %pad_maximum_fusion.2), channel_id=1, source_target_pairs={{0,4},{1,5},{2,6},{3,7},{4,0},{5,1},{6,2},{7,3},{8,12},{9,13},{10,... | collective-permute-start | bytes 1769480 | tf_op jit(solution)/shard_map/ppermute | solution.py:1014
  30.8 12.5 %collective-permute-start.6 = (bf16[96,768]{1,0:T(8,128)(2,1)S(1)}, bf16[96,768]{1,0:T(8,128)(2,1)S(1)}, u32[]{:S(2)}, u32[]{:S(2)}) collective-permute-start(bf16[96,768]{1,0:T(8,128)(2,1)S(1)} %reshape.90), channel_id=1, source_target_pairs={{0,24},{1,25},{2,26},{3,27},{4,28},{5,29},{6,30},{7,31},{8,16},{9,... | collective-permute-start | bytes 442376 | tf_op jit(solution)/shard_map/ppermute | solution.py:1014
  34.8 21.2 %collective-permute-start.5 = (bf16[96,768]{1,0:T(8,128)(2,1)S(1)}, bf16[96,768]{1,0:T(8,128)(2,1)S(1)}, u32[]{:S(2)}, u32[]{:S(2)}) collective-permute-start(bf16[96,768]{1,0:T(8,128)(2,1)S(1)} %reshape.90), channel_id=1, source_target_pairs={{0,16},{1,17},{2,18},{3,19},{4,20},{5,21},{6,22},{7,23},{8,24},{9,... | collective-permute-start | bytes 442376 | tf_op jit(solution)/shard_map/ppermute | solution.py:1014
  39.5 16.5 %collective-permute-start.4 = (bf16[96,768]{1,0:T(8,128)(2,1)S(1)}, bf16[96,768]{1,0:T(8,128)(2,1)}, u32[]{:S(2)}, u32[]{:S(2)}) collective-permute-start(bf16[96,768]{1,0:T(8,128)(2,1)S(1)} %reshape.90), channel_id=1, source_target_pairs={{0,8},{1,9},{2,10},{3,11},{4,12},{5,13},{6,14},{7,15},{8,0},{9,1},... | collective-permute-start | bytes 442376 | tf_op jit(solution)/shard_map/ppermute | solution.py:1014
  40.0 27.3 %collective-permute-start.8 = (bf16[4,96,768]{2,1,0:T(8,128)(2,1)S(1)}, bf16[4,96,768]{2,1,0:T(8,128)(2,1)}, u32[]{:S(2)}, u32[]{:S(2)}) collective-permute-start(bf16[4,96,768]{2,1,0:T(8,128)(2,1)S(1)} %pad_maximum_fusion.2), channel_id=1, source_target_pairs={{0,2},{1,3},{2,0},{3,1},{4,6},{5,7},{6,4},{7,5},{8,10},{9,11},{10,... | collective-permute-start | bytes 1769480 | tf_op jit(solution)/shard_map/ppermute | solution.py:1014
  42.7 25.8 %collective-permute-start.9 = (bf16[4,96,768]{2,1,0:T(8,128)(2,1)}, bf16[4,96,768]{2,1,0:T(8,128)(2,1)}, u32[]{:S(2)}, u32[]{:S(2)}) collective-permute-start(bf16[4,96,768]{2,1,0:T(8,128)(2,1)} %collective-permute-done.3), channel_id=1, source_target_pairs={{0,2},{1,3},{2,0},{3,1},{4,6},{5,7},{6,4},{7,5},{8,10},{9,11},{10,... | collective-permute-start | bytes 1769480 | tf_op jit(solution)/shard_map/ppermute | solution.py:1014
  57.8 38.6 %all-to-all-start = ((bf16[8,96,768]{2,1,0:T(8,128)(2,1)}), bf16[8,96,768]{2,1,0:T(8,128)(2,1)S(1)}, u32[]{:S(2)}, u32[]{:S(2)}) async-start(bf16[8,96,768]{2,1,0:T(8,128)(2,1)} %param.20), calls=%async_computation | async-start | bytes 2359296 | tf_op jit(solution)/shard_map/all_to_all | solution.py:1106
  67.3 27.6 %collective-permute-start.7 = (bf16[8,96,768]{2,1,0:T(8,128)(2,1)}, bf16[8,96,768]{2,1,0:T(8,128)(2,1)}, u32[]{:S(2)}, u32[]{:S(2)}) collective-permute-start(bf16[8,96,768]{2,1,0:T(8,128)(2,1)} %constant_dynamic-update-slice_fusion.refs_2_.refs_5_.refs_3_), channel_id=1, source_target_pairs={{0,1},{1,0},{2,3},{3,2},{4,5},{5,4},{6,7},{7,6},{8,9},{9,8},{10,11... | collective-permute-start | bytes 3538952 | tf_op jit(solution)/shard_map/ppermute | solution.py:1014
  69.6 25.3 %collective-permute-start.10 = (bf16[8,96,768]{2,1,0:T(8,128)(2,1)S(1)}, bf16[8,96,768]{2,1,0:T(8,128)(2,1)}, u32[]{:S(2)}, u32[]{:S(2)}) collective-permute-start(bf16[8,96,768]{2,1,0:T(8,128)(2,1)S(1)} %constant_dynamic-update-slice_fusion.5.refs_4_.refs_7_.refs_5_), channel_id=1, source_target_pairs={{0,1},{1,0},{2,3},{3,2},{4,5},{5,4},{6,7},{7,6},{8,9},{9,8},{10,11... | collective-permute-start | bytes 3538952 | tf_op jit(solution)/shard_map/ppermute | solution.py:1014
  72.9 23.5 %copy-start.9 = (f32[8,768]{1,0:T(8,128)S(1)}, f32[8,768]{1,0:T(8,128)}, u32[]{:S(2)}) copy-start(f32[8,768]{1,0:T(8,128)} %refs_5_.3) | copy-start | bytes 73732
  72.9 23.5 %copy-start.10 = (f32[768]{0:T(1024)S(1)}, f32[768]{0:T(1024)}, u32[]{:S(2)}) copy-start(f32[768]{0:T(1024)} %refs_2_.6) | copy-start | bytes 9220
  72.9 23.5 %copy-start.11 = (f32[768]{0:T(1024)S(1)}, f32[768]{0:T(1024)}, u32[]{:S(2)}) copy-start(f32[768]{0:T(1024)} %refs_4_.2) | copy-start | bytes 9220
  72.9 23.5 %copy-start.12 = (f32[768]{0:T(1024)S(1)}, f32[768]{0:T(1024)}, u32[]{:S(2)}) copy-start(f32[768]{0:T(1024)} %refs_7_.4) | copy-start | bytes 9220
  72.9 23.5 %copy-start.16 = (f32[768]{0:T(1024)S(1)}, f32[768]{0:T(1024)}, u32[]{:S(2)}) copy-start(f32[768]{0:T(1024)} %refs_8_.3) | copy-start | bytes 9220
  73.6 19.9 %collective-permute-start.11 = (bf16[4,96,768]{2,1,0:T(8,128)(2,1)}, bf16[4,96,768]{2,1,0:T(8,128)(2,1)S(1)}, u32[]{:S(2)}, u32[]{:S(2)}) collective-permute-start(bf16[4,96,768]{2,1,0:T(8,128)(2,1)} %pad_maximum_fusion.3), channel_id=1, source_target_pairs={{0,4},{1,5},{2,6},{3,7},{4,0},{5,1},{6,2},{7,3},{8,12},{9,13},{10,... | collective-permute-start | bytes 1769480 | tf_op jit(solution)/shard_map/ppermute | solution.py:1014
  94.3 38.9 %collective-permute-start.13 = (bf16[8,96,768]{2,1,0:T(8,128)(2,1)}, bf16[8,96,768]{2,1,0:T(8,128)(2,1)}, u32[]{:S(2)}, u32[]{:S(2)}) collective-permute-start(bf16[8,96,768]{2,1,0:T(8,128)(2,1)} %constant_dynamic-update-slice_fusion.7.refs_9_.refs_10_), channel_id=1, source_target_pairs={{0,1},{1,0},{2,3},{3,2},{4,5},{5,4},{6,7},{7,6},{8,9},{9,8},{10,11... | collective-permute-start | bytes 3538952 | tf_op jit(solution)/shard_map/ppermute | solution.py:1014
  94.4 32.1 %collective-permute-start.12 = (bf16[8,96,768]{2,1,0:T(8,128)(2,1)}, bf16[8,96,768]{2,1,0:T(8,128)(2,1)}, u32[]{:S(2)}, u32[]{:S(2)}) collective-permute-start(bf16[8,96,768]{2,1,0:T(8,128)(2,1)} %bitcast.102), channel_id=1, source_target_pairs={{0,1},{1,0},{2,3},{3,2},{4,5},{5,4},{6,7},{7,6},{8,9},{9,8},{10,11... | collective-permute-start | bytes 3538952 | tf_op jit(solution)/shard_map/ppermute | solution.py:1014
  94.9 49.4 %collective-permute-start.14 = (bf16[8,96,768]{2,1,0:T(8,128)(2,1)}, bf16[8,96,768]{2,1,0:T(8,128)(2,1)}, u32[]{:S(2)}, u32[]{:S(2)}) collective-permute-start(bf16[8,96,768]{2,1,0:T(8,128)(2,1)} %constant_dynamic-update-slice_fusion.7.refs_9_.refs_10_), channel_id=1, source_target_pairs={{0,2},{1,3},{2,0},{3,1},{4,6},{5,7},{6,4},{7,5},{8,10},{9,11},{10,... | collective-permute-start | bytes 3538952 | tf_op jit(solution)/shard_map/ppermute | solution.py:1014
  108.3 18.2 %copy-start.13 = (f32[768]{0:T(1024)S(1)}, f32[768]{0:T(1024)}, u32[]{:S(2)}) copy-start(f32[768]{0:T(1024)} %refs_8_.2) | copy-start | bytes 9220
  108.3 18.2 %copy-start.15 = (f32[768]{0:T(1024)S(1)}, f32[768]{0:T(1024)}, u32[]{:S(2)}) copy-start(f32[768]{0:T(1024)} %refs_4_.3) | copy-start | bytes 9220
  126.5 21.9 %collective-permute-start.16 = (bf16[8,96,768]{2,1,0:T(8,128)(2,1)}, bf16[8,96,768]{2,1,0:T(8,128)(2,1)S(1)}, u32[]{:S(2)}, u32[]{:S(2)}) collective-permute-start(bf16[8,96,768]{2,1,0:T(8,128)(2,1)} %bitcast.104), channel_id=1, source_target_pairs={{0,1},{1,0},{2,3},{3,2},{4,5},{5,4},{6,7},{7,6},{8,9},{9,8},{10,11... | collective-permute-start | bytes 3538952 | tf_op jit(solution)/shard_map/ppermute | solution.py:1014
  144.3 4.1 %collective-permute-start.15 = (bf16[8,96,768]{2,1,0:T(8,128)(2,1)}, bf16[8,96,768]{2,1,0:T(8,128)(2,1)S(1)}, u32[]{:S(2)}, u32[]{:S(2)}) collective-permute-start(bf16[8,96,768]{2,1,0:T(8,128)(2,1)} %collective-permute-done.14.refs_10_), channel_id=1, source_target_pairs={{0,1},{1,0},{2,3},{3,2},{4,5},{5,4},{6,7},{7,6},{8,9},{9,8},{10,11... | collective-permute-start | bytes 3538952 | tf_op jit(solution)/shard_map/ppermute | solution.py:1014
  148.3 23.2 %collective-permute-start.17 = (bf16[2,8,96,768]{3,2,1,0:T(8,128)(2,1)S(1)}, bf16[2,8,96,768]{3,2,1,0:T(8,128)(2,1)S(1)}, u32[]{:S(2)}, u32[]{:S(2)}) collective-permute-start(bf16[2,8,96,768]{3,2,1,0:T(8,128)(2,1)S(1)} %shard_map.329.refs_14_), channel_id=1, source_target_pairs={{0,1},{1,0},{2,3},{3,2},{4,5},{5,4},{6,7},{7,6},{8,9},{9,8},{10,11... | collective-permute-start | bytes 7077896 | tf_op jit(solution)/shard_map/ppermute | solution.py:1014
  166.6 5.0 %collective-permute-start.18 = (bf16[2,8,96,768]{3,2,1,0:T(8,128)(2,1)S(1)}, bf16[2,8,96,768]{3,2,1,0:T(8,128)(2,1)S(1)}, u32[]{:S(2)}, u32[]{:S(2)}) collective-permute-start(bf16[2,8,96,768]{3,2,1,0:T(8,128)(2,1)S(1)} %shard_map.331.refs_9_), channel_id=1, source_target_pairs={{0,1},{1,0},{2,3},{3,2},{4,5},{5,4},{6,7},{7,6},{8,9},{9,8},{10,11... | collective-permute-start | bytes 7077896 | tf_op jit(solution)/shard_map/ppermute | solution.py:1014
  180.0 34.7 %collective-permute-start.21 = (bf16[2,4,96,768]{3,2,1,0:T(8,128)(2,1)S(1)}, bf16[2,4,96,768]{3,2,1,0:T(8,128)(2,1)S(1)}, u32[]{:S(2)}, u32[]{:S(2)}) collective-permute-start(bf16[2,4,96,768]{3,2,1,0:T(8,128)(2,1)S(1)} %get-tuple-element.129), channel_id=1, source_target_pairs={{0,4},{1,5},{2,6},{3,7},{4,0},{5,1},{6,2},{7,3},{8,12},{9,13},{10,... | collective-permute-start | bytes 3538952 | tf_op jit(solution)/shard_map/ppermute | solution.py:1014
  180.3 34.4 %collective-permute-start.23 = (bf16[2,4,96,768]{3,2,1,0:T(8,128)(2,1)S(1)}, bf16[2,4,96,768]{3,2,1,0:T(8,128)(2,1)S(1)}, u32[]{:S(2)}, u32[]{:S(2)}) collective-permute-start(bf16[2,4,96,768]{3,2,1,0:T(8,128)(2,1)S(1)} %get-tuple-element.131), channel_id=1, source_target_pairs={{0,2},{1,3},{2,0},{3,1},{4,6},{5,7},{6,4},{7,5},{8,10},{9,11},{10,... | collective-permute-start | bytes 3538952 | tf_op jit(solution)/shard_map/ppermute | solution.py:1014
  181.2 13.1 %copy-start.26 = (bf16[784,768]{1,0:T(8,128)(2,1)S(1)}, bf16[784,768]{1,0:T(8,128)(2,1)}, u32[]{:S(2)}) copy-start(bf16[784,768]{1,0:T(8,128)(2,1)} %copy-done.25) | copy-start | bytes 3612676
  197.5 20.4 %collective-permute-start.20 = (bf16[2,8,96,384]{3,2,1,0:T(8,128)(2,1)S(1)}, bf16[2,8,96,384]{3,2,1,0:T(8,128)(2,1)S(1)}, u32[]{:S(2)}, u32[]{:S(2)}) collective-permute-start(bf16[2,8,96,384]{3,2,1,0:T(8,128)(2,1)S(1)} %shard_map.336.refs_9_), channel_id=1, source_target_pairs={{0,1},{1,0},{2,3},{3,2},{4,5},{5,4},{6,7},{7,6},{8,9},{9,8},{10,11... | collective-permute-start | bytes 3538952 | tf_op jit(solution)/shard_map/ppermute | solution.py:1014
  214.1 20.7 %collective-permute-start.19 = (bf16[2,8,96,384]{3,2,1,0:T(8,128)(2,1)S(1)}, bf16[2,8,96,384]{3,2,1,0:T(8,128)(2,1)S(1)}, u32[]{:S(2)}, u32[]{:S(2)}) collective-permute-start(bf16[2,8,96,384]{3,2,1,0:T(8,128)(2,1)S(1)} %shard_map.338.refs_6_), channel_id=1, source_target_pairs={{0,1},{1,0},{2,3},{3,2},{4,5},{5,4},{6,7},{7,6},{8,9},{9,8},{10,11... | collective-permute-start | bytes 3538952 | tf_op jit(solution)/shard_map/ppermute | solution.py:1014
  214.8 15.3 %collective-permute-start.22 = (bf16[4,96,768]{2,1,0:T(8,128)(2,1)S(1)}, bf16[4,96,768]{2,1,0:T(8,128)(2,1)S(1)}, u32[]{:S(2)}, u32[]{:S(2)}) collective-permute-start(bf16[4,96,768]{2,1,0:T(8,128)(2,1)S(1)} %fusion.10), channel_id=1, source_target_pairs={{0,2},{1,3},{2,0},{3,1},{4,6},{5,7},{6,4},{7,5},{8,10},{9,11},{10,... | collective-permute-start | bytes 1769480 | tf_op jit(solution)/shard_map/ppermute | solution.py:1014
  216.1 15.1 %collective-permute-start.24 = (bf16[4,96,768]{2,1,0:T(8,128)(2,1)S(1)}, bf16[4,96,768]{2,1,0:T(8,128)(2,1)S(1)}, u32[]{:S(2)}, u32[]{:S(2)}) collective-permute-start(bf16[4,96,768]{2,1,0:T(8,128)(2,1)S(1)} %fusion.6), channel_id=1, source_target_pairs={{0,4},{1,5},{2,6},{3,7},{4,0},{5,1},{6,2},{7,3},{8,12},{9,13},{10,... | collective-permute-start | bytes 1769480 | tf_op jit(solution)/shard_map/ppermute | solution.py:1014
  231.4 28.6 %collective-permute-start.28 = (bf16[2,2,96,768]{3,2,1,0:T(8,128)(2,1)S(1)}, bf16[2,2,96,768]{3,2,1,0:T(8,128)(2,1)S(1)}, u32[]{:S(2)}, u32[]{:S(2)}) collective-permute-start(bf16[2,2,96,768]{3,2,1,0:T(8,128)(2,1)S(1)} %fusion.3), channel_id=1, source_target_pairs={{0,16},{1,17},{2,18},{3,19},{4,20},{5,21},{6,22},{7,23},{8,24},{9,... | collective-permute-start | bytes 1769480 | tf_op jit(solution)/shard_map/ppermute | solution.py:1014
  238.1 26.7 %collective-permute-start.27 = (bf16[2,4,96,768]{3,2,1,0:T(8,128)(2,1)S(1)}, bf16[2,4,96,768]{3,2,1,0:T(8,128)(2,1)S(1)}, u32[]{:S(2)}, u32[]{:S(2)}) collective-permute-start(bf16[2,4,96,768]{3,2,1,0:T(8,128)(2,1)S(1)} %get-tuple-element.144), channel_id=1, source_target_pairs={{0,2},{1,3},{2,0},{3,1},{4,6},{5,7},{6,4},{7,5},{8,10},{9,11},{10,... | collective-permute-start | bytes 3538952 | tf_op jit(solution)/shard_map/ppermute | solution.py:1014
  250.7 9.3 %collective-permute-start.25 = (bf16[8,56,768]{2,1,0:T(8,128)(2,1)S(1)}, bf16[8,56,768]{2,1,0:T(8,128)(2,1)S(1)}, u32[]{:S(2)}, u32[]{:S(2)}) collective-permute-start(bf16[8,56,768]{2,1,0:T(8,128)(2,1)S(1)} %get-tuple-element.141), channel_id=1, source_target_pairs={{0,1},{1,0},{2,3},{3,2},{4,5},{5,4},{6,7},{7,6},{8,9},{9,8},{10,11... | collective-permute-start | bytes 2064392 | tf_op jit(solution)/shard_map/ppermute | solution.py:1014
  250.9 10.0 %collective-permute-start.26 = (bf16[8,56,768]{2,1,0:T(8,128)(2,1)S(1)}, bf16[8,56,768]{2,1,0:T(8,128)(2,1)S(1)}, u32[]{:S(2)}, u32[]{:S(2)}) collective-permute-start(bf16[8,56,768]{2,1,0:T(8,128)(2,1)S(1)} %get-tuple-element.143), channel_id=1, source_target_pairs={{0,1},{1,0},{2,3},{3,2},{4,5},{5,4},{6,7},{7,6},{8,9},{9,8},{10,11... | collective-permute-start | bytes 2064392 | tf_op jit(solution)/shard_map/ppermute | solution.py:1014
  265.8 24.9 %collective-permute-start.29 = (bf16[4,56,768]{2,1,0:T(8,128)(2,1)}, bf16[4,56,768]{2,1,0:T(8,128)(2,1)S(1)}, u32[]{:S(2)}, u32[]{:S(2)}) collective-permute-start(bf16[4,56,768]{2,1,0:T(8,128)(2,1)} %get-tuple-element.146), channel_id=1, source_target_pairs={{0,4},{1,5},{2,6},{3,7},{4,0},{5,1},{6,2},{7,3},{8,12},{9,13},{10,... | collective-permute-start | bytes 1032200 | tf_op jit(solution)/shard_map/ppermute | solution.py:1014
  267.4 23.4 %collective-permute-start.30 = (bf16[4,56,768]{2,1,0:T(8,128)(2,1)}, bf16[4,56,768]{2,1,0:T(8,128)(2,1)}, u32[]{:S(2)}, u32[]{:S(2)}) collective-permute-start(bf16[4,56,768]{2,1,0:T(8,128)(2,1)} %get-tuple-element.147), channel_id=1, source_target_pairs={{0,2},{1,3},{2,0},{3,1},{4,6},{5,7},{6,4},{7,5},{8,10},{9,11},{10,... | collective-permute-start | bytes 1032200 | tf_op jit(solution)/shard_map/ppermute | solution.py:1014
  268.1 22.7 %collective-permute-start.31 = (bf16[4,56,768]{2,1,0:T(8,128)(2,1)}, bf16[4,56,768]{2,1,0:T(8,128)(2,1)}, u32[]{:S(2)}, u32[]{:S(2)}) collective-permute-start(bf16[4,56,768]{2,1,0:T(8,128)(2,1)} %get-tuple-element.148), channel_id=1, source_target_pairs={{0,6},{1,7},{2,4},{3,5},{4,2},{5,3},{6,0},{7,1},{8,14},{9,15},{10,... | collective-permute-start | bytes 1032200 | tf_op jit(solution)/shard_map/ppermute | solution.py:1014
  269.3 64.0 %all-to-all-start.1 = ((bf16[8,96,768]{2,1,0:T(8,128)(2,1)}), bf16[8,96,768]{2,1,0:T(8,128)(2,1)S(1)}, u32[]{:S(2)}, u32[]{:S(2)}) async-start(bf16[8,96,768]{2,1,0:T(8,128)(2,1)} %bitcast.44), calls=%async_computation.1 | async-start | bytes 2359296 | tf_op jit(solution)/shard_map/all_to_all | solution.py:1224
  292.7 7.0 %collective-permute-start.32 = (bf16[56,768]{1,0:T(8,128)(2,1)}, bf16[56,768]{1,0:T(8,128)(2,1)S(1)}, u32[]{:S(2)}, u32[]{:S(2)}) collective-permute-start(bf16[56,768]{1,0:T(8,128)(2,1)} %get-tuple-element.153), channel_id=1, source_target_pairs={{0,8},{1,9},{2,10},{3,11},{4,12},{5,13},{6,14},{7,15},{8,0},{9,1},... | collective-permute-start | bytes 258056 | tf_op jit(solution)/shard_map/ppermute | solution.py:1014
  292.7 13.1 %collective-permute-start.33 = (bf16[56,768]{1,0:T(8,128)(2,1)}, bf16[56,768]{1,0:T(8,128)(2,1)S(1)}, u32[]{:S(2)}, u32[]{:S(2)}) collective-permute-start(bf16[56,768]{1,0:T(8,128)(2,1)} %get-tuple-element.154), channel_id=1, source_target_pairs={{0,16},{1,17},{2,18},{3,19},{4,20},{5,21},{6,22},{7,23},{8,24},{9,... | collective-permute-start | bytes 258056 | tf_op jit(solution)/shard_map/ppermute | solution.py:1014
  292.7 13.1 %collective-permute-start.34 = (bf16[56,768]{1,0:T(8,128)(2,1)}, bf16[56,768]{1,0:T(8,128)(2,1)S(1)}, u32[]{:S(2)}, u32[]{:S(2)}) collective-permute-start(bf16[56,768]{1,0:T(8,128)(2,1)} %get-tuple-element.155), channel_id=1, source_target_pairs={{0,24},{1,25},{2,26},{3,27},{4,28},{5,29},{6,30},{7,31},{8,16},{9,... | collective-permute-start | bytes 258056 | tf_op jit(solution)/shard_map/ppermute | solution.py:1014
  297.1 12.1 %collective-permute-start.35 = (bf16[4,96,768]{2,1,0:T(8,128)(2,1)}, bf16[4,96,768]{2,1,0:T(8,128)(2,1)}, u32[]{:S(2)}, u32[]{:S(2)}) collective-permute-start(bf16[4,96,768]{2,1,0:T(8,128)(2,1)} %get-tuple-element.157), channel_id=1, source_target_pairs={{0,4},{1,5},{2,6},{3,7},{4,0},{5,1},{6,2},{7,3},{8,12},{9,13},{10,... | collective-permute-start | bytes 1769480 | tf_op jit(solution)/shard_map/ppermute | solution.py:1014
  299.0 10.1 %collective-permute-start.36 = (bf16[2,96,768]{2,1,0:T(8,128)(2,1)S(1)}, bf16[2,96,768]{2,1,0:T(8,128)(2,1)S(1)}, u32[]{:S(2)}, u32[]{:S(2)}) collective-permute-start(bf16[2,96,768]{2,1,0:T(8,128)(2,1)S(1)} %slice_bitcast_fusion.2), channel_id=1, source_target_pairs={{0,8},{1,9},{2,10},{3,11},{4,12},{5,13},{6,14},{7,15},{8,0},{9,1},... | collective-permute-start | bytes 884744 | tf_op jit(solution)/shard_map/ppermute | solution.py:1014
  310.4 8.4 %collective-permute-start.39 = (bf16[56,768]{1,0:T(8,128)(2,1)S(1)}, bf16[56,768]{1,0:T(8,128)(2,1)S(1)}, u32[]{:S(2)}, u32[]{:S(2)}) collective-permute-start(bf16[56,768]{1,0:T(8,128)(2,1)S(1)} %add_add_fusion), channel_id=1, source_target_pairs={{0,24},{1,25},{2,26},{3,27},{4,28},{5,29},{6,30},{7,31},{8,16},{9,... | collective-permute-start | bytes 258056 | tf_op jit(solution)/shard_map/ppermute | solution.py:1014
  311.3 13.5 %collective-permute-start.38 = (bf16[56,768]{1,0:T(8,128)(2,1)S(1)}, bf16[56,768]{1,0:T(8,128)(2,1)S(1)}, u32[]{:S(2)}, u32[]{:S(2)}) collective-permute-start(bf16[56,768]{1,0:T(8,128)(2,1)S(1)} %add_add_fusion), channel_id=1, source_target_pairs={{0,16},{1,17},{2,18},{3,19},{4,20},{5,21},{6,22},{7,23},{8,24},{9,... | collective-permute-start | bytes 258056 | tf_op jit(solution)/shard_map/ppermute | solution.py:1014
  311.5 13.3 %collective-permute-start.37 = (bf16[56,768]{1,0:T(8,128)(2,1)S(1)}, bf16[56,768]{1,0:T(8,128)(2,1)S(1)}, u32[]{:S(2)}, u32[]{:S(2)}) collective-permute-start(bf16[56,768]{1,0:T(8,128)(2,1)S(1)} %add_add_fusion), channel_id=1, source_target_pairs={{0,8},{1,9},{2,10},{3,11},{4,12},{5,13},{6,14},{7,15},{8,0},{9,1},... | collective-permute-start | bytes 258056 | tf_op jit(solution)/shard_map/ppermute | solution.py:1014
  314.8 13.3 %collective-permute-start.40 = (bf16[2,96,768]{2,1,0:T(8,128)(2,1)S(1)}, bf16[2,96,768]{2,1,0:T(8,128)(2,1)S(1)}, u32[]{:S(2)}, u32[]{:S(2)}) collective-permute-start(bf16[2,96,768]{2,1,0:T(8,128)(2,1)S(1)} %slice.212), channel_id=1, source_target_pairs={{0,16},{1,17},{2,18},{3,19},{4,20},{5,21},{6,22},{7,23},{8,24},{9,... | collective-permute-start | bytes 884744 | tf_op jit(solution)/shard_map/ppermute | solution.py:1014
  317.7 10.5 %collective-permute-start.41 = (bf16[2,96,768]{2,1,0:T(8,128)(2,1)S(1)}, bf16[2,96,768]{2,1,0:T(8,128)(2,1)S(1)}, u32[]{:S(2)}, u32[]{:S(2)}) collective-permute-start(bf16[2,96,768]{2,1,0:T(8,128)(2,1)S(1)} %bitcast_add_fusion.refs_1_), channel_id=1, source_target_pairs={{0,2},{1,3},{2,0},{3,1},{4,6},{5,7},{6,4},{7,5},{8,10},{9,11},{10,... | collective-permute-start | bytes 884744 | tf_op jit(solution)/shard_map/ppermute | solution.py:1014
  325.5 7.9 %copy-start.4 = (bf16[768,768]{1,0:T(8,128)(2,1)S(1)}, bf16[768,768]{1,0:T(8,128)(2,1)}, u32[]{:S(2)}) copy-start(bf16[768,768]{1,0:T(8,128)(2,1)} %refs_2_.7) | copy-start | bytes 3538948
  328.2 12.3 %collective-permute-start.44 = (bf16[4,56,768]{2,1,0:T(8,128)(2,1)}, bf16[4,56,768]{2,1,0:T(8,128)(2,1)}, u32[]{:S(2)}, u32[]{:S(2)}) collective-permute-start(bf16[4,56,768]{2,1,0:T(8,128)(2,1)} %pad_maximum_fusion.5), channel_id=1, source_target_pairs={{0,6},{1,7},{2,4},{3,5},{4,2},{5,3},{6,0},{7,1},{8,14},{9,15},{10,... | collective-permute-start | bytes 1032200 | tf_op jit(solution)/shard_map/ppermute | solution.py:1014
  330.3 14.6 %collective-permute-start.43 = (bf16[4,56,768]{2,1,0:T(8,128)(2,1)}, bf16[4,56,768]{2,1,0:T(8,128)(2,1)}, u32[]{:S(2)}, u32[]{:S(2)}) collective-permute-start(bf16[4,56,768]{2,1,0:T(8,128)(2,1)} %pad_maximum_fusion.5), channel_id=1, source_target_pairs={{0,2},{1,3},{2,0},{3,1},{4,6},{5,7},{6,4},{7,5},{8,10},{9,11},{10,... | collective-permute-start | bytes 1032200 | tf_op jit(solution)/shard_map/ppermute | solution.py:1014
  331.0 13.9 %collective-permute-start.42 = (bf16[4,56,768]{2,1,0:T(8,128)(2,1)}, bf16[4,56,768]{2,1,0:T(8,128)(2,1)}, u32[]{:S(2)}, u32[]{:S(2)}) collective-permute-start(bf16[4,56,768]{2,1,0:T(8,128)(2,1)} %pad_maximum_fusion.5), channel_id=1, source_target_pairs={{0,4},{1,5},{2,6},{3,7},{4,0},{5,1},{6,2},{7,3},{8,12},{9,13},{10,... | collective-permute-start | bytes 1032200 | tf_op jit(solution)/shard_map/ppermute | solution.py:1014
  332.4 5.5 %collective-permute-start.45 = (bf16[96,768]{1,0:T(8,128)(2,1)}, bf16[96,768]{1,0:T(8,128)(2,1)}, u32[]{:S(2)}, u32[]{:S(2)}) collective-permute-start(bf16[96,768]{1,0:T(8,128)(2,1)} %slice_bitcast_fusion.7), channel_id=1, source_target_pairs={{0,8},{1,9},{2,10},{3,11},{4,12},{5,13},{6,14},{7,15},{8,0},{9,1},... | collective-permute-start | bytes 442376 | tf_op jit(solution)/shard_map/ppermute | solution.py:1014
  333.4 13.1 %collective-permute-start.46 = (bf16[2,2,96,768]{3,2,1,0:T(8,128)(2,1)}, bf16[2,2,96,768]{3,2,1,0:T(8,128)(2,1)S(1)}, u32[]{:S(2)}, u32[]{:S(2)}) collective-permute-start(bf16[2,2,96,768]{3,2,1,0:T(8,128)(2,1)} %pad_maximum_fusion.4), channel_id=1, source_target_pairs={{0,1},{1,0},{2,3},{3,2},{4,5},{5,4},{6,7},{7,6},{8,9},{9,8},{10,11... | collective-permute-start | bytes 1769480 | tf_op jit(solution)/shard_map/ppermute | solution.py:1014
  346.4 6.3 %collective-permute-start.47 = (bf16[16,56,768]{2,1,0:T(8,128)(2,1)S(1)}, bf16[16,56,768]{2,1,0:T(8,128)(2,1)S(1)}, u32[]{:S(2)}, u32[]{:S(2)}) collective-permute-start(bf16[16,56,768]{2,1,0:T(8,128)(2,1)S(1)} %pad_maximum_fusion.1.refs_1_), channel_id=1, source_target_pairs={{0,1},{1,0},{2,3},{3,2},{4,5},{5,4},{6,7},{7,6},{8,9},{9,8},{10,11... | collective-permute-start | bytes 4128776 | tf_op jit(solution)/shard_map/ppermute | solution.py:1014
  346.5 6.3 %collective-permute-start.48 = (bf16[96,768]{1,0:T(8,128)(2,1)S(1)}, bf16[96,768]{1,0:T(8,128)(2,1)S(1)}, u32[]{:S(2)}, u32[]{:S(2)}) collective-permute-start(bf16[96,768]{1,0:T(8,128)(2,1)S(1)} %bitcast_add_fusion.1.refs_1_), channel_id=1, source_target_pairs={{0,2},{1,3},{2,0},{3,1},{4,6},{5,7},{6,4},{7,5},{8,10},{9,11},{10,... | collective-permute-start | bytes 442376 | tf_op jit(solution)/shard_map/ppermute | solution.py:1014
  352.8 5.4 %collective-permute-start.49 = (bf16[2,96,768]{2,1,0:T(8,128)(2,1)S(1)}, bf16[2,96,768]{2,1,0:T(8,128)(2,1)S(1)}, u32[]{:S(2)}, u32[]{:S(2)}) collective-permute-start(bf16[2,96,768]{2,1,0:T(8,128)(2,1)S(1)} %pad_maximum_fusion.6), channel_id=1, source_target_pairs={{0,1},{1,0},{2,3},{3,2},{4,5},{5,4},{6,7},{7,6},{8,9},{9,8},{10,11... | collective-permute-start | bytes 884744 | tf_op jit(solution)/shard_map/ppermute | solution.py:1014
  (24 other events, 69.6 us)
Sparse Core Ops, SparseCore 0:
  10.8 49.4 all-gather.4
  63.0 46.9 all-gather.6

commit v6 on v5

--- a/solution.py
+++ b/solution.py
@@ -1102,7 +1102,7 @@
         first_y = grid.swap(first_z, **Y)
         first_x = grid.swap(first_z, **X)
         up_z = gather_z(grid, tie(piece_up, first_z))
-        raw_rows = tie(raw_rows, first_y, up_z)
+        raw_rows = tie(raw_rows, first_y)
     received = lax.all_to_all(raw_rows, "mod", split_axis=0, concat_axis=0, tiled=True)
     rows = received.reshape(capacity, D)
     branch, down_bias_grad = prepare(out_cotangent[0], recv_counts, read_counts, block_rows, total)

time: 374 us -> 375 us (level)
  waiting for transfers between devices: 105 us -> 100 us
    all_to_all x1, starting transfers between devices: 6.93 us -> 11.7 us  [per_device(): lax.all_to_all(raw_rows, 'mod', split_axis=0, concat_axis=0, tiled=True)]
    ppermute x50, waiting for transfers between devices: 105 us -> 100 us  [swap(): return lax.ppermute(value, AXES, pairs)]
    unnamed x76 -> x74, local copies, waits for them, and re-layouts: 19 us -> 22 us
  transfers between devices with their start and end apart: 54 -> 54, of which waited for: 18 -> 17; matrix products, arithmetic and copies ran while one was open for 9% -> 9% of each run, Pallas kernels for 34% -> 34%
where the time goes in v6:
time: 375 us; the launch traced here: 369 us
  Pallas kernels  135 us (36%)
  waiting for transfers between devices  100 us (27%)
  starting transfers between devices  67.9 us (18%)
  local copies, waits for them, and re-layouts  36.3 us (10%)
  between operations  15.9 us (4%)
  other arithmetic  13.7 us (4%)
    pallas_call x24, Pallas kernels, call(): return lambda *args: built(*args, *deps)  135 us
    ppermute x50, waiting for transfers between devices, swap(): return lax.ppermute(value, AXES, pairs)  100 us
    ppermute x50, starting transfers between devices, swap(): return lax.ppermute(value, AXES, pairs)  52.5 us
    unnamed x74, local copies, waits for them, and re-layouts  22 us
    all_to_all x1, starting transfers between devices, per_device(): lax.all_to_all(raw_rows, 'mod', split_axis=0, concat_axis=0, tiled=True)  11.7 us
  transfers between devices with their start and end apart: 54, of which 17 were waited for; matrix products, arithmetic and copies ran while one was open for 9% of the time, Pallas kernels for 34%

profile of v6, /device:TPU:0, one launch (start us, length us, event | category | flops | bytes accessed | tf_op | source)
XLA Modules:
  0.0 368.7 jit_solution(6904344556641401567)
XLA Ops:
  7.2 1.7 constant_dynamic-slice_fusion
  9.1 1.6 constant_dynamic-update-slice_fusion.4
  10.7 4.0 %collective-permute-start.1 = (bf16[96,768]{1,0:T(8,128)(2,1)S(1)}, bf16[96,768]{1,0:T(8,128)(2,1)S(1)}, u32[]{:S(2)}, u32[]{:S(2)}) collective-permute-start(bf16[96,768]{1,0:T(8,128)(2,1)S(1)} %get-tuple-element.189), channel_id=1, source_target_pairs={{0,16},{1,17},{2,18},{3,19},{4,20},{5,21},{6,22},{7,23},{8,24},{9,... | collective-permute-start | bytes 442376 | tf_op jit(solution)/shard_map/ppermute | solution.py:1014
  16.3 7.1 %collective-permute-done.1 = bf16[96,768]{1,0:T(8,128)(2,1)S(1)} collective-permute-done((bf16[96,768]{1,0:T(8,128)(2,1)S(1)}, bf16[96,768]{1,0:T(8,128)(2,1)S(1)}, u32[]{:S(2)}, u32[]{:S(2)}) %collective-permute-start.1) | collective-permute-done | bytes 147488 | tf_op jit(solution)/shard_map/ppermute | solution.py:1014
  23.4 2.8 collective-permute-done.2
  26.3 1.6 collective-permute-start.3
  28.9 2.3 reshape.91
  36.4 3.9 %collective-permute-start.10 = (bf16[96,768]{1,0:T(8,128)(2,1)S(1)}, bf16[96,768]{1,0:T(8,128)(2,1)}, u32[]{:S(2)}, u32[]{:S(2)}) collective-permute-start(bf16[96,768]{1,0:T(8,128)(2,1)S(1)} %reshape.92), channel_id=1, source_target_pairs={{0,24},{1,25},{2,26},{3,27},{4,28},{5,29},{6,30},{7,31},{8,16},{9,... | collective-permute-start | bytes 442376 | tf_op jit(solution)/shard_map/ppermute | solution.py:1014
  40.3 4.5 %collective-permute-start.9 = (bf16[96,768]{1,0:T(8,128)(2,1)S(1)}, bf16[96,768]{1,0:T(8,128)(2,1)}, u32[]{:S(2)}, u32[]{:S(2)}) collective-permute-start(bf16[96,768]{1,0:T(8,128)(2,1)S(1)} %reshape.92), channel_id=1, source_target_pairs={{0,16},{1,17},{2,18},{3,19},{4,20},{5,21},{6,22},{7,23},{8,24},{9,... | collective-permute-start | bytes 442376 | tf_op jit(solution)/shard_map/ppermute | solution.py:1014
  45.4 1.6 collective-permute-start.5
  47.0 11.7 %all-to-all-start = ((bf16[8,96,768]{2,1,0:T(8,128)(2,1)}), bf16[8,96,768]{2,1,0:T(8,128)(2,1)S(1)}, u32[]{:S(2)}, u32[]{:S(2)}) async-start(bf16[8,96,768]{2,1,0:T(8,128)(2,1)} %param.20), calls=%async_computation | async-start | bytes 2359296 | tf_op jit(solution)/shard_map/all_to_all | solution.py:1106
  62.3 1.9 constant_dynamic-update-slice_fusion.refs_2_.refs_5_.refs_3_
  65.3 7.1 %collective-permute-done.6 = bf16[4,96,768]{2,1,0:T(8,128)(2,1)S(1)} collective-permute-done((bf16[4,96,768]{2,1,0:T(8,128)(2,1)}, bf16[4,96,768]{2,1,0:T(8,128)(2,1)S(1)}, u32[]{:S(2)}, u32[]{:S(2)}) %collective-permute-start.6) | collective-permute-done | bytes 589856 | tf_op jit(solution)/shard_map/ppermute | solution.py:1014
  75.7 1.6 constant_dynamic-update-slice_fusion.10
  77.3 1.6 constant_dynamic-update-slice_fusion.9
  78.9 1.6 constant_dynamic-update-slice_fusion.8
  80.4 13.2 %collective-permute-done.11 = bf16[4,96,768]{2,1,0:T(8,128)(2,1)S(1)} collective-permute-done((bf16[4,96,768]{2,1,0:T(8,128)(2,1)S(1)}, bf16[4,96,768]{2,1,0:T(8,128)(2,1)S(1)}, u32[]{:S(2)}, u32[]{:S(2)}) %collective-permute-start.11) | collective-permute-done | bytes 589856 | tf_op jit(solution)/shard_map/ppermute | solution.py:1014
  99.2 1.7 shard_map.323
  102.4 6.1 %shard_map.324.refs_0_ = bf16[3,784,768]{2,1,0:T(8,128)(2,1)S(1)} custom-call(s32[2]{0:T(128)S(1)} %pad_add_fusion.refs_0_, bf16[784,768]{1,0:T(8,128)(2,1)S(1)} %get-tuple-element.100.refs_1_, bf16[8,96,768]{2,1,0:T(8,128)(2,1)} %constant_dynamic-update-slice_fusion.refs_2_.refs_5_.refs_3_, ...), custom_call_target="tpu_custom_call" | custom-call | flops 8049999872 | bytes 1048576 | tf_op jit(solution)/shard_map/pallas_call | solution.py:87
  108.5 15.3 %shard_map.325 = (bf16[784,768]{1,0:T(8,128)(2,1)S(1)}, f32[16,768]{1,0:T(8,128)S(1)}, f32[96,128]{1,0:T(8,128)S(1)}) custom-call(bf16[3,784,768]{2,1,0:T(8,128)(2,1)S(1)} %shard_map.324.refs_0_, s32[1,8]{1,0:T(1,128)S(1)} %copy-done.17, s32[1,1]{1,0:T(1,128)S(6)} %copy.56.refs_2_.refs_6_, s32[1,768]{1,0:T(1,128)S(1)} %copy-done.1, ...), custom_call_target="tpu_custom_call" | custom-call | flops 24149999616 | bytes 1048576 | tf_op jit(solution)/shard_map/pallas_call | solution.py:87
  123.8 1.8 copy-done.20
  126.7 1.7 copy-done.23
  129.6 3.7 %shard_map.326 = (f32[784,768]{1,0:T(8,128)S(1)}, bf16[784,768]{1,0:T(8,128)(2,1)S(1)}) custom-call(s32[2]{0:T(128)S(1)} %pad_add_fusion.refs_0_, bf16[784,768]{1,0:T(8,128)(2,1)S(1)} %copy-done.28, bf16[8,96,768]{2,1,0:T(8,128)(2,1)} %constant_dynamic-update-slice_fusion.refs_2_.refs_5_.refs_3_, ...), custom_call_target="tpu_custom_call" | custom-call | flops 7360000000 | bytes 1048576 | tf_op jit(solution)/shard_map/pallas_call | solution.py:87
  133.4 11.0 %shard_map.328 = (bf16[2,784,768]{2,1,0:T(8,128)(2,1)S(1)}, bf16[2,784,768]{2,1,0:T(8,128)(2,1)S(1)}, f32[784,768]{1,0:T(8,128)S(1)}, f32[784,768]{1,0:T(8,128)S(1)}, f32[4,768]{1,0:T(4,128)S(1)}) custom-call(s32[2]{0:T(128)S(1)} %pad_add_fusion.refs_0_, s32[1,8]{1,0:T(1,128)S(1)} %copy-done.17, s32[1,1]{1,0:T(1,128)S(6)} %copy.56.refs_2_.refs_6_, ...), custom_call_target="tpu_custom_call" | custom-call | flops 23000000512 | bytes 1048576 | tf_op jit(solution)/shard_map/pallas_call | solution.py:87
  145.3 3.2 shard_map.329.refs_14_
  148.6 14.9 %shard_map.330 = (bf16[2,784,768]{2,1,0:T(8,128)(2,1)S(1)}, bf16[2,784,768]{2,1,0:T(8,128)(2,1)S(1)}, f32[784,768]{1,0:T(8,128)S(1)}, f32[784,768]{1,0:T(8,128)S(1)}, f32[4,768]{1,0:T(4,128)S(1)}) custom-call(s32[2]{0:T(128)S(1)} %pad_add_fusion.refs_0_, s32[1,8]{1,0:T(1,128)S(1)} %copy-done.17, s32[1,1]{1,0:T(1,128)S(6)} %copy.56.refs_2_.refs_6_, ...), custom_call_target="tpu_custom_call" | custom-call | flops 23000000512 | bytes 1048576 | tf_op jit(solution)/shard_map/pallas_call | solution.py:87
  163.5 3.2 shard_map.331.refs_9_
  167.3 4.5 %shard_map.332 = (f32[784,768]{1,0:T(8,128)S(1)}, bf16[784,768]{1,0:T(8,128)(2,1)S(1)}, bf16[784,768]{1,0:T(8,128)(2,1)S(1)}, f32[2,768]{1,0:T(2,128)S(1)}) custom-call(s32[2]{0:T(128)S(1)} %pad_add_fusion.refs_0_, f32[784,768]{1,0:T(8,128)S(1)} %get-tuple-element.117.refs_1_, f32[784,768]{1,0:T(8,128)S(1)} %get-tuple-element.108.refs_7_.refs_8_.refs_2_, ...), custom_call_target="tpu_custom_call" | custom-call | flops 9774999552 | bytes 1048576 | tf_op jit(solution)/shard_map/pallas_call | solution.py:87
  171.8 3.3 shard_map.333
  175.1 5.1 %shard_map.334 = (bf16[2,4,96,768]{3,2,1,0:T(8,128)(2,1)S(1)}, bf16[2,4,96,768]{3,2,1,0:T(8,128)(2,1)S(1)}) custom-call(s32[2]{0:T(128)S(1)} %pad_add_fusion.refs_0_, bf16[784,768]{1,0:T(8,128)(2,1)S(1)} %get-tuple-element.106.refs_3_.refs_1_, bf16[2,784,768]{2,1,0:T(8,128)(2,1)S(1)} %get-tuple-element.116.refs_3_.refs_2_, ...), custom_call_target="tpu_custom_call" | custom-call | flops 9200000000 | bytes 1048576 | tf_op jit(solution)/shard_map/pallas_call | solution.py:87
  180.2 2.5 collective-permute-start.21
  182.8 13.0 %shard_map.335.refs_3_.refs_1_ = bf16[3,784,384]{2,1,0:T(8,128)(2,1)S(1)} custom-call(bf16[3,784,768]{2,1,0:T(8,128)(2,1)S(1)} %copy-done.21, bf16[784,768]{1,0:T(8,128)(2,1)S(1)} %copy-done.29, bf16[784,768]{1,0:T(8,128)(2,1)S(1)} %get-tuple-element.120.refs_2_, f32[16,768]{1,0:T(8,128)S(1)} %get-tuple-element.121.refs_3_, ...), custom_call_target="tpu_custom_call" | custom-call | flops 17250000896 | bytes 1048576 | tf_op jit(solution)/shard_map/pallas_call | solution.py:87
  195.9 3.3 shard_map.336.refs_9_
  199.3 13.0 %shard_map.337.refs_3_.refs_2_ = bf16[3,784,384]{2,1,0:T(8,128)(2,1)S(1)} custom-call(bf16[3,784,768]{2,1,0:T(8,128)(2,1)S(1)} %copy-done.21, bf16[784,768]{1,0:T(8,128)(2,1)S(1)} %copy-done.29, bf16[784,768]{1,0:T(8,128)(2,1)S(1)} %get-tuple-element.120.refs_2_, f32[16,768]{1,0:T(8,128)S(1)} %get-tuple-element.121.refs_3_, ...), custom_call_target="tpu_custom_call" | custom-call | flops 17250000896 | bytes 1048576 | tf_op jit(solution)/shard_map/pallas_call | solution.py:87
  212.3 3.5 shard_map.338.refs_6_
  216.5 2.1 collective-permute-start.22
  218.7 3.2 shard_map.339
  221.8 10.3 %collective-permute-done.22 = bf16[4,96,768]{2,1,0:T(8,128)(2,1)S(1)} collective-permute-done((bf16[4,96,768]{2,1,0:T(8,128)(2,1)S(1)}, bf16[4,96,768]{2,1,0:T(8,128)(2,1)S(1)}, u32[]{:S(2)}, u32[]{:S(2)}) %collective-permute-start.22) | collective-permute-done | bytes 589856 | tf_op jit(solution)/shard_map/ppermute | solution.py:1014
  233.7 1.8 collective-permute-start.28
  235.7 3.2 shard_map.340
  239.4 7.5 %shard_map.341 = (bf16[768,768]{1,0:T(8,128)(2,1)}, f32[8,768]{1,0:T(8,128)S(1)}, f32[2,768]{1,0:T(2,128)S(1)}) custom-call(s32[2]{0:T(128)S(1)} %pad_add_fusion.refs_0_, bf16[3,784,384]{2,1,0:T(8,128)(2,1)S(1)} %shard_map.335.refs_3_.refs_1_, bf16[3,784,384]{2,1,0:T(8,128)(2,1)S(1)} %shard_map.337.refs_3_.refs_2_, ...), custom_call_target="tpu_custom_call" | custom-call | flops 11500000256 | bytes 1048576 | tf_op jit(solution)/shard_map/pallas_call | solution.py:87
  246.9 4.7 %shard_map.342 = (bf16[8,56,768]{2,1,0:T(8,128)(2,1)S(1)}, bf16[8,56,768]{2,1,0:T(8,128)(2,1)S(1)}, bf16[8,56,768]{2,1,0:T(8,128)(2,1)S(1)}, bf16[8,56,768]{2,1,0:T(8,128)(2,1)S(1)}) custom-call(s32[2]{0:T(128)S(1)} %pad_add_fusion.refs_0_, bf16[768,768]{1,0:T(8,128)(2,1)S(1)} %bitcast.94, bf16[768,768]{1,0:T(8,128)(2,1)} %get-tuple-element.134.refs_2_, ...), custom_call_target="tpu_custom_call" | custom-call | flops 6899999744 | bytes 1048576 | tf_op jit(solution)/shard_map/pallas_call | solution.py:87
  252.4 9.1 %collective-permute-done.28 = bf16[2,2,96,768]{3,2,1,0:T(8,128)(2,1)S(1)} collective-permute-done((bf16[2,2,96,768]{3,2,1,0:T(8,128)(2,1)S(1)}, bf16[2,2,96,768]{3,2,1,0:T(8,128)(2,1)S(1)}, u32[]{:S(2)}, u32[]{:S(2)}) %collective-permute-start.28) | collective-permute-done | bytes 589856 | tf_op jit(solution)/shard_map/ppermute | solution.py:1014
  263.3 2.3 collective-permute-done.27
  270.2 3.6 all-to-all-start.1
  273.8 17.5 %collective-permute-done.29 = bf16[4,56,768]{2,1,0:T(8,128)(2,1)S(1)} collective-permute-done((bf16[4,56,768]{2,1,0:T(8,128)(2,1)}, bf16[4,56,768]{2,1,0:T(8,128)(2,1)S(1)}, u32[]{:S(2)}, u32[]{:S(2)}) %collective-permute-start.29) | collective-permute-done | bytes 344096 | tf_op jit(solution)/shard_map/ppermute | solution.py:1014
  291.3 1.9 fusion.15
  293.6 2.0 collective-permute-start.33
  295.6 2.0 collective-permute-start.34
  297.6 2.1 collective-permute-start.35
  299.9 7.1 %collective-permute-done.33 = bf16[56,768]{1,0:T(8,128)(2,1)S(1)} collective-permute-done((bf16[56,768]{1,0:T(8,128)(2,1)}, bf16[56,768]{1,0:T(8,128)(2,1)S(1)}, u32[]{:S(2)}, u32[]{:S(2)}) %collective-permute-start.33) | collective-permute-done | bytes 86048 | tf_op jit(solution)/shard_map/ppermute | solution.py:1014
  307.1 3.1 collective-permute-done.36
  312.4 3.5 collective-permute-start.37
  316.0 2.8 fusion
  319.6 5.6 %collective-permute-done.38 = bf16[56,768]{1,0:T(8,128)(2,1)S(1)} collective-permute-done((bf16[56,768]{1,0:T(8,128)(2,1)S(1)}, bf16[56,768]{1,0:T(8,128)(2,1)S(1)}, u32[]{:S(2)}, u32[]{:S(2)}) %collective-permute-start.38) | collective-permute-done | bytes 86048 | tf_op jit(solution)/shard_map/ppermute | solution.py:1014
  326.0 3.3 collective-permute-done.40
  329.3 1.9 collective-permute-start.44
  335.8 2.5 shard_map.343
  340.0 1.7 collective-permute-done.44
  341.7 4.8 %collective-permute-done.43 = bf16[4,56,768]{2,1,0:T(8,128)(2,1)} collective-permute-done((bf16[4,56,768]{2,1,0:T(8,128)(2,1)}, bf16[4,56,768]{2,1,0:T(8,128)(2,1)}, u32[]{:S(2)}, u32[]{:S(2)}) %collective-permute-start.43) | collective-permute-done | bytes 344096 | tf_op jit(solution)/shard_map/ppermute | solution.py:1014
  348.8 2.4 shard_map.344
  351.2 3.1 collective-permute-done.48.refs_2_
  354.4 3.3 shard_map.345
  359.7 1.6 shard_map.346
  (192 shorter events, 51.8 us)
Async XLA Ops:
  7.2 87.3 %all-gather.5.cloned.1.call-start = ((), (), s32[]{:S(2)}) async-start(), calls=%async_computation.2 | async-start | bytes 1327104 | tf_op jit(solution)/shard_map/all_gather | solution.py:1115
  9.0 19.6 %copy-start.32 = (f32[3072]{0:T(1024)S(1)}, f32[3072]{0:T(1024)}, u32[]{:S(2)}) copy-start(f32[3072]{0:T(1024)} %param.36) | copy-start | bytes 36868
  9.0 19.7 %copy-start.1 = (s32[1,768]{1,0:T(1,128)S(1)}, s32[1,768]{1,0:T(1,128)}, u32[]{:S(2)}) copy-start(s32[1,768]{1,0:T(1,128)} %refs_7_.7) | copy-start | bytes 9220
  9.0 117.7 %all-gather.7.cloned.1.call-start = ((), (), s32[]{:S(2)}) async-start(), calls=%async_computation.3 | async-start | bytes 1327104 | tf_op jit(solution)/shard_map/all_gather | solution.py:1117
  10.7 12.7 %collective-permute-start.1 = (bf16[96,768]{1,0:T(8,128)(2,1)S(1)}, bf16[96,768]{1,0:T(8,128)(2,1)S(1)}, u32[]{:S(2)}, u32[]{:S(2)}) collective-permute-start(bf16[96,768]{1,0:T(8,128)(2,1)S(1)} %get-tuple-element.189), channel_id=1, source_target_pairs={{0,16},{1,17},{2,18},{3,19},{4,20},{5,21},{6,22},{7,23},{8,24},{9,... | collective-permute-start | bytes 442376 | tf_op jit(solution)/shard_map/ppermute | solution.py:1014
  14.7 8.7 %collective-permute-start = (bf16[96,768]{1,0:T(8,128)(2,1)S(1)}, bf16[96,768]{1,0:T(8,128)(2,1)S(1)}, u32[]{:S(2)}, u32[]{:S(2)}) collective-permute-start(bf16[96,768]{1,0:T(8,128)(2,1)S(1)} %get-tuple-element.189), channel_id=1, source_target_pairs={{0,8},{1,9},{2,10},{3,11},{4,12},{5,13},{6,14},{7,15},{8,0},{9,1},... | collective-permute-start | bytes 442376 | tf_op jit(solution)/shard_map/ppermute | solution.py:1014
  16.3 9.9 %collective-permute-start.2 = (bf16[96,768]{1,0:T(8,128)(2,1)S(1)}, bf16[96,768]{1,0:T(8,128)(2,1)S(1)}, u32[]{:S(2)}, u32[]{:S(2)}) collective-permute-start(bf16[96,768]{1,0:T(8,128)(2,1)S(1)} %get-tuple-element.189), channel_id=1, source_target_pairs={{0,24},{1,25},{2,26},{3,27},{4,28},{5,29},{6,30},{7,31},{8,16},{9,... | collective-permute-start | bytes 442376 | tf_op jit(solution)/shard_map/ppermute | solution.py:1014
  26.3 20.7 %collective-permute-start.3 = (bf16[4,96,768]{2,1,0:T(8,128)(2,1)S(1)}, bf16[4,96,768]{2,1,0:T(8,128)(2,1)}, u32[]{:S(2)}, u32[]{:S(2)}) collective-permute-start(bf16[4,96,768]{2,1,0:T(8,128)(2,1)S(1)} %pad_maximum_fusion.2), channel_id=1, source_target_pairs={{0,4},{1,5},{2,6},{3,7},{4,0},{5,1},{6,2},{7,3},{8,12},{9,13},{10,... | collective-permute-start | bytes 1769480 | tf_op jit(solution)/shard_map/ppermute | solution.py:1014
  36.4 36.9 %collective-permute-start.10 = (bf16[96,768]{1,0:T(8,128)(2,1)S(1)}, bf16[96,768]{1,0:T(8,128)(2,1)}, u32[]{:S(2)}, u32[]{:S(2)}) collective-permute-start(bf16[96,768]{1,0:T(8,128)(2,1)S(1)} %reshape.92), channel_id=1, source_target_pairs={{0,24},{1,25},{2,26},{3,27},{4,28},{5,29},{6,30},{7,31},{8,16},{9,... | collective-permute-start | bytes 442376 | tf_op jit(solution)/shard_map/ppermute | solution.py:1014
  40.3 33.0 %collective-permute-start.9 = (bf16[96,768]{1,0:T(8,128)(2,1)S(1)}, bf16[96,768]{1,0:T(8,128)(2,1)}, u32[]{:S(2)}, u32[]{:S(2)}) collective-permute-start(bf16[96,768]{1,0:T(8,128)(2,1)S(1)} %reshape.92), channel_id=1, source_target_pairs={{0,16},{1,17},{2,18},{3,19},{4,20},{5,21},{6,22},{7,23},{8,24},{9,... | collective-permute-start | bytes 442376 | tf_op jit(solution)/shard_map/ppermute | solution.py:1014
  44.8 28.4 %collective-permute-start.8 = (bf16[96,768]{1,0:T(8,128)(2,1)S(1)}, bf16[96,768]{1,0:T(8,128)(2,1)}, u32[]{:S(2)}, u32[]{:S(2)}) collective-permute-start(bf16[96,768]{1,0:T(8,128)(2,1)S(1)} %reshape.92), channel_id=1, source_target_pairs={{0,8},{1,9},{2,10},{3,11},{4,12},{5,13},{6,14},{7,15},{8,0},{9,1},... | collective-permute-start | bytes 442376 | tf_op jit(solution)/shard_map/ppermute | solution.py:1014
  45.4 18.8 %collective-permute-start.5 = (bf16[4,96,768]{2,1,0:T(8,128)(2,1)S(1)}, bf16[4,96,768]{2,1,0:T(8,128)(2,1)}, u32[]{:S(2)}, u32[]{:S(2)}) collective-permute-start(bf16[4,96,768]{2,1,0:T(8,128)(2,1)S(1)} %pad_maximum_fusion.2), channel_id=1, source_target_pairs={{0,2},{1,3},{2,0},{3,1},{4,6},{5,7},{6,4},{7,5},{8,10},{9,11},{10,... | collective-permute-start | bytes 1769480 | tf_op jit(solution)/shard_map/ppermute | solution.py:1014
  47.0 49.6 %all-to-all-start = ((bf16[8,96,768]{2,1,0:T(8,128)(2,1)}), bf16[8,96,768]{2,1,0:T(8,128)(2,1)S(1)}, u32[]{:S(2)}, u32[]{:S(2)}) async-start(bf16[8,96,768]{2,1,0:T(8,128)(2,1)} %param.20), calls=%async_computation | async-start | bytes 2359296 | tf_op jit(solution)/shard_map/all_to_all | solution.py:1106
  59.4 13.1 %collective-permute-start.6 = (bf16[4,96,768]{2,1,0:T(8,128)(2,1)}, bf16[4,96,768]{2,1,0:T(8,128)(2,1)S(1)}, u32[]{:S(2)}, u32[]{:S(2)}) collective-permute-start(bf16[4,96,768]{2,1,0:T(8,128)(2,1)} %collective-permute-done.3), channel_id=1, source_target_pairs={{0,2},{1,3},{2,0},{3,1},{4,6},{5,7},{6,4},{7,5},{8,10},{9,11},{10,... | collective-permute-start | bytes 1769480 | tf_op jit(solution)/shard_map/ppermute | solution.py:1014
  64.2 30.8 %collective-permute-start.4 = (bf16[8,96,768]{2,1,0:T(8,128)(2,1)}, bf16[8,96,768]{2,1,0:T(8,128)(2,1)}, u32[]{:S(2)}, u32[]{:S(2)}) collective-permute-start(bf16[8,96,768]{2,1,0:T(8,128)(2,1)} %constant_dynamic-update-slice_fusion.refs_2_.refs_5_.refs_3_), channel_id=1, source_target_pairs={{0,1},{1,0},{2,3},{3,2},{4,5},{5,4},{6,7},{7,6},{8,9},{9,8},{10,11... | collective-permute-start | bytes 3538952 | tf_op jit(solution)/shard_map/ppermute | solution.py:1014
  72.5 22.6 %collective-permute-start.7 = (bf16[8,96,768]{2,1,0:T(8,128)(2,1)S(1)}, bf16[8,96,768]{2,1,0:T(8,128)(2,1)}, u32[]{:S(2)}, u32[]{:S(2)}) collective-permute-start(bf16[8,96,768]{2,1,0:T(8,128)(2,1)S(1)} %constant_dynamic-update-slice_fusion.5.refs_4_.refs_7_.refs_5_), channel_id=1, source_target_pairs={{0,1},{1,0},{2,3},{3,2},{4,5},{5,4},{6,7},{7,6},{8,9},{9,8},{10,11... | collective-permute-start | bytes 3538952 | tf_op jit(solution)/shard_map/ppermute | solution.py:1014
  74.4 22.2 %copy-start.9 = (f32[8,768]{1,0:T(8,128)S(1)}, f32[8,768]{1,0:T(8,128)}, u32[]{:S(2)}) copy-start(f32[8,768]{1,0:T(8,128)} %refs_5_.3) | copy-start | bytes 73732
  74.4 22.2 %copy-start.10 = (f32[768]{0:T(1024)S(1)}, f32[768]{0:T(1024)}, u32[]{:S(2)}) copy-start(f32[768]{0:T(1024)} %refs_2_.6) | copy-start | bytes 9220
  74.4 22.2 %copy-start.11 = (f32[768]{0:T(1024)S(1)}, f32[768]{0:T(1024)}, u32[]{:S(2)}) copy-start(f32[768]{0:T(1024)} %refs_4_.2) | copy-start | bytes 9220
  74.4 22.2 %copy-start.12 = (f32[768]{0:T(1024)S(1)}, f32[768]{0:T(1024)}, u32[]{:S(2)}) copy-start(f32[768]{0:T(1024)} %refs_7_.4) | copy-start | bytes 9220
  74.4 22.2 %copy-start.16 = (f32[768]{0:T(1024)S(1)}, f32[768]{0:T(1024)}, u32[]{:S(2)}) copy-start(f32[768]{0:T(1024)} %refs_8_.3) | copy-start | bytes 9220
  74.4 19.2 %collective-permute-start.11 = (bf16[4,96,768]{2,1,0:T(8,128)(2,1)S(1)}, bf16[4,96,768]{2,1,0:T(8,128)(2,1)S(1)}, u32[]{:S(2)}, u32[]{:S(2)}) collective-permute-start(bf16[4,96,768]{2,1,0:T(8,128)(2,1)S(1)} %pad_maximum_fusion.3), channel_id=1, source_target_pairs={{0,4},{1,5},{2,6},{3,7},{4,0},{5,1},{6,2},{7,3},{8,12},{9,13},{10,... | collective-permute-start | bytes 1769480 | tf_op jit(solution)/shard_map/ppermute | solution.py:1014
  94.5 38.9 %collective-permute-start.13 = (bf16[8,96,768]{2,1,0:T(8,128)(2,1)}, bf16[8,96,768]{2,1,0:T(8,128)(2,1)}, u32[]{:S(2)}, u32[]{:S(2)}) collective-permute-start(bf16[8,96,768]{2,1,0:T(8,128)(2,1)} %constant_dynamic-update-slice_fusion.7.refs_9_.refs_10_), channel_id=1, source_target_pairs={{0,1},{1,0},{2,3},{3,2},{4,5},{5,4},{6,7},{7,6},{8,9},{9,8},{10,11... | collective-permute-start | bytes 3538952 | tf_op jit(solution)/shard_map/ppermute | solution.py:1014
  94.5 32.1 %collective-permute-start.12 = (bf16[8,96,768]{2,1,0:T(8,128)(2,1)}, bf16[8,96,768]{2,1,0:T(8,128)(2,1)}, u32[]{:S(2)}, u32[]{:S(2)}) collective-permute-start(bf16[8,96,768]{2,1,0:T(8,128)(2,1)} %bitcast.102), channel_id=1, source_target_pairs={{0,1},{1,0},{2,3},{3,2},{4,5},{5,4},{6,7},{7,6},{8,9},{9,8},{10,11... | collective-permute-start | bytes 3538952 | tf_op jit(solution)/shard_map/ppermute | solution.py:1014
  95.0 49.4 %collective-permute-start.14 = (bf16[8,96,768]{2,1,0:T(8,128)(2,1)}, bf16[8,96,768]{2,1,0:T(8,128)(2,1)}, u32[]{:S(2)}, u32[]{:S(2)}) collective-permute-start(bf16[8,96,768]{2,1,0:T(8,128)(2,1)} %constant_dynamic-update-slice_fusion.7.refs_9_.refs_10_), channel_id=1, source_target_pairs={{0,2},{1,3},{2,0},{3,1},{4,6},{5,7},{6,4},{7,5},{8,10},{9,11},{10,... | collective-permute-start | bytes 3538952 | tf_op jit(solution)/shard_map/ppermute | solution.py:1014
  108.5 18.2 %copy-start.13 = (f32[768]{0:T(1024)S(1)}, f32[768]{0:T(1024)}, u32[]{:S(2)}) copy-start(f32[768]{0:T(1024)} %refs_8_.2) | copy-start | bytes 9220
  108.5 18.2 %copy-start.15 = (f32[768]{0:T(1024)S(1)}, f32[768]{0:T(1024)}, u32[]{:S(2)}) copy-start(f32[768]{0:T(1024)} %refs_4_.3) | copy-start | bytes 9220
  126.7 21.9 %collective-permute-start.16 = (bf16[8,96,768]{2,1,0:T(8,128)(2,1)}, bf16[8,96,768]{2,1,0:T(8,128)(2,1)S(1)}, u32[]{:S(2)}, u32[]{:S(2)}) collective-permute-start(bf16[8,96,768]{2,1,0:T(8,128)(2,1)} %bitcast.104), channel_id=1, source_target_pairs={{0,1},{1,0},{2,3},{3,2},{4,5},{5,4},{6,7},{7,6},{8,9},{9,8},{10,11... | collective-permute-start | bytes 3538952 | tf_op jit(solution)/shard_map/ppermute | solution.py:1014
  144.5 4.1 %collective-permute-start.15 = (bf16[8,96,768]{2,1,0:T(8,128)(2,1)}, bf16[8,96,768]{2,1,0:T(8,128)(2,1)S(1)}, u32[]{:S(2)}, u32[]{:S(2)}) collective-permute-start(bf16[8,96,768]{2,1,0:T(8,128)(2,1)} %collective-permute-done.14.refs_10_), channel_id=1, source_target_pairs={{0,1},{1,0},{2,3},{3,2},{4,5},{5,4},{6,7},{7,6},{8,9},{9,8},{10,11... | collective-permute-start | bytes 3538952 | tf_op jit(solution)/shard_map/ppermute | solution.py:1014
  148.5 23.3 %collective-permute-start.17 = (bf16[2,8,96,768]{3,2,1,0:T(8,128)(2,1)S(1)}, bf16[2,8,96,768]{3,2,1,0:T(8,128)(2,1)S(1)}, u32[]{:S(2)}, u32[]{:S(2)}) collective-permute-start(bf16[2,8,96,768]{3,2,1,0:T(8,128)(2,1)S(1)} %shard_map.329.refs_14_), channel_id=1, source_target_pairs={{0,1},{1,0},{2,3},{3,2},{4,5},{5,4},{6,7},{7,6},{8,9},{9,8},{10,11... | collective-permute-start | bytes 7077896 | tf_op jit(solution)/shard_map/ppermute | solution.py:1014
  166.7 5.0 %collective-permute-start.18 = (bf16[2,8,96,768]{3,2,1,0:T(8,128)(2,1)S(1)}, bf16[2,8,96,768]{3,2,1,0:T(8,128)(2,1)S(1)}, u32[]{:S(2)}, u32[]{:S(2)}) collective-permute-start(bf16[2,8,96,768]{3,2,1,0:T(8,128)(2,1)S(1)} %shard_map.331.refs_9_), channel_id=1, source_target_pairs={{0,1},{1,0},{2,3},{3,2},{4,5},{5,4},{6,7},{7,6},{8,9},{9,8},{10,11... | collective-permute-start | bytes 7077896 | tf_op jit(solution)/shard_map/ppermute | solution.py:1014
  180.2 36.2 %collective-permute-start.21 = (bf16[2,4,96,768]{3,2,1,0:T(8,128)(2,1)S(1)}, bf16[2,4,96,768]{3,2,1,0:T(8,128)(2,1)S(1)}, u32[]{:S(2)}, u32[]{:S(2)}) collective-permute-start(bf16[2,4,96,768]{3,2,1,0:T(8,128)(2,1)S(1)} %get-tuple-element.129), channel_id=1, source_target_pairs={{0,4},{1,5},{2,6},{3,7},{4,0},{5,1},{6,2},{7,3},{8,12},{9,13},{10,... | collective-permute-start | bytes 3538952 | tf_op jit(solution)/shard_map/ppermute | solution.py:1014
  182.8 33.6 %collective-permute-start.23 = (bf16[2,4,96,768]{3,2,1,0:T(8,128)(2,1)S(1)}, bf16[2,4,96,768]{3,2,1,0:T(8,128)(2,1)S(1)}, u32[]{:S(2)}, u32[]{:S(2)}) collective-permute-start(bf16[2,4,96,768]{3,2,1,0:T(8,128)(2,1)S(1)} %get-tuple-element.131), channel_id=1, source_target_pairs={{0,2},{1,3},{2,0},{3,1},{4,6},{5,7},{6,4},{7,5},{8,10},{9,11},{10,... | collective-permute-start | bytes 3538952 | tf_op jit(solution)/shard_map/ppermute | solution.py:1014
  182.8 13.1 %copy-start.26 = (bf16[784,768]{1,0:T(8,128)(2,1)S(1)}, bf16[784,768]{1,0:T(8,128)(2,1)}, u32[]{:S(2)}) copy-start(bf16[784,768]{1,0:T(8,128)(2,1)} %copy-done.25) | copy-start | bytes 3612676
  199.2 19.5 %collective-permute-start.20 = (bf16[2,8,96,384]{3,2,1,0:T(8,128)(2,1)S(1)}, bf16[2,8,96,384]{3,2,1,0:T(8,128)(2,1)S(1)}, u32[]{:S(2)}, u32[]{:S(2)}) collective-permute-start(bf16[2,8,96,384]{3,2,1,0:T(8,128)(2,1)S(1)} %shard_map.336.refs_9_), channel_id=1, source_target_pairs={{0,1},{1,0},{2,3},{3,2},{4,5},{5,4},{6,7},{7,6},{8,9},{9,8},{10,11... | collective-permute-start | bytes 3538952 | tf_op jit(solution)/shard_map/ppermute | solution.py:1014
  215.8 19.9 %collective-permute-start.19 = (bf16[2,8,96,384]{3,2,1,0:T(8,128)(2,1)S(1)}, bf16[2,8,96,384]{3,2,1,0:T(8,128)(2,1)S(1)}, u32[]{:S(2)}, u32[]{:S(2)}) collective-permute-start(bf16[2,8,96,384]{3,2,1,0:T(8,128)(2,1)S(1)} %shard_map.338.refs_6_), channel_id=1, source_target_pairs={{0,1},{1,0},{2,3},{3,2},{4,5},{5,4},{6,7},{7,6},{8,9},{9,8},{10,11... | collective-permute-start | bytes 3538952 | tf_op jit(solution)/shard_map/ppermute | solution.py:1014
  216.5 15.6 %collective-permute-start.22 = (bf16[4,96,768]{2,1,0:T(8,128)(2,1)S(1)}, bf16[4,96,768]{2,1,0:T(8,128)(2,1)S(1)}, u32[]{:S(2)}, u32[]{:S(2)}) collective-permute-start(bf16[4,96,768]{2,1,0:T(8,128)(2,1)S(1)} %fusion.10), channel_id=1, source_target_pairs={{0,2},{1,3},{2,0},{3,1},{4,6},{5,7},{6,4},{7,5},{8,10},{9,11},{10,... | collective-permute-start | bytes 1769480 | tf_op jit(solution)/shard_map/ppermute | solution.py:1014
  218.6 15.0 %collective-permute-start.24 = (bf16[4,96,768]{2,1,0:T(8,128)(2,1)S(1)}, bf16[4,96,768]{2,1,0:T(8,128)(2,1)S(1)}, u32[]{:S(2)}, u32[]{:S(2)}) collective-permute-start(bf16[4,96,768]{2,1,0:T(8,128)(2,1)S(1)} %fusion.6), channel_id=1, source_target_pairs={{0,4},{1,5},{2,6},{3,7},{4,0},{5,1},{6,2},{7,3},{8,12},{9,13},{10,... | collective-permute-start | bytes 1769480 | tf_op jit(solution)/shard_map/ppermute | solution.py:1014
  233.7 27.7 %collective-permute-start.28 = (bf16[2,2,96,768]{3,2,1,0:T(8,128)(2,1)S(1)}, bf16[2,2,96,768]{3,2,1,0:T(8,128)(2,1)S(1)}, u32[]{:S(2)}, u32[]{:S(2)}) collective-permute-start(bf16[2,2,96,768]{3,2,1,0:T(8,128)(2,1)S(1)} %fusion.3), channel_id=1, source_target_pairs={{0,16},{1,17},{2,18},{3,19},{4,20},{5,21},{6,22},{7,23},{8,24},{9,... | collective-permute-start | bytes 1769480 | tf_op jit(solution)/shard_map/ppermute | solution.py:1014
  238.9 26.7 %collective-permute-start.27 = (bf16[2,4,96,768]{3,2,1,0:T(8,128)(2,1)S(1)}, bf16[2,4,96,768]{3,2,1,0:T(8,128)(2,1)S(1)}, u32[]{:S(2)}, u32[]{:S(2)}) collective-permute-start(bf16[2,4,96,768]{3,2,1,0:T(8,128)(2,1)S(1)} %get-tuple-element.144), channel_id=1, source_target_pairs={{0,2},{1,3},{2,0},{3,1},{4,6},{5,7},{6,4},{7,5},{8,10},{9,11},{10,... | collective-permute-start | bytes 3538952 | tf_op jit(solution)/shard_map/ppermute | solution.py:1014
  251.6 9.9 %collective-permute-start.25 = (bf16[8,56,768]{2,1,0:T(8,128)(2,1)S(1)}, bf16[8,56,768]{2,1,0:T(8,128)(2,1)S(1)}, u32[]{:S(2)}, u32[]{:S(2)}) collective-permute-start(bf16[8,56,768]{2,1,0:T(8,128)(2,1)S(1)} %get-tuple-element.141), channel_id=1, source_target_pairs={{0,1},{1,0},{2,3},{3,2},{4,5},{5,4},{6,7},{7,6},{8,9},{9,8},{10,11... | collective-permute-start | bytes 2064392 | tf_op jit(solution)/shard_map/ppermute | solution.py:1014
  251.7 10.6 %collective-permute-start.26 = (bf16[8,56,768]{2,1,0:T(8,128)(2,1)S(1)}, bf16[8,56,768]{2,1,0:T(8,128)(2,1)S(1)}, u32[]{:S(2)}, u32[]{:S(2)}) collective-permute-start(bf16[8,56,768]{2,1,0:T(8,128)(2,1)S(1)} %get-tuple-element.143), channel_id=1, source_target_pairs={{0,1},{1,0},{2,3},{3,2},{4,5},{5,4},{6,7},{7,6},{8,9},{9,8},{10,11... | collective-permute-start | bytes 2064392 | tf_op jit(solution)/shard_map/ppermute | solution.py:1014
  266.7 24.6 %collective-permute-start.29 = (bf16[4,56,768]{2,1,0:T(8,128)(2,1)}, bf16[4,56,768]{2,1,0:T(8,128)(2,1)S(1)}, u32[]{:S(2)}, u32[]{:S(2)}) collective-permute-start(bf16[4,56,768]{2,1,0:T(8,128)(2,1)} %get-tuple-element.146), channel_id=1, source_target_pairs={{0,4},{1,5},{2,6},{3,7},{4,0},{5,1},{6,2},{7,3},{8,12},{9,13},{10,... | collective-permute-start | bytes 1032200 | tf_op jit(solution)/shard_map/ppermute | solution.py:1014
  268.2 23.1 %collective-permute-start.30 = (bf16[4,56,768]{2,1,0:T(8,128)(2,1)}, bf16[4,56,768]{2,1,0:T(8,128)(2,1)}, u32[]{:S(2)}, u32[]{:S(2)}) collective-permute-start(bf16[4,56,768]{2,1,0:T(8,128)(2,1)} %get-tuple-element.147), channel_id=1, source_target_pairs={{0,2},{1,3},{2,0},{3,1},{4,6},{5,7},{6,4},{7,5},{8,10},{9,11},{10,... | collective-permute-start | bytes 1032200 | tf_op jit(solution)/shard_map/ppermute | solution.py:1014
  268.9 22.4 %collective-permute-start.31 = (bf16[4,56,768]{2,1,0:T(8,128)(2,1)}, bf16[4,56,768]{2,1,0:T(8,128)(2,1)}, u32[]{:S(2)}, u32[]{:S(2)}) collective-permute-start(bf16[4,56,768]{2,1,0:T(8,128)(2,1)} %get-tuple-element.148), channel_id=1, source_target_pairs={{0,6},{1,7},{2,4},{3,5},{4,2},{5,3},{6,0},{7,1},{8,14},{9,15},{10,... | collective-permute-start | bytes 1032200 | tf_op jit(solution)/shard_map/ppermute | solution.py:1014
  270.2 64.3 %all-to-all-start.1 = ((bf16[8,96,768]{2,1,0:T(8,128)(2,1)}), bf16[8,96,768]{2,1,0:T(8,128)(2,1)S(1)}, u32[]{:S(2)}, u32[]{:S(2)}) async-start(bf16[8,96,768]{2,1,0:T(8,128)(2,1)} %bitcast.44), calls=%async_computation.1 | async-start | bytes 2359296 | tf_op jit(solution)/shard_map/all_to_all | solution.py:1224
  293.2 6.6 %collective-permute-start.32 = (bf16[56,768]{1,0:T(8,128)(2,1)}, bf16[56,768]{1,0:T(8,128)(2,1)S(1)}, u32[]{:S(2)}, u32[]{:S(2)}) collective-permute-start(bf16[56,768]{1,0:T(8,128)(2,1)} %get-tuple-element.153), channel_id=1, source_target_pairs={{0,8},{1,9},{2,10},{3,11},{4,12},{5,13},{6,14},{7,15},{8,0},{9,1},... | collective-permute-start | bytes 258056 | tf_op jit(solution)/shard_map/ppermute | solution.py:1014
  293.6 13.4 %collective-permute-start.33 = (bf16[56,768]{1,0:T(8,128)(2,1)}, bf16[56,768]{1,0:T(8,128)(2,1)S(1)}, u32[]{:S(2)}, u32[]{:S(2)}) collective-permute-start(bf16[56,768]{1,0:T(8,128)(2,1)} %get-tuple-element.154), channel_id=1, source_target_pairs={{0,16},{1,17},{2,18},{3,19},{4,20},{5,21},{6,22},{7,23},{8,24},{9,... | collective-permute-start | bytes 258056 | tf_op jit(solution)/shard_map/ppermute | solution.py:1014
  295.6 11.4 %collective-permute-start.34 = (bf16[56,768]{1,0:T(8,128)(2,1)}, bf16[56,768]{1,0:T(8,128)(2,1)S(1)}, u32[]{:S(2)}, u32[]{:S(2)}) collective-permute-start(bf16[56,768]{1,0:T(8,128)(2,1)} %get-tuple-element.155), channel_id=1, source_target_pairs={{0,24},{1,25},{2,26},{3,27},{4,28},{5,29},{6,30},{7,31},{8,16},{9,... | collective-permute-start | bytes 258056 | tf_op jit(solution)/shard_map/ppermute | solution.py:1014
  297.6 12.6 %collective-permute-start.35 = (bf16[4,96,768]{2,1,0:T(8,128)(2,1)}, bf16[4,96,768]{2,1,0:T(8,128)(2,1)}, u32[]{:S(2)}, u32[]{:S(2)}) collective-permute-start(bf16[4,96,768]{2,1,0:T(8,128)(2,1)} %get-tuple-element.157), channel_id=1, source_target_pairs={{0,4},{1,5},{2,6},{3,7},{4,0},{5,1},{6,2},{7,3},{8,12},{9,13},{10,... | collective-permute-start | bytes 1769480 | tf_op jit(solution)/shard_map/ppermute | solution.py:1014
  299.8 10.4 %collective-permute-start.36 = (bf16[2,96,768]{2,1,0:T(8,128)(2,1)S(1)}, bf16[2,96,768]{2,1,0:T(8,128)(2,1)S(1)}, u32[]{:S(2)}, u32[]{:S(2)}) collective-permute-start(bf16[2,96,768]{2,1,0:T(8,128)(2,1)S(1)} %slice_bitcast_fusion.2), channel_id=1, source_target_pairs={{0,8},{1,9},{2,10},{3,11},{4,12},{5,13},{6,14},{7,15},{8,0},{9,1},... | collective-permute-start | bytes 884744 | tf_op jit(solution)/shard_map/ppermute | solution.py:1014
  311.4 8.2 %collective-permute-start.39 = (bf16[56,768]{1,0:T(8,128)(2,1)S(1)}, bf16[56,768]{1,0:T(8,128)(2,1)S(1)}, u32[]{:S(2)}, u32[]{:S(2)}) collective-permute-start(bf16[56,768]{1,0:T(8,128)(2,1)S(1)} %add_add_fusion), channel_id=1, source_target_pairs={{0,24},{1,25},{2,26},{3,27},{4,28},{5,29},{6,30},{7,31},{8,16},{9,... | collective-permute-start | bytes 258056 | tf_op jit(solution)/shard_map/ppermute | solution.py:1014
  312.4 12.8 %collective-permute-start.38 = (bf16[56,768]{1,0:T(8,128)(2,1)S(1)}, bf16[56,768]{1,0:T(8,128)(2,1)S(1)}, u32[]{:S(2)}, u32[]{:S(2)}) collective-permute-start(bf16[56,768]{1,0:T(8,128)(2,1)S(1)} %add_add_fusion), channel_id=1, source_target_pairs={{0,16},{1,17},{2,18},{3,19},{4,20},{5,21},{6,22},{7,23},{8,24},{9,... | collective-permute-start | bytes 258056 | tf_op jit(solution)/shard_map/ppermute | solution.py:1014
  312.4 12.8 %collective-permute-start.37 = (bf16[56,768]{1,0:T(8,128)(2,1)S(1)}, bf16[56,768]{1,0:T(8,128)(2,1)S(1)}, u32[]{:S(2)}, u32[]{:S(2)}) collective-permute-start(bf16[56,768]{1,0:T(8,128)(2,1)S(1)} %add_add_fusion), channel_id=1, source_target_pairs={{0,8},{1,9},{2,10},{3,11},{4,12},{5,13},{6,14},{7,15},{8,0},{9,1},... | collective-permute-start | bytes 258056 | tf_op jit(solution)/shard_map/ppermute | solution.py:1014
  315.9 13.4 %collective-permute-start.40 = (bf16[2,96,768]{2,1,0:T(8,128)(2,1)S(1)}, bf16[2,96,768]{2,1,0:T(8,128)(2,1)S(1)}, u32[]{:S(2)}, u32[]{:S(2)}) collective-permute-start(bf16[2,96,768]{2,1,0:T(8,128)(2,1)S(1)} %slice.212), channel_id=1, source_target_pairs={{0,16},{1,17},{2,18},{3,19},{4,20},{5,21},{6,22},{7,23},{8,24},{9,... | collective-permute-start | bytes 884744 | tf_op jit(solution)/shard_map/ppermute | solution.py:1014
  318.8 10.5 %collective-permute-start.41 = (bf16[2,96,768]{2,1,0:T(8,128)(2,1)S(1)}, bf16[2,96,768]{2,1,0:T(8,128)(2,1)S(1)}, u32[]{:S(2)}, u32[]{:S(2)}) collective-permute-start(bf16[2,96,768]{2,1,0:T(8,128)(2,1)S(1)} %bitcast_add_fusion.refs_1_), channel_id=1, source_target_pairs={{0,2},{1,3},{2,0},{3,1},{4,6},{5,7},{6,4},{7,5},{8,10},{9,11},{10,... | collective-permute-start | bytes 884744 | tf_op jit(solution)/shard_map/ppermute | solution.py:1014
  329.3 12.3 %collective-permute-start.44 = (bf16[4,56,768]{2,1,0:T(8,128)(2,1)}, bf16[4,56,768]{2,1,0:T(8,128)(2,1)}, u32[]{:S(2)}, u32[]{:S(2)}) collective-permute-start(bf16[4,56,768]{2,1,0:T(8,128)(2,1)} %pad_maximum_fusion.5), channel_id=1, source_target_pairs={{0,6},{1,7},{2,4},{3,5},{4,2},{5,3},{6,0},{7,1},{8,14},{9,15},{10,... | collective-permute-start | bytes 1032200 | tf_op jit(solution)/shard_map/ppermute | solution.py:1014
  331.3 15.2 %collective-permute-start.43 = (bf16[4,56,768]{2,1,0:T(8,128)(2,1)}, bf16[4,56,768]{2,1,0:T(8,128)(2,1)}, u32[]{:S(2)}, u32[]{:S(2)}) collective-permute-start(bf16[4,56,768]{2,1,0:T(8,128)(2,1)} %pad_maximum_fusion.5), channel_id=1, source_target_pairs={{0,2},{1,3},{2,0},{3,1},{4,6},{5,7},{6,4},{7,5},{8,10},{9,11},{10,... | collective-permute-start | bytes 1032200 | tf_op jit(solution)/shard_map/ppermute | solution.py:1014
  332.5 13.9 %collective-permute-start.42 = (bf16[4,56,768]{2,1,0:T(8,128)(2,1)}, bf16[4,56,768]{2,1,0:T(8,128)(2,1)}, u32[]{:S(2)}, u32[]{:S(2)}) collective-permute-start(bf16[4,56,768]{2,1,0:T(8,128)(2,1)} %pad_maximum_fusion.5), channel_id=1, source_target_pairs={{0,4},{1,5},{2,6},{3,7},{4,0},{5,1},{6,2},{7,3},{8,12},{9,13},{10,... | collective-permute-start | bytes 1032200 | tf_op jit(solution)/shard_map/ppermute | solution.py:1014
  333.6 5.5 %collective-permute-start.45 = (bf16[96,768]{1,0:T(8,128)(2,1)}, bf16[96,768]{1,0:T(8,128)(2,1)}, u32[]{:S(2)}, u32[]{:S(2)}) collective-permute-start(bf16[96,768]{1,0:T(8,128)(2,1)} %slice_bitcast_fusion.7), channel_id=1, source_target_pairs={{0,8},{1,9},{2,10},{3,11},{4,12},{5,13},{6,14},{7,15},{8,0},{9,1},... | collective-permute-start | bytes 442376 | tf_op jit(solution)/shard_map/ppermute | solution.py:1014
  334.5 13.5 %collective-permute-start.46 = (bf16[2,2,96,768]{3,2,1,0:T(8,128)(2,1)}, bf16[2,2,96,768]{3,2,1,0:T(8,128)(2,1)S(1)}, u32[]{:S(2)}, u32[]{:S(2)}) collective-permute-start(bf16[2,2,96,768]{3,2,1,0:T(8,128)(2,1)} %pad_maximum_fusion.4), channel_id=1, source_target_pairs={{0,1},{1,0},{2,3},{3,2},{4,5},{5,4},{6,7},{7,6},{8,9},{9,8},{10,11... | collective-permute-start | bytes 1769480 | tf_op jit(solution)/shard_map/ppermute | solution.py:1014
  348.0 6.3 %collective-permute-start.47 = (bf16[16,56,768]{2,1,0:T(8,128)(2,1)S(1)}, bf16[16,56,768]{2,1,0:T(8,128)(2,1)S(1)}, u32[]{:S(2)}, u32[]{:S(2)}) collective-permute-start(bf16[16,56,768]{2,1,0:T(8,128)(2,1)S(1)} %pad_maximum_fusion.1.refs_1_), channel_id=1, source_target_pairs={{0,1},{1,0},{2,3},{3,2},{4,5},{5,4},{6,7},{7,6},{8,9},{9,8},{10,11... | collective-permute-start | bytes 4128776 | tf_op jit(solution)/shard_map/ppermute | solution.py:1014
  348.1 6.3 %collective-permute-start.48 = (bf16[96,768]{1,0:T(8,128)(2,1)S(1)}, bf16[96,768]{1,0:T(8,128)(2,1)S(1)}, u32[]{:S(2)}, u32[]{:S(2)}) collective-permute-start(bf16[96,768]{1,0:T(8,128)(2,1)S(1)} %bitcast_add_fusion.1.refs_1_), channel_id=1, source_target_pairs={{0,2},{1,3},{2,0},{3,1},{4,6},{5,7},{6,4},{7,5},{8,10},{9,11},{10,... | collective-permute-start | bytes 442376 | tf_op jit(solution)/shard_map/ppermute | solution.py:1014
  354.4 5.4 %collective-permute-start.49 = (bf16[2,96,768]{2,1,0:T(8,128)(2,1)S(1)}, bf16[2,96,768]{2,1,0:T(8,128)(2,1)S(1)}, u32[]{:S(2)}, u32[]{:S(2)}) collective-permute-start(bf16[2,96,768]{2,1,0:T(8,128)(2,1)S(1)} %pad_maximum_fusion.6), channel_id=1, source_target_pairs={{0,1},{1,0},{2,3},{3,2},{4,5},{5,4},{6,7},{7,6},{8,9},{9,8},{10,11... | collective-permute-start | bytes 884744 | tf_op jit(solution)/shard_map/ppermute | solution.py:1014
  (23 other events, 75.6 us)
Sparse Core Ops, SparseCore 0:
  10.8 51.8 all-gather.4
  65.4 51.2 all-gather.6
